TPU v7x, 32 devices: a whole 2x2x4 slice. The times are simulated.
32 devices in a mesh: grp: 4 (over z), dp: 2 (over y), width: 4 (over x, core).
Axes of the slice: x: 2, y: 2, z: 4, core: 2. Of those that a mesh axis runs over, the one named last changes fastest.
Arguments:
- query_out: bfloat16 [512, 8192], P(None, ('grp', 'dp')), may hold values from -0.09375 to 0.09375
- query_in: bfloat16 [512, 14336], P(None, 'width'), may hold values from -0.046875 to 0.046875
- eigen_out: bfloat16 [8192, 8192], P(('grp', 'dp'), 'width'), may hold values from -0.0625 to 0.0625
- eigen_in: bfloat16 [14336, 14336], P('width', ('grp', 'dp')), may hold values from -0.046875 to 0.046875
- eigvals: float32 [8192, 14336], P('width', ('grp', 'dp')), may hold values from 0.001 to 5
- start: bfloat16 [14336, 256], P(('grp', 'dp')), may hold values from -6 to 6
- grads_out: bfloat16 [4096, 8192], P(('grp', 'dp'), 'width'), may hold values from -0.0625 to 0.0625
- gate_pre: bfloat16 [4096, 14336], P(('grp', 'dp'), 'width'), may hold values from -6 to 6
- up_pre: bfloat16 [4096, 14336], P(('grp', 'dp'), 'width'), may hold values from -0.046875 to 0.046875
Outputs:
- scores: float32 [16, 4096], P(None, ('grp', 'dp', 'width'))
- out_factor: bfloat16 [8192, 256], P('width')
- in_factor: bfloat16 [14336, 256], P('width')
All inputs are finite; a program needn't handle non-finite values.
Results may differ from a plain program's by a relative error of at most 0.0095.
Values may be sent and summed in bfloat16 or wider, within the bound.
No kernel may reach another device: no remote copies, remote signals or barrier semaphores. Data moves between devices by JAX's collectives and lax.ppermute only.
A program may use at most 256 MiB of HBM per device.

v0:
```python
import jax
import jax.numpy as jnp
from jax import lax
from jax.sharding import PartitionSpec as P

D = 8192
NQ = 16
QTOK = 32
RANK = 16
ITERS = 2


damping = 0.01
ridge_scale = 1e-06


def local_gram(image_cols):
    return jnp.einsum("dqr,dqs->qrs", image_cols, image_cols, precision=lax.Precision.HIGHEST) / D


def factor_inverse(gram_mat, identity):
    trace_mean = jnp.trace(gram_mat, axis1=1, axis2=2) / RANK
    gram_mat = gram_mat + ridge_scale * trace_mean[:, None, None] * identity[None, :, :]
    lower_factor = jnp.linalg.cholesky(gram_mat)

    def invert_one(single_lower):
        return jax.scipy.linalg.solve_triangular(single_lower, identity, lower=True)

    return jax.vmap(invert_one)(lower_factor)


def per_device(
    query_out, query_in, eigen_out, eigen_in, eigvals, start, grads_out, gate_pre, up_pre
):
    part_out = jnp.dot(query_out, eigen_out, preferred_element_type=jnp.float32)
    part_in = jnp.dot(query_in, eigen_in, preferred_element_type=jnp.float32)
    rot_in = lax.psum(part_in, "width").astype(jnp.bfloat16)
    share_out = lax.psum_scatter(part_out, ("grp", "dp"), scatter_dimension=0, tiled=True).astype(
        jnp.bfloat16
    )
    rot_out = lax.all_gather(share_out, ("grp", "dp"), axis=0, tiled=True)
    rows_out = rot_out.shape[1]
    cols_in = rot_in.shape[1]
    rotated = jnp.einsum(
        "qkd,qkf->qdf",
        rot_out.reshape(NQ, QTOK, rows_out),
        rot_in.reshape(NQ, QTOK, cols_in),
        preferred_element_type=jnp.float32,
    )
    rotated = (rotated / (eigvals + damping)).astype(jnp.bfloat16)
    basis_in = start.reshape(cols_in, NQ, RANK)
    identity = jnp.eye(RANK, dtype=jnp.float32)
    basis_out = None
    for iteration in range(ITERS):
        image_cols = jnp.einsum(
            "qdf,fqr->dqr", rotated, basis_in, preferred_element_type=jnp.float32
        )
        image_cols = lax.psum_scatter(image_cols, ("grp", "dp"), scatter_dimension=0, tiled=True)
        gram_mat = lax.psum(local_gram(image_cols), ("grp", "dp", "width"))
        inverse = factor_inverse(gram_mat, identity)
        basis_out = jnp.einsum(
            "dqr,qsr->dqs", image_cols, inverse, precision=lax.Precision.HIGHEST
        ).astype(jnp.bfloat16)
        basis_out = lax.all_gather(basis_out, ("grp", "dp"), axis=0, tiled=True)
        returned = jnp.einsum(
            "qdf,dqr->fqr", rotated, basis_out, preferred_element_type=jnp.float32
        )
        basis_in = lax.psum(returned, "width").astype(jnp.bfloat16)
    out_cols = basis_out.reshape(rows_out, NQ * RANK)
    in_cols = basis_in.reshape(cols_in, NQ * RANK)
    part_factor_in = jnp.dot(eigen_in, in_cols, preferred_element_type=jnp.float32)
    part_factor_out = jnp.dot(eigen_out, out_cols, preferred_element_type=jnp.float32)
    share_in = lax.psum_scatter(
        part_factor_in, ("grp", "dp"), scatter_dimension=0, tiled=True
    ).astype(jnp.bfloat16)
    in_factor = lax.all_gather(share_in, ("grp", "dp"), axis=0, tiled=True)
    share_factor = lax.psum_scatter(
        part_factor_out, "width", scatter_dimension=0, tiled=True
    ).astype(jnp.bfloat16)
    whole_out = lax.all_gather(share_factor, ("grp", "dp", "width"), axis=0, tiled=True)
    width_rows = grads_out.shape[1]
    out_factor = lax.dynamic_slice_in_dim(
        whole_out, lax.axis_index("width") * width_rows, width_rows, 0
    )
    hidden = (jax.nn.silu(gate_pre.astype(jnp.float32)) * up_pre.astype(jnp.float32)).astype(
        jnp.bfloat16
    )
    proj_out = jnp.dot(grads_out, out_factor, preferred_element_type=jnp.float32)
    proj_in = jnp.dot(hidden, in_factor, preferred_element_type=jnp.float32)
    proj_out, proj_in = (
        lax.psum_scatter(proj_out, "width", scatter_dimension=0, tiled=True),
        lax.psum_scatter(proj_in, "width", scatter_dimension=0, tiled=True),
    )
    scores = (proj_out * proj_in).reshape(proj_out.shape[0], NQ, RANK).sum(axis=2).T
    return (scores, out_factor, in_factor)


def solution(mesh):
    return jax.shard_map(
        per_device,
        mesh=mesh,
        in_specs=(
            P(None, ("grp", "dp")),
            P(None, "width"),
            P(("grp", "dp"), "width"),
            P("width", ("grp", "dp")),
            P("width", ("grp", "dp")),
            P(("grp", "dp"), None),
            P(("grp", "dp"), "width"),
            P(("grp", "dp"), "width"),
            P(("grp", "dp"), "width"),
        ),
        out_specs=(P(None, ("grp", "dp", "width")), P("width", None), P("width", None)),
        check_vma=False,
    )
```

profile of v0, /device:TPU:0, one launch (start us, length us, event | category | flops | bytes accessed | tf_op | source)
XLA Modules:
  0.0 1137.6 jit_solution(18045563970328782984)
XLA Ops:
  7.2 6.9 fusion.20
  14.2 13.5 %fusion.21 = f32[512,1792]{1,0:T(8,128)} fusion(bf16[512,3584]{1,0:T(8,128)(2,1)} %param.13, bf16[3584,1792]{1,0:T(8,128)(2,1)} %param.15), kind=kOutput, calls=%fused_computation.54 | convolution fusion | flops 6576668672 | bytes 20185088 | tf_op jit(solution)/shard_map/dot_general | solution.py:36
  29.1 11.7 %broadcast_add_fusion = f32[2048,1792]{1,0:T(8,128)} fusion(f32[2048,1792]{1,0:T(8,128)} %param.16), kind=kLoop, calls=%fused_computation.7 | loop fusion | flops 3670016 | bytes 29360128 | tf_op jit(solution)/shard_map/add | solution.py:50
  40.8 64.2 %reduce-scatter.10.cloned.1.call-done = f32[64,2048]{1,0:T(8,128)} async-done(((f32[512,2048]{1,0:T(8,128)}), f32[64,2048]{1,0:T(8,128)}) %reduce-scatter.10.cloned.1.call-update) | async-done | bytes 524304 | tf_op jit(solution)/shard_map/reduce_scatter | solution.py:38
  106.8 69.2 %all-reduce.3 = bf16[512,1792]{1,0:T(8,128)(2,1)} all-reduce(f32[512,1792]{1,0:T(8,128)} %fusion.21), channel_id=1, replica_groups=mesh['grp'=4,'dp'=2,'width'=4] {'width'}, use_global_device_ids=true, to_apply=%region_1.0 | all-reduce | flops 917504 | bytes 5505024 | tf_op jit(solution)/shard_map/psum | solution.py:37
  176.0 53.1 %divide_convert_fusion = bf16[16,2048,1792]{2,1,0:T(8,128)(2,1)} fusion(f32[2048,1792]{1,0:T(8,128)} %broadcast_add_fusion, bf16[16,32,2048]{2,1,0:T(8,128)(2,1)} %bitcast.79, bf16[16,32,1792]{2,1,0:T(8,128)(2,1)} %bitcast.75), kind=kOutput, calls=%fused_computation | convolution fusion | flops 3875536896 | bytes 136052736 | tf_op jit(solution)/shard_map/qkd,qkf->qdf/dot_general | solution.py:44
  229.0 42.5 %convolution_bitcast_fusion.4 = f32[2048,16,16]{0,2,1:T(8,128)} fusion(bf16[16,2048,1792]{2,1,0:T(8,128)(2,1)} %divide_convert_fusion, bf16[1792,16,16]{0,2,1:T(8,128)(2,1)S(1)} %bitcast.74), kind=kOutput, calls=%fused_computation.14 | convolution fusion | flops 1879048192 | bytes 120455168 | tf_op jit(solution)/shard_map/qdf,fqr->dqr/dot_general | solution.py:55
  271.9 66.9 %reduce-scatter.12.cloned.1.call-done = f32[256,16,16]{0,2,1:T(8,128)} async-done(((f32[2048,16,16]{0,2,1:T(8,128)}), f32[256,16,16]{0,2,1:T(8,128)}) %reduce-scatter.12.cloned.1.call-update) | async-done | bytes 262160 | tf_op jit(solution)/shard_map/reduce_scatter | solution.py:58
  340.2 40.6 %psum.36 = f32[16,16,16]{1,2,0:T(8,128)S(1)} all-reduce(f32[16,16,16]{1,2,0:T(8,128)S(1)} %convolution_multiply_fusion.1), channel_id=1, replica_groups=mesh['grp'=4,'dp'=2,'width'=4] {'grp','dp','width'}, use_global_device_ids=true, to_apply=%region_3.0 | all-reduce | flops 4096 | bytes 32768 | tf_op jit(solution)/shard_map/psum | solution.py:59
  381.4 23.5 %custom-call.8 = f32[16,16,16]{2,1,0:T(8,128)S(1)} custom-call(f32[16,16,16]{2,1,0:T(8,128)S(1)} %fusion.15), custom_call_target="Cholesky" | custom-call | tf_op jit(solution)/shard_map/jit(cholesky)/cholesky | solution.py:24
  405.1 19.8 %custom-call.9 = f32[16,1,16,16]{2,3,1,0:T(8,128)S(1)} custom-call(f32[16,1,16,16]{3,2,1,0:T(8,128)S(1)} %select_bitcast_fusion.1), custom_call_target="InvertDiagBlocksLowerTriangular" | custom-call | tf_op jit(solution)/shard_map/vmap(jit(_solve_triangular))/triangular_solve | solution.py:27
  427.4 39.0 %all-gather.8.cloned.1.call-done = bf16[2048,16,16]{0,2,1:T(8,128)(2,1)} async-done(((bf16[256,16,16]{0,2,1:T(8,128)(2,1)}), bf16[2048,16,16]{0,2,1:T(8,128)(2,1)}) %all-gather.8.cloned.1.call-update) | async-done | bytes 1048592 | tf_op jit(solution)/shard_map/all_gather | solution.py:64
  466.4 39.7 %convolution_bitcast_fusion.3 = f32[1792,16,16]{0,2,1:T(8,128)} fusion(bf16[2048,16,16]{0,2,1:T(8,128)(2,1)} %all-gather.8.cloned.1.call-done, bf16[16,2048,1792]{2,1,0:T(8,128)(2,1)} %divide_convert_fusion), kind=kOutput, calls=%fused_computation.13 | convolution fusion | flops 1879048192 | bytes 120324096 | tf_op jit(solution)/shard_map/qdf,dqr->fqr/dot_general | solution.py:65
  506.1 36.9 %all-reduce.4 = bf16[1792,16,16]{0,2,1:T(8,128)(2,1)S(1)} all-reduce(f32[1792,16,16]{0,2,1:T(8,128)} %convolution_bitcast_fusion.3), channel_id=1, replica_groups=mesh['grp'=4,'dp'=2,'width'=4] {'width'}, use_global_device_ids=true, to_apply=%region_7.10 | all-reduce | flops 458752 | bytes 2752512 | tf_op jit(solution)/shard_map/psum | solution.py:68
  543.0 42.5 %convolution_bitcast_fusion.2 = f32[2048,16,16]{0,2,1:T(8,128)} fusion(bf16[16,2048,1792]{2,1,0:T(8,128)(2,1)} %divide_convert_fusion, bf16[1792,16,16]{0,2,1:T(8,128)(2,1)S(1)} %all-reduce.4), kind=kOutput, calls=%fused_computation.12 | convolution fusion | flops 1879048192 | bytes 120455168 | tf_op jit(solution)/shard_map/qdf,fqr->dqr/dot_general | solution.py:55
  585.6 67.2 %reduce-scatter.14.cloned.1.call-done = f32[256,16,16]{0,2,1:T(8,128)} async-done(((f32[2048,16,16]{0,2,1:T(8,128)}), f32[256,16,16]{0,2,1:T(8,128)}) %reduce-scatter.14.cloned.1.call-update) | async-done | bytes 262160 | tf_op jit(solution)/shard_map/reduce_scatter | solution.py:58
  654.2 40.7 %psum.38 = f32[16,16,16]{1,2,0:T(8,128)S(1)} all-reduce(f32[16,16,16]{1,2,0:T(8,128)S(1)} %convolution_multiply_fusion), channel_id=1, replica_groups=mesh['grp'=4,'dp'=2,'width'=4] {'grp','dp','width'}, use_global_device_ids=true, to_apply=%region_9.12 | all-reduce | flops 4096 | bytes 32768 | tf_op jit(solution)/shard_map/psum | solution.py:59
  695.3 23.5 %custom-call.10 = f32[16,16,16]{2,1,0:T(8,128)S(1)} custom-call(f32[16,16,16]{2,1,0:T(8,128)S(1)} %fusion.12), custom_call_target="Cholesky" | custom-call | tf_op jit(solution)/shard_map/jit(cholesky)/cholesky | solution.py:24
  719.1 19.8 %custom-call.11 = f32[16,1,16,16]{2,3,1,0:T(8,128)S(1)} custom-call(f32[16,1,16,16]{3,2,1,0:T(8,128)S(1)} %select_bitcast_fusion), custom_call_target="InvertDiagBlocksLowerTriangular" | custom-call | tf_op jit(solution)/shard_map/vmap(jit(_solve_triangular))/triangular_solve | solution.py:27
  741.6 38.8 %all-gather.10.cloned.1.call-done = bf16[2048,16,16]{0,2,1:T(8,128)(2,1)} async-done(((bf16[256,16,16]{0,2,1:T(8,128)(2,1)}), bf16[2048,16,16]{0,2,1:T(8,128)(2,1)}) %all-gather.10.cloned.1.call-update) | async-done | bytes 1048592 | tf_op jit(solution)/shard_map/all_gather | solution.py:64
  780.4 39.8 %convolution_bitcast_fusion.1 = f32[1792,16,16]{0,2,1:T(8,128)} fusion(bf16[2048,16,16]{0,2,1:T(8,128)(2,1)} %all-gather.10.cloned.1.call-done, bf16[16,2048,1792]{2,1,0:T(8,128)(2,1)} %divide_convert_fusion), kind=kOutput, calls=%fused_computation.11 | convolution fusion | flops 1879048192 | bytes 120324096 | tf_op jit(solution)/shard_map/qdf,dqr->fqr/dot_general | solution.py:65
  820.2 4.4 convolution_bitcast_fusion.5
  824.7 40.3 %all-reduce.5 = bf16[1792,16,16]{0,2,1:T(8,128)(2,1)S(1)} all-reduce(f32[1792,16,16]{0,2,1:T(8,128)} %convolution_bitcast_fusion.1), channel_id=1, replica_groups=mesh['grp'=4,'dp'=2,'width'=4] {'width'}, use_global_device_ids=true, to_apply=%region_13.16 | all-reduce | flops 458752 | bytes 2752512 | tf_op jit(solution)/shard_map/psum | solution.py:68
  865.0 10.0 convolution_bitcast_fusion
  875.0 5.1 copy.73
  881.9 78.8 %reduce-scatter.22.cloned.1.call-done = f32[448,256]{1,0:T(8,128)} async-done(((f32[3584,256]{1,0:T(8,128)}), f32[448,256]{1,0:T(8,128)}) %reduce-scatter.22.cloned.1.call-update) | async-done | bytes 458768 | tf_op jit(solution)/shard_map/reduce_scatter | solution.py:73
  962.5 67.9 %all-gather.12.cloned.1.call-done = bf16[8192,256]{0,1:T(8,128)(2,1)} async-done(((bf16[256,256]{0,1:T(8,128)(2,1)}), bf16[8192,256]{0,1:T(8,128)(2,1)}) %all-gather.12.cloned.1.call-update) | async-done | bytes 4194320 | tf_op jit(solution)/shard_map/all_gather | solution.py:80
  1033.6 44.8 %all-gather.14.cloned.1.call-done = bf16[3584,256]{1,0:T(8,128)(2,1)} async-done(((bf16[448,256]{1,0:T(8,128)(2,1)}), bf16[3584,256]{1,0:T(8,128)(2,1)}) %all-gather.14.cloned.1.call-update) | async-done | bytes 1835024 | tf_op jit(solution)/shard_map/all_gather | solution.py:76
  1078.3 7.2 fusion.5
  1086.9 15.3 %reduce-scatter.18.cloned.1.call-done = f32[128,256]{0,1:T(8,128)} async-done(((f32[512,256]{0,1:T(8,128)}), f32[128,256]{0,1:T(8,128)}) %reduce-scatter.18.cloned.1.call-update) | async-done | bytes 131088 | tf_op jit(solution)/shard_map/reduce_scatter | solution.py:91
  1102.1 24.2 %reduce-scatter.20.cloned.1.call-done = f32[128,256]{0,1:T(8,128)} async-done(((f32[512,256]{0,1:T(8,128)}), f32[128,256]{0,1:T(8,128)}) %reduce-scatter.20.cloned.1.call-update) | async-done | bytes 131088 | tf_op jit(solution)/shard_map/reduce_scatter | solution.py:92
  1127.9 2.8 copy.82
  (68 shorter events, 22.8 us)
Async XLA Ops:
  7.2 1024.5 %copy-start = (bf16[512,2048]{1,0:T(8,128)(2,1)S(1)}, bf16[512,2048]{1,0:T(8,128)(2,1)}, u32[]{:S(2)}) copy-start(bf16[512,2048]{1,0:T(8,128)(2,1)} %param.18) | copy-start | bytes 6291460
  7.2 97.8 %reduce-scatter.10.cloned.1.call-start = ((), (), s32[]{:S(2)}) async-start(), calls=%async_computation.7 | async-start | bytes 4718592 | tf_op jit(solution)/shard_map/reduce_scatter | solution.py:38
  14.2 13.6 %copy-start.3 = (bf16[1792,256]{1,0:T(8,128)(2,1)S(1)}, bf16[1792,256]{1,0:T(8,128)(2,1)}, u32[]{:S(2)}) copy-start(bf16[1792,256]{1,0:T(8,128)(2,1)} %param.17) | copy-start | bytes 2752516
  14.2 161.8 %all-gather.6.cloned.1.call-start = ((), (), s32[]{:S(2)}) async-start(), calls=%async_computation.8 | async-start | bytes 2359296 | tf_op jit(solution)/shard_map/all_gather | solution.py:41
  106.7 232.1 %reduce-scatter.12.cloned.1.call-start = ((), (), s32[]{:S(2)}) async-start(), calls=%async_computation.9 | async-start | bytes 2359296 | tf_op jit(solution)/shard_map/reduce_scatter | solution.py:58
  176.0 53.1 %copy-start.1 = (bf16[1792,256]{0,1:T(8,128)(2,1)S(1)}, bf16[1792,256]{0,1:T(8,128)(2,1)}, u32[]{:S(2)}) copy-start(bf16[1792,256]{0,1:T(8,128)(2,1)} %copy.56) | copy-start | bytes 2752516
  271.6 194.8 %all-gather.8.cloned.1.call-start = ((), (), s32[]{:S(2)}) async-start(), calls=%async_computation.10 | async-start | bytes 1179648 | tf_op jit(solution)/shard_map/all_gather | solution.py:64
  427.3 225.4 %reduce-scatter.14.cloned.1.call-start = ((), (), s32[]{:S(2)}) async-start(), calls=%async_computation.11 | async-start | bytes 2359296 | tf_op jit(solution)/shard_map/reduce_scatter | solution.py:58
  585.5 194.8 %all-gather.10.cloned.1.call-start = ((), (), s32[]{:S(2)}) async-start(), calls=%async_computation.12 | async-start | bytes 1179648 | tf_op jit(solution)/shard_map/all_gather | solution.py:64
  741.3 138.9 %reduce-scatter.16.cloned.1.call-start = ((), (), s32[]{:S(2)}) async-start(), calls=%async_computation.13 | async-start | bytes 1310720 | tf_op jit(solution)/shard_map/reduce_scatter | solution.py:77
  780.4 39.8 %copy-start.2 = (bf16[2048,16,16]{0,2,1:T(8,128)(2,1)S(1)}, bf16[2048,16,16]{0,2,1:T(8,128)(2,1)}, u32[]{:S(2)}) copy-start(bf16[2048,16,16]{0,2,1:T(8,128)(2,1)} %all-gather.10.cloned.1.call-done) | copy-start | bytes 3145732
  824.6 136.1 %reduce-scatter.22.cloned.1.call-start = ((), (), s32[]{:S(2)}) async-start(), calls=%async_computation.18 | async-start | bytes 4128768 | tf_op jit(solution)/shard_map/reduce_scatter | solution.py:73
  880.1 150.3 %all-gather.12.cloned.1.call-start = ((), (), s32[]{:S(2)}) async-start(), calls=%async_computation.14 | async-start | bytes 4325376 | tf_op jit(solution)/shard_map/all_gather | solution.py:80
  881.8 196.5 %all-gather.14.cloned.1.call-start = ((), (), s32[]{:S(2)}) async-start(), calls=%async_computation.16 | async-start | bytes 2064384 | tf_op jit(solution)/shard_map/all_gather | solution.py:76
  962.5 139.7 %reduce-scatter.18.cloned.1.call-start = ((), (), s32[]{:S(2)}) async-start(), calls=%async_computation.15 | async-start | bytes 655360 | tf_op jit(solution)/shard_map/reduce_scatter | solution.py:91
  1033.2 93.1 %reduce-scatter.20.cloned.1.call-start = ((), (), s32[]{:S(2)}) async-start(), calls=%async_computation.17 | async-start | bytes 655360 | tf_op jit(solution)/shard_map/reduce_scatter | solution.py:92
Sparse Core Ops, SparseCore 0:
  14.3 90.6 reduce-scatter.9
  107.3 49.0 all-gather.5
  271.7 67.0 reduce-scatter.11
  427.5 38.9 all-gather.7
  585.7 67.0 reduce-scatter.13
  741.4 38.9 all-gather.9
  824.8 27.0 reduce-scatter.15
  880.2 80.4 reduce-scatter.21
  964.2 66.1 all-gather.11
  1033.0 45.3 all-gather.13
  1081.4 20.6 reduce-scatter.17
  1104.6 21.6 reduce-scatter.19
where the time goes:
time: 1140 us
  waiting for transfers between devices  507 us (44%)
  matrix products  269 us (24%)
  blocking collectives  228 us (20%)
  other arithmetic  106 us (9%)
  between operations  14.4 us (1%)
  local copies, waits for them, and re-layouts  12.2 us (1%)
    reduce_scatter x2, waiting for transfers between devices, per_device(): lax.psum_scatter(image_cols, ('grp', 'dp'), scatter_dimension=0, tiled=True)  134 us
    dot_general x2, matrix products, per_device(): jnp.einsum('qdf,fqr->dqr', rotated, basis_in, preferred_element_type=jnp....  85.1 us
    psum x2, blocking collectives, per_device(): gram_mat = lax.psum(local_gram(image_cols), ('grp', 'dp', 'width'))  81.3 us
    dot_general x2, matrix products, per_device(): jnp.einsum('qdf,dqr->fqr', rotated, basis_out, preferred_element_type=jnp...  79.5 us
    reduce_scatter x1, waiting for transfers between devices, per_device(): lax.psum_scatter(part_factor_in, ('grp', 'dp'), scatter_dimension=0, tile...  78.8 us
    all_gather x2, waiting for transfers between devices, per_device(): basis_out = lax.all_gather(basis_out, ('grp', 'dp'), axis=0, tiled=True)  77.9 us
    psum x2, blocking collectives, per_device(): basis_in = lax.psum(returned, 'width').astype(jnp.bfloat16)  77.2 us
    psum x1, blocking collectives, per_device(): rot_in = lax.psum(part_in, 'width').astype(jnp.bfloat16)  69.2 us
  transfers between devices with their start and end apart: 12, of which 10 were waited for; matrix products, arithmetic and copies ran while one was open for 5% of the time, Pallas kernels for 0%

commit v1 on v0

v1 whole, which is shorter than its diff:
```python
import jax
import jax.numpy as jnp
from jax import lax
from jax.experimental import pallas as pl
from jax.experimental.pallas import tpu as pltpu
from jax.sharding import PartitionSpec as P

NQ = 16
QTOK = 32
RANK = 16
ITERS = 2

damping = 0.01
ridge_scale = 1e-06

GD = ("grp", "dp")


def inverse_kernel(gram_ref, out_ref):
    gram = gram_ref[...]
    count = gram.shape[0]
    row = lax.broadcasted_iota(jnp.int32, (count, RANK, RANK), 1)
    col = lax.broadcasted_iota(jnp.int32, (count, RANK, RANK), 2)
    eye = jnp.where(row == col, 1.0, 0.0).astype(jnp.float32)
    trace = jnp.sum(jnp.sum(gram * eye, axis=2, keepdims=True), axis=1, keepdims=True)
    left = gram + ridge_scale * (trace / RANK) * eye
    right = eye
    for step in range(RANK):
        pivot = left[:, step : step + 1, step : step + 1]
        factor = jnp.where(row > step, left[:, :, step : step + 1] / pivot, 0.0)
        right = right - factor * right[:, step : step + 1, :]
        left = left - factor * left[:, step : step + 1, :]
    diagonal = jnp.sum(left * eye, axis=2, keepdims=True)
    out_ref[...] = right * lax.rsqrt(diagonal)


def lower_inverse(gram):
    return pl.pallas_call(
        inverse_kernel, out_shape=jax.ShapeDtypeStruct(gram.shape, jnp.float32)
    )(gram)


def sum_scatter(part, axes, count):
    pieces = lax.all_to_all(part.astype(jnp.bfloat16), axes, 0, 0, tiled=True)
    pieces = pieces.reshape((count, part.shape[0] // count) + part.shape[1:])
    return jnp.sum(pieces.astype(jnp.float32), axis=0)


def gather_rows(piece, axes, count):
    copies = jnp.broadcast_to(piece[None], (count,) + piece.shape)
    whole = lax.all_to_all(copies, axes, 0, 0, tiled=True)
    return whole.reshape((count * piece.shape[0],) + piece.shape[1:])


def sum_width(part, count, kind=jnp.bfloat16):
    step = 1
    total = part
    while step < count:
        sent = total.astype(kind)
        got = lax.ppermute(sent, "width", [(i, i ^ step) for i in range(count)])
        total = sent.astype(jnp.float32) + got.astype(jnp.float32)
        step *= 2
    return total


def sum_width_small(part, count):
    total = part
    for step in range(1, count):
        total = total + lax.ppermute(part, "width", [(i, i ^ step) for i in range(count)])
    return total


def make_per_device(n_gd, n_width):
    def per_device(
        query_out, query_in, eigen_out, eigen_in, eigvals, start, grads_out, gate_pre, up_pre
    ):
        D = eigen_out.shape[0] * n_gd
        part_out = jnp.dot(query_out, eigen_out, preferred_element_type=jnp.float32)
        part_in = jnp.dot(query_in, eigen_in, preferred_element_type=jnp.float32)
        rot_in = sum_width(part_in, n_width).astype(jnp.bfloat16)
        share_out = sum_scatter(part_out, GD, n_gd).astype(jnp.bfloat16)
        rot_out = gather_rows(share_out, GD, n_gd)
        rows_out = rot_out.shape[1]
        cols_in = rot_in.shape[1]
        rotated = jnp.einsum(
            "qkd,qkf->qdf",
            rot_out.reshape(NQ, QTOK, rows_out),
            rot_in.reshape(NQ, QTOK, cols_in),
            preferred_element_type=jnp.float32,
        )
        weight = 1.0 / (eigvals + damping)
        rotated = (rotated * weight).astype(jnp.bfloat16)
        basis_in = start.reshape(cols_in, NQ, RANK)
        basis_out = None
        for iteration in range(ITERS):
            image = jnp.einsum(
                "qdf,fqr->dqr", rotated, basis_in, preferred_element_type=jnp.float32
            ).reshape(rows_out, NQ * RANK)
            image = sum_scatter(image, GD, n_gd).astype(jnp.bfloat16)
            image = gather_rows(image, GD, n_gd).reshape(rows_out, NQ, RANK)
            gram = (
                jnp.einsum("dqr,dqs->qrs", image, image, preferred_element_type=jnp.float32) / D
            )
            inverse = lower_inverse(sum_width_small(gram, n_width))
            basis_out = jnp.einsum(
                "dqr,qsr->dqs",
                image.astype(jnp.float32),
                inverse,
                precision=lax.Precision.HIGHEST,
            ).astype(jnp.bfloat16)
            returned = jnp.einsum(
                "qdf,dqr->fqr", rotated, basis_out, preferred_element_type=jnp.float32
            ).reshape(cols_in, NQ * RANK)
            basis_in = (
                sum_width(returned, n_width).astype(jnp.bfloat16).reshape(cols_in, NQ, RANK)
            )
        out_cols = basis_out.reshape(rows_out, NQ * RANK)
        in_cols = basis_in.reshape(cols_in, NQ * RANK)
        part_factor_out = jnp.dot(eigen_out, out_cols, preferred_element_type=jnp.float32)
        share = sum_scatter(part_factor_out, "width", n_width).astype(jnp.bfloat16)
        piece_rows = share.shape[0]
        gathered = gather_rows(share, GD, n_gd)
        mixed = lax.all_to_all(gathered, "width", 0, 0, tiled=True)
        out_factor = (
            mixed.reshape(n_width, n_gd // n_width, piece_rows, NQ * RANK)
            .transpose(1, 0, 2, 3)
            .reshape(rows_out, NQ * RANK)
        )
        part_factor_in = jnp.dot(eigen_in, in_cols, preferred_element_type=jnp.float32)
        share_in = sum_scatter(part_factor_in, GD, n_gd).astype(jnp.bfloat16)
        in_factor = gather_rows(share_in, GD, n_gd)
        hidden = (jax.nn.silu(gate_pre.astype(jnp.float32)) * up_pre.astype(jnp.float32)).astype(
            jnp.bfloat16
        )
        proj_out = jnp.dot(grads_out, out_factor, preferred_element_type=jnp.float32)
        proj_in = jnp.dot(hidden, in_factor, preferred_element_type=jnp.float32)
        proj_out = sum_scatter(proj_out, "width", n_width)
        proj_in = sum_scatter(proj_in, "width", n_width)
        scores = (proj_out * proj_in).reshape(proj_out.shape[0], NQ, RANK).sum(axis=2).T
        return (scores, out_factor, in_factor)

    return per_device


def solution(mesh):
    n_gd = mesh.shape["grp"] * mesh.shape["dp"]
    n_width = mesh.shape["width"]
    return jax.shard_map(
        make_per_device(n_gd, n_width),
        mesh=mesh,
        in_specs=(
            P(None, GD),
            P(None, "width"),
            P(GD, "width"),
            P("width", GD),
            P("width", GD),
            P(GD, None),
            P(GD, "width"),
            P(GD, "width"),
            P(GD, "width"),
        ),
        out_specs=(P(None, GD + ("width",)), P("width", None), P("width", None)),
        check_vma=False,
    )
```

time: 1140 us -> 710 us (0.62)
  waiting for transfers between devices: 507 us -> 175 us
  other arithmetic: 106 us -> 29.7 us
  blocking collectives: 228 us -> 162 us
  starting transfers between devices: 1.16 us -> 44.2 us
  between operations: 14.4 us -> 1.17 us
    reduce_scatter x7 -> x0, waiting for transfers between devices: 317 us -> none  [the longest x2 134 us: per_device(): lax.psum_scatter(image_cols, ('grp', 'dp'), scatter_dimension=0, tiled=True)]
    psum x5 -> x0, blocking collectives: 228 us -> none  [the longest x2 81.3 us: per_device(): gram_mat = lax.psum(local_gram(image_cols), ('grp', 'dp', 'width'))]
    all_gather x5 -> x0, waiting for transfers between devices: 191 us -> none  [the longest x2 77.9 us: per_device(): basis_out = lax.all_gather(basis_out, ('grp', 'dp'), axis=0, tiled=True)]
    all_to_all x0 -> x5, blocking collectives: none -> 162 us  [the longest x3 105 us: sum_scatter(): pieces = lax.all_to_all(part.astype(jnp.bfloat16), axes, 0, 0, tiled=True)]
    all_to_all x0 -> x8, waiting for transfers between devices: none -> 99.5 us  [the longest x4 46.8 us: sum_scatter(): pieces = lax.all_to_all(part.astype(jnp.bfloat16), axes, 0, 0, tiled=True)]
    another operation x11 -> x0, other arithmetic: 87 us -> none  [the longest x6 47.1 us: factor_inverse(): lower_factor = jnp.linalg.cholesky(gram_mat)]
    ppermute x0 -> x12, waiting for transfers between devices: none -> 75.9 us  [the longest x6 63 us: sum_width(): got = lax.ppermute(sent, 'width', [(i, i ^ step) for i in range(count)])]
    all_to_all x0 -> x8, starting transfers between devices: none -> 34.8 us  [the longest x4 17.6 us: sum_scatter(): pieces = lax.all_to_all(part.astype(jnp.bfloat16), axes, 0, 0, tiled=True)]
  transfers between devices with their start and end apart: 12 -> 20, of which waited for: 10 -> 13; matrix products, arithmetic and copies ran while one was open for 5% -> 10% of each run, Pallas kernels for 0% -> 0%
where the time goes in v1:
time: 710 us; the launch traced here: 704 us
  matrix products  262 us (37%)
  waiting for transfers between devices  175 us (25%)
  blocking collectives  162 us (23%)
  starting transfers between devices  44.2 us (6%)
  other arithmetic  29.7 us (4%)
  local copies, waits for them, and re-layouts  23.1 us (3%)
    all_to_all x3, blocking collectives, sum_scatter(): pieces = lax.all_to_all(part.astype(jnp.bfloat16), axes, 0, 0, tiled=True)  105 us
    dot_general x2, matrix products, per_device(): jnp.einsum('qdf,fqr->dqr', rotated, basis_in, preferred_element_type=jnp....  84 us
    dot_general x2, matrix products, per_device(): jnp.einsum('qdf,dqr->fqr', rotated, basis_out, preferred_element_type=jnp...  78.6 us
    ppermute x6, waiting for transfers between devices, sum_width(): got = lax.ppermute(sent, 'width', [(i, i ^ step) for i in range(count)])  63 us
    all_to_all x2, blocking collectives, gather_rows(): whole = lax.all_to_all(copies, axes, 0, 0, tiled=True)  57.1 us
    dot_general x1, matrix products, per_device(): jnp.einsum('qkd,qkf->qdf', rot_out.reshape(NQ, QTOK, rows_out), rot_in.re...  53 us
    all_to_all x4, waiting for transfers between devices, sum_scatter(): pieces = lax.all_to_all(part.astype(jnp.bfloat16), axes, 0, 0, tiled=True)  46.8 us
    all_to_all x3, waiting for transfers between devices, gather_rows(): whole = lax.all_to_all(copies, axes, 0, 0, tiled=True)  40.1 us
  transfers between devices with their start and end apart: 20, of which 13 were waited for; matrix products, arithmetic and copies ran while one was open for 10% of the time, Pallas kernels for 0%

profile of v1, /device:TPU:0, one launch (start us, length us, event | category | flops | bytes accessed | tf_op | source)
XLA Modules:
  0.0 704.2 jit_solution(4106437497385878658)
XLA Ops:
  0.6 6.3 convolution_convert_fusion.2
  6.9 7.3 %all-to-all-start = ((bf16[8,64,2048]{2,1,0:T(8,128)(2,1)}), bf16[8,64,2048]{2,1,0:T(8,128)(2,1)}, u32[]{:S(2)}, u32[]{:S(2)}) async-start(bf16[8,64,2048]{2,1,0:T(8,128)(2,1)} %bitcast.99), calls=%async_computation | async-start | bytes 4194304 | tf_op jit(solution)/shard_map/all_to_all | solution.py:44
  14.2 13.1 %convolution_convert_fusion.1 = bf16[512,1792]{1,0:T(8,128)(2,1)} fusion(bf16[512,3584]{1,0:T(8,128)(2,1)} %param.10, bf16[3584,1792]{1,0:T(8,128)(2,1)} %param.12), kind=kOutput, calls=%fused_computation.14 | convolution fusion | flops 6577586176 | bytes 18350080 | tf_op jit(solution)/shard_map/dot_general | solution.py:79
  27.3 35.2 %all-to-all-done = bf16[8,64,2048]{2,1,0:T(8,128)(2,1)} async-done(((bf16[8,64,2048]{2,1,0:T(8,128)(2,1)}), bf16[8,64,2048]{2,1,0:T(8,128)(2,1)}, u32[]{:S(2)}, u32[]{:S(2)}) %all-to-all-start) | async-done | bytes 2097184 | tf_op jit(solution)/shard_map/all_to_all | solution.py:44
  66.2 4.9 all-to-all-start.1
  72.4 3.7 add_convert_fusion.1
  77.6 12.3 %add_divide_fusion = f32[2048,1792]{1,0:T(8,128)} fusion(f32[2048,1792]{1,0:T(8,128)} %param.13), kind=kLoop, calls=%fused_computation.1 | loop fusion | flops 7340032 | bytes 29360128 | tf_op jit(solution)/shard_map/div | solution.py:91
  89.9 27.5 %collective-permute-done.1 = bf16[512,1792]{1,0:T(8,128)(2,1)} collective-permute-done((bf16[512,1792]{1,0:T(8,128)(2,1)}, bf16[512,1792]{1,0:T(8,128)(2,1)}, u32[]{:S(2)}, u32[]{:S(2)}) %collective-permute-start.1) | collective-permute-done | bytes 1835040 | tf_op jit(solution)/shard_map/ppermute | solution.py:60
  121.1 53.0 %multiply_convert_fusion = bf16[16,2048,1792]{2,1,0:T(8,128)(2,1)} fusion(f32[2048,1792]{1,0:T(8,128)} %add_divide_fusion, bf16[16,32,2048]{2,1,0:T(8,128)(2,1)} %bitcast.1, bf16[16,32,1792]{2,1,0:T(8,128)(2,1)} %bitcast.87), kind=kOutput, calls=%fused_computation | convolution fusion | flops 3875536896 | bytes 136052736 | tf_op jit(solution)/shard_map/qkd,qkf->qdf/dot_general | solution.py:85
  174.1 42.0 %convolution_convert_fusion.8 = bf16[16,2048,16]{1,2,0:T(8,128)(2,1)S(1)} fusion(bf16[16,2048,1792]{2,1,0:T(8,128)(2,1)} %multiply_convert_fusion, bf16[1792,16,16]{0,2,1:T(8,128)(2,1)} %bitcast.95), kind=kOutput, calls=%fused_computation.21 | convolution fusion | flops 1879572480 | bytes 119406592 | tf_op jit(solution)/shard_map/qdf,fqr->dqr/dot_general | solution.py:96
  216.6 29.3 %all_to_all.91 = bf16[8,256,256]{1,2,0:T(8,128)(2,1)S(1)} all-to-all(bf16[8,256,256]{1,2,0:T(8,128)(2,1)S(1)} %copy.31), channel_id=1, replica_groups=mesh['grp'=4,'dp'=2,'width'=4] {'grp','dp'}, dimensions={0} | all-to-all | bytes 2097152 | tf_op jit(solution)/shard_map/all_to_all | solution.py:44
  246.2 28.2 %all_to_all.92 = bf16[8,256,256]{1,2,0:T(8,128)(2,1)S(1)} all-to-all(bf16[8,256,256]{1,2,0:T(8,128)(2,1)S(1)} %broadcast_in_dim.11), channel_id=1, replica_groups=mesh['grp'=4,'dp'=2,'width'=4] {'grp','dp'}, dimensions={0} | all-to-all | bytes 2097152 | tf_op jit(solution)/shard_map/all_to_all | solution.py:51
  279.9 4.5 collective-permute-done.3
  292.9 39.0 %convolution_convert_fusion.7 = bf16[16,16,1792]{2,1,0:T(8,128)(2,1)S(1)} fusion(bf16[2048,16,16]{0,2,1:T(8,128)(2,1)} %fusion.8, bf16[16,2048,1792]{2,1,0:T(8,128)(2,1)} %multiply_convert_fusion), kind=kOutput, calls=%fused_computation.20 | convolution fusion | flops 1879506944 | bytes 119406592 | tf_op jit(solution)/shard_map/qdf,dqr->fqr/dot_general | solution.py:111
  336.3 21.0 %collective-permute-done.6 = bf16[1792,256]{0,1:T(8,128)(2,1)S(1)} collective-permute-done((bf16[1792,256]{0,1:T(8,128)(2,1)S(1)}, bf16[1792,256]{0,1:T(8,128)(2,1)S(1)}, u32[]{:S(2)}, u32[]{:S(2)}) %collective-permute-start.6) | collective-permute-done | bytes 917536 | tf_op jit(solution)/shard_map/ppermute | solution.py:60
  358.5 42.0 %convolution_convert_fusion.6 = bf16[16,16,2048]{2,1,0:T(8,128)(2,1)S(1)} fusion(bf16[1792,16,16]{0,2,1:T(8,128)(2,1)} %bitcast.98, bf16[16,2048,1792]{2,1,0:T(8,128)(2,1)} %multiply_convert_fusion), kind=kOutput, calls=%fused_computation.19 | convolution fusion | flops 1879572480 | bytes 119406592 | tf_op jit(solution)/shard_map/qdf,fqr->dqr/dot_general | solution.py:96
  401.0 28.8 %all_to_all.93 = bf16[8,256,256]{1,2,0:T(8,128)(2,1)S(1)} all-to-all(bf16[8,256,256]{1,2,0:T(8,128)(2,1)S(1)} %copy.33), channel_id=1, replica_groups=mesh['grp'=4,'dp'=2,'width'=4] {'grp','dp'}, dimensions={0} | all-to-all | bytes 2097152 | tf_op jit(solution)/shard_map/all_to_all | solution.py:44
  430.0 28.9 %all_to_all.94 = bf16[8,256,256]{1,2,0:T(8,128)(2,1)S(1)} all-to-all(bf16[8,256,256]{1,2,0:T(8,128)(2,1)S(1)} %broadcast_in_dim.12), channel_id=1, replica_groups=mesh['grp'=4,'dp'=2,'width'=4] {'grp','dp'}, dimensions={0} | all-to-all | bytes 2097152 | tf_op jit(solution)/shard_map/all_to_all | solution.py:51
  464.4 4.5 collective-permute-done.8
  477.4 39.7 %convolution_convert_fusion.5 = bf16[16,16,1792]{2,1,0:T(8,128)(2,1)} fusion(bf16[16,2048,1792]{2,1,0:T(8,128)(2,1)} %multiply_convert_fusion, bf16[16,16,2048]{2,1,0:T(8,128)(2,1)} %convolution_convert_fusion.3), kind=kOutput, calls=%fused_computation.18 | convolution fusion | flops 1879506944 | bytes 119406592 | tf_op jit(solution)/shard_map/qdf,dqr->fqr/dot_general | solution.py:111
  528.9 5.6 all-to-all-done.6
  537.2 4.2 all-to-all-start.7
  541.5 12.3 %collective-permute-done.11 = bf16[1792,256]{0,1:T(8,128)(2,1)} collective-permute-done((bf16[1792,256]{0,1:T(8,128)(2,1)S(1)}, bf16[1792,256]{0,1:T(8,128)(2,1)}, u32[]{:S(2)}, u32[]{:S(2)}) %collective-permute-start.11) | collective-permute-done | bytes 917536 | tf_op jit(solution)/shard_map/ppermute | solution.py:60
  553.7 9.7 %fusion.5 = bf16[3584,256]{0,1:T(8,128)(2,1)} fusion(bf16[3584,1792]{1,0:T(8,128)(2,1)} %param.12, bf16[1792,256]{0,1:T(8,128)(2,1)} %collective-permute-done.11, bf16[1792,256]{0,1:T(8,128)(2,1)S(1)} %add_convert_fusion.3), kind=kOutput, calls=%fused_computation.10 | convolution fusion | flops 3291086848 | bytes 16515072 | tf_op jit(solution)/shard_map/dot_general | solution.py:129
  563.4 3.8 copy.40
  567.2 47.0 %all_to_all.95 = bf16[8,448,256]{2,1,0:T(8,128)(2,1)} all-to-all(bf16[8,448,256]{2,1,0:T(8,128)(2,1)} %bitcast.88), channel_id=1, replica_groups=mesh['grp'=4,'dp'=2,'width'=4] {'grp','dp'}, dimensions={0} | all-to-all | bytes 3670016 | tf_op jit(solution)/shard_map/all_to_all | solution.py:44
  614.2 3.8 all-to-all-start.8
  619.8 12.6 %all-to-all-done.8 = bf16[4,512,256]{2,1,0:T(8,128)(2,1)S(1)} async-done(((bf16[4,512,256]{2,1,0:T(8,128)(2,1)}), bf16[4,512,256]{2,1,0:T(8,128)(2,1)S(1)}, u32[]{:S(2)}, u32[]{:S(2)}) %all-to-all-start.8) | async-done | bytes 1048608 | tf_op jit(solution)/shard_map/all_to_all | solution.py:123
  633.8 4.3 all-to-all-start.11
  640.7 40.1 %all-to-all-done.11 = bf16[8,448,256]{2,1,0:T(8,128)(2,1)} async-done(((bf16[8,448,256]{2,1,0:T(8,128)(2,1)}), bf16[8,448,256]{2,1,0:T(8,128)(2,1)}, u32[]{:S(2)}, u32[]{:S(2)}) %all-to-all-start.11) | async-done | bytes 1835040 | tf_op jit(solution)/shard_map/all_to_all | solution.py:51
  684.2 6.7 fusion.9
  694.4 6.0 all-to-all-done.12
  (75 shorter events, 75.9 us)
Async XLA Ops:
  0.6 638.5 %copy-start = (bf16[512,2048]{1,0:T(8,128)(2,1)S(1)}, bf16[512,2048]{1,0:T(8,128)(2,1)}, u32[]{:S(2)}) copy-start(bf16[512,2048]{1,0:T(8,128)(2,1)} %param.15) | copy-start | bytes 6291460
  6.9 55.6 %all-to-all-start = ((bf16[8,64,2048]{2,1,0:T(8,128)(2,1)}), bf16[8,64,2048]{2,1,0:T(8,128)(2,1)}, u32[]{:S(2)}, u32[]{:S(2)}) async-start(bf16[8,64,2048]{2,1,0:T(8,128)(2,1)} %bitcast.99), calls=%async_computation | async-start | bytes 4194304 | tf_op jit(solution)/shard_map/all_to_all | solution.py:44
  27.3 45.1 %collective-permute-start = (bf16[512,1792]{1,0:T(8,128)(2,1)}, bf16[512,1792]{1,0:T(8,128)(2,1)}, u32[]{:S(2)}, u32[]{:S(2)}) collective-permute-start(bf16[512,1792]{1,0:T(8,128)(2,1)} %convolution_convert_fusion.1), channel_id=1, source_target_pairs={{0,1},{1,0},{2,3},{3,2},{4,5},{5,4},{6,7},{7,6},{8,9},{9,8},{10,11... | collective-permute-start | bytes 5505032 | tf_op jit(solution)/shard_map/ppermute | solution.py:60
  64.5 6.5 copy-start.3
  66.2 55.0 %all-to-all-start.1 = ((bf16[8,64,2048]{2,1,0:T(8,128)(2,1)}), bf16[8,64,2048]{2,1,0:T(8,128)(2,1)}, u32[]{:S(2)}, u32[]{:S(2)}) async-start(bf16[8,64,2048]{2,1,0:T(8,128)(2,1)} %broadcast_in_dim.10), calls=%async_computation.1 | async-start | bytes 4194304 | tf_op jit(solution)/shard_map/all_to_all | solution.py:51
  76.1 41.3 %collective-permute-start.1 = (bf16[512,1792]{1,0:T(8,128)(2,1)}, bf16[512,1792]{1,0:T(8,128)(2,1)}, u32[]{:S(2)}, u32[]{:S(2)}) collective-permute-start(bf16[512,1792]{1,0:T(8,128)(2,1)} %add_convert_fusion.1), channel_id=1, source_target_pairs={{0,2},{1,3},{2,0},{3,1},{4,6},{5,7},{6,4},{7,5},{8,10},{9,11},{10,... | collective-permute-start | bytes 5505032 | tf_op jit(solution)/shard_map/ppermute | solution.py:60
  278.0 1.9 collective-permute-start.2
  278.0 6.4 collective-permute-start.3
  279.6 6.7 collective-permute-start.4
  331.9 2.5 collective-permute-start.5
  334.7 22.6 %collective-permute-start.6 = (bf16[1792,256]{0,1:T(8,128)(2,1)S(1)}, bf16[1792,256]{0,1:T(8,128)(2,1)S(1)}, u32[]{:S(2)}, u32[]{:S(2)}) collective-permute-start(bf16[1792,256]{0,1:T(8,128)(2,1)S(1)} %add_convert_fusion.5), channel_id=1, source_target_pairs={{0,2},{1,3},{2,0},{3,1},{4,6},{5,7},{6,4},{7,5},{8,10},{9,11},{10,... | collective-permute-start | bytes 2752520 | tf_op jit(solution)/shard_map/ppermute | solution.py:60
  462.5 1.9 collective-permute-start.7
  462.5 6.4 collective-permute-start.8
  464.1 6.7 collective-permute-start.9
  477.4 39.9 %copy-start.1 = (bf16[16,16,2048]{2,1,0:T(8,128)(2,1)S(1)}, bf16[16,16,2048]{2,1,0:T(8,128)(2,1)}, u32[]{:S(2)}) copy-start(bf16[16,16,2048]{2,1,0:T(8,128)(2,1)} %convolution_convert_fusion.3) | copy-start | bytes 3145732
  517.1 8.0 %collective-permute-start.10 = (bf16[1792,256]{0,1:T(8,128)(2,1)}, bf16[1792,256]{0,1:T(8,128)(2,1)}, u32[]{:S(2)}, u32[]{:S(2)}) collective-permute-start(bf16[1792,256]{0,1:T(8,128)(2,1)} %bitcast.96), channel_id=1, source_target_pairs={{0,1},{1,0},{2,3},{3,2},{4,5},{5,4},{6,7},{7,6},{8,9},{9,8},{10,11... | collective-permute-start | bytes 2752520 | tf_op jit(solution)/shard_map/ppermute | solution.py:60
  521.7 12.8 %all-to-all-start.6 = ((bf16[4,256,256]{1,2,0:T(8,128)(2,1)}), bf16[4,256,256]{1,2,0:T(8,128)(2,1)S(1)}, u32[]{:S(2)}, u32[]{:S(2)}) async-start(bf16[4,256,256]{1,2,0:T(8,128)(2,1)} %bitcast.85), calls=%async_computation.6 | async-start | bytes 1048576 | tf_op jit(solution)/shard_map/all_to_all | solution.py:44
  526.8 26.9 %collective-permute-start.11 = (bf16[1792,256]{0,1:T(8,128)(2,1)S(1)}, bf16[1792,256]{0,1:T(8,128)(2,1)}, u32[]{:S(2)}, u32[]{:S(2)}) collective-permute-start(bf16[1792,256]{0,1:T(8,128)(2,1)S(1)} %add_convert_fusion.3), channel_id=1, source_target_pairs={{0,2},{1,3},{2,0},{3,1},{4,6},{5,7},{6,4},{7,5},{8,10},{9,11},{10,... | collective-permute-start | bytes 2752520 | tf_op jit(solution)/shard_map/ppermute | solution.py:60
  537.2 30.0 %all-to-all-start.7 = ((bf16[8,256,256]{2,1,0:T(8,128)(2,1)}), bf16[8,256,256]{2,1,0:T(8,128)(2,1)}, u32[]{:S(2)}, u32[]{:S(2)}) async-start(bf16[8,256,256]{2,1,0:T(8,128)(2,1)} %broadcast_in_dim.13), calls=%async_computation.7 | async-start | bytes 2097152 | tf_op jit(solution)/shard_map/all_to_all | solution.py:51
  614.2 18.2 %all-to-all-start.8 = ((bf16[4,512,256]{2,1,0:T(8,128)(2,1)}), bf16[4,512,256]{2,1,0:T(8,128)(2,1)S(1)}, u32[]{:S(2)}, u32[]{:S(2)}) async-start(bf16[4,512,256]{2,1,0:T(8,128)(2,1)} %bitcast.14), calls=%async_computation.8 | async-start | bytes 2097152 | tf_op jit(solution)/shard_map/all_to_all | solution.py:123
  633.8 47.0 %all-to-all-start.11 = ((bf16[8,448,256]{2,1,0:T(8,128)(2,1)}), bf16[8,448,256]{2,1,0:T(8,128)(2,1)}, u32[]{:S(2)}, u32[]{:S(2)}) async-start(bf16[8,448,256]{2,1,0:T(8,128)(2,1)} %broadcast_in_dim.14), calls=%async_computation.11 | async-start | bytes 3670016 | tf_op jit(solution)/shard_map/all_to_all | solution.py:51
  638.2 1.0 copy-start.2
  680.8 10.1 %all-to-all-start.9 = ((bf16[4,128,256]{1,2,0:T(8,128)(2,1)}), bf16[4,128,256]{1,2,0:T(8,128)(2,1)S(1)}, u32[]{:S(2)}, u32[]{:S(2)}) async-start(bf16[4,128,256]{1,2,0:T(8,128)(2,1)} %bitcast.86), calls=%async_computation.9 | async-start | bytes 524288 | tf_op jit(solution)/shard_map/all_to_all | solution.py:44
  690.9 9.4 %all-to-all-start.12 = ((bf16[4,128,256]{2,1,0:T(8,128)(2,1)}), bf16[4,128,256]{2,1,0:T(8,128)(2,1)S(1)}, u32[]{:S(2)}, u32[]{:S(2)}) async-start(bf16[4,128,256]{2,1,0:T(8,128)(2,1)} %bitcast.25), calls=%async_computation.12 | async-start | bytes 524288 | tf_op jit(solution)/shard_map/all_to_all | solution.py:44

commit v2 on v1

v2 whole, which is shorter than its diff:
```python
import functools

import jax
import jax.numpy as jnp
from jax import lax
from jax.experimental import pallas as pl
from jax.experimental.pallas import tpu as pltpu
from jax.sharding import PartitionSpec as P

NQ = 16
QTOK = 32
RANK = 16
ITERS = 2
GROUPS = 2
NG = NQ // GROUPS
COLS = NG * RANK
LANES = 256

damping = 0.01
ridge_scale = 1e-06

GD = ("grp", "dp")
f32 = jnp.float32
bf16 = jnp.bfloat16
VMEM_LIMIT = 56 * 1024 * 1024


def params():
    return pltpu.CompilerParams(vmem_limit_bytes=VMEM_LIMIT)


def chunks(extent):
    return [(at, min(LANES, extent - at)) for at in range(0, extent, LANES)]


def lane_mask(rows, query):
    lane = lax.broadcasted_iota(jnp.int32, (rows, COLS), 1)
    return (lane >= query * RANK) & (lane < (query + 1) * RANK)


def image_block(rotated_ref, basis, query, image):
    product = jnp.dot(rotated_ref[query], basis, preferred_element_type=f32)
    return jnp.where(lane_mask(image.shape[0], query), product, image)


def form_kernel(place_ref, out_ref, in_ref, eig_ref, basis_ref, rotated_ref, image_ref, weight):
    rows, cols = eig_ref.shape
    weight[...] = 1.0 / (eig_ref[...] + damping)
    image = jnp.zeros((rows, COLS), f32)
    basis = basis_ref[...]
    for query in range(NG):
        left = out_ref[:, query * QTOK : (query + 1) * QTOK]
        for at, width in chunks(cols):
            right = in_ref[query * QTOK : (query + 1) * QTOK, at : at + width]
            block = jnp.dot(left, right, preferred_element_type=f32)
            rotated_ref[query, :, at : at + width] = (
                block * weight[:, at : at + width]
            ).astype(bf16)
        image = image_block(rotated_ref, basis, query, image)
    image_ref[...] = image.astype(image_ref.dtype)


def form_piece(place, out_piece, rot_in, eigvals, basis, piece, n_grp, n_dp, kind):
    rows = out_piece.shape[0]
    sub = rows // n_grp
    cols = rot_in.shape[1]

    def eig_block(j, place_ref):
        piece_at = lax.rem(place_ref[1] + piece + 1, n_dp)
        return piece_at * n_grp + lax.rem(place_ref[0] + j + 1, n_grp), 0

    return pl.pallas_call(
        form_kernel,
        grid_spec=pltpu.PrefetchScalarGridSpec(
            num_scalar_prefetch=1,
            grid=(n_grp,),
            in_specs=[
                pl.BlockSpec((sub, NG * QTOK), lambda j, _: (j, 0)),
                pl.BlockSpec((NG * QTOK, cols), lambda j, _: (0, 0)),
                pl.BlockSpec((sub, cols), eig_block),
                pl.BlockSpec((cols, COLS), lambda j, _: (0, 0)),
            ],
            out_specs=[
                pl.BlockSpec((NG, sub, cols), lambda j, _: (0, j, 0)),
                pl.BlockSpec((sub, COLS), lambda j, _: (j, 0)),
            ],
            scratch_shapes=[pltpu.VMEM((sub, cols), f32)],
        ),
        out_shape=[
            jax.ShapeDtypeStruct((NG, rows, cols), bf16),
            jax.ShapeDtypeStruct((rows, COLS), kind),
        ],
        compiler_params=params(),
        cost_estimate=pl.CostEstimate(
            flops=2 * NG * rows * cols * 512, bytes_accessed=NG * rows * cols * 2, transcendentals=0
        ),
        name="form",
    )(place, out_piece, rot_in, eigvals, basis)


def image_kernel(basis_ref, rotated_ref, image_ref):
    image = jnp.zeros((rotated_ref.shape[1], COLS), f32)
    basis = basis_ref[...]
    for query in range(NG):
        image = image_block(rotated_ref, basis, query, image)
    image_ref[...] = image.astype(image_ref.dtype)


def image_piece(basis, rotated, n_grp, kind):
    _, rows, cols = rotated.shape
    sub = rows // n_grp
    return pl.pallas_call(
        image_kernel,
        grid=(n_grp,),
        in_specs=[
            pl.BlockSpec((cols, COLS), lambda j: (0, 0)),
            pl.BlockSpec((NG, sub, cols), lambda j: (0, j, 0)),
        ],
        out_specs=pl.BlockSpec((sub, COLS), lambda j: (j, 0)),
        out_shape=jax.ShapeDtypeStruct((rows, COLS), kind),
        compiler_params=params(),
        cost_estimate=pl.CostEstimate(
            flops=2 * NG * rows * cols * 256, bytes_accessed=NG * rows * cols * 2, transcendentals=0
        ),
        name="image",
    )(basis, rotated)


def return_kernel(first, basis_ref, rotated_ref, *refs):
    total_ref = refs[-1]

    @pl.when(pl.program_id(0) == 0)
    def _():
        total_ref[...] = jnp.zeros_like(total_ref) if first else refs[0][...]

    for query in range(NG):
        rows = slice(query * RANK, (query + 1) * RANK)
        total_ref[rows, :] += jnp.dot(
            basis_ref[0, rows, :], rotated_ref[query], preferred_element_type=f32
        )


def return_piece(basis, rotated, piece, n_grp, total):
    _, rows, cols = rotated.shape
    sub = rows // n_grp
    first = total is None
    whole = pl.BlockSpec((COLS, cols), lambda j: (0, 0))
    return pl.pallas_call(
        functools.partial(return_kernel, first),
        grid=(n_grp,),
        in_specs=[
            pl.BlockSpec((1, COLS, sub), lambda j: (piece * n_grp + j, 0, 0)),
            pl.BlockSpec((NG, sub, cols), lambda j: (0, j, 0)),
        ]
        + ([] if first else [whole]),
        out_specs=whole,
        out_shape=jax.ShapeDtypeStruct((COLS, cols), f32),
        compiler_params=params(),
        cost_estimate=pl.CostEstimate(
            flops=2 * NG * rows * cols * 256, bytes_accessed=NG * rows * cols * 2, transcendentals=0
        ),
        name="returned",
    )(basis, rotated, *([] if first else [total]))


def roll_kernel(place_ref, part_ref, out_ref):
    out_ref[...] = part_ref[...].astype(out_ref.dtype)


def roll_piece(place, part, piece, n_grp, n_dp, kind):
    rows, cols = part.shape
    sub = rows // (n_grp * n_dp)

    def block(j, place_ref):
        piece_at = lax.rem(place_ref[1] + piece + 1, n_dp)
        return piece_at * n_grp + lax.rem(place_ref[0] + j + 1, n_grp), 0

    return pl.pallas_call(
        roll_kernel,
        grid_spec=pltpu.PrefetchScalarGridSpec(
            num_scalar_prefetch=1,
            grid=(n_grp,),
            in_specs=[pl.BlockSpec((sub, cols), block)],
            out_specs=pl.BlockSpec((sub, cols), lambda j, _: (j, 0)),
        ),
        out_shape=jax.ShapeDtypeStruct((rows // n_dp, cols), kind),
        name="roll",
    )(place, part)


def first_sum_kernel(n_grp, keep_ref, *refs):
    arrived, outs = refs[: -n_grp], refs[-n_grp:]
    sub = keep_ref.shape[0] // n_grp
    for j in range(n_grp):
        rows = slice(j * sub, (j + 1) * sub)
        total = keep_ref[rows, :]
        for ref in arrived:
            total = total + ref[rows, :].astype(f32)
        outs[j][...] = total.astype(outs[j].dtype)


def first_sum(keep, arrived, n_grp):
    rows, cols = keep.shape
    sub = rows // n_grp
    shapes = [jax.ShapeDtypeStruct((sub, cols), bf16) for _ in range(n_grp - 1)]
    return pl.pallas_call(
        functools.partial(first_sum_kernel, n_grp),
        out_shape=shapes + [jax.ShapeDtypeStruct((sub, cols), f32)],
        compiler_params=params(),
        name="first_sum",
    )(keep, *arrived)


def second_sum_kernel(keep_ref, *refs):
    total = keep_ref[...]
    for ref in refs[:-1]:
        total = total + ref[...].astype(f32)
    refs[-1][...] = total.astype(bf16)


def second_sum(keep, arrived):
    return pl.pallas_call(
        second_sum_kernel,
        out_shape=jax.ShapeDtypeStruct(keep.shape, bf16),
        compiler_params=params(),
        name="second_sum",
    )(keep, *arrived)


def reduce_gather(sends, keep, n_grp, n_dp):
    arrived = [
        lax.ppermute(send, "dp", [(i, (i + step + 1) % n_dp) for i in range(n_dp)])
        for step, send in enumerate(sends)
    ]
    *quarters, own = first_sum(keep, arrived, n_grp)
    arrived = [
        lax.ppermute(quarter, "grp", [(i, (i + step + 1) % n_grp) for i in range(n_grp)])
        for step, quarter in enumerate(quarters)
    ]
    block = second_sum(own, arrived)
    blocks = []
    for piece in range(n_dp):
        for j in range(n_grp):
            far_dp, far_grp = n_dp - 1 - piece, n_grp - 1 - j
            if far_dp == 0 and far_grp == 0:
                blocks.append(block)
                continue
            pairs = [
                (g * n_dp + d, ((g + far_grp) % n_grp) * n_dp + (d + far_dp) % n_dp)
                for g in range(n_grp)
                for d in range(n_dp)
            ]
            blocks.append(lax.ppermute(block, GD, pairs))
    return blocks


def gram_kernel(scale, *refs):
    out_ref = refs[-1]
    gram = jnp.zeros((COLS, COLS), f32)
    for ref in refs[:-1]:
        block = ref[...]
        gram = gram + lax.dot_general(
            block, block, (((0,), (0,)), ((), ())), preferred_element_type=f32
        )
    gram = jnp.where(same_query(), gram * scale, 0.0)
    compact = gram[:RANK]
    for query in range(1, NG):
        compact = compact + gram[query * RANK : (query + 1) * RANK]
    out_ref[...] = compact


def same_query():
    row = lax.broadcasted_iota(jnp.int32, (COLS, COLS), 0)
    col = lax.broadcasted_iota(jnp.int32, (COLS, COLS), 1)
    return row // RANK == col // RANK


def local_gram(blocks, scale):
    return pl.pallas_call(
        functools.partial(gram_kernel, scale),
        out_shape=jax.ShapeDtypeStruct((RANK, COLS), f32),
        compiler_params=params(),
        name="gram",
    )(*blocks)


def lower_inverse(compact):
    row = lax.broadcasted_iota(jnp.int32, (COLS, COLS), 0)
    col = lax.broadcasted_iota(jnp.int32, (COLS, COLS), 1)
    same = row // RANK == col // RANK
    eye = row == col
    gram = jnp.where(same, jnp.concatenate([compact] * NG, axis=0), 0.0)
    shape = (NG, RANK, COLS)
    gram = gram.reshape(shape)
    eye = eye.reshape(shape)
    row = lax.broadcasted_iota(jnp.int32, shape, 1)
    col = lax.broadcasted_iota(jnp.int32, shape, 2) % RANK
    trace = jnp.sum(
        jnp.sum(jnp.where(eye, gram, 0.0), axis=2, keepdims=True), axis=1, keepdims=True
    )
    left = gram + jnp.where(eye, ridge_scale * (trace / RANK), 0.0)
    right = jnp.where(eye, 1.0, 0.0)
    for step in range(RANK):
        column = jnp.sum(jnp.where(col == step, left, 0.0), axis=2, keepdims=True)
        pivot = column[:, step : step + 1, :]
        factor = jnp.where(row[:, :, :1] > step, column / pivot, 0.0)
        right = right - factor * right[:, step : step + 1, :]
        left = left - factor * left[:, step : step + 1, :]
    diagonal = jnp.sum(jnp.where(eye, left, 0.0), axis=2, keepdims=True)
    return (right * lax.rsqrt(diagonal)).reshape(COLS, COLS)


def basis_kernel(n_gram, *refs):
    grams, blocks, out_ref = refs[:n_gram], refs[n_gram:-1], refs[-1]
    compact = grams[0][...]
    for ref in grams[1:]:
        compact = compact + ref[...]
    inverse = lower_inverse(compact)
    for at, ref in enumerate(blocks):
        out_ref[at] = lax.dot_general(
            inverse,
            ref[...].astype(f32),
            (((1,), (1,)), ((), ())),
            precision=lax.Precision.HIGHEST,
            preferred_element_type=f32,
        ).astype(bf16)


def orthonormal(grams, blocks):
    sub = blocks[0].shape[0]
    return pl.pallas_call(
        functools.partial(basis_kernel, len(grams)),
        out_shape=jax.ShapeDtypeStruct((len(blocks), COLS, sub), bf16),
        compiler_params=params(),
        name="orthonormal",
    )(*grams, *blocks)


def sum_width(part, count):
    total = part + lax.ppermute(part, "width", [(i, i ^ 1) for i in range(count)])
    step = 2
    while step < count:
        sent = total.astype(bf16)
        got = lax.ppermute(sent, "width", [(i, i ^ step) for i in range(count)])
        total = total + got.astype(f32)
        step *= 2
    return total


def sum_scatter(part, axes, count):
    pieces = lax.all_to_all(part.astype(bf16), axes, 0, 0, tiled=True)
    pieces = pieces.reshape((count, part.shape[0] // count) + part.shape[1:])
    return jnp.sum(pieces.astype(f32), axis=0)


def gather_rows(piece, axes, count):
    copies = jnp.broadcast_to(piece[None], (count,) + piece.shape)
    whole = lax.all_to_all(copies, axes, 0, 0, tiled=True)
    return whole.reshape((count * piece.shape[0],) + piece.shape[1:])


def unroll_blocks(place, blocks, n_grp, n_dp):
    sub = blocks.shape[2]
    grid = blocks.reshape(n_dp, n_grp, COLS, sub)
    grid = jnp.roll(grid, place[1] + 1, axis=0)
    grid = jnp.roll(grid, place[0] + 1, axis=1)
    return grid.reshape(n_dp * n_grp, COLS, sub).transpose(1, 0, 2).reshape(COLS, -1)


def make_per_device(n_grp, n_dp, n_width):
    n_gd = n_grp * n_dp

    def per_device(
        query_out, query_in, eigen_out, eigen_in, eigvals, start, grads_out, gate_pre, up_pre
    ):
        place = jnp.stack([lax.axis_index("grp"), lax.axis_index("dp")]).astype(jnp.int32)
        scale = 1.0 / (eigen_out.shape[0] * n_gd)
        rows_out = eigvals.shape[0]
        kinds = [bf16] * (n_dp - 1) + [f32]
        finals, out_cols = [], []
        for group in range(GROUPS):
            span = slice(group * NG * QTOK, (group + 1) * NG * QTOK)
            part_out = lax.dot_general(
                eigen_out, query_out[span], (((0,), (1,)), ((), ())), preferred_element_type=f32
            )
            pieces = [
                roll_piece(place, part_out, piece, n_grp, n_dp, kind)
                for piece, kind in enumerate(kinds)
            ]
            rot_out = reduce_gather(pieces[:-1], pieces[-1], n_grp, n_dp)
            part_in = jnp.dot(query_in[span], eigen_in, preferred_element_type=f32)
            rot_in = sum_width(part_in, n_width).astype(bf16)
            basis = start[:, group * COLS : (group + 1) * COLS]
            rotated = []
            for iteration in range(ITERS):
                images = []
                for piece, kind in enumerate(kinds):
                    if iteration == 0:
                        out_piece = jnp.concatenate(
                            rot_out[piece * n_grp : (piece + 1) * n_grp], axis=0
                        )
                        block, image = form_piece(
                            place, out_piece, rot_in, eigvals, basis, piece, n_grp, n_dp, kind
                        )
                        rotated.append(block)
                    else:
                        image = image_piece(basis, rotated[piece], n_grp, kind)
                    images.append(image)
                blocks = reduce_gather(images[:-1], images[-1], n_grp, n_dp)
                gram = local_gram(blocks, scale)
                grams = [gram] + [
                    lax.ppermute(gram, "width", [(i, i ^ step) for i in range(n_width)])
                    for step in range(1, n_width)
                ]
                basis_out = orthonormal(grams, blocks)
                total = None
                for piece in range(n_dp):
                    total = return_piece(basis_out, rotated[piece], piece, n_grp, total)
                basis = sum_width(total, n_width).astype(bf16).T
            finals.append(basis)
            out_cols.append(unroll_blocks(place, basis_out, n_grp, n_dp))
        out_cols = jnp.concatenate(out_cols, axis=0)
        part_factor_out = lax.dot_general(
            eigen_out, out_cols, (((1,), (1,)), ((), ())), preferred_element_type=f32
        )
        share = sum_scatter(part_factor_out, "width", n_width).astype(bf16)
        piece_rows = share.shape[0]
        gathered = gather_rows(share, GD, n_gd)
        mixed = lax.all_to_all(gathered, "width", 0, 0, tiled=True)
        out_factor = (
            mixed.reshape(n_width, n_gd // n_width, piece_rows, NQ * RANK)
            .transpose(1, 0, 2, 3)
            .reshape(rows_out, NQ * RANK)
        )
        hidden = (jax.nn.silu(gate_pre.astype(f32)) * up_pre.astype(f32)).astype(bf16)
        in_factors = []
        for group in range(GROUPS):
            part = jnp.dot(eigen_in, finals[group], preferred_element_type=f32)
            pieces = [
                roll_piece(place, part, piece, n_grp, n_dp, kind)
                for piece, kind in enumerate(kinds)
            ]
            blocks = reduce_gather(pieces[:-1], pieces[-1], n_grp, n_dp)
            grid = jnp.stack(blocks).reshape(n_dp, n_grp, -1, COLS)
            grid = jnp.roll(grid, place[1] + 1, axis=0)
            grid = jnp.roll(grid, place[0] + 1, axis=1)
            in_factors.append(grid.reshape(-1, COLS))
        in_factor = jnp.concatenate(in_factors, axis=1)
        proj_out = jnp.dot(grads_out, out_factor, preferred_element_type=f32)
        proj_in = jnp.dot(hidden, in_factor, preferred_element_type=f32)
        proj_out = sum_scatter(proj_out, "width", n_width)
        proj_in = sum_scatter(proj_in, "width", n_width)
        scores = (proj_out * proj_in).reshape(proj_out.shape[0], NQ, RANK).sum(axis=2).T
        return (scores, out_factor, in_factor)

    return per_device


def solution(mesh):
    return jax.shard_map(
        make_per_device(mesh.shape["grp"], mesh.shape["dp"], mesh.shape["width"]),
        mesh=mesh,
        in_specs=(
            P(None, GD),
            P(None, "width"),
            P(GD, "width"),
            P("width", GD),
            P("width", GD),
            P(GD, None),
            P(GD, "width"),
            P(GD, "width"),
            P(GD, "width"),
        ),
        out_specs=(P(None, GD + ("width",)), P("width", None), P("width", None)),
        check_vma=False,
    )
```

time: 710 us -> 729 us (1.027)
  Pallas kernels: 6.1 us -> 324 us
  matrix products: 262 us -> 57.2 us
  blocking collectives: 162 us -> 0 us
  starting transfers between devices: 44.2 us -> 169 us
  waiting for transfers between devices: 175 us -> 120 us
  other arithmetic: 29.7 us -> 21.4 us
    pallas_call x2 -> x48, Pallas kernels: 6.1 us -> 324 us  [the longest x8 95.4 us: return_piece(): pl.pallas_call(functools.partial(return_kernel, first), grid=(n_grp,), in...]
    dot_general x15 -> x9, matrix products: 262 us -> 57.2 us  [the longest x2 18.8 us: per_device(): part = jnp.dot(eigen_in, finals[group], preferred_element_type=f32)]
    all_to_all x5 -> x0, blocking collectives: 162 us -> none  [the longest x3 105 us: sum_scatter(): pieces = lax.all_to_all(part.astype(jnp.bfloat16), axes, 0, 0, tiled=True)]
    ppermute x6 -> x106, starting transfers between devices: 3.76 us -> 143 us  [the longest x56 88.9 us: reduce_gather(): blocks.append(lax.ppermute(block, GD, pairs))]
    ppermute x6 -> x106, waiting for transfers between devices: 12.8 us -> 67.3 us  [the longest x56 67.1 us: reduce_gather(): blocks.append(lax.ppermute(block, GD, pairs))]
    all_to_all x3 -> x1, waiting for transfers between devices: 40.1 us -> 0.01 us  [gather_rows(): whole = lax.all_to_all(copies, axes, 0, 0, tiled=True)]
    all_to_all x4 -> x3, waiting for transfers between devices: 46.8 us -> 9.31 us  [sum_scatter(): pieces = lax.all_to_all(part.astype(bf16), axes, 0, 0, tiled=True)]
    ppermute x6, waiting for transfers between devices: 63 us -> 35.3 us  [sum_width(): got = lax.ppermute(sent, 'width', [(i, i ^ step) for i in range(count)])]
  transfers between devices with their start and end apart: 20 -> 117, of which waited for: 13 -> 22; matrix products, arithmetic and copies ran while one was open for 10% -> 12% of each run, Pallas kernels for 0% -> 45%
where the time goes in v2:
time: 729 us; the launch traced here: 719 us
  Pallas kernels  324 us (44%)
  starting transfers between devices  169 us (23%)
  waiting for transfers between devices  120 us (16%)
  matrix products  57.2 us (8%)
  local copies, waits for them, and re-layouts  25 us (3%)
  other arithmetic  21.4 us (3%)
    pallas_call x8, Pallas kernels, return_piece(): pl.pallas_call(functools.partial(return_kernel, first), grid=(n_grp,), in...  95.4 us
    ppermute x56, starting transfers between devices, reduce_gather(): blocks.append(lax.ppermute(block, GD, pairs))  88.9 us
    pallas_call x4, Pallas kernels, form_piece(): pl.pallas_call(form_kernel, grid_spec=pltpu.PrefetchScalarGridSpec(num_sc...  87.6 us
    ppermute x56, waiting for transfers between devices, reduce_gather(): blocks.append(lax.ppermute(block, GD, pairs))  67.1 us
    pallas_call x4, Pallas kernels, image_piece(): pl.pallas_call(image_kernel, grid=(n_grp,), in_specs=[pl.BlockSpec((cols,...  53.9 us
    ppermute x24, starting transfers between devices, reduce_gather(): lax.ppermute(quarter, 'grp', [(i, (i + step + 1) % n_grp) for i in range(...  36.2 us
    ppermute x6, waiting for transfers between devices, sum_width(): got = lax.ppermute(sent, 'width', [(i, i ^ step) for i in range(count)])  35.3 us
    pallas_call x8, Pallas kernels, roll_piece(): pl.pallas_call(roll_kernel, grid_spec=pltpu.PrefetchScalarGridSpec(num_sc...  32.1 us
  transfers between devices with their start and end apart: 117, of which 22 were waited for; matrix products, arithmetic and copies ran while one was open for 12% of the time, Pallas kernels for 45%

profile of v2, /device:TPU:0, one launch (start us, length us, event | category | flops | bytes accessed | tf_op | source)
XLA Modules:
  0.0 718.7 jit_solution(15126187897481495554)
XLA Ops:
  1.3 5.0 fusion.28.part_ref
  13.2 5.0 fusion.26.part_ref
  35.2 9.9 %fusion.9 = f32[256,1792]{1,0:T(8,128)} fusion(bf16[3584,1792]{1,0:T(8,128)(2,1)} %param.20, bf16[512,3584]{1,0:T(8,128)(2,1)} %param.18), kind=kOutput, calls=%fused_computation.23 | convolution fusion | flops 3288334336 | bytes 16515072 | tf_op jit(solution)/shard_map/dot_general | solution.py:391
  61.5 7.5 %fusion.7 = f32[256,1792]{1,0:T(8,128)S(1)} fusion(bf16[3584,1792]{1,0:T(8,128)(2,1)} %param.20, bf16[512,3584]{1,0:T(8,128)(2,1)} %param.18), kind=kOutput, calls=%fused_computation.20 | convolution fusion | flops 3288334336 | bytes 16515072 | tf_op jit(solution)/shard_map/dot_general | solution.py:391
  76.5 10.6 %collective-permute-start.11 = (bf16[256,256]{1,0:T(8,128)(2,1)S(1)}, bf16[256,256]{1,0:T(8,128)(2,1)S(1)}, u32[]{:S(2)}, u32[]{:S(2)}) collective-permute-start(bf16[256,256]{1,0:T(8,128)(2,1)S(1)} %copy-done.12), channel_id=1, source_target_pairs={{0,12},{4,8},{8,20},{12,16},{16,28},{20,24},{24,4},{28,0},{1,13},{... | collective-permute-start | bytes 393224 | tf_op jit(solution)/shard_map/ppermute | solution.py:253
  107.5 11.3 %collective-permute-done.48 = bf16[256,256]{1,0:T(8,128)(2,1)S(1)} collective-permute-done((bf16[256,256]{1,0:T(8,128)(2,1)}, bf16[256,256]{1,0:T(8,128)(2,1)S(1)}, u32[]{:S(2)}, u32[]{:S(2)}) %collective-permute-start.48) | collective-permute-done | bytes 131104 | tf_op jit(solution)/shard_map/ppermute | solution.py:253
  127.3 15.4 %collective-permute-done.8 = bf16[256,1792]{1,0:T(8,128)(2,1)S(1)} collective-permute-done((bf16[256,1792]{1,0:T(8,128)(2,1)S(1)}, bf16[256,1792]{1,0:T(8,128)(2,1)S(1)}, u32[]{:S(2)}, u32[]{:S(2)}) %collective-permute-start.8) | collective-permute-done | bytes 917536 | tf_op jit(solution)/shard_map/ppermute | solution.py:344
  143.8 22.0 %form.5 = (bf16[8,1024,1792]{2,1,0:T(8,128)(2,1)}, bf16[1024,128]{1,0:T(8,128)(2,1)}) custom-call(s32[2]{0:T(128)} %pad_add_fusion.place_ref, bf16[1024,256]{1,0:T(8,128)(2,1)} %pad_maximum_fusion.2.out_ref, bf16[256,1792]{1,0:T(8,128)(2,1)} %add_convert_fusion.1.in_ref, f32[2048,1792]{1,0:T(8,128)} %eig_ref.7, bf16[1792,128]{1,0:T(8,128)(2,1)} %get-tuple-element.99.basis_ref), custom_call_target="tpu_custom_call" | custom-call | flops 15032385536 | bytes 29360128 | tf_op jit(solution)/shard_map/form/pallas_call | solution.py:72
  167.2 21.7 %form.4 = (bf16[8,1024,1792]{2,1,0:T(8,128)(2,1)}, f32[1024,128]{1,0:T(8,128)}) custom-call(s32[2]{0:T(128)} %pad_add_fusion.place_ref, bf16[1024,256]{1,0:T(8,128)(2,1)} %pad_maximum_fusion.1.out_ref, bf16[256,1792]{1,0:T(8,128)(2,1)} %add_convert_fusion.1.in_ref, f32[2048,1792]{1,0:T(8,128)} %eig_ref.7, bf16[1792,128]{1,0:T(8,128)(2,1)} %get-tuple-element.99.basis_ref), custom_call_target="tpu_custom_call" | custom-call | flops 15032385536 | bytes 29360128 | tf_op jit(solution)/shard_map/form/pallas_call | solution.py:72
  189.9 22.1 %form.7 = (bf16[8,1024,1792]{2,1,0:T(8,128)(2,1)}, bf16[1024,128]{1,0:T(8,128)(2,1)}) custom-call(s32[2]{0:T(128)} %pad_add_fusion.place_ref, bf16[1024,256]{1,0:T(8,128)(2,1)} %pad_maximum_fusion.4.out_ref, bf16[256,1792]{1,0:T(8,128)(2,1)} %add_convert_fusion.in_ref, f32[2048,1792]{1,0:T(8,128)} %eig_ref.7, bf16[1792,128]{1,0:T(8,128)(2,1)} %get-tuple-element.100.basis_ref), custom_call_target="tpu_custom_call" | custom-call | flops 15032385536 | bytes 29360128 | tf_op jit(solution)/shard_map/form/pallas_call | solution.py:72
  219.1 21.8 %form.6 = (bf16[8,1024,1792]{2,1,0:T(8,128)(2,1)}, f32[1024,128]{1,0:T(8,128)}) custom-call(s32[2]{0:T(128)} %pad_add_fusion.place_ref, bf16[1024,256]{1,0:T(8,128)(2,1)} %pad_maximum_fusion.3.out_ref, bf16[256,1792]{1,0:T(8,128)(2,1)} %add_convert_fusion.in_ref, f32[2048,1792]{1,0:T(8,128)} %eig_ref.7, bf16[1792,128]{1,0:T(8,128)(2,1)} %get-tuple-element.100.basis_ref), custom_call_target="tpu_custom_call" | custom-call | flops 15032385536 | bytes 29360128 | tf_op jit(solution)/shard_map/form/pallas_call | solution.py:72
  287.4 12.1 %returned.8.refs_0_ = f32[128,1792]{1,0:T(8,128)} custom-call(bf16[8,128,256]{2,1,0:T(8,128)(2,1)} %orthonormal.4.basis_ref, bf16[8,1024,1792]{2,1,0:T(8,128)(2,1)} %get-tuple-element.58.rotated_ref), custom_call_target="tpu_custom_call" | custom-call | flops 7516192768 | bytes 29360128 | tf_op jit(solution)/shard_map/returned/pallas_call | solution.py:148
  299.5 11.9 %returned.9 = f32[128,1792]{1,0:T(8,128)} custom-call(bf16[8,128,256]{2,1,0:T(8,128)(2,1)} %orthonormal.4.basis_ref, bf16[8,1024,1792]{2,1,0:T(8,128)(2,1)} %get-tuple-element.57.rotated_ref, f32[128,1792]{1,0:T(8,128)} %returned.8.refs_0_), custom_call_target="tpu_custom_call" | custom-call | flops 7516192768 | bytes 29360128 | tf_op jit(solution)/shard_map/returned/pallas_call | solution.py:148
  318.8 11.7 %returned.10.refs_0_ = f32[128,1792]{1,0:T(8,128)} custom-call(bf16[8,128,256]{2,1,0:T(8,128)(2,1)} %orthonormal.6.basis_ref, bf16[8,1024,1792]{2,1,0:T(8,128)(2,1)} %get-tuple-element.74.rotated_ref), custom_call_target="tpu_custom_call" | custom-call | flops 7516192768 | bytes 29360128 | tf_op jit(solution)/shard_map/returned/pallas_call | solution.py:148
  330.5 11.9 %returned.11 = f32[128,1792]{1,0:T(8,128)} custom-call(bf16[8,128,256]{2,1,0:T(8,128)(2,1)} %orthonormal.6.basis_ref, bf16[8,1024,1792]{2,1,0:T(8,128)(2,1)} %get-tuple-element.73.rotated_ref, f32[128,1792]{1,0:T(8,128)} %returned.10.refs_0_), custom_call_target="tpu_custom_call" | custom-call | flops 7516192768 | bytes 29360128 | tf_op jit(solution)/shard_map/returned/pallas_call | solution.py:148
  349.3 10.6 %collective-permute-done.28 = bf16[128,1792]{0,1:T(8,128)(2,1)S(1)} collective-permute-done((bf16[128,1792]{0,1:T(8,128)(2,1)S(1)}, bf16[128,1792]{0,1:T(8,128)(2,1)S(1)}, u32[]{:S(2)}, u32[]{:S(2)}) %collective-permute-start.28) | collective-permute-done | bytes 458784 | tf_op jit(solution)/shard_map/ppermute | solution.py:344
  360.8 13.4 %image.5 = bf16[1024,128]{1,0:T(8,128)(2,1)} custom-call(bf16[1792,128]{1,0:T(8,128)(2,1)} %fusion.30.basis_ref, bf16[8,1024,1792]{2,1,0:T(8,128)(2,1)} %get-tuple-element.58.rotated_ref), custom_call_target="tpu_custom_call" | custom-call | flops 7516192768 | bytes 29360128 | tf_op jit(solution)/shard_map/image/pallas_call | solution.py:112
  375.4 13.5 %image.4.keep_ref = f32[1024,128]{1,0:T(8,128)} custom-call(bf16[1792,128]{1,0:T(8,128)(2,1)} %fusion.30.basis_ref, bf16[8,1024,1792]{2,1,0:T(8,128)(2,1)} %get-tuple-element.57.rotated_ref), custom_call_target="tpu_custom_call" | custom-call | flops 7516192768 | bytes 29360128 | tf_op jit(solution)/shard_map/image/pallas_call | solution.py:112
  389.8 13.6 %image.7 = bf16[1024,128]{1,0:T(8,128)(2,1)} custom-call(bf16[1792,128]{1,0:T(8,128)(2,1)} %fusion.31.basis_ref, bf16[8,1024,1792]{2,1,0:T(8,128)(2,1)} %get-tuple-element.74.rotated_ref), custom_call_target="tpu_custom_call" | custom-call | flops 7516192768 | bytes 29360128 | tf_op jit(solution)/shard_map/image/pallas_call | solution.py:112
  410.6 13.5 %image.6.keep_ref = f32[1024,128]{1,0:T(8,128)} custom-call(bf16[1792,128]{1,0:T(8,128)(2,1)} %fusion.31.basis_ref, bf16[8,1024,1792]{2,1,0:T(8,128)(2,1)} %get-tuple-element.73.rotated_ref), custom_call_target="tpu_custom_call" | custom-call | flops 7516192768 | bytes 29360128 | tf_op jit(solution)/shard_map/image/pallas_call | solution.py:112
  473.4 11.9 %returned.12.refs_0_ = f32[128,1792]{1,0:T(8,128)} custom-call(bf16[8,128,256]{2,1,0:T(8,128)(2,1)} %orthonormal.5.basis_ref, bf16[8,1024,1792]{2,1,0:T(8,128)(2,1)} %get-tuple-element.58.rotated_ref), custom_call_target="tpu_custom_call" | custom-call | flops 7516192768 | bytes 29360128 | tf_op jit(solution)/shard_map/returned/pallas_call | solution.py:148
  485.3 11.9 %returned.13 = f32[128,1792]{1,0:T(8,128)} custom-call(bf16[8,128,256]{2,1,0:T(8,128)(2,1)} %orthonormal.5.basis_ref, bf16[8,1024,1792]{2,1,0:T(8,128)(2,1)} %get-tuple-element.57.rotated_ref, f32[128,1792]{1,0:T(8,128)} %returned.12.refs_0_), custom_call_target="tpu_custom_call" | custom-call | flops 7516192768 | bytes 29360128 | tf_op jit(solution)/shard_map/returned/pallas_call | solution.py:148
  503.1 11.7 %returned.14.refs_0_ = f32[128,1792]{1,0:T(8,128)} custom-call(bf16[8,128,256]{2,1,0:T(8,128)(2,1)} %orthonormal.7.basis_ref, bf16[8,1024,1792]{2,1,0:T(8,128)(2,1)} %get-tuple-element.74.rotated_ref), custom_call_target="tpu_custom_call" | custom-call | flops 7516192768 | bytes 29360128 | tf_op jit(solution)/shard_map/returned/pallas_call | solution.py:148
  514.8 12.2 %returned.15 = f32[128,1792]{1,0:T(8,128)} custom-call(bf16[8,128,256]{2,1,0:T(8,128)(2,1)} %orthonormal.7.basis_ref, bf16[8,1024,1792]{2,1,0:T(8,128)(2,1)} %get-tuple-element.73.rotated_ref, f32[128,1792]{1,0:T(8,128)} %returned.14.refs_0_), custom_call_target="tpu_custom_call" | custom-call | flops 7516192768 | bytes 29360128 | tf_op jit(solution)/shard_map/returned/pallas_call | solution.py:148
  537.5 9.2 %collective-permute-done.87 = bf16[128,1792]{1,0:T(8,128)(2,1)S(1)} collective-permute-done((bf16[128,1792]{1,0:T(8,128)(2,1)S(1)}, bf16[128,1792]{1,0:T(8,128)(2,1)S(1)}, u32[]{:S(2)}, u32[]{:S(2)}) %collective-permute-start.87) | collective-permute-done | bytes 458784 | tf_op jit(solution)/shard_map/ppermute | solution.py:344
  546.8 9.4 %convolution_bitcast_fusion.1.part_ref = f32[3584,128]{1,0:T(8,128)} fusion(bf16[3584,1792]{1,0:T(8,128)(2,1)} %param.20, f32[128,1792]{1,0:T(8,128)S(1)} %get-tuple-element.88, bf16[128,1792]{1,0:T(8,128)(2,1)S(1)} %collective-permute-done.87), kind=kOutput, calls=%fused_computation.8 | convolution fusion | flops 1644855296 | bytes 16056320 | tf_op jit(solution)/shard_map/dot_general | solution.py:438
  562.1 9.4 %convolution_bitcast_fusion.part_ref = f32[3584,128]{1,0:T(8,128)} fusion(bf16[3584,1792]{1,0:T(8,128)(2,1)} %param.20, f32[128,1792]{1,0:T(8,128)S(1)} %get-tuple-element.90, bf16[128,1792]{1,0:T(8,128)(2,1)S(1)} %collective-permute-done.100), kind=kOutput, calls=%fused_computation.7 | convolution fusion | flops 1644855296 | bytes 16056320 | tf_op jit(solution)/shard_map/dot_general | solution.py:438
  625.1 26.3 %collective-permute-done.93 = bf16[448,128]{1,0:T(8,128)(2,1)S(1)} collective-permute-done((bf16[448,128]{1,0:T(8,128)(2,1)S(1)}, bf16[448,128]{1,0:T(8,128)(2,1)S(1)}, u32[]{:S(2)}, u32[]{:S(2)}) %collective-permute-start.93) | collective-permute-done | bytes 114720 | tf_op jit(solution)/shard_map/ppermute | solution.py:253
  663.2 8.0 %collective-permute-done.106 = bf16[448,128]{1,0:T(8,128)(2,1)S(1)} collective-permute-done((bf16[448,128]{1,0:T(8,128)(2,1)}, bf16[448,128]{1,0:T(8,128)(2,1)S(1)}, u32[]{:S(2)}, u32[]{:S(2)}) %collective-permute-start.106) | collective-permute-done | bytes 114720 | tf_op jit(solution)/shard_map/ppermute | solution.py:253
  684.3 6.7 fusion.11
  691.0 7.7 %all-to-all-done.2 = bf16[4,512,256]{2,1,0:T(8,128)(2,1)S(1)} async-done(((bf16[4,512,256]{2,1,0:T(8,128)(2,1)}), bf16[4,512,256]{2,1,0:T(8,128)(2,1)S(1)}, u32[]{:S(2)}, u32[]{:S(2)}) %all-to-all-start.2) | async-done | bytes 1048608 | tf_op jit(solution)/shard_map/all_to_all | solution.py:429
  711.7 5.9 all-to-all-done.3
  (480 shorter events, 321.6 us)
Async XLA Ops:
  22.1 27.1 %collective-permute-start.43 = (bf16[1024,256]{1,0:T(8,128)(2,1)}, bf16[1024,256]{1,0:T(8,128)(2,1)S(1)}, u32[]{:S(2)}, u32[]{:S(2)}) collective-permute-start(bf16[1024,256]{1,0:T(8,128)(2,1)} %roll.11), channel_id=1, source_target_pairs={{0,4},{4,0},{1,5},{5,1},{2,6},{6,2},{3,7},{7,3},{8,12},{12,8},{9,1... | collective-permute-start | bytes 1572872 | tf_op jit(solution)/shard_map/ppermute | solution.py:232
  29.2 23.7 %collective-permute-start.1 = (bf16[256,256]{1,0:T(8,128)(2,1)}, bf16[256,256]{1,0:T(8,128)(2,1)S(1)}, u32[]{:S(2)}, u32[]{:S(2)}) collective-permute-start(bf16[256,256]{1,0:T(8,128)(2,1)} %get-tuple-element.48), channel_id=1, source_target_pairs={{0,8},{8,16},{16,24},{24,0},{1,9},{9,17},{17,25},{25,1},{2,10},{10... | collective-permute-start | bytes 393224 | tf_op jit(solution)/shard_map/ppermute | solution.py:237
  45.1 54.5 %collective-permute-start.7 = (f32[256,1792]{1,0:T(8,128)}, f32[256,1792]{1,0:T(8,128)}, u32[]{:S(2)}, u32[]{:S(2)}) collective-permute-start(f32[256,1792]{1,0:T(8,128)} %fusion.9), channel_id=1, source_target_pairs={{0,1},{1,0},{2,3},{3,2},{4,5},{5,4},{6,7},{7,6},{8,9},{9,8},{10,11... | collective-permute-start | bytes 5505032 | tf_op jit(solution)/shard_map/ppermute | solution.py:340
  69.1 55.6 %collective-permute-start.50 = (f32[256,1792]{1,0:T(8,128)S(1)}, f32[256,1792]{1,0:T(8,128)S(1)}, u32[]{:S(2)}, u32[]{:S(2)}) collective-permute-start(f32[256,1792]{1,0:T(8,128)S(1)} %fusion.7), channel_id=1, source_target_pairs={{0,1},{1,0},{2,3},{3,2},{4,5},{5,4},{6,7},{7,6},{8,9},{9,8},{10,11... | collective-permute-start | bytes 5505032 | tf_op jit(solution)/shard_map/ppermute | solution.py:340
  96.2 22.6 %collective-permute-start.48 = (bf16[256,256]{1,0:T(8,128)(2,1)}, bf16[256,256]{1,0:T(8,128)(2,1)S(1)}, u32[]{:S(2)}, u32[]{:S(2)}) collective-permute-start(bf16[256,256]{1,0:T(8,128)(2,1)} %second_sum.11), channel_id=1, source_target_pairs={{0,16},{4,20},{8,24},{12,28},{16,0},{20,4},{24,8},{28,12},{1,17},{... | collective-permute-start | bytes 393224 | tf_op jit(solution)/shard_map/ppermute | solution.py:253
  119.4 23.3 %collective-permute-start.8 = (bf16[256,1792]{1,0:T(8,128)(2,1)S(1)}, bf16[256,1792]{1,0:T(8,128)(2,1)S(1)}, u32[]{:S(2)}, u32[]{:S(2)}) collective-permute-start(bf16[256,1792]{1,0:T(8,128)(2,1)S(1)} %get-tuple-element.93), channel_id=1, source_target_pairs={{0,2},{1,3},{2,0},{3,1},{4,6},{5,7},{6,4},{7,5},{8,10},{9,11},{10,... | collective-permute-start | bytes 2752520 | tf_op jit(solution)/shard_map/ppermute | solution.py:344
  125.8 63.1 %collective-permute-start.51 = (bf16[256,1792]{1,0:T(8,128)(2,1)}, bf16[256,1792]{1,0:T(8,128)(2,1)S(1)}, u32[]{:S(2)}, u32[]{:S(2)}) collective-permute-start(bf16[256,1792]{1,0:T(8,128)(2,1)} %get-tuple-element.97), channel_id=1, source_target_pairs={{0,2},{1,3},{2,0},{3,1},{4,6},{5,7},{6,4},{7,5},{8,10},{9,11},{10,... | collective-permute-start | bytes 2752520 | tf_op jit(solution)/shard_map/ppermute | solution.py:344
  165.8 46.9 %collective-permute-start.13 = (bf16[1024,128]{1,0:T(8,128)(2,1)}, bf16[1024,128]{1,0:T(8,128)(2,1)S(1)}, u32[]{:S(2)}, u32[]{:S(2)}) collective-permute-start(bf16[1024,128]{1,0:T(8,128)(2,1)} %get-tuple-element.52), channel_id=1, source_target_pairs={{0,4},{4,0},{1,5},{5,1},{2,6},{6,2},{3,7},{7,3},{8,12},{12,8},{9,1... | collective-permute-start | bytes 786440 | tf_op jit(solution)/shard_map/ppermute | solution.py:232
  212.0 28.9 %collective-permute-start.56 = (bf16[1024,128]{1,0:T(8,128)(2,1)}, bf16[1024,128]{1,0:T(8,128)(2,1)S(1)}, u32[]{:S(2)}, u32[]{:S(2)}) collective-permute-start(bf16[1024,128]{1,0:T(8,128)(2,1)} %get-tuple-element.68), channel_id=1, source_target_pairs={{0,4},{4,0},{1,5},{5,1},{2,6},{6,2},{3,7},{7,3},{8,12},{12,8},{9,1... | collective-permute-start | bytes 786440 | tf_op jit(solution)/shard_map/ppermute | solution.py:232
  215.2 30.2 %collective-permute-start.14 = (bf16[256,128]{1,0:T(8,128)(2,1)}, bf16[256,128]{1,0:T(8,128)(2,1)S(1)}, u32[]{:S(2)}, u32[]{:S(2)}) collective-permute-start(bf16[256,128]{1,0:T(8,128)(2,1)} %get-tuple-element.54), channel_id=1, source_target_pairs={{0,8},{8,16},{16,24},{24,0},{1,9},{9,17},{17,25},{25,1},{2,10},{10... | collective-permute-start | bytes 196616 | tf_op jit(solution)/shard_map/ppermute | solution.py:237
  215.2 33.2 %collective-permute-start.15 = (bf16[256,128]{1,0:T(8,128)(2,1)}, bf16[256,128]{1,0:T(8,128)(2,1)S(1)}, u32[]{:S(2)}, u32[]{:S(2)}) collective-permute-start(bf16[256,128]{1,0:T(8,128)(2,1)} %get-tuple-element.55), channel_id=1, source_target_pairs={{0,16},{8,24},{16,0},{24,8},{1,17},{9,25},{17,1},{25,9},{2,18},{10... | collective-permute-start | bytes 196616 | tf_op jit(solution)/shard_map/ppermute | solution.py:237
  215.3 33.2 %collective-permute-start.16 = (bf16[256,128]{1,0:T(8,128)(2,1)}, bf16[256,128]{1,0:T(8,128)(2,1)S(1)}, u32[]{:S(2)}, u32[]{:S(2)}) collective-permute-start(bf16[256,128]{1,0:T(8,128)(2,1)} %get-tuple-element.56), channel_id=1, source_target_pairs={{0,24},{8,0},{16,8},{24,16},{1,25},{9,1},{17,9},{25,17},{2,26},{10... | collective-permute-start | bytes 196616 | tf_op jit(solution)/shard_map/ppermute | solution.py:237
  279.9 33.3 %collective-permute-start.67 = (f32[16,128]{1,0:T(8,128)}, f32[16,128]{1,0:T(8,128)S(1)}, u32[]{:S(2)}, u32[]{:S(2)}) collective-permute-start(f32[16,128]{1,0:T(8,128)} %gram.6.refs_0_), channel_id=1, source_target_pairs={{0,1},{1,0},{2,3},{3,2},{4,5},{5,4},{6,7},{7,6},{8,9},{9,8},{10,11... | collective-permute-start | bytes 24584 | tf_op jit(solution)/shard_map/ppermute | solution.py:412
  279.9 33.3 %collective-permute-start.68 = (f32[16,128]{1,0:T(8,128)}, f32[16,128]{1,0:T(8,128)S(1)}, u32[]{:S(2)}, u32[]{:S(2)}) collective-permute-start(f32[16,128]{1,0:T(8,128)} %gram.6.refs_0_), channel_id=1, source_target_pairs={{0,2},{1,3},{2,0},{3,1},{4,6},{5,7},{6,4},{7,5},{8,10},{9,11},{10,... | collective-permute-start | bytes 24584 | tf_op jit(solution)/shard_map/ppermute | solution.py:412
  281.5 31.8 %collective-permute-start.69 = (f32[16,128]{1,0:T(8,128)}, f32[16,128]{1,0:T(8,128)S(1)}, u32[]{:S(2)}, u32[]{:S(2)}) collective-permute-start(f32[16,128]{1,0:T(8,128)} %gram.6.refs_0_), channel_id=1, source_target_pairs={{0,3},{1,2},{2,1},{3,0},{4,7},{5,6},{6,5},{7,4},{8,11},{9,10},{10,... | collective-permute-start | bytes 24584 | tf_op jit(solution)/shard_map/ppermute | solution.py:412
  312.9 32.2 %collective-permute-start.27 = (f32[128,1792]{0,1:T(8,128)S(1)}, f32[128,1792]{0,1:T(8,128)}, u32[]{:S(2)}, u32[]{:S(2)}) collective-permute-start(f32[128,1792]{0,1:T(8,128)S(1)} %copy.50), channel_id=1, source_target_pairs={{0,1},{1,0},{2,3},{3,2},{4,5},{5,4},{6,7},{7,6},{8,9},{9,8},{10,11... | collective-permute-start | bytes 2752520 | tf_op jit(solution)/shard_map/ppermute | solution.py:340
  348.2 40.7 %collective-permute-start.71 = (bf16[128,1792]{0,1:T(8,128)(2,1)S(1)}, bf16[128,1792]{0,1:T(8,128)(2,1)S(1)}, u32[]{:S(2)}, u32[]{:S(2)}) collective-permute-start(bf16[128,1792]{0,1:T(8,128)(2,1)S(1)} %get-tuple-element.95), channel_id=1, source_target_pairs={{0,2},{1,3},{2,0},{3,1},{4,6},{5,7},{6,4},{7,5},{8,10},{9,11},{10,... | collective-permute-start | bytes 1376264 | tf_op jit(solution)/shard_map/ppermute | solution.py:344
  374.2 30.0 %collective-permute-start.29 = (bf16[1024,128]{1,0:T(8,128)(2,1)}, bf16[1024,128]{1,0:T(8,128)(2,1)S(1)}, u32[]{:S(2)}, u32[]{:S(2)}) collective-permute-start(bf16[1024,128]{1,0:T(8,128)(2,1)} %image.5), channel_id=1, source_target_pairs={{0,4},{4,0},{1,5},{5,1},{2,6},{6,2},{3,7},{7,3},{8,12},{12,8},{9,1... | collective-permute-start | bytes 786440 | tf_op jit(solution)/shard_map/ppermute | solution.py:232
  408.2 23.3 %collective-permute-start.31 = (bf16[256,128]{1,0:T(8,128)(2,1)}, bf16[256,128]{1,0:T(8,128)(2,1)S(1)}, u32[]{:S(2)}, u32[]{:S(2)}) collective-permute-start(bf16[256,128]{1,0:T(8,128)(2,1)} %get-tuple-element.61), channel_id=1, source_target_pairs={{0,16},{8,24},{16,0},{24,8},{1,17},{9,25},{17,1},{25,9},{2,18},{10... | collective-permute-start | bytes 196616 | tf_op jit(solution)/shard_map/ppermute | solution.py:237
  466.0 31.6 %collective-permute-start.83 = (f32[16,128]{1,0:T(8,128)}, f32[16,128]{1,0:T(8,128)S(1)}, u32[]{:S(2)}, u32[]{:S(2)}) collective-permute-start(f32[16,128]{1,0:T(8,128)} %gram.7.refs_0_), channel_id=1, source_target_pairs={{0,1},{1,0},{2,3},{3,2},{4,5},{5,4},{6,7},{7,6},{8,9},{9,8},{10,11... | collective-permute-start | bytes 24584 | tf_op jit(solution)/shard_map/ppermute | solution.py:412
  466.0 31.6 %collective-permute-start.84 = (f32[16,128]{1,0:T(8,128)}, f32[16,128]{1,0:T(8,128)S(1)}, u32[]{:S(2)}, u32[]{:S(2)}) collective-permute-start(f32[16,128]{1,0:T(8,128)} %gram.7.refs_0_), channel_id=1, source_target_pairs={{0,2},{1,3},{2,0},{3,1},{4,6},{5,7},{6,4},{7,5},{8,10},{9,11},{10,... | collective-permute-start | bytes 24584 | tf_op jit(solution)/shard_map/ppermute | solution.py:412
  467.4 30.1 %collective-permute-start.85 = (f32[16,128]{1,0:T(8,128)}, f32[16,128]{1,0:T(8,128)S(1)}, u32[]{:S(2)}, u32[]{:S(2)}) collective-permute-start(f32[16,128]{1,0:T(8,128)} %gram.7.refs_0_), channel_id=1, source_target_pairs={{0,3},{1,2},{2,1},{3,0},{4,7},{5,6},{6,5},{7,4},{8,11},{9,10},{10,... | collective-permute-start | bytes 24584 | tf_op jit(solution)/shard_map/ppermute | solution.py:412
  497.2 34.8 %collective-permute-start.86 = (f32[128,1792]{1,0:T(8,128)}, f32[128,1792]{1,0:T(8,128)}, u32[]{:S(2)}, u32[]{:S(2)}) collective-permute-start(f32[128,1792]{1,0:T(8,128)} %returned.13), channel_id=1, source_target_pairs={{0,1},{1,0},{2,3},{3,2},{4,5},{5,4},{6,7},{7,6},{8,9},{9,8},{10,11... | collective-permute-start | bytes 2752520 | tf_op jit(solution)/shard_map/ppermute | solution.py:340
  537.0 25.1 %collective-permute-start.100 = (bf16[128,1792]{1,0:T(8,128)(2,1)}, bf16[128,1792]{1,0:T(8,128)(2,1)S(1)}, u32[]{:S(2)}, u32[]{:S(2)}) collective-permute-start(bf16[128,1792]{1,0:T(8,128)(2,1)} %get-tuple-element.89), channel_id=1, source_target_pairs={{0,2},{1,3},{2,0},{3,1},{4,6},{5,7},{6,4},{7,5},{8,10},{9,11},{10,... | collective-permute-start | bytes 1376264 | tf_op jit(solution)/shard_map/ppermute | solution.py:344
  560.3 27.3 %collective-permute-start.88 = (bf16[1792,128]{1,0:T(8,128)(2,1)}, bf16[1792,128]{1,0:T(8,128)(2,1)}, u32[]{:S(2)}, u32[]{:S(2)}) collective-permute-start(bf16[1792,128]{1,0:T(8,128)(2,1)} %roll.13), channel_id=1, source_target_pairs={{0,4},{4,0},{1,5},{5,1},{2,6},{6,2},{3,7},{7,3},{8,12},{12,8},{9,1... | collective-permute-start | bytes 1376264 | tf_op jit(solution)/shard_map/ppermute | solution.py:232
  580.2 28.6 %all-to-all-start = ((bf16[4,256,256]{1,2,0:T(8,128)(2,1)}), bf16[4,256,256]{1,2,0:T(8,128)(2,1)S(1)}, u32[]{:S(2)}, u32[]{:S(2)}) async-start(bf16[4,256,256]{1,2,0:T(8,128)(2,1)} %bitcast.86), calls=%async_computation | async-start | bytes 1048576 | tf_op jit(solution)/shard_map/all_to_all | solution.py:351
  610.0 70.5 %all-to-all-start.1 = ((bf16[8,256,256]{2,1,0:T(8,128)(2,1)}), bf16[8,256,256]{2,1,0:T(8,128)(2,1)}, u32[]{:S(2)}, u32[]{:S(2)}) async-start(bf16[8,256,256]{2,1,0:T(8,128)(2,1)} %broadcast_in_dim.2), calls=%async_computation.1 | async-start | bytes 2097152 | tf_op jit(solution)/shard_map/all_to_all | solution.py:358
  614.3 37.2 %collective-permute-start.93 = (bf16[448,128]{1,0:T(8,128)(2,1)S(1)}, bf16[448,128]{1,0:T(8,128)(2,1)S(1)}, u32[]{:S(2)}, u32[]{:S(2)}) collective-permute-start(bf16[448,128]{1,0:T(8,128)(2,1)S(1)} %copy-done.14), channel_id=1, source_target_pairs={{0,20},{4,16},{8,28},{12,24},{16,4},{20,0},{24,12},{28,8},{1,21},{... | collective-permute-start | bytes 344072 | tf_op jit(solution)/shard_map/ppermute | solution.py:253
  618.0 33.5 %collective-permute-start.94 = (bf16[448,128]{1,0:T(8,128)(2,1)S(1)}, bf16[448,128]{1,0:T(8,128)(2,1)S(1)}, u32[]{:S(2)}, u32[]{:S(2)}) collective-permute-start(bf16[448,128]{1,0:T(8,128)(2,1)S(1)} %copy-done.14), channel_id=1, source_target_pairs={{0,12},{4,8},{8,20},{12,16},{16,28},{20,24},{24,4},{28,0},{1,13},{... | collective-permute-start | bytes 344072 | tf_op jit(solution)/shard_map/ppermute | solution.py:253
  619.5 36.5 %collective-permute-start.95 = (bf16[448,128]{1,0:T(8,128)(2,1)S(1)}, bf16[448,128]{1,0:T(8,128)(2,1)S(1)}, u32[]{:S(2)}, u32[]{:S(2)}) collective-permute-start(bf16[448,128]{1,0:T(8,128)(2,1)S(1)} %copy-done.14), channel_id=1, source_target_pairs={{0,4},{4,0},{8,12},{12,8},{16,20},{20,16},{24,28},{28,24},{1,5},{5... | collective-permute-start | bytes 344072 | tf_op jit(solution)/shard_map/ppermute | solution.py:253
  620.9 35.2 %collective-permute-start.96 = (bf16[448,128]{1,0:T(8,128)(2,1)S(1)}, bf16[448,128]{1,0:T(8,128)(2,1)S(1)}, u32[]{:S(2)}, u32[]{:S(2)}) collective-permute-start(bf16[448,128]{1,0:T(8,128)(2,1)S(1)} %copy-done.14), channel_id=1, source_target_pairs={{0,24},{4,28},{8,0},{12,4},{16,8},{20,12},{24,16},{28,20},{1,25},{... | collective-permute-start | bytes 344072 | tf_op jit(solution)/shard_map/ppermute | solution.py:253
  625.1 32.0 %collective-permute-start.97 = (bf16[448,128]{1,0:T(8,128)(2,1)S(1)}, bf16[448,128]{1,0:T(8,128)(2,1)S(1)}, u32[]{:S(2)}, u32[]{:S(2)}) collective-permute-start(bf16[448,128]{1,0:T(8,128)(2,1)S(1)} %copy-done.14), channel_id=1, source_target_pairs={{0,16},{4,20},{8,24},{12,28},{16,0},{20,4},{24,8},{28,12},{1,17},{... | collective-permute-start | bytes 344072 | tf_op jit(solution)/shard_map/ppermute | solution.py:253
  (169 other events, 2136.4 us)

commit v3 on v1

v3 whole, which is shorter than its diff:
```python
import functools

import jax
import jax.numpy as jnp
from jax import lax
from jax.experimental import pallas as pl
from jax.experimental.pallas import tpu as pltpu
from jax.sharding import PartitionSpec as P

NQ = 16
QTOK = 32
RANK = 16
ITERS = 2
CORES = 2
NG = NQ // CORES
COLS = NG * RANK
TOKS = NG * QTOK
LANES = 256
PIECES = 2

damping = 0.01
ridge_scale = 1e-06

GD = ("grp", "dp")
f32 = jnp.float32
bf16 = jnp.bfloat16


def params():
    return pltpu.CompilerParams(vmem_limit_bytes=48 * 1024 * 1024)


def chunks(extent):
    return [(at, min(LANES, extent - at)) for at in range(0, extent, LANES)]


def cost(shape, columns):
    count = shape[0] * shape[1] * shape[2]
    return pl.CostEstimate(
        flops=2 * count * columns, bytes_accessed=2 * count, transcendentals=0
    )


def add_image(product, query, image):
    lane = lax.broadcasted_iota(jnp.int32, image.shape, 1)
    image[...] = jnp.where(lane // RANK == query, product, image[...])


def write_image(image, send_ref, keep_ref):
    part, parts = pl.program_id(0), pl.num_programs(0)
    last = pl.program_id(1) == NG - 1

    @pl.when(last & (part < parts - 1))
    def _():
        send_ref[...] = image[...].astype(bf16)

    @pl.when(last & (part == parts - 1))
    def _():
        keep_ref[...] = image[...]


def form_kernel(n_dp, place_ref, *refs):
    out_refs = refs[:n_dp]
    in_ref, eig_ref, basis_ref, rotated_ref, send_ref, keep_ref = refs[n_dp : n_dp + 6]
    weight, left, right, image = refs[n_dp + 6 :]
    part, query = pl.program_id(0), pl.program_id(1)
    cols = eig_ref.shape[1]

    @pl.when(query == 0)
    def _():
        weight[...] = 1.0 / (eig_ref[...] + damping)
        right[...] = jnp.zeros_like(right)

    for at in range(n_dp):

        @pl.when((query == 0) & (part == at))
        def _(at=at):
            left[...] = out_refs[at][...]

    @pl.when(query > 0)
    def _():
        before = pl.ds(pl.multiple_of((query - 1) * QTOK, QTOK), QTOK)
        right[before, :] = jnp.zeros((QTOK, cols), bf16)

    own = pl.ds(pl.multiple_of(query * QTOK, QTOK), QTOK)
    right[own, :] = in_ref[own, :]
    for at, width in chunks(cols):
        span = slice(at, at + width)
        block = jnp.dot(left[...], right[:, span], preferred_element_type=f32)
        rotated_ref[0, :, span] = (block * weight[:, span]).astype(bf16)
    add_image(
        jnp.dot(rotated_ref[0], basis_ref[...], preferred_element_type=f32), query, image
    )
    write_image(image, send_ref, keep_ref)


def form_piece(place, out_parts, rot_in, eigvals, basis, piece):
    n_dp = len(out_parts)
    rows = out_parts[0].shape[0]
    cols = rot_in.shape[1]

    def eig_block(part, query, place_ref):
        return piece * n_dp + lax.rem(place_ref[0] + 1 + part, n_dp), 0

    def fixed(shape):
        return pl.BlockSpec(shape, lambda part, query, _: (0, 0))

    shape = (NG, n_dp * rows, cols)
    return pl.pallas_call(
        functools.partial(form_kernel, n_dp),
        grid_spec=pltpu.PrefetchScalarGridSpec(
            num_scalar_prefetch=1,
            grid=(n_dp, NG),
            in_specs=[fixed((rows, TOKS))] * n_dp
            + [
                fixed((TOKS, cols)),
                pl.BlockSpec((rows, cols), eig_block),
                fixed((cols, COLS)),
            ],
            out_specs=[
                pl.BlockSpec((1, rows, cols), lambda part, query, _: (query, part, 0)),
                pl.BlockSpec(
                    (rows, COLS), lambda part, query, _: (jnp.minimum(part, n_dp - 2), 0)
                ),
                fixed((rows, COLS)),
            ],
            scratch_shapes=[
                pltpu.VMEM((rows, cols), f32),
                pltpu.VMEM((rows, TOKS), bf16),
                pltpu.VMEM((TOKS, cols), bf16),
                pltpu.VMEM((rows, COLS), f32),
            ],
        ),
        out_shape=[
            jax.ShapeDtypeStruct(shape, bf16),
            jax.ShapeDtypeStruct(((n_dp - 1) * rows, COLS), bf16),
            jax.ShapeDtypeStruct((rows, COLS), f32),
        ],
        compiler_params=params(),
        cost_estimate=cost(shape, 600),
        name="form",
    )(place, *out_parts, rot_in, eigvals, basis)


def image_kernel(basis_ref, rotated_ref, send_ref, keep_ref, image):
    add_image(
        jnp.dot(rotated_ref[0], basis_ref[...], preferred_element_type=f32),
        pl.program_id(1),
        image,
    )
    write_image(image, send_ref, keep_ref)


def image_piece(basis, rotated, n_dp):
    _, rows, cols = rotated.shape
    rows = rows // n_dp
    return pl.pallas_call(
        image_kernel,
        grid=(n_dp, NG),
        in_specs=[
            pl.BlockSpec((cols, COLS), lambda part, query: (0, 0)),
            pl.BlockSpec((1, rows, cols), lambda part, query: (query, part, 0)),
        ],
        out_specs=[
            pl.BlockSpec((rows, COLS), lambda part, query: (jnp.minimum(part, n_dp - 2), 0)),
            pl.BlockSpec((rows, COLS), lambda part, query: (0, 0)),
        ],
        out_shape=[
            jax.ShapeDtypeStruct(((n_dp - 1) * rows, COLS), bf16),
            jax.ShapeDtypeStruct((rows, COLS), f32),
        ],
        scratch_shapes=[pltpu.VMEM((rows, COLS), f32)],
        compiler_params=params(),
        cost_estimate=cost(rotated.shape, 300),
        name="image",
    )(basis, rotated)


def return_kernel(n_dp, first, *refs):
    image_refs, rotated_ref = refs[:n_dp], refs[n_dp]
    total_ref, gram_ref, turned = refs[-3:]
    part, query = pl.program_id(0), pl.program_id(1)

    @pl.when((part == 0) & (query == 0))
    def _():
        if first:
            total_ref[...] = jnp.zeros_like(total_ref)
            gram_ref[...] = jnp.zeros_like(gram_ref)
        else:
            total_ref[...] = refs[n_dp + 1][...]
            gram_ref[...] = refs[n_dp + 2][...]

    for at in range(n_dp):

        @pl.when((query == 0) & (part == at))
        def _(at=at):
            image = image_refs[at][...]
            turned[...] = image.astype(f32).T.astype(bf16)
            gram_ref[...] += lax.dot_general(
                image, image, (((0,), (0,)), ((), ())), preferred_element_type=f32
            )

    own = pl.ds(pl.multiple_of(query * RANK, RANK), RANK)
    total_ref[own, :] += jnp.dot(turned[own, :], rotated_ref[0], preferred_element_type=f32)


def return_piece(images, rotated, before):
    n_dp = len(images)
    _, rows, cols = rotated.shape
    rows = rows // n_dp
    first = before is None

    def fixed(shape):
        return pl.BlockSpec(shape, lambda part, query: (0, 0))

    sums = [fixed((COLS, cols)), fixed((COLS, COLS))]
    return pl.pallas_call(
        functools.partial(return_kernel, n_dp, first),
        grid=(n_dp, NG),
        in_specs=[fixed((rows, COLS))] * n_dp
        + [pl.BlockSpec((1, rows, cols), lambda part, query: (query, part, 0))]
        + ([] if first else sums),
        out_specs=sums,
        out_shape=[
            jax.ShapeDtypeStruct((COLS, cols), f32),
            jax.ShapeDtypeStruct((COLS, COLS), f32),
        ],
        scratch_shapes=[pltpu.VMEM((COLS, rows), bf16)],
        compiler_params=params(),
        cost_estimate=cost(rotated.shape, 300),
        name="returned",
    )(*images, rotated, *([] if first else before))


def lower_inverse(gram):
    shape = (NG, RANK, COLS)
    row = lax.broadcasted_iota(jnp.int32, shape, 1)
    lane = lax.broadcasted_iota(jnp.int32, shape, 2)
    same = lane // RANK == lax.broadcasted_iota(jnp.int32, shape, 0)
    col = lane % RANK
    eye = same & (col == row)
    gram = jnp.where(same, gram.reshape(shape), 0.0)
    trace = jnp.sum(
        jnp.sum(jnp.where(eye, gram, 0.0), axis=2, keepdims=True), axis=1, keepdims=True
    )
    left = gram + jnp.where(eye, ridge_scale * (trace / RANK), 0.0)
    right = jnp.where(eye, 1.0, 0.0)
    for step in range(RANK):
        column = jnp.sum(jnp.where(col == step, left, 0.0), axis=2, keepdims=True)
        pivot = column[:, step : step + 1, :]
        factor = jnp.where(row[:, :, :1] > step, column / pivot, 0.0)
        right = right - factor * right[:, step : step + 1, :]
        left = left - factor * left[:, step : step + 1, :]
    diagonal = jnp.sum(jnp.where(eye, left, 0.0), axis=2, keepdims=True)
    return (right * lax.rsqrt(diagonal)).reshape(COLS, COLS)


def normalize_kernel(scale, total_ref, got_ref, gram_ref, gram_got_ref, basis_ref, inverse_ref):
    inverse = lower_inverse((gram_ref[...] + gram_got_ref[...]) * scale)
    inverse_ref[...] = inverse
    total = total_ref[...] + got_ref[...].astype(f32)
    basis_ref[...] = lax.dot_general(
        total,
        inverse,
        (((0,), (1,)), ((), ())),
        precision=lax.Precision.HIGHEST,
        preferred_element_type=f32,
    ).astype(bf16)


def normalize(total, got, gram, gram_got, scale):
    return pl.pallas_call(
        functools.partial(normalize_kernel, scale),
        out_shape=[
            jax.ShapeDtypeStruct((total.shape[1], COLS), bf16),
            jax.ShapeDtypeStruct((COLS, COLS), f32),
        ],
        compiler_params=params(),
        name="normalize",
    )(total, got, gram, gram_got)


def turned_by(count, step):
    return [(i, (i + step) % count) for i in range(count)]


def crossed(count, step):
    return [(i, i ^ step) for i in range(count)]


def swap_cores(part, n_width):
    return lax.ppermute(part, "width", crossed(n_width, 1))


def reduce_gather(sends, keep, n_grp, n_dp, even=False):
    rows = keep.shape[0]
    total = keep
    for part in range(n_dp - 1):
        send = sends[part * rows : (part + 1) * rows]
        total = total + lax.ppermute(send, "dp", turned_by(n_dp, part + 1)).astype(f32)
    step = 1
    while step < n_grp:
        sent = total.astype(bf16)
        got = lax.ppermute(sent, "grp", crossed(n_grp, step)).astype(f32)
        total = (sent.astype(f32) if even else total) + got
        step *= 2
    own = total.astype(bf16)
    others = [
        lax.ppermute(own, "dp", turned_by(n_dp, n_dp - 1 - part)) for part in range(n_dp - 1)
    ]
    return others + [own]


def unrolled(parts, dp):
    whole = jnp.stack(parts)
    whole = jnp.roll(whole, dp + 1, axis=0)
    return whole.reshape((-1,) + whole.shape[2:])


def split_parts(part, dp, n_dp, piece, pieces):
    rows = part.shape[0] // (pieces * n_dp)
    taken = [
        lax.dynamic_slice_in_dim(part, piece * n_dp * rows + (dp + 1 + at) % n_dp * rows, rows, 0)
        for at in range(n_dp)
    ]
    return jnp.concatenate(taken[:-1], axis=0).astype(bf16), taken[-1].astype(f32)


def sum_scatter(part, axes, count):
    pieces = lax.all_to_all(part.astype(bf16), axes, 0, 0, tiled=True)
    pieces = pieces.reshape((count, part.shape[0] // count) + part.shape[1:])
    return jnp.sum(pieces.astype(f32), axis=0)


def gather_rows(piece, axes, count):
    copies = jnp.broadcast_to(piece[None], (count,) + piece.shape)
    whole = lax.all_to_all(copies, axes, 0, 0, tiled=True)
    return whole.reshape((count * piece.shape[0],) + piece.shape[1:])


def make_per_device(n_grp, n_dp, n_width):
    n_gd = n_grp * n_dp

    def per_device(
        query_out, query_in, eigen_out, eigen_in, eigvals, start, grads_out, gate_pre, up_pre
    ):
        dp = lax.axis_index("dp")
        core = lax.axis_index("width") % CORES
        place = jnp.stack([dp]).astype(jnp.int32)
        scale = 1.0 / (eigen_out.shape[0] * n_gd)
        rows_out = eigvals.shape[0]

        def rows_of(array, index):
            return lax.dynamic_slice_in_dim(array, index * TOKS, TOKS, 0)

        def rotate_out(queries):
            return lax.dot_general(
                eigen_out, queries, (((0,), (1,)), ((), ())), preferred_element_type=f32
            )

        theirs_out = rotate_out(rows_of(query_out, 1 - core)).astype(bf16)
        theirs_out = swap_cores(theirs_out, n_width)
        mine_out = rotate_out(rows_of(query_out, core))
        theirs_in = jnp.dot(rows_of(query_in, 1 - core), eigen_in, preferred_element_type=f32)
        theirs_in = swap_cores(theirs_in, n_width)
        mine_in = jnp.dot(rows_of(query_in, core), eigen_in, preferred_element_type=f32)
        total_in = mine_in + theirs_in
        step = 2
        while step < n_width:
            got = lax.ppermute(total_in.astype(bf16), "width", crossed(n_width, step))
            total_in = total_in + got.astype(f32)
            step *= 2
        rot_in = total_in.astype(bf16)
        eig_sent, _, _ = lax.optimization_barrier((eigvals, theirs_out, theirs_in))
        eig_theirs = swap_cores(eig_sent, n_width)

        rot_out = []
        for part in (mine_out, theirs_out):
            for piece in range(PIECES):
                sends, keep = split_parts(part, dp, n_dp, piece, PIECES)
                rot_out.append(reduce_gather(sends, keep, n_grp, n_dp))
        basis = lax.dynamic_slice_in_dim(start, core * COLS, COLS, 1)
        count = len(rot_out)
        rotated = []
        for iteration in range(ITERS):
            images = []
            for at in range(count):
                if iteration == 0:
                    eig = eigvals if at < PIECES else eig_theirs
                    block, sends, keep = form_piece(
                        place, rot_out[at], rot_in, eig, basis, at % PIECES
                    )
                    rotated.append(block)
                else:
                    sends, keep = image_piece(basis, rotated[at], n_dp)
                images.append(reduce_gather(sends, keep, n_grp, n_dp))
            sums = None
            for at in range(count):
                sums = return_piece(images[at], rotated[at], sums)
            total, gram = sums
            step = 2
            while True:
                got = lax.ppermute(total.astype(bf16), "width", crossed(n_width, step))
                gram_got = lax.ppermute(gram, "width", crossed(n_width, step))
                step *= 2
                if step >= n_width:
                    break
                total = total + got.astype(f32)
                gram = gram + gram_got
            basis, inverse = normalize(total, got, gram, gram_got, scale)

        def columns(mine, theirs):
            return jnp.where(
                core == 0,
                jnp.concatenate([mine, theirs], axis=1),
                jnp.concatenate([theirs, mine], axis=1),
            )

        image = jnp.concatenate([unrolled(parts, dp) for parts in images], axis=0)
        basis_out = lax.dot_general(
            image.astype(f32),
            inverse,
            (((1,), (1,)), ((), ())),
            precision=lax.Precision.HIGHEST,
            preferred_element_type=f32,
        ).astype(bf16)
        out_cols = columns(basis_out[:rows_out], swap_cores(basis_out[rows_out:], n_width))
        part_factor_out = jnp.dot(eigen_out, out_cols, preferred_element_type=f32)
        share = sum_scatter(part_factor_out, "width", n_width).astype(bf16)
        piece_rows = share.shape[0]
        gathered = gather_rows(share, GD, n_gd)
        mixed = lax.all_to_all(gathered, "width", 0, 0, tiled=True)
        out_factor = (
            mixed.reshape(n_width, n_gd // n_width, piece_rows, NQ * RANK)
            .transpose(1, 0, 2, 3)
            .reshape(rows_out, NQ * RANK)
        )
        hidden = (jax.nn.silu(gate_pre.astype(f32)) * up_pre.astype(f32)).astype(bf16)
        hidden = lax.optimization_barrier(hidden)
        in_cols = columns(basis, swap_cores(basis, n_width))
        part_factor_in = jnp.dot(eigen_in, in_cols, preferred_element_type=f32)
        in_factors = []
        for piece in range(2 * PIECES):
            sends, keep = split_parts(part_factor_in, dp, n_dp, piece, 2 * PIECES)
            in_factors.append(unrolled(reduce_gather(sends, keep, n_grp, n_dp, even=True), dp))
        in_factor = jnp.concatenate(in_factors, axis=0)
        proj_out = jnp.dot(grads_out, out_factor, preferred_element_type=f32)
        proj_in = jnp.dot(hidden, in_factor, preferred_element_type=f32)
        proj_out = sum_scatter(proj_out, "width", n_width)
        proj_in = sum_scatter(proj_in, "width", n_width)
        scores = (proj_out * proj_in).reshape(proj_out.shape[0], NQ, RANK).sum(axis=2).T
        return (scores, out_factor, in_factor)

    return per_device


def solution(mesh):
    return jax.shard_map(
        make_per_device(mesh.shape["grp"], mesh.shape["dp"], mesh.shape["width"]),
        mesh=mesh,
        in_specs=(
            P(None, GD),
            P(None, "width"),
            P(GD, "width"),
            P("width", GD),
            P("width", GD),
            P(GD, None),
            P(GD, "width"),
            P(GD, "width"),
            P(GD, "width"),
        ),
        out_specs=(P(None, GD + ("width",)), P("width", None), P("width", None)),
        check_vma=False,
    )
```

time: 710 us -> 702 us (0.989)
  Pallas kernels: 6.1 us -> 322 us
  matrix products: 262 us -> 36.1 us
  blocking collectives: 162 us -> 0 us
  starting transfers between devices: 44.2 us -> 97.5 us
  waiting for transfers between devices: 175 us -> 190 us
  local copies, waits for them, and re-layouts: 23.1 us -> 13.6 us
    pallas_call x2 -> x18, Pallas kernels: 6.1 us -> 322 us  [the longest x8 132 us: return_piece(): pl.pallas_call(functools.partial(return_kernel, n_dp, first), grid=(n_dp,...]
    dot_general x15 -> x9, matrix products: 262 us -> 36.1 us  [the longest x1 8.63 us: per_device(): jnp.dot(rows_of(query_in, core), eigen_in, preferred_element_type=f32)]
    all_to_all x5 -> x0, blocking collectives: 162 us -> none  [the longest x3 105 us: sum_scatter(): pieces = lax.all_to_all(part.astype(jnp.bfloat16), axes, 0, 0, tiled=True)]
    ppermute x12 -> x74, waiting for transfers between devices: 75.9 us -> 171 us  [the longest x32 119 us: reduce_gather(): got = lax.ppermute(sent, 'grp', crossed(n_grp, step)).astype(f32)]
    ppermute x12 -> x74, starting transfers between devices: 9.44 us -> 79.4 us  [the longest x32 32.8 us: reduce_gather(): got = lax.ppermute(sent, 'grp', crossed(n_grp, step)).astype(f32)]
    all_to_all x3 -> x1, waiting for transfers between devices: 40.1 us -> 0.01 us  [gather_rows(): whole = lax.all_to_all(copies, axes, 0, 0, tiled=True)]
    all_to_all x4 -> x3, waiting for transfers between devices: 46.8 us -> 9.27 us  [sum_scatter(): pieces = lax.all_to_all(part.astype(bf16), axes, 0, 0, tiled=True)]
    convert_element_type x5 -> x45, other arithmetic: 10.5 us -> 23.7 us  [the longest x25 12.7 us: reduce_gather(): sent = total.astype(bf16)]
  transfers between devices with their start and end apart: 20 -> 79, of which waited for: 13 -> 43; matrix products, arithmetic and copies ran while one was open for 10% -> 10% of each run, Pallas kernels for 0% -> 33%
where the time goes in v3:
time: 702 us; the launch traced here: 691 us
  Pallas kernels  322 us (46%)
  waiting for transfers between devices  190 us (27%)
  starting transfers between devices  97.5 us (14%)
  matrix products  36.1 us (5%)
  other arithmetic  29.8 us (4%)
  local copies, waits for them, and re-layouts  13.6 us (2%)
    pallas_call x8, Pallas kernels, return_piece(): pl.pallas_call(functools.partial(return_kernel, n_dp, first), grid=(n_dp,...  132 us
    ppermute x32, waiting for transfers between devices, reduce_gather(): got = lax.ppermute(sent, 'grp', crossed(n_grp, step)).astype(f32)  119 us
    pallas_call x4, Pallas kernels, form_piece(): pl.pallas_call(functools.partial(form_kernel, n_dp), grid_spec=pltpu.Pref...  109 us
    pallas_call x4, Pallas kernels, image_piece(): pl.pallas_call(image_kernel, grid=(n_dp, NG), in_specs=[pl.BlockSpec((col...  75.5 us
    ppermute x32, starting transfers between devices, reduce_gather(): got = lax.ppermute(sent, 'grp', crossed(n_grp, step)).astype(f32)  32.8 us
    ppermute x16, waiting for transfers between devices, reduce_gather(): lax.ppermute(send, 'dp', turned_by(n_dp, part + 1)).astype(f32)  29.9 us
    ppermute x16, starting transfers between devices, reduce_gather(): lax.ppermute(own, 'dp', turned_by(n_dp, n_dp - 1 - part))  20.9 us
    ppermute x16, starting transfers between devices, reduce_gather(): lax.ppermute(send, 'dp', turned_by(n_dp, part + 1)).astype(f32)  18 us
  transfers between devices with their start and end apart: 79, of which 43 were waited for; matrix products, arithmetic and copies ran while one was open for 10% of the time, Pallas kernels for 33%

profile of v3, /device:TPU:0, one launch (start us, length us, event | category | flops | bytes accessed | tf_op | source)
XLA Modules:
  0.0 691.2 jit_solution(1718555898022817673)
XLA Ops:
  0.7 7.7 %fusion.6 = f32[256,1792]{1,0:T(8,128)S(1)} fusion(bf16[3584,1792]{1,0:T(8,128)(2,1)} %param.16, bf16[512,3584]{1,0:T(8,128)(2,1)} %param.14, s32[]{:T(128)S(6)} %select_n.128), kind=kOutput, calls=%fused_computation.13 | convolution fusion | flops 3288334336 | bytes 16515076 | tf_op jit(solution)/shard_map/dot_general | solution.py:364
  23.1 7.3 %collective-permute-done.28 = bf16[512,256]{1,0:T(8,128)(2,1)S(1)} collective-permute-done((bf16[512,256]{1,0:T(8,128)(2,1)}, bf16[512,256]{1,0:T(8,128)(2,1)S(1)}, u32[]{:S(2)}, u32[]{:S(2)}) %collective-permute-start.28) | collective-permute-done | bytes 262176 | tf_op jit(solution)/shard_map/ppermute | solution.py:300
  49.0 7.4 %collective-permute-done.30 = bf16[512,256]{1,0:T(8,128)(2,1)} collective-permute-done((bf16[512,256]{1,0:T(8,128)(2,1)}, bf16[512,256]{1,0:T(8,128)(2,1)}, u32[]{:S(2)}, u32[]{:S(2)}) %collective-permute-start.30) | collective-permute-done | bytes 262176 | tf_op jit(solution)/shard_map/ppermute | solution.py:304
  66.0 8.6 %fusion.99 = (bf16[256,1792]{1,0:T(8,128)(2,1)S(1)}, f32[256,1792]{1,0:T(8,128)S(1)}) fusion(f32[256,1792]{1,0:T(8,128)} %collective-permute-done.5, bf16[3584,1792]{1,0:T(8,128)(2,1)} %param.16, bf16[512,3584]{1,0:T(8,128)(2,1)S(1)} %copy-done.10, s32[]{:T(128)S(6)} %select_n.133), kind=kOutput, calls=%fused_computation.205 | convolution fusion | flops 3289251840 | bytes 19267588 | tf_op jit(solution)/shard_map/dot_general | solution.py:366
  76.5 7.1 %collective-permute-done.14 = bf16[512,256]{1,0:T(8,128)(2,1)S(1)} collective-permute-done((bf16[512,256]{1,0:T(8,128)(2,1)S(1)}, bf16[512,256]{1,0:T(8,128)(2,1)S(1)}, u32[]{:S(2)}, u32[]{:S(2)}) %collective-permute-start.14) | collective-permute-done | bytes 262176 | tf_op jit(solution)/shard_map/ppermute | solution.py:304
  87.4 9.4 %collective-permute-done.3 = bf16[512,256]{1,0:T(8,128)(2,1)S(1)} collective-permute-done((bf16[512,256]{1,0:T(8,128)(2,1)S(1)}, bf16[512,256]{1,0:T(8,128)(2,1)S(1)}, u32[]{:S(2)}, u32[]{:S(2)}) %collective-permute-start.3) | collective-permute-done | bytes 262176 | tf_op jit(solution)/shard_map/ppermute | solution.py:304
  99.3 27.3 %form.7 = (bf16[8,1024,1792]{2,1,0:T(8,128)(2,1)}, bf16[512,128]{1,0:T(8,128)(2,1)S(1)}, f32[512,128]{1,0:T(8,128)S(1)}) custom-call(s32[1]{0:T(128)} %bitcast.place_ref, bf16[512,256]{1,0:T(8,128)(2,1)S(1)} %collective-permute-done.31.refs_0_, bf16[512,256]{1,0:T(8,128)(2,1)S(1)} %get-tuple-element.93.refs_1_, ...), custom_call_target="tpu_custom_call" | custom-call | flops 17616076800 | bytes 29360128 | tf_op jit(solution)/shard_map/form/pallas_call | solution.py:109
  126.6 27.2 %form.6 = (bf16[8,1024,1792]{2,1,0:T(8,128)(2,1)}, bf16[512,128]{1,0:T(8,128)(2,1)S(1)}, f32[512,128]{1,0:T(8,128)S(1)}) custom-call(s32[1]{0:T(128)} %bitcast.place_ref, bf16[512,256]{1,0:T(8,128)(2,1)S(1)} %collective-permute-done.23.refs_0_, bf16[512,256]{1,0:T(8,128)(2,1)S(1)} %add_convert_fusion.10.refs_1_, ...), custom_call_target="tpu_custom_call" | custom-call | flops 17616076800 | bytes 29360128 | tf_op jit(solution)/shard_map/form/pallas_call | solution.py:109
  179.3 16.5 %returned.8 = (f32[128,1792]{1,0:T(8,128)S(1)}, f32[128,128]{1,0:T(8,128)S(1)}) custom-call(bf16[512,128]{1,0:T(8,128)(2,1)S(1)} %collective-permute-done.35.refs_0_, bf16[512,128]{1,0:T(8,128)(2,1)S(1)} %add_convert_fusion.17.refs_1_, bf16[8,1024,1792]{2,1,0:T(8,128)(2,1)} %get-tuple-element.57.refs_2_.rotated_ref), custom_call_target="tpu_custom_call" | custom-call | flops 8808038400 | bytes 29360128 | tf_op jit(solution)/shard_map/returned/pallas_call | solution.py:217
  195.8 16.5 %returned.9 = (f32[128,1792]{1,0:T(8,128)S(1)}, f32[128,128]{1,0:T(8,128)S(1)}) custom-call(bf16[512,128]{1,0:T(8,128)(2,1)S(1)} %collective-permute-done.27.refs_0_, bf16[512,128]{1,0:T(8,128)(2,1)S(1)} %add_convert_fusion.18.refs_1_, bf16[8,1024,1792]{2,1,0:T(8,128)(2,1)} %get-tuple-element.54.refs_2_.rotated_ref, ...), custom_call_target="tpu_custom_call" | custom-call | flops 8808038400 | bytes 29360128 | tf_op jit(solution)/shard_map/returned/pallas_call | solution.py:217
  212.3 27.2 %form.5 = (bf16[8,1024,1792]{2,1,0:T(8,128)(2,1)}, bf16[512,128]{1,0:T(8,128)(2,1)S(1)}, f32[512,128]{1,0:T(8,128)S(1)}) custom-call(s32[1]{0:T(128)} %bitcast.place_ref, bf16[512,256]{1,0:T(8,128)(2,1)S(1)} %collective-permute-done.15.refs_0_, bf16[512,256]{1,0:T(8,128)(2,1)S(1)} %get-tuple-element.101.refs_1_, ...), custom_call_target="tpu_custom_call" | custom-call | flops 17616076800 | bytes 29360128 | tf_op jit(solution)/shard_map/form/pallas_call | solution.py:109
  241.2 27.2 %form.4 = (bf16[8,1024,1792]{2,1,0:T(8,128)(2,1)}, bf16[512,128]{1,0:T(8,128)(2,1)S(1)}, f32[512,128]{1,0:T(8,128)S(1)}) custom-call(s32[1]{0:T(128)} %bitcast.place_ref, bf16[512,256]{1,0:T(8,128)(2,1)S(1)} %collective-permute-done.4.refs_0_, bf16[512,256]{1,0:T(8,128)(2,1)S(1)} %add_convert_fusion.12.refs_1_, ...), custom_call_target="tpu_custom_call" | custom-call | flops 17616076800 | bytes 29360128 | tf_op jit(solution)/shard_map/form/pallas_call | solution.py:109
  287.5 16.5 %returned.10 = (f32[128,1792]{1,0:T(8,128)S(1)}, f32[128,128]{1,0:T(8,128)S(1)}) custom-call(bf16[512,128]{1,0:T(8,128)(2,1)S(1)} %collective-permute-done.19.refs_0_, bf16[512,128]{1,0:T(8,128)(2,1)S(1)} %add_convert_fusion.19.refs_1_, bf16[8,1024,1792]{2,1,0:T(8,128)(2,1)} %get-tuple-element.51.refs_2_.rotated_ref, ...), custom_call_target="tpu_custom_call" | custom-call | flops 8808038400 | bytes 29360128 | tf_op jit(solution)/shard_map/returned/pallas_call | solution.py:217
  304.0 16.7 %returned.11 = (f32[128,1792]{1,0:T(8,128)S(1)}, f32[128,128]{1,0:T(8,128)S(1)}) custom-call(bf16[512,128]{1,0:T(8,128)(2,1)S(1)} %collective-permute-done.11.refs_0_, bf16[512,128]{1,0:T(8,128)(2,1)S(1)} %add_convert_fusion.20.refs_1_, bf16[8,1024,1792]{2,1,0:T(8,128)(2,1)} %get-tuple-element.48.refs_2_.rotated_ref, ...), custom_call_target="tpu_custom_call" | custom-call | flops 8808038400 | bytes 29360128 | tf_op jit(solution)/shard_map/returned/pallas_call | solution.py:217
  323.6 7.5 %collective-permute-done.37.gram_got_ref = f32[128,128]{1,0:T(8,128)} collective-permute-done((f32[128,128]{1,0:T(8,128)S(1)}, f32[128,128]{1,0:T(8,128)}, u32[]{:S(2)}, u32[]{:S(2)}) %collective-permute-start.37) | collective-permute-done | bytes 65568 | tf_op jit(solution)/shard_map/ppermute | solution.py:404
  334.3 18.9 %image.7 = (bf16[512,128]{1,0:T(8,128)(2,1)S(1)}, f32[512,128]{1,0:T(8,128)S(1)}) custom-call(bf16[1792,128]{1,0:T(8,128)(2,1)S(1)} %get-tuple-element.66.basis_ref, bf16[8,1024,1792]{2,1,0:T(8,128)(2,1)} %get-tuple-element.48.refs_2_.rotated_ref), custom_call_target="tpu_custom_call" | custom-call | flops 8808038400 | bytes 29360128 | tf_op jit(solution)/shard_map/image/pallas_call | solution.py:157
  353.2 18.9 %image.6 = (bf16[512,128]{1,0:T(8,128)(2,1)S(1)}, f32[512,128]{1,0:T(8,128)S(1)}) custom-call(bf16[1792,128]{1,0:T(8,128)(2,1)S(1)} %get-tuple-element.66.basis_ref, bf16[8,1024,1792]{2,1,0:T(8,128)(2,1)} %get-tuple-element.51.refs_2_.rotated_ref), custom_call_target="tpu_custom_call" | custom-call | flops 8808038400 | bytes 29360128 | tf_op jit(solution)/shard_map/image/pallas_call | solution.py:157
  372.0 18.9 %image.5 = (bf16[512,128]{1,0:T(8,128)(2,1)S(1)}, f32[512,128]{1,0:T(8,128)S(1)}) custom-call(bf16[1792,128]{1,0:T(8,128)(2,1)S(1)} %get-tuple-element.66.basis_ref, bf16[8,1024,1792]{2,1,0:T(8,128)(2,1)} %get-tuple-element.54.refs_2_.rotated_ref), custom_call_target="tpu_custom_call" | custom-call | flops 8808038400 | bytes 29360128 | tf_op jit(solution)/shard_map/image/pallas_call | solution.py:157
  391.8 18.9 %image.4 = (bf16[512,128]{1,0:T(8,128)(2,1)S(1)}, f32[512,128]{1,0:T(8,128)S(1)}) custom-call(bf16[1792,128]{1,0:T(8,128)(2,1)S(1)} %get-tuple-element.66.basis_ref, bf16[8,1024,1792]{2,1,0:T(8,128)(2,1)} %get-tuple-element.57.refs_2_.rotated_ref), custom_call_target="tpu_custom_call" | custom-call | flops 8808038400 | bytes 29360128 | tf_op jit(solution)/shard_map/image/pallas_call | solution.py:157
  430.8 4.9 collective-permute-done.48
  443.7 16.5 %returned.12 = (f32[128,1792]{1,0:T(8,128)S(1)}, f32[128,128]{1,0:T(8,128)S(1)}) custom-call(bf16[512,128]{1,0:T(8,128)(2,1)S(1)} %collective-permute-done.41.refs_0_, bf16[512,128]{1,0:T(8,128)(2,1)S(1)} %add_convert_fusion.16.refs_1_, bf16[8,1024,1792]{2,1,0:T(8,128)(2,1)} %get-tuple-element.57.refs_2_.rotated_ref), custom_call_target="tpu_custom_call" | custom-call | flops 8808038400 | bytes 29360128 | tf_op jit(solution)/shard_map/returned/pallas_call | solution.py:217
  460.2 16.5 %returned.13 = (f32[128,1792]{1,0:T(8,128)S(1)}, f32[128,128]{1,0:T(8,128)S(1)}) custom-call(bf16[512,128]{1,0:T(8,128)(2,1)S(1)} %collective-permute-done.45.refs_0_, bf16[512,128]{1,0:T(8,128)(2,1)S(1)} %add_convert_fusion.15.refs_1_, bf16[8,1024,1792]{2,1,0:T(8,128)(2,1)} %get-tuple-element.54.refs_2_.rotated_ref, ...), custom_call_target="tpu_custom_call" | custom-call | flops 8808038400 | bytes 29360128 | tf_op jit(solution)/shard_map/returned/pallas_call | solution.py:217
  476.7 16.5 %returned.14 = (f32[128,1792]{1,0:T(8,128)S(1)}, f32[128,128]{1,0:T(8,128)S(1)}) custom-call(bf16[512,128]{1,0:T(8,128)(2,1)S(1)} %collective-permute-done.49.refs_0_, bf16[512,128]{1,0:T(8,128)(2,1)S(1)} %add_convert_fusion.14.refs_1_, bf16[8,1024,1792]{2,1,0:T(8,128)(2,1)} %get-tuple-element.51.refs_2_.rotated_ref, ...), custom_call_target="tpu_custom_call" | custom-call | flops 8808038400 | bytes 29360128 | tf_op jit(solution)/shard_map/returned/pallas_call | solution.py:217
  493.2 16.5 %returned.15 = (f32[128,1792]{1,0:T(8,128)S(1)}, f32[128,128]{1,0:T(8,128)S(1)}) custom-call(bf16[512,128]{1,0:T(8,128)(2,1)S(1)} %collective-permute-done.53.refs_0_, bf16[512,128]{1,0:T(8,128)(2,1)S(1)} %add_convert_fusion.13.refs_1_, bf16[8,1024,1792]{2,1,0:T(8,128)(2,1)} %get-tuple-element.48.refs_2_.rotated_ref, ...), custom_call_target="tpu_custom_call" | custom-call | flops 8808038400 | bytes 29360128 | tf_op jit(solution)/shard_map/returned/pallas_call | solution.py:217
  512.7 6.3 collective-permute-done.55.gram_got_ref
  523.3 6.9 fusion.23
  546.9 5.6 collective-permute-done.66
  577.7 22.6 %collective-permute-done.63 = bf16[448,256]{0,1:T(8,128)(2,1)} collective-permute-done((bf16[448,256]{0,1:T(8,128)(2,1)S(1)}, bf16[448,256]{0,1:T(8,128)(2,1)}, u32[]{:S(2)}, u32[]{:S(2)}) %collective-permute-start.63) | collective-permute-done | bytes 229408 | tf_op jit(solution)/shard_map/ppermute | solution.py:304
  607.4 17.9 %collective-permute-done.72 = bf16[448,256]{0,1:T(8,128)(2,1)S(1)} collective-permute-done((bf16[448,256]{0,1:T(8,128)(2,1)S(1)}, bf16[448,256]{0,1:T(8,128)(2,1)S(1)}, u32[]{:S(2)}, u32[]{:S(2)}) %collective-permute-start.72) | collective-permute-done | bytes 229408 | tf_op jit(solution)/shard_map/ppermute | solution.py:304
  641.6 5.0 fusion.4
  661.6 9.7 %all-to-all-done.2 = bf16[4,512,256]{2,1,0:T(8,128)(2,1)S(1)} async-done(((bf16[4,512,256]{2,1,0:T(8,128)(2,1)}), bf16[4,512,256]{2,1,0:T(8,128)(2,1)S(1)}, u32[]{:S(2)}, u32[]{:S(2)}) %all-to-all-start.2) | async-done | bytes 1048608 | tf_op jit(solution)/shard_map/all_to_all | solution.py:432
  684.2 5.9 all-to-all-done.3
  (248 shorter events, 233.0 us)
Async XLA Ops:
  13.8 198.5 %collective-permute-start.7 = (f32[2048,1792]{1,0:T(8,128)}, f32[2048,1792]{1,0:T(8,128)}, u32[]{:S(2)}, u32[]{:S(2)}) collective-permute-start(f32[2048,1792]{1,0:T(8,128)} %refs_3_.3), channel_id=1, source_target_pairs={{0,1},{1,0},{2,3},{3,2},{4,5},{5,4},{6,7},{7,6},{8,9},{9,8},{10,11... | collective-permute-start | bytes 44040200 | tf_op jit(solution)/shard_map/ppermute | solution.py:292
  48.5 15.5 %collective-permute-start.13 = (bf16[512,256]{1,0:T(8,128)(2,1)S(1)}, bf16[512,256]{1,0:T(8,128)(2,1)S(1)}, u32[]{:S(2)}, u32[]{:S(2)}) collective-permute-start(bf16[512,256]{1,0:T(8,128)(2,1)S(1)} %fusion.50), channel_id=1, source_target_pairs={{0,8},{8,0},{16,24},{24,16},{1,9},{9,1},{17,25},{25,17},{2,10},{10... | collective-permute-start | bytes 786440 | tf_op jit(solution)/shard_map/ppermute | solution.py:304
  61.2 23.3 %collective-permute-start.22 = (bf16[512,256]{1,0:T(8,128)(2,1)S(1)}, bf16[512,256]{1,0:T(8,128)(2,1)S(1)}, u32[]{:S(2)}, u32[]{:S(2)}) collective-permute-start(bf16[512,256]{1,0:T(8,128)(2,1)S(1)} %get-tuple-element.94), channel_id=1, source_target_pairs={{0,16},{8,24},{16,0},{24,8},{1,17},{9,25},{17,1},{25,9},{2,18},{10... | collective-permute-start | bytes 786440 | tf_op jit(solution)/shard_map/ppermute | solution.py:304
  64.2 19.4 %collective-permute-start.14 = (bf16[512,256]{1,0:T(8,128)(2,1)S(1)}, bf16[512,256]{1,0:T(8,128)(2,1)S(1)}, u32[]{:S(2)}, u32[]{:S(2)}) collective-permute-start(bf16[512,256]{1,0:T(8,128)(2,1)S(1)} %get-tuple-element.103), channel_id=1, source_target_pairs={{0,16},{8,24},{16,0},{24,8},{1,17},{9,25},{17,1},{25,9},{2,18},{10... | collective-permute-start | bytes 786440 | tf_op jit(solution)/shard_map/ppermute | solution.py:304
  64.4 19.1 %collective-permute-start.2 = (bf16[512,256]{1,0:T(8,128)(2,1)S(1)}, bf16[512,256]{1,0:T(8,128)(2,1)S(1)}, u32[]{:S(2)}, u32[]{:S(2)}) collective-permute-start(bf16[512,256]{1,0:T(8,128)(2,1)S(1)} %get-tuple-element.104), channel_id=1, source_target_pairs={{0,8},{8,0},{16,24},{24,16},{1,9},{9,1},{17,25},{25,17},{2,10},{10... | collective-permute-start | bytes 786440 | tf_op jit(solution)/shard_map/ppermute | solution.py:304
  74.6 22.4 %collective-permute-start.6 = (bf16[256,1792]{1,0:T(8,128)(2,1)S(1)}, bf16[256,1792]{1,0:T(8,128)(2,1)S(1)}, u32[]{:S(2)}, u32[]{:S(2)}) collective-permute-start(bf16[256,1792]{1,0:T(8,128)(2,1)S(1)} %get-tuple-element.107), channel_id=1, source_target_pairs={{0,2},{1,3},{2,0},{3,1},{4,6},{5,7},{6,4},{7,5},{8,10},{9,11},{10,... | collective-permute-start | bytes 2752520 | tf_op jit(solution)/shard_map/ppermute | solution.py:370
  83.9 15.3 %collective-permute-start.31 = (bf16[512,256]{1,0:T(8,128)(2,1)S(1)}, bf16[512,256]{1,0:T(8,128)(2,1)S(1)}, u32[]{:S(2)}, u32[]{:S(2)}) collective-permute-start(bf16[512,256]{1,0:T(8,128)(2,1)S(1)} %get-tuple-element.93.refs_1_), channel_id=1, source_target_pairs={{0,4},{4,0},{1,5},{5,1},{2,6},{6,2},{3,7},{7,3},{8,12},{12,8},{9,1... | collective-permute-start | bytes 786440 | tf_op jit(solution)/shard_map/ppermute | solution.py:309
  85.8 40.8 %collective-permute-start.23 = (bf16[512,256]{1,0:T(8,128)(2,1)S(1)}, bf16[512,256]{1,0:T(8,128)(2,1)S(1)}, u32[]{:S(2)}, u32[]{:S(2)}) collective-permute-start(bf16[512,256]{1,0:T(8,128)(2,1)S(1)} %add_convert_fusion.10.refs_1_), channel_id=1, source_target_pairs={{0,4},{4,0},{1,5},{5,1},{2,6},{6,2},{3,7},{7,3},{8,12},{12,8},{9,1... | collective-permute-start | bytes 786440 | tf_op jit(solution)/shard_map/ppermute | solution.py:309
  96.9 115.4 %collective-permute-start.15 = (bf16[512,256]{1,0:T(8,128)(2,1)S(1)}, bf16[512,256]{1,0:T(8,128)(2,1)S(1)}, u32[]{:S(2)}, u32[]{:S(2)}) collective-permute-start(bf16[512,256]{1,0:T(8,128)(2,1)S(1)} %get-tuple-element.101.refs_1_), channel_id=1, source_target_pairs={{0,4},{4,0},{1,5},{5,1},{2,6},{6,2},{3,7},{7,3},{8,12},{12,8},{9,1... | collective-permute-start | bytes 786440 | tf_op jit(solution)/shard_map/ppermute | solution.py:309
  97.0 144.2 %collective-permute-start.4 = (bf16[512,256]{1,0:T(8,128)(2,1)S(1)}, bf16[512,256]{1,0:T(8,128)(2,1)S(1)}, u32[]{:S(2)}, u32[]{:S(2)}) collective-permute-start(bf16[512,256]{1,0:T(8,128)(2,1)S(1)} %add_convert_fusion.12.refs_1_), channel_id=1, source_target_pairs={{0,4},{4,0},{1,5},{5,1},{2,6},{6,2},{3,7},{7,3},{8,12},{12,8},{9,1... | collective-permute-start | bytes 786440 | tf_op jit(solution)/shard_map/ppermute | solution.py:309
  126.6 29.2 %collective-permute-start.32 = (bf16[512,128]{1,0:T(8,128)(2,1)S(1)}, bf16[512,128]{1,0:T(8,128)(2,1)S(1)}, u32[]{:S(2)}, u32[]{:S(2)}) collective-permute-start(bf16[512,128]{1,0:T(8,128)(2,1)S(1)} %get-tuple-element.56), channel_id=1, source_target_pairs={{0,4},{4,0},{1,5},{5,1},{2,6},{6,2},{3,7},{7,3},{8,12},{12,8},{9,1... | collective-permute-start | bytes 393224 | tf_op jit(solution)/shard_map/ppermute | solution.py:300
  175.6 20.2 %collective-permute-start.27 = (bf16[512,128]{1,0:T(8,128)(2,1)S(1)}, bf16[512,128]{1,0:T(8,128)(2,1)S(1)}, u32[]{:S(2)}, u32[]{:S(2)}) collective-permute-start(bf16[512,128]{1,0:T(8,128)(2,1)S(1)} %add_convert_fusion.18.refs_1_), channel_id=1, source_target_pairs={{0,4},{4,0},{1,5},{5,1},{2,6},{6,2},{3,7},{7,3},{8,12},{12,8},{9,1... | collective-permute-start | bytes 393224 | tf_op jit(solution)/shard_map/ppermute | solution.py:309
  239.5 29.2 %collective-permute-start.16 = (bf16[512,128]{1,0:T(8,128)(2,1)S(1)}, bf16[512,128]{1,0:T(8,128)(2,1)S(1)}, u32[]{:S(2)}, u32[]{:S(2)}) collective-permute-start(bf16[512,128]{1,0:T(8,128)(2,1)S(1)} %get-tuple-element.50), channel_id=1, source_target_pairs={{0,4},{4,0},{1,5},{5,1},{2,6},{6,2},{3,7},{7,3},{8,12},{12,8},{9,1... | collective-permute-start | bytes 393224 | tf_op jit(solution)/shard_map/ppermute | solution.py:300
  285.4 18.6 %collective-permute-start.11 = (bf16[512,128]{1,0:T(8,128)(2,1)S(1)}, bf16[512,128]{1,0:T(8,128)(2,1)S(1)}, u32[]{:S(2)}, u32[]{:S(2)}) collective-permute-start(bf16[512,128]{1,0:T(8,128)(2,1)S(1)} %add_convert_fusion.20.refs_1_), channel_id=1, source_target_pairs={{0,4},{4,0},{1,5},{5,1},{2,6},{6,2},{3,7},{7,3},{8,12},{12,8},{9,1... | collective-permute-start | bytes 393224 | tf_op jit(solution)/shard_map/ppermute | solution.py:309
  390.9 23.1 %collective-permute-start.50 = (bf16[512,128]{1,0:T(8,128)(2,1)S(1)}, bf16[512,128]{1,0:T(8,128)(2,1)S(1)}, u32[]{:S(2)}, u32[]{:S(2)}) collective-permute-start(bf16[512,128]{1,0:T(8,128)(2,1)S(1)} %get-tuple-element.74), channel_id=1, source_target_pairs={{0,4},{4,0},{1,5},{5,1},{2,6},{6,2},{3,7},{7,3},{8,12},{12,8},{9,1... | collective-permute-start | bytes 393224 | tf_op jit(solution)/shard_map/ppermute | solution.py:300
  430.2 63.0 %collective-permute-start.53 = (bf16[512,128]{1,0:T(8,128)(2,1)S(1)}, bf16[512,128]{1,0:T(8,128)(2,1)S(1)}, u32[]{:S(2)}, u32[]{:S(2)}) collective-permute-start(bf16[512,128]{1,0:T(8,128)(2,1)S(1)} %add_convert_fusion.13.refs_1_), channel_id=1, source_target_pairs={{0,4},{4,0},{1,5},{5,1},{2,6},{6,2},{3,7},{7,3},{8,12},{12,8},{9,1... | collective-permute-start | bytes 393224 | tf_op jit(solution)/shard_map/ppermute | solution.py:309
  435.8 40.9 %collective-permute-start.49 = (bf16[512,128]{1,0:T(8,128)(2,1)S(1)}, bf16[512,128]{1,0:T(8,128)(2,1)S(1)}, u32[]{:S(2)}, u32[]{:S(2)}) collective-permute-start(bf16[512,128]{1,0:T(8,128)(2,1)S(1)} %add_convert_fusion.14.refs_1_), channel_id=1, source_target_pairs={{0,4},{4,0},{1,5},{5,1},{2,6},{6,2},{3,7},{7,3},{8,12},{12,8},{9,1... | collective-permute-start | bytes 393224 | tf_op jit(solution)/shard_map/ppermute | solution.py:309
  439.0 21.2 %collective-permute-start.45 = (bf16[512,128]{1,0:T(8,128)(2,1)S(1)}, bf16[512,128]{1,0:T(8,128)(2,1)S(1)}, u32[]{:S(2)}, u32[]{:S(2)}) collective-permute-start(bf16[512,128]{1,0:T(8,128)(2,1)S(1)} %add_convert_fusion.15.refs_1_), channel_id=1, source_target_pairs={{0,4},{4,0},{1,5},{5,1},{2,6},{6,2},{3,7},{7,3},{8,12},{12,8},{9,1... | collective-permute-start | bytes 393224 | tf_op jit(solution)/shard_map/ppermute | solution.py:309
  533.8 18.7 %collective-permute-start.66 = (bf16[448,256]{0,1:T(8,128)(2,1)S(1)}, bf16[448,256]{0,1:T(8,128)(2,1)}, u32[]{:S(2)}, u32[]{:S(2)}) collective-permute-start(bf16[448,256]{0,1:T(8,128)(2,1)S(1)} %get-tuple-element.91), channel_id=1, source_target_pairs={{0,4},{4,0},{1,5},{5,1},{2,6},{6,2},{3,7},{7,3},{8,12},{12,8},{9,1... | collective-permute-start | bytes 688136 | tf_op jit(solution)/shard_map/ppermute | solution.py:300
  534.0 23.3 %collective-permute-start.62 = (bf16[448,256]{0,1:T(8,128)(2,1)S(1)}, bf16[448,256]{0,1:T(8,128)(2,1)}, u32[]{:S(2)}, u32[]{:S(2)}) collective-permute-start(bf16[448,256]{0,1:T(8,128)(2,1)S(1)} %get-tuple-element.92), channel_id=1, source_target_pairs={{0,4},{4,0},{1,5},{5,1},{2,6},{6,2},{3,7},{7,3},{8,12},{12,8},{9,1... | collective-permute-start | bytes 688136 | tf_op jit(solution)/shard_map/ppermute | solution.py:300
  540.1 24.5 %all-to-all-start = ((bf16[4,256,256]{1,2,0:T(8,128)(2,1)}), bf16[4,256,256]{1,2,0:T(8,128)(2,1)S(1)}, u32[]{:S(2)}, u32[]{:S(2)}) async-start(bf16[4,256,256]{1,2,0:T(8,128)(2,1)} %bitcast.100), calls=%async_computation | async-start | bytes 1048576 | tf_op jit(solution)/shard_map/all_to_all | solution.py:330
  560.6 16.0 %collective-permute-start.67 = (bf16[448,256]{0,1:T(8,128)(2,1)S(1)}, bf16[448,256]{0,1:T(8,128)(2,1)}, u32[]{:S(2)}, u32[]{:S(2)}) collective-permute-start(bf16[448,256]{0,1:T(8,128)(2,1)S(1)} %get-tuple-element.87), channel_id=1, source_target_pairs={{0,8},{8,0},{16,24},{24,16},{1,9},{9,1},{17,25},{25,17},{2,10},{10... | collective-permute-start | bytes 688136 | tf_op jit(solution)/shard_map/ppermute | solution.py:304
  562.6 37.7 %collective-permute-start.63 = (bf16[448,256]{0,1:T(8,128)(2,1)S(1)}, bf16[448,256]{0,1:T(8,128)(2,1)}, u32[]{:S(2)}, u32[]{:S(2)}) collective-permute-start(bf16[448,256]{0,1:T(8,128)(2,1)S(1)} %get-tuple-element.88), channel_id=1, source_target_pairs={{0,8},{8,0},{16,24},{24,16},{1,9},{9,1},{17,25},{25,17},{2,10},{10... | collective-permute-start | bytes 688136 | tf_op jit(solution)/shard_map/ppermute | solution.py:304
  562.6 43.3 %collective-permute-start.59 = (bf16[448,256]{0,1:T(8,128)(2,1)S(1)}, bf16[448,256]{0,1:T(8,128)(2,1)}, u32[]{:S(2)}, u32[]{:S(2)}) collective-permute-start(bf16[448,256]{0,1:T(8,128)(2,1)S(1)} %get-tuple-element.85), channel_id=1, source_target_pairs={{0,8},{8,0},{16,24},{24,16},{1,9},{9,1},{17,25},{25,17},{2,10},{10... | collective-permute-start | bytes 688136 | tf_op jit(solution)/shard_map/ppermute | solution.py:304
  565.8 87.5 %all-to-all-start.1 = ((bf16[8,256,256]{2,1,0:T(8,128)(2,1)}), bf16[8,256,256]{2,1,0:T(8,128)(2,1)}, u32[]{:S(2)}, u32[]{:S(2)}) async-start(bf16[8,256,256]{2,1,0:T(8,128)(2,1)} %broadcast_in_dim.2), calls=%async_computation.1 | async-start | bytes 2097152 | tf_op jit(solution)/shard_map/all_to_all | solution.py:337
  571.4 53.9 %collective-permute-start.72 = (bf16[448,256]{0,1:T(8,128)(2,1)S(1)}, bf16[448,256]{0,1:T(8,128)(2,1)S(1)}, u32[]{:S(2)}, u32[]{:S(2)}) collective-permute-start(bf16[448,256]{0,1:T(8,128)(2,1)S(1)} %add_convert_fusion.2), channel_id=1, source_target_pairs={{0,16},{8,24},{16,0},{24,8},{1,17},{9,25},{17,1},{25,9},{2,18},{10... | collective-permute-start | bytes 688136 | tf_op jit(solution)/shard_map/ppermute | solution.py:304
  577.6 53.3 %collective-permute-start.68 = (bf16[448,256]{0,1:T(8,128)(2,1)S(1)}, bf16[448,256]{0,1:T(8,128)(2,1)S(1)}, u32[]{:S(2)}, u32[]{:S(2)}) collective-permute-start(bf16[448,256]{0,1:T(8,128)(2,1)S(1)} %add_convert_fusion.4), channel_id=1, source_target_pairs={{0,16},{8,24},{16,0},{24,8},{1,17},{9,25},{17,1},{25,9},{2,18},{10... | collective-permute-start | bytes 688136 | tf_op jit(solution)/shard_map/ppermute | solution.py:304
  601.3 35.3 %collective-permute-start.64 = (bf16[448,256]{0,1:T(8,128)(2,1)S(1)}, bf16[448,256]{0,1:T(8,128)(2,1)S(1)}, u32[]{:S(2)}, u32[]{:S(2)}) collective-permute-start(bf16[448,256]{0,1:T(8,128)(2,1)S(1)} %add_convert_fusion.6), channel_id=1, source_target_pairs={{0,16},{8,24},{16,0},{24,8},{1,17},{9,25},{17,1},{25,9},{2,18},{10... | collective-permute-start | bytes 688136 | tf_op jit(solution)/shard_map/ppermute | solution.py:304
  606.9 32.5 %collective-permute-start.60 = (bf16[448,256]{0,1:T(8,128)(2,1)S(1)}, bf16[448,256]{0,1:T(8,128)(2,1)S(1)}, u32[]{:S(2)}, u32[]{:S(2)}) collective-permute-start(bf16[448,256]{0,1:T(8,128)(2,1)S(1)} %add_convert_fusion.8), channel_id=1, source_target_pairs={{0,16},{8,24},{16,0},{24,8},{1,17},{9,25},{17,1},{25,9},{2,18},{10... | collective-permute-start | bytes 688136 | tf_op jit(solution)/shard_map/ppermute | solution.py:304
  625.4 21.2 %collective-permute-start.73 = (bf16[448,256]{0,1:T(8,128)(2,1)S(1)}, bf16[448,256]{0,1:T(8,128)(2,1)S(1)}, u32[]{:S(2)}, u32[]{:S(2)}) collective-permute-start(bf16[448,256]{0,1:T(8,128)(2,1)S(1)} %add_convert_fusion.1), channel_id=1, source_target_pairs={{0,4},{4,0},{1,5},{5,1},{2,6},{6,2},{3,7},{7,3},{8,12},{12,8},{9,1... | collective-permute-start | bytes 688136 | tf_op jit(solution)/shard_map/ppermute | solution.py:309
  631.0 15.5 %collective-permute-start.69 = (bf16[448,256]{0,1:T(8,128)(2,1)S(1)}, bf16[448,256]{0,1:T(8,128)(2,1)S(1)}, u32[]{:S(2)}, u32[]{:S(2)}) collective-permute-start(bf16[448,256]{0,1:T(8,128)(2,1)S(1)} %add_convert_fusion.3), channel_id=1, source_target_pairs={{0,4},{4,0},{1,5},{5,1},{2,6},{6,2},{3,7},{7,3},{8,12},{12,8},{9,1... | collective-permute-start | bytes 688136 | tf_op jit(solution)/shard_map/ppermute | solution.py:309
  653.3 18.0 %all-to-all-start.2 = ((bf16[4,512,256]{2,1,0:T(8,128)(2,1)}), bf16[4,512,256]{2,1,0:T(8,128)(2,1)S(1)}, u32[]{:S(2)}, u32[]{:S(2)}) async-start(bf16[4,512,256]{2,1,0:T(8,128)(2,1)} %bitcast.19), calls=%async_computation.2 | async-start | bytes 2097152 | tf_op jit(solution)/shard_map/all_to_all | solution.py:432
  (59 other events, 1239.7 us)

commit v4 on v3

v4 whole, which is shorter than its diff:
```python
import functools

import jax
import jax.numpy as jnp
from jax import lax
from jax.experimental import pallas as pl
from jax.experimental.pallas import tpu as pltpu
from jax.sharding import PartitionSpec as P

NQ = 16
QTOK = 32
RANK = 16
ITERS = 2
CORES = 2
NG = NQ // CORES
COLS = NG * RANK
TOKS = NG * QTOK
LANES = 256
PIECES = 2
BLOCK = 4
FACTOR_PIECES = 4

damping = 0.01
ridge_scale = 1e-06

GD = ("grp", "dp")
f32 = jnp.float32
bf16 = jnp.bfloat16


def params():
    return pltpu.CompilerParams(vmem_limit_bytes=48 * 1024 * 1024)


def chunks(extent):
    return [(at, min(LANES, extent - at)) for at in range(0, extent, LANES)]


def cost(shape, columns):
    count = shape[0] * shape[1] * shape[2]
    return pl.CostEstimate(
        flops=2 * count * columns, bytes_accessed=2 * count, transcendentals=0
    )


def add_images(product, first, rows, image):
    lane = lax.broadcasted_iota(jnp.int32, (rows, COLS), 1) // RANK
    for at in range(BLOCK):
        image[...] = jnp.where(
            lane == first + at, product[at * rows : (at + 1) * rows], image[...]
        )


def write_image(image, send_ref, keep_ref):
    part, parts = pl.program_id(0), pl.num_programs(0)
    last = pl.program_id(1) == pl.num_programs(1) - 1

    @pl.when(last & (part < parts - 1))
    def _():
        send_ref[...] = image[...].astype(bf16)

    @pl.when(last & (part == parts - 1))
    def _():
        keep_ref[...] = image[...]


def image_of(rotated_ref, basis_ref):
    _, rows, cols = rotated_ref.shape
    return jnp.dot(
        rotated_ref[...].reshape(BLOCK * rows, cols), basis_ref[...], preferred_element_type=f32
    )


def form_kernel(n_dp, n_ties, place_ref, *refs):
    out_refs = refs[:n_dp]
    in_ref, eig_ref, basis_ref = refs[n_dp : n_dp + 3]
    rotated_ref, send_ref, keep_ref, weight, left, image = refs[n_dp + 3 + n_ties :]
    part, first = pl.program_id(0), pl.program_id(1) * BLOCK
    rows, cols = eig_ref.shape

    @pl.when(first == 0)
    def _():
        weight[...] = 1.0 / (eig_ref[...] + damping)

    for at in range(n_dp):

        @pl.when((first == 0) & (part == at))
        def _(at=at):
            for query in range(NG):
                left[query] = out_refs[at][:, query * QTOK : (query + 1) * QTOK]

    for at in range(BLOCK):
        query = first + at
        own = left[query]
        right = in_ref[pl.ds(pl.multiple_of(query * QTOK, QTOK), QTOK), :]
        for begin, width in chunks(cols):
            span = slice(begin, begin + width)
            block = jnp.dot(own, right[:, span], preferred_element_type=f32)
            rotated_ref[at, :, span] = (block * weight[:, span]).astype(bf16)
    add_images(image_of(rotated_ref, basis_ref), first, rows, image)
    write_image(image, send_ref, keep_ref)


def tied(ties):
    return [pl.BlockSpec(memory_space=pl.ANY)] * len(ties)


def form_piece(place, out_parts, rot_in, eigvals, basis, piece, ties):
    n_dp = len(out_parts)
    rows = out_parts[0].shape[0]
    cols = rot_in.shape[1]

    def eig_block(part, query, place_ref):
        return piece * n_dp + lax.rem(place_ref[0] + 1 + part, n_dp), 0

    def fixed(shape):
        return pl.BlockSpec(shape, lambda part, query, _: (0, 0))

    shape = (NG, n_dp * rows, cols)
    return pl.pallas_call(
        functools.partial(form_kernel, n_dp, len(ties)),
        grid_spec=pltpu.PrefetchScalarGridSpec(
            num_scalar_prefetch=1,
            grid=(n_dp, NG // BLOCK),
            in_specs=[fixed((rows, TOKS))] * n_dp
            + [
                fixed((TOKS, cols)),
                pl.BlockSpec((rows, cols), eig_block),
                fixed((cols, COLS)),
            ]
            + tied(ties),
            out_specs=[
                pl.BlockSpec((BLOCK, rows, cols), lambda part, query, _: (query, part, 0)),
                pl.BlockSpec(
                    (rows, COLS), lambda part, query, _: (jnp.minimum(part, n_dp - 2), 0)
                ),
                fixed((rows, COLS)),
            ],
            scratch_shapes=[
                pltpu.VMEM((rows, cols), f32),
                pltpu.VMEM((NG, rows, QTOK), bf16),
                pltpu.VMEM((rows, COLS), f32),
            ],
        ),
        out_shape=[
            jax.ShapeDtypeStruct(shape, bf16),
            jax.ShapeDtypeStruct(((n_dp - 1) * rows, COLS), bf16),
            jax.ShapeDtypeStruct((rows, COLS), f32),
        ],
        compiler_params=params(),
        cost_estimate=cost(shape, 400),
        name="form",
    )(place, *out_parts, rot_in, eigvals, basis, *ties)


def image_kernel(n_ties, basis_ref, rotated_ref, *refs):
    send_ref, keep_ref, image = refs[n_ties:]
    rows = image.shape[0]
    add_images(image_of(rotated_ref, basis_ref), pl.program_id(1) * BLOCK, rows, image)
    write_image(image, send_ref, keep_ref)


def image_piece(basis, rotated, n_dp, ties):
    _, rows, cols = rotated.shape
    rows = rows // n_dp
    return pl.pallas_call(
        functools.partial(image_kernel, len(ties)),
        grid=(n_dp, NG // BLOCK),
        in_specs=[
            pl.BlockSpec((cols, COLS), lambda part, query: (0, 0)),
            pl.BlockSpec((BLOCK, rows, cols), lambda part, query: (query, part, 0)),
        ]
        + tied(ties),
        out_specs=[
            pl.BlockSpec((rows, COLS), lambda part, query: (jnp.minimum(part, n_dp - 2), 0)),
            pl.BlockSpec((rows, COLS), lambda part, query: (0, 0)),
        ],
        out_shape=[
            jax.ShapeDtypeStruct(((n_dp - 1) * rows, COLS), bf16),
            jax.ShapeDtypeStruct((rows, COLS), f32),
        ],
        scratch_shapes=[pltpu.VMEM((rows, COLS), f32)],
        compiler_params=params(),
        cost_estimate=cost(rotated.shape, 256),
        name="image",
    )(basis, rotated, *ties)


def return_kernel(n_dp, first, *refs):
    image_refs, rotated_ref = refs[:n_dp], refs[n_dp]
    total_ref, gram_ref, turned = refs[-3:]
    part, step = pl.program_id(0), pl.program_id(1)

    @pl.when((part == 0) & (step == 0))
    def _():
        if first:
            total_ref[...] = jnp.zeros_like(total_ref)
            gram_ref[...] = jnp.zeros_like(gram_ref)
        else:
            total_ref[...] = refs[n_dp + 1][...]
            gram_ref[...] = refs[n_dp + 2][...]

    for at in range(n_dp):

        @pl.when((step == 0) & (part == at))
        def _(at=at):
            image = image_refs[at][...]
            turned[...] = image.astype(f32).T.astype(bf16)
            gram_ref[...] += lax.dot_general(
                image, image, (((0,), (0,)), ((), ())), preferred_element_type=f32
            )

    for at in range(BLOCK):
        own = pl.ds(pl.multiple_of((step * BLOCK + at) * RANK, RANK), RANK)
        total_ref[own, :] += jnp.dot(
            turned[own, :], rotated_ref[at], preferred_element_type=f32
        )


def return_piece(images, rotated, before, ties):
    n_dp = len(images)
    _, rows, cols = rotated.shape
    rows = rows // n_dp
    first = before is None

    def fixed(shape):
        return pl.BlockSpec(shape, lambda part, query: (0, 0))

    sums = [fixed((COLS, cols)), fixed((COLS, COLS))]
    return pl.pallas_call(
        functools.partial(return_kernel, n_dp, first),
        grid=(n_dp, NG // BLOCK),
        in_specs=[fixed((rows, COLS))] * n_dp
        + [pl.BlockSpec((BLOCK, rows, cols), lambda part, query: (query, part, 0))]
        + ([] if first else sums)
        + tied(ties),
        out_specs=sums,
        out_shape=[
            jax.ShapeDtypeStruct((COLS, cols), f32),
            jax.ShapeDtypeStruct((COLS, COLS), f32),
        ],
        scratch_shapes=[pltpu.VMEM((COLS, rows), bf16)],
        compiler_params=params(),
        cost_estimate=cost(rotated.shape, 256),
        name="returned",
    )(*images, rotated, *([] if first else before), *ties)


def rotate_in_kernel(place_ref, query_ref, eigen_ref, theirs_ref, mine_ref):
    for out_ref, index in ((theirs_ref, 1 - place_ref[1]), (mine_ref, place_ref[1])):
        rows = pl.ds(pl.multiple_of(index * TOKS, TOKS), TOKS)
        out_ref[...] = jnp.dot(query_ref[rows, :], eigen_ref[...], preferred_element_type=f32)


def rotate_in(place, query_in, eigen_in):
    depth, cols = eigen_in.shape
    width = LANES if cols % LANES == 0 else cols
    out = jax.ShapeDtypeStruct((TOKS, cols), f32)
    return pl.pallas_call(
        rotate_in_kernel,
        grid_spec=pltpu.PrefetchScalarGridSpec(
            num_scalar_prefetch=1,
            grid=(cols // width,),
            in_specs=[
                pl.BlockSpec(query_in.shape, lambda at, _: (0, 0)),
                pl.BlockSpec((depth, width), lambda at, _: (0, at)),
            ],
            out_specs=[pl.BlockSpec((TOKS, width), lambda at, _: (0, at))] * 2,
        ),
        out_shape=[out, out],
        compiler_params=params(),
        name="rotate_in",
    )(place, query_in, eigen_in)


def factor_kernel(n_ties, place_ref, eigen_ref, cols_ref, *refs):
    send_ref, keep_ref = refs[n_ties:]
    part, parts = pl.program_id(0), pl.num_programs(0)
    product = jnp.dot(eigen_ref[...], cols_ref[...], preferred_element_type=f32)

    @pl.when(part < parts - 1)
    def _():
        send_ref[...] = product.astype(bf16)

    @pl.when(part == parts - 1)
    def _():
        keep_ref[...] = product


def factor_piece(place, eigen_in, in_cols, piece, pieces, n_dp, ties):
    rows, depth = eigen_in.shape
    rows = rows // (pieces * n_dp)
    width = in_cols.shape[1]
    return pl.pallas_call(
        functools.partial(factor_kernel, len(ties)),
        grid_spec=pltpu.PrefetchScalarGridSpec(
            num_scalar_prefetch=1,
            grid=(n_dp,),
            in_specs=[
                pl.BlockSpec(
                    (rows, depth),
                    lambda part, place_ref: (
                        piece * n_dp + lax.rem(place_ref[0] + 1 + part, n_dp),
                        0,
                    ),
                ),
                pl.BlockSpec((depth, width), lambda part, _: (0, 0)),
            ]
            + tied(ties),
            out_specs=[
                pl.BlockSpec((rows, width), lambda part, _: (jnp.minimum(part, n_dp - 2), 0)),
                pl.BlockSpec((rows, width), lambda part, _: (0, 0)),
            ],
        ),
        out_shape=[
            jax.ShapeDtypeStruct(((n_dp - 1) * rows, width), bf16),
            jax.ShapeDtypeStruct((rows, width), f32),
        ],
        compiler_params=params(),
        name="factor",
    )(place, eigen_in, in_cols, *ties)


def project_kernel(n_dp, place_ref, hidden_ref, *refs):
    *part_refs, factor_ref, proj_ref = refs
    rows = part_refs[0].shape[0]
    for at, ref in enumerate(part_refs):
        owner = lax.rem(place_ref[0] + 1 + at % n_dp, n_dp)
        begin = (at // n_dp * n_dp + owner) * rows
        factor_ref[pl.ds(pl.multiple_of(begin, 8), rows), :] = ref[...]
    proj_ref[...] = jnp.dot(
        hidden_ref[...], factor_ref[...], preferred_element_type=f32
    ).astype(bf16)


def project(place, hidden, parts, n_dp):
    tokens, depth = hidden.shape
    width = parts[0].shape[1]
    vmem = pl.BlockSpec(memory_space=pltpu.VMEM)
    return pl.pallas_call(
        functools.partial(project_kernel, n_dp),
        in_specs=[pl.BlockSpec(memory_space=pltpu.SMEM)] + [vmem] * (1 + len(parts)),
        out_specs=[vmem, vmem],
        out_shape=[
            jax.ShapeDtypeStruct((depth, width), bf16),
            jax.ShapeDtypeStruct((tokens, width), bf16),
        ],
        compiler_params=params(),
        name="project",
    )(place, hidden, *parts)


def gram_kernel(*refs):
    gram = jnp.zeros((COLS, COLS), f32)
    for ref in refs[:-1]:
        image = ref[...]
        gram = gram + lax.dot_general(
            image, image, (((0,), (0,)), ((), ())), preferred_element_type=f32
        )
    refs[-1][...] = gram


def gram_of(images):
    return pl.pallas_call(
        gram_kernel,
        out_shape=jax.ShapeDtypeStruct((COLS, COLS), f32),
        compiler_params=params(),
        name="gram",
    )(*images)


def lower_inverse(gram):
    shape = (NG, RANK, COLS)
    row = lax.broadcasted_iota(jnp.int32, shape, 1)
    lane = lax.broadcasted_iota(jnp.int32, shape, 2)
    same = lane // RANK == lax.broadcasted_iota(jnp.int32, shape, 0)
    col = lane % RANK
    eye = same & (col == row)
    gram = jnp.where(same, gram.reshape(shape), 0.0)
    trace = jnp.sum(
        jnp.sum(jnp.where(eye, gram, 0.0), axis=2, keepdims=True), axis=1, keepdims=True
    )
    left = gram + jnp.where(eye, ridge_scale * (trace / RANK), 0.0)
    right = jnp.where(eye, 1.0, 0.0)
    for step in range(RANK):
        column = jnp.sum(jnp.where(col == step, left, 0.0), axis=2, keepdims=True)
        pivot = column[:, step : step + 1, :]
        factor = jnp.where(row[:, :, :1] > step, column / pivot, 0.0)
        right = right - factor * right[:, step : step + 1, :]
        left = left - factor * left[:, step : step + 1, :]
    diagonal = jnp.sum(jnp.where(eye, left, 0.0), axis=2, keepdims=True)
    return (right * lax.rsqrt(diagonal)).reshape(COLS, COLS)


def inverse_kernel(scale, gram_ref, gram_got_ref, inverse_ref):
    inverse_ref[...] = lower_inverse((gram_ref[...] + gram_got_ref[...]) * scale)


def inverse_of(gram, gram_got, scale):
    return pl.pallas_call(
        functools.partial(inverse_kernel, scale),
        out_shape=jax.ShapeDtypeStruct((COLS, COLS), f32),
        compiler_params=params(),
        name="inverse",
    )(gram, gram_got)


def normalize_kernel(total_ref, got_ref, inverse_ref, basis_ref):
    total = total_ref[...] + got_ref[...].astype(f32)
    basis_ref[...] = lax.dot_general(
        total,
        inverse_ref[...],
        (((0,), (1,)), ((), ())),
        precision=lax.Precision.HIGHEST,
        preferred_element_type=f32,
    ).astype(bf16)


def normalize(total, got, inverse):
    return pl.pallas_call(
        normalize_kernel,
        out_shape=jax.ShapeDtypeStruct((total.shape[1], COLS), bf16),
        compiler_params=params(),
        name="normalize",
    )(total, got, inverse)


def turned_by(count, step):
    return [(i, (i + step) % count) for i in range(count)]


def crossed(count, step):
    return [(i, i ^ step) for i in range(count)]


def swap_cores(part, n_width):
    return lax.ppermute(part, "width", crossed(n_width, 1))


class Reduction:
    def __init__(self, sends, keep, n_grp, n_dp, even=False):
        self.parts = None
        self.steps = self.run(sends, keep, n_grp, n_dp, even)
        next(self.steps)

    def advance(self):
        return next(self.steps, None) or []

    def run(self, sends, keep, n_grp, n_dp, even):
        rows = keep.shape[0]
        got = [
            lax.ppermute(
                sends[at * rows : (at + 1) * rows], "dp", turned_by(n_dp, at + 1)
            )
            for at in range(n_dp - 1)
        ]
        yield []
        total = keep
        for part in got:
            total = total + part.astype(f32)
        step = 1
        while step < n_grp:
            sent = total.astype(bf16)
            got = lax.ppermute(sent, "grp", crossed(n_grp, step))
            yield [sent]
            total = (sent.astype(f32) if even else total) + got.astype(f32)
            step *= 2
        own = total.astype(bf16)
        others = [
            lax.ppermute(own, "dp", turned_by(n_dp, n_dp - 1 - at)) for at in range(n_dp - 1)
        ]
        yield [own]
        self.parts = others + [own]


def advance_all(reductions):
    ties = []
    for reduction in reductions:
        if reduction.parts is None:
            ties += reduction.advance()
    return ties


def finish(reduction, reductions):
    ties = []
    while reduction.parts is None:
        ties = advance_all(reductions)
    return ties


def unrolled(parts, dp):
    whole = jnp.stack(parts)
    whole = jnp.roll(whole, dp + 1, axis=0)
    return whole.reshape((-1,) + whole.shape[2:])


def split_parts(part, dp, n_dp, piece, pieces):
    rows = part.shape[0] // (pieces * n_dp)
    taken = [
        lax.dynamic_slice_in_dim(part, piece * n_dp * rows + (dp + 1 + at) % n_dp * rows, rows, 0)
        for at in range(n_dp)
    ]
    return jnp.concatenate(taken[:-1], axis=0).astype(bf16), taken[-1].astype(f32)


def sum_scatter(part, axes, count):
    pieces = lax.all_to_all(part.astype(bf16), axes, 0, 0, tiled=True)
    pieces = pieces.reshape((count, part.shape[0] // count) + part.shape[1:])
    return jnp.sum(pieces.astype(f32), axis=0)


def gather_rows(piece, axes, count):
    copies = jnp.broadcast_to(piece[None], (count,) + piece.shape)
    whole = lax.all_to_all(copies, axes, 0, 0, tiled=True)
    return whole.reshape((count * piece.shape[0],) + piece.shape[1:])


def make_per_device(n_grp, n_dp, n_width):
    n_gd = n_grp * n_dp

    def per_device(
        query_out, query_in, eigen_out, eigen_in, eigvals, start, grads_out, gate_pre, up_pre
    ):
        dp = lax.axis_index("dp")
        core = lax.axis_index("width") % CORES
        place = jnp.stack([dp, core]).astype(jnp.int32)
        scale = 1.0 / (eigen_out.shape[0] * n_gd)
        rows_out = eigvals.shape[0]

        def rows_of(array, index):
            return lax.dynamic_slice_in_dim(array, index * TOKS, TOKS, 0)

        def rotate_out(queries):
            return lax.dot_general(
                eigen_out, queries, (((0,), (1,)), ((), ())), preferred_element_type=f32
            )

        def reduction(sends, keep, even=False):
            return Reduction(sends, keep, n_grp, n_dp, even)

        theirs_in, mine_in = rotate_in(place, query_in, eigen_in)
        total_in = mine_in + swap_cores(theirs_in, n_width)
        mine_out = rotate_out(rows_of(query_out, core))
        theirs_out = rotate_out(rows_of(query_out, 1 - core)).astype(bf16)
        theirs_out = swap_cores(theirs_out, n_width)
        step = 2
        while step < n_width:
            got = lax.ppermute(total_in.astype(bf16), "width", crossed(n_width, step))
            total_in = total_in + got.astype(f32)
            step *= 2
        rot_in = total_in.astype(bf16)
        eig_sent, _, _ = lax.optimization_barrier((eigvals, theirs_out, total_in))
        eig_theirs = swap_cores(eig_sent, n_width)

        turning = []
        for part in (mine_out, theirs_out):
            for piece in range(PIECES):
                advance_all(turning)
                turning.append(reduction(*split_parts(part, dp, n_dp, piece, PIECES)))
        basis = lax.dynamic_slice_in_dim(start, core * COLS, COLS, 1)
        count = len(turning)
        rotated = []
        for iteration in range(ITERS):
            summing, ties = [], []
            for at in range(count):
                if iteration == 0:
                    finish(turning[at], turning)
                    eig = eigvals if at < PIECES else eig_theirs
                    block, sends, keep = form_piece(
                        place, turning[at].parts, rot_in, eig, basis, at % PIECES, ties
                    )
                    rotated.append(block)
                    ties = advance_all(turning)
                else:
                    sends, keep = image_piece(basis, rotated[at], n_dp, ties)
                    ties = []
                ties += advance_all(summing)
                summing.append(reduction(sends, keep))
            sums = None
            for at in range(count):
                finish(summing[at], summing)
                if at == count - 1:
                    gram = gram_of([part for each in summing for part in each.parts])
                    step = 2
                    while step < n_width:
                        gram_got = lax.ppermute(gram, "width", crossed(n_width, step))
                        step *= 2
                        if step < n_width:
                            gram = gram + gram_got
                    ties = [gram]
                sums = return_piece(summing[at].parts, rotated[at], sums, ties)
                ties = advance_all(summing)
            inverse = inverse_of(gram, gram_got, scale)
            total = sums[0]
            step = 2
            while step < n_width:
                got = lax.ppermute(total.astype(bf16), "width", crossed(n_width, step))
                step *= 2
                if step < n_width:
                    total = total + got.astype(f32)
            basis = normalize(total, got, inverse)

        def columns(mine, theirs):
            return jnp.where(
                core == 0,
                jnp.concatenate([mine, theirs], axis=1),
                jnp.concatenate([theirs, mine], axis=1),
            )

        hidden = (jax.nn.silu(gate_pre.astype(f32)) * up_pre.astype(f32)).astype(bf16)
        image = jnp.concatenate([unrolled(each.parts, dp) for each in summing], axis=0)
        basis_out = lax.dot_general(
            image.astype(f32),
            inverse,
            (((1,), (1,)), ((), ())),
            precision=lax.Precision.HIGHEST,
            preferred_element_type=f32,
        ).astype(bf16)
        out_cols = columns(basis_out[:rows_out], swap_cores(basis_out[rows_out:], n_width))
        part_factor_out = jnp.dot(eigen_out, out_cols, preferred_element_type=f32)
        share = sum_scatter(part_factor_out, "width", n_width).astype(bf16)
        piece_rows = share.shape[0]
        gathered = gather_rows(share, GD, n_gd)
        mixed = lax.all_to_all(gathered, "width", 0, 0, tiled=True)
        out_factor = (
            mixed.reshape(n_width, n_gd // n_width, piece_rows, NQ * RANK)
            .transpose(1, 0, 2, 3)
            .reshape(rows_out, NQ * RANK)
        )
        in_cols = columns(basis, swap_cores(basis, n_width))
        factors, ties = [], []
        for piece in range(FACTOR_PIECES):
            sends, keep = factor_piece(
                place, eigen_in, in_cols, piece, FACTOR_PIECES, n_dp, ties
            )
            ties = advance_all(factors)
            factors.append(reduction(sends, keep, even=True))
        for each in factors:
            finish(each, factors)
        parts = [part for each in factors for part in each.parts]
        in_factor, proj_in = project(place, hidden, parts, n_dp)
        proj_out = jnp.dot(grads_out, out_factor, preferred_element_type=f32)
        proj_out = sum_scatter(proj_out, "width", n_width)
        proj_in = sum_scatter(proj_in, "width", n_width)
        scores = (proj_out * proj_in).reshape(proj_out.shape[0], NQ, RANK).sum(axis=2).T
        return (scores, out_factor, in_factor)

    return per_device


def solution(mesh):
    return jax.shard_map(
        make_per_device(mesh.shape["grp"], mesh.shape["dp"], mesh.shape["width"]),
        mesh=mesh,
        in_specs=(
            P(None, GD),
            P(None, "width"),
            P(GD, "width"),
            P("width", GD),
            P("width", GD),
            P(GD, None),
            P(GD, "width"),
            P(GD, "width"),
            P(GD, "width"),
        ),
        out_specs=(P(None, GD + ("width",)), P("width", None), P("width", None)),
        check_vma=False,
    )
```

time: 702 us -> 629 us (0.90)
  Pallas kernels: 322 us -> 273 us
  matrix products: 36.1 us -> 15.5 us
    pallas_call x8, Pallas kernels: 132 us -> 88.4 us  [return_piece(): pl.pallas_call(functools.partial(return_kernel, n_dp, first), grid=(n_dp,...]
    ppermute x64, waiting for transfers between devices: 154 us -> 122 us  [the longest x32 98.5 us: run(): got = lax.ppermute(sent, 'grp', crossed(n_grp, step))]
    dot_general x4 -> x0, matrix products: 25 us -> none  [the longest x1 8.63 us: per_device(): jnp.dot(rows_of(query_in, core), eigen_in, preferred_element_type=f32)]
    ppermute x1, waiting for transfers between devices: 0.01 us -> 16.4 us  [per_device(): got = lax.ppermute(total_in.astype(bf16), 'width', crossed(n_width, step))]
    ppermute x2, waiting for transfers between devices: 0.01 us -> 11.6 us  [per_device(): got = lax.ppermute(total.astype(bf16), 'width', crossed(n_width, step))]
    pallas_call x10 -> x20, Pallas kernels: 190 us -> 185 us  [the longest x4 97.1 us: form_piece(): pl.pallas_call(functools.partial(form_kernel, n_dp, len(ties)), grid_spec...]
    convert_element_type x42 -> x45, other arithmetic: 17.9 us -> 18 us  [the longest x28 10.3 us: run(): sent = total.astype(bf16)]
  transfers between devices with their start and end apart: 79 -> 79, of which waited for: 43 -> 36; matrix products, arithmetic and copies ran while one was open for 10% -> 8% of each run, Pallas kernels for 33% -> 36%
where the time goes in v4:
time: 629 us; the launch traced here: 622 us
  Pallas kernels  273 us (43%)
  waiting for transfers between devices  183 us (29%)
  starting transfers between devices  104 us (17%)
  other arithmetic  30.1 us (5%)
  matrix products  15.5 us (2%)
  local copies, waits for them, and re-layouts  14.2 us (2%)
    ppermute x32, waiting for transfers between devices, run(): got = lax.ppermute(sent, 'grp', crossed(n_grp, step))  98.5 us
    pallas_call x4, Pallas kernels, form_piece(): pl.pallas_call(functools.partial(form_kernel, n_dp, len(ties)), grid_spec...  97.1 us
    pallas_call x8, Pallas kernels, return_piece(): pl.pallas_call(functools.partial(return_kernel, n_dp, first), grid=(n_dp,...  88.4 us
    pallas_call x4, Pallas kernels, image_piece(): pl.pallas_call(functools.partial(image_kernel, len(ties)), grid=(n_dp, NG...  51.1 us
    ppermute x32, starting transfers between devices, run(): got = lax.ppermute(sent, 'grp', crossed(n_grp, step))  40.1 us
    ppermute x16, waiting for transfers between devices, run(): lax.ppermute(sends[at * rows:(at + 1) * rows], 'dp', turned_by(n_dp, at +...  21.5 us
    ppermute x16, starting transfers between devices, run(): lax.ppermute(sends[at * rows:(at + 1) * rows], 'dp', turned_by(n_dp, at +...  19.7 us
    ppermute x1, waiting for transfers between devices, per_device(): got = lax.ppermute(total_in.astype(bf16), 'width', crossed(n_width, step))  16.4 us
  transfers between devices with their start and end apart: 79, of which 36 were waited for; matrix products, arithmetic and copies ran while one was open for 8% of the time, Pallas kernels for 36%

profile of v4, /device:TPU:0, one launch (start us, length us, event | category | flops | bytes accessed | tf_op | source)
XLA Modules:
  0.0 621.7 jit_solution(11585769178212527009)
XLA Ops:
  0.7 12.3 %rotate_in.1 = (f32[256,1792]{1,0:T(8,128)S(1)}, f32[256,1792]{1,0:T(8,128)S(1)}) custom-call(s32[2]{0:T(128)S(1)} %pad_add_fusion.place_ref, bf16[512,3584]{1,0:T(8,128)(2,1)} %query_ref.1, bf16[3584,1792]{1,0:T(8,128)(2,1)} %eigen_ref.9), custom_call_target="tpu_custom_call" | custom-call | tf_op jit(solution)/shard_map/rotate_in/pallas_call | solution.py:259
  25.6 16.4 %collective-permute-done.6 = bf16[256,1792]{1,0:T(8,128)(2,1)} collective-permute-done((bf16[256,1792]{1,0:T(8,128)(2,1)S(1)}, bf16[256,1792]{1,0:T(8,128)(2,1)}, u32[]{:S(2)}, u32[]{:S(2)}) %collective-permute-start.6) | collective-permute-done | bytes 917536 | tf_op jit(solution)/shard_map/ppermute | solution.py:548
  43.5 5.4 fusion.20
  65.6 6.0 collective-permute-done.18
  93.3 5.4 collective-permute-done.9
  108.8 13.9 %collective-permute-done.10 = bf16[512,256]{1,0:T(8,128)(2,1)S(1)} collective-permute-done((bf16[512,256]{1,0:T(8,128)(2,1)S(1)}, bf16[512,256]{1,0:T(8,128)(2,1)S(1)}, u32[]{:S(2)}, u32[]{:S(2)}) %collective-permute-start.10) | collective-permute-done | bytes 262176 | tf_op jit(solution)/shard_map/ppermute | solution.py:464
  133.2 24.4 %form.4 = (bf16[8,1024,1792]{2,1,0:T(8,128)(2,1)}, bf16[512,128]{1,0:T(8,128)(2,1)S(1)}, f32[512,128]{1,0:T(8,128)S(1)}) custom-call(s32[2]{0:T(128)S(1)} %pad_add_fusion.place_ref, bf16[512,256]{1,0:T(8,128)(2,1)S(1)} %collective-permute-done.11.refs_0_, bf16[512,256]{1,0:T(8,128)(2,1)S(1)} %add_convert_fusion.2.refs_1_, ...), custom_call_target="tpu_custom_call" | custom-call | flops 11744051200 | bytes 29360128 | tf_op jit(solution)/shard_map/form/pallas_call | solution.py:120
  159.1 24.1 %form.5 = (bf16[8,1024,1792]{2,1,0:T(8,128)(2,1)}, bf16[512,128]{1,0:T(8,128)(2,1)S(1)}, f32[512,128]{1,0:T(8,128)S(1)}) custom-call(s32[2]{0:T(128)S(1)} %pad_add_fusion.place_ref, bf16[512,256]{1,0:T(8,128)(2,1)S(1)} %collective-permute-done.17.refs_0_, bf16[512,256]{1,0:T(8,128)(2,1)S(1)} %get-tuple-element.100.refs_1_, ...), custom_call_target="tpu_custom_call" | custom-call | flops 11744051200 | bytes 29360128 | tf_op jit(solution)/shard_map/form/pallas_call | solution.py:120
  194.4 6.7 %collective-permute-done.34 = bf16[512,128]{1,0:T(8,128)(2,1)S(1)} collective-permute-done((bf16[512,128]{1,0:T(8,128)(2,1)S(1)}, bf16[512,128]{1,0:T(8,128)(2,1)S(1)}, u32[]{:S(2)}, u32[]{:S(2)}) %collective-permute-start.34) | collective-permute-done | bytes 131104 | tf_op jit(solution)/shard_map/ppermute | solution.py:464
  203.4 24.6 %form.7 = (bf16[8,1024,1792]{2,1,0:T(8,128)(2,1)}, bf16[512,128]{1,0:T(8,128)(2,1)S(1)}, f32[512,128]{1,0:T(8,128)S(1)}) custom-call(s32[2]{0:T(128)S(1)} %pad_add_fusion.place_ref, bf16[512,256]{1,0:T(8,128)(2,1)S(1)} %collective-permute-done.26.refs_0_, bf16[512,256]{1,0:T(8,128)(2,1)S(1)} %get-tuple-element.108.refs_5_.refs_1_, ...), custom_call_target="tpu_custom_call" | custom-call | flops 11744051200 | bytes 29360128 | tf_op jit(solution)/shard_map/form/pallas_call | solution.py:120
  229.2 24.1 %form.6 = (bf16[8,1024,1792]{2,1,0:T(8,128)(2,1)}, bf16[512,128]{1,0:T(8,128)(2,1)S(1)}, f32[512,128]{1,0:T(8,128)S(1)}) custom-call(s32[2]{0:T(128)S(1)} %pad_add_fusion.place_ref, bf16[512,256]{1,0:T(8,128)(2,1)S(1)} %collective-permute-done.4.refs_0_, bf16[512,256]{1,0:T(8,128)(2,1)S(1)} %add_convert_fusion.3.refs_1_.refs_5_, ...), custom_call_target="tpu_custom_call" | custom-call | flops 11744051200 | bytes 29360128 | tf_op jit(solution)/shard_map/form/pallas_call | solution.py:120
  258.4 11.0 %returned.8 = (f32[128,1792]{1,0:T(8,128)S(1)}, f32[128,128]{1,0:T(8,128)S(1)}) custom-call(bf16[512,128]{1,0:T(8,128)(2,1)S(1)} %collective-permute-done.35.refs_0_, bf16[512,128]{1,0:T(8,128)(2,1)S(1)} %add_convert_fusion.20.refs_1_.refs_3_, bf16[8,1024,1792]{2,1,0:T(8,128)(2,1)} %get-tuple-element.65.refs_2_.rotated_ref, ...), custom_call_target="tpu_custom_call" | custom-call | flops 7516192768 | bytes 29360128 | tf_op jit(solution)/shard_map/returned/pallas_call | solution.py:230
  272.6 7.1 %collective-permute-done.29 = bf16[512,128]{1,0:T(8,128)(2,1)S(1)} collective-permute-done((bf16[512,128]{1,0:T(8,128)(2,1)S(1)}, bf16[512,128]{1,0:T(8,128)(2,1)S(1)}, u32[]{:S(2)}, u32[]{:S(2)}) %collective-permute-start.29) | collective-permute-done | bytes 131104 | tf_op jit(solution)/shard_map/ppermute | solution.py:464
  282.0 10.9 %returned.9 = (f32[128,1792]{1,0:T(8,128)S(1)}, f32[128,128]{1,0:T(8,128)S(1)}) custom-call(bf16[512,128]{1,0:T(8,128)(2,1)S(1)} %collective-permute-done.33.refs_0_.refs_2_, bf16[512,128]{1,0:T(8,128)(2,1)S(1)} %add_convert_fusion.21.refs_1_.refs_3_, bf16[8,1024,1792]{2,1,0:T(8,128)(2,1)} %get-tuple-element.64.refs_2_.rotated_ref, ...), custom_call_target="tpu_custom_call" | custom-call | flops 7516192768 | bytes 29360128 | tf_op jit(solution)/shard_map/returned/pallas_call | solution.py:230
  293.4 10.9 %returned.10 = (f32[128,1792]{1,0:T(8,128)S(1)}, f32[128,128]{1,0:T(8,128)S(1)}) custom-call(bf16[512,128]{1,0:T(8,128)(2,1)S(1)} %collective-permute-done.30.refs_0_.refs_4_, bf16[512,128]{1,0:T(8,128)(2,1)S(1)} %add_convert_fusion.22.refs_5_.refs_1_, bf16[8,1024,1792]{2,1,0:T(8,128)(2,1)} %get-tuple-element.63.refs_2_.rotated_ref, ...), custom_call_target="tpu_custom_call" | custom-call | flops 7516192768 | bytes 29360128 | tf_op jit(solution)/shard_map/returned/pallas_call | solution.py:230
  304.3 11.4 %returned.11 = (f32[128,1792]{1,0:T(8,128)S(1)}, f32[128,128]{1,0:T(8,128)}) custom-call(bf16[512,128]{1,0:T(8,128)(2,1)S(1)} %collective-permute-done.25.refs_6_.refs_0_, bf16[512,128]{1,0:T(8,128)(2,1)S(1)} %add_convert_fusion.23.refs_5_.refs_7_.refs_1_, bf16[8,1024,1792]{2,1,0:T(8,128)(2,1)} %get-tuple-element.60.refs_2_.rotated_ref, ...), custom_call_target="tpu_custom_call" | custom-call | flops 7516192768 | bytes 29360128 | tf_op jit(solution)/shard_map/returned/pallas_call | solution.py:230
  318.5 10.3 %collective-permute-done.37.gram_got_ref = f32[128,128]{1,0:T(8,128)} collective-permute-done((f32[128,128]{1,0:T(8,128)S(1)}, f32[128,128]{1,0:T(8,128)}, u32[]{:S(2)}, u32[]{:S(2)}) %collective-permute-start.37) | collective-permute-done | bytes 65568 | tf_op jit(solution)/shard_map/ppermute | solution.py:586
  332.1 12.7 %image.4 = (bf16[512,128]{1,0:T(8,128)(2,1)S(1)}, f32[512,128]{1,0:T(8,128)S(1)}) custom-call(bf16[1792,128]{1,0:T(8,128)(2,1)S(1)} %normalize.2.basis_ref, bf16[8,1024,1792]{2,1,0:T(8,128)(2,1)} %get-tuple-element.65.refs_2_.rotated_ref), custom_call_target="tpu_custom_call" | custom-call | flops 7516192768 | bytes 29360128 | tf_op jit(solution)/shard_map/image/pallas_call | solution.py:166
  346.7 12.7 %image.5 = (bf16[512,128]{1,0:T(8,128)(2,1)S(1)}, f32[512,128]{1,0:T(8,128)S(1)}) custom-call(bf16[1792,128]{1,0:T(8,128)(2,1)S(1)} %normalize.2.basis_ref, bf16[8,1024,1792]{2,1,0:T(8,128)(2,1)} %get-tuple-element.64.refs_2_.rotated_ref), custom_call_target="tpu_custom_call" | custom-call | flops 7516192768 | bytes 29360128 | tf_op jit(solution)/shard_map/image/pallas_call | solution.py:166
  359.8 12.9 %image.6 = (bf16[512,128]{1,0:T(8,128)(2,1)S(1)}, f32[512,128]{1,0:T(8,128)S(1)}) custom-call(bf16[1792,128]{1,0:T(8,128)(2,1)S(1)} %normalize.2.basis_ref, bf16[8,1024,1792]{2,1,0:T(8,128)(2,1)} %get-tuple-element.63.refs_2_.rotated_ref, bf16[512,128]{1,0:T(8,128)(2,1)S(1)} %fusion.47.refs_0_), custom_call_target="tpu_custom_call" | custom-call | flops 7516192768 | bytes 29360128 | tf_op jit(solution)/shard_map/image/pallas_call | solution.py:166
  379.9 12.7 %image.7 = (bf16[512,128]{1,0:T(8,128)(2,1)S(1)}, f32[512,128]{1,0:T(8,128)S(1)}) custom-call(bf16[1792,128]{1,0:T(8,128)(2,1)S(1)} %normalize.2.basis_ref, bf16[8,1024,1792]{2,1,0:T(8,128)(2,1)} %get-tuple-element.60.refs_2_.rotated_ref, bf16[512,128]{1,0:T(8,128)(2,1)S(1)} %fusion.57.refs_0_, bf16[512,128]{1,0:T(8,128)(2,1)S(1)} %fusion.48.refs_1_), custom_call_target="tpu_custom_call" | custom-call | flops 7516192768 | bytes 29360128 | tf_op jit(solution)/shard_map/image/pallas_call | solution.py:166
  401.5 5.7 collective-permute-done.44
  409.6 10.9 %returned.12 = (f32[128,1792]{1,0:T(8,128)S(1)}, f32[128,128]{1,0:T(8,128)S(1)}) custom-call(bf16[512,128]{1,0:T(8,128)(2,1)S(1)} %collective-permute-done.41.refs_0_, bf16[512,128]{1,0:T(8,128)(2,1)S(1)} %add_convert_fusion.19.refs_1_.refs_3_, bf16[8,1024,1792]{2,1,0:T(8,128)(2,1)} %get-tuple-element.65.refs_2_.rotated_ref, ...), custom_call_target="tpu_custom_call" | custom-call | flops 7516192768 | bytes 29360128 | tf_op jit(solution)/shard_map/returned/pallas_call | solution.py:230
  420.5 10.9 %returned.13 = (f32[128,1792]{1,0:T(8,128)S(1)}, f32[128,128]{1,0:T(8,128)S(1)}) custom-call(bf16[512,128]{1,0:T(8,128)(2,1)S(1)} %collective-permute-done.45.refs_2_.refs_0_, bf16[512,128]{1,0:T(8,128)(2,1)S(1)} %add_convert_fusion.18.refs_3_.refs_1_, bf16[8,1024,1792]{2,1,0:T(8,128)(2,1)} %get-tuple-element.64.refs_2_.rotated_ref, ...), custom_call_target="tpu_custom_call" | custom-call | flops 7516192768 | bytes 29360128 | tf_op jit(solution)/shard_map/returned/pallas_call | solution.py:230
  433.1 10.9 %returned.14 = (f32[128,1792]{1,0:T(8,128)S(1)}, f32[128,128]{1,0:T(8,128)S(1)}) custom-call(bf16[512,128]{1,0:T(8,128)(2,1)S(1)} %collective-permute-done.49.refs_4_.refs_0_, bf16[512,128]{1,0:T(8,128)(2,1)S(1)} %add_convert_fusion.17.refs_5_.refs_1_, bf16[8,1024,1792]{2,1,0:T(8,128)(2,1)} %get-tuple-element.63.refs_2_.rotated_ref, ...), custom_call_target="tpu_custom_call" | custom-call | flops 7516192768 | bytes 29360128 | tf_op jit(solution)/shard_map/returned/pallas_call | solution.py:230
  452.6 11.6 %returned.15 = (f32[128,1792]{1,0:T(8,128)S(1)}, f32[128,128]{1,0:T(8,128)}) custom-call(bf16[512,128]{1,0:T(8,128)(2,1)S(1)} %collective-permute-done.53.refs_6_.refs_0_, bf16[512,128]{1,0:T(8,128)(2,1)S(1)} %add_convert_fusion.16.refs_7_.refs_5_.refs_1_, bf16[8,1024,1792]{2,1,0:T(8,128)(2,1)} %get-tuple-element.60.refs_2_.rotated_ref, ...), custom_call_target="tpu_custom_call" | custom-call | flops 7516192768 | bytes 29360128 | tf_op jit(solution)/shard_map/returned/pallas_call | solution.py:230
  466.5 11.6 %collective-permute-done.56.got_ref = bf16[128,1792]{1,0:T(8,128)(2,1)S(1)} collective-permute-done((bf16[128,1792]{1,0:T(8,128)(2,1)}, bf16[128,1792]{1,0:T(8,128)(2,1)S(1)}, u32[]{:S(2)}, u32[]{:S(2)}) %collective-permute-start.56) | collective-permute-done | bytes 458784 | tf_op jit(solution)/shard_map/ppermute | solution.py:597
  521.7 13.8 %collective-permute-done.59 = bf16[448,256]{1,0:T(8,128)(2,1)S(1)} collective-permute-done((bf16[448,256]{1,0:T(8,128)(2,1)S(1)}, bf16[448,256]{1,0:T(8,128)(2,1)S(1)}, u32[]{:S(2)}, u32[]{:S(2)}) %collective-permute-start.59) | collective-permute-done | bytes 229408 | tf_op jit(solution)/shard_map/ppermute | solution.py:464
  549.5 8.5 %collective-permute-done.67 = bf16[448,256]{1,0:T(8,128)(2,1)S(1)} collective-permute-done((bf16[448,256]{1,0:T(8,128)(2,1)S(1)}, bf16[448,256]{1,0:T(8,128)(2,1)S(1)}, u32[]{:S(2)}, u32[]{:S(2)}) %collective-permute-start.67) | collective-permute-done | bytes 229408 | tf_op jit(solution)/shard_map/ppermute | solution.py:464
  558.2 12.1 %collective-permute-done.64 = bf16[448,256]{1,0:T(8,128)(2,1)S(1)} collective-permute-done((bf16[448,256]{1,0:T(8,128)(2,1)S(1)}, bf16[448,256]{1,0:T(8,128)(2,1)S(1)}, u32[]{:S(2)}, u32[]{:S(2)}) %collective-permute-start.64) | collective-permute-done | bytes 229408 | tf_op jit(solution)/shard_map/ppermute | solution.py:464
  595.1 6.7 %all-to-all-done.2 = bf16[4,512,256]{2,1,0:T(8,128)(2,1)} async-done(((bf16[4,512,256]{2,1,0:T(8,128)(2,1)}), bf16[4,512,256]{2,1,0:T(8,128)(2,1)}, u32[]{:S(2)}, u32[]{:S(2)}) %all-to-all-start.2) | async-done | bytes 1048608 | tf_op jit(solution)/shard_map/all_to_all | solution.py:624
  614.8 5.9 all-to-all-done.3
  (244 shorter events, 235.4 us)
Async XLA Ops:
  18.4 23.6 %collective-permute-start.6 = (bf16[256,1792]{1,0:T(8,128)(2,1)S(1)}, bf16[256,1792]{1,0:T(8,128)(2,1)}, u32[]{:S(2)}, u32[]{:S(2)}) collective-permute-start(bf16[256,1792]{1,0:T(8,128)(2,1)S(1)} %get-tuple-element.98), channel_id=1, source_target_pairs={{0,2},{1,3},{2,0},{3,1},{4,6},{5,7},{6,4},{7,5},{8,10},{9,11},{10,... | collective-permute-start | bytes 2752520 | tf_op jit(solution)/shard_map/ppermute | solution.py:548
  25.5 17.9 %collective-permute-start = (bf16[2048,256]{1,0:T(8,128)(2,1)S(1)}, bf16[2048,256]{1,0:T(8,128)(2,1)}, u32[]{:S(2)}, u32[]{:S(2)}) collective-permute-start(bf16[2048,256]{1,0:T(8,128)(2,1)S(1)} %fusion.5), channel_id=1, source_target_pairs={{0,1},{1,0},{2,3},{3,2},{4,5},{5,4},{6,7},{7,6},{8,9},{9,8},{10,11... | collective-permute-start | bytes 3145736 | tf_op jit(solution)/shard_map/ppermute | solution.py:437
  43.4 160.0 %collective-permute-start.7 = (f32[2048,1792]{1,0:T(8,128)}, f32[2048,1792]{1,0:T(8,128)}, u32[]{:S(2)}, u32[]{:S(2)}) collective-permute-start(f32[2048,1792]{1,0:T(8,128)} %refs_3_.3), channel_id=1, source_target_pairs={{0,1},{1,0},{2,3},{3,2},{4,5},{5,4},{6,7},{7,6},{8,9},{9,8},{10,11... | collective-permute-start | bytes 44040200 | tf_op jit(solution)/shard_map/ppermute | solution.py:437
  52.8 22.3 %collective-permute-start.8 = (bf16[512,256]{1,0:T(8,128)(2,1)}, bf16[512,256]{1,0:T(8,128)(2,1)}, u32[]{:S(2)}, u32[]{:S(2)}) collective-permute-start(bf16[512,256]{1,0:T(8,128)(2,1)} %get-tuple-element.105), channel_id=1, source_target_pairs={{0,4},{4,0},{1,5},{5,1},{2,6},{6,2},{3,7},{7,3},{8,12},{12,8},{9,1... | collective-permute-start | bytes 786440 | tf_op jit(solution)/shard_map/ppermute | solution.py:452
  80.0 18.6 %collective-permute-start.9 = (bf16[512,256]{1,0:T(8,128)(2,1)}, bf16[512,256]{1,0:T(8,128)(2,1)}, u32[]{:S(2)}, u32[]{:S(2)}) collective-permute-start(bf16[512,256]{1,0:T(8,128)(2,1)} %get-tuple-element.103), channel_id=1, source_target_pairs={{0,8},{8,0},{16,24},{24,16},{1,9},{9,1},{17,25},{25,17},{2,10},{10... | collective-permute-start | bytes 786440 | tf_op jit(solution)/shard_map/ppermute | solution.py:464
  85.9 17.7 %collective-permute-start.2 = (bf16[512,256]{1,0:T(8,128)(2,1)S(1)}, bf16[512,256]{1,0:T(8,128)(2,1)S(1)}, u32[]{:S(2)}, u32[]{:S(2)}) collective-permute-start(bf16[512,256]{1,0:T(8,128)(2,1)S(1)} %get-tuple-element.111), channel_id=1, source_target_pairs={{0,8},{8,0},{16,24},{24,16},{1,9},{9,1},{17,25},{25,17},{2,10},{10... | collective-permute-start | bytes 786440 | tf_op jit(solution)/shard_map/ppermute | solution.py:464
  85.9 18.0 %collective-permute-start.20 = (bf16[512,256]{1,0:T(8,128)(2,1)S(1)}, bf16[512,256]{1,0:T(8,128)(2,1)S(1)}, u32[]{:S(2)}, u32[]{:S(2)}) collective-permute-start(bf16[512,256]{1,0:T(8,128)(2,1)S(1)} %get-tuple-element.110), channel_id=1, source_target_pairs={{0,16},{8,24},{16,0},{24,8},{1,17},{9,25},{17,1},{25,9},{2,18},{10... | collective-permute-start | bytes 786440 | tf_op jit(solution)/shard_map/ppermute | solution.py:464
  100.4 22.2 %collective-permute-start.10 = (bf16[512,256]{1,0:T(8,128)(2,1)S(1)}, bf16[512,256]{1,0:T(8,128)(2,1)S(1)}, u32[]{:S(2)}, u32[]{:S(2)}) collective-permute-start(bf16[512,256]{1,0:T(8,128)(2,1)S(1)} %get-tuple-element.101), channel_id=1, source_target_pairs={{0,16},{8,24},{16,0},{24,8},{1,17},{9,25},{17,1},{25,9},{2,18},{10... | collective-permute-start | bytes 786440 | tf_op jit(solution)/shard_map/ppermute | solution.py:464
  105.3 22.9 %collective-permute-start.3 = (bf16[512,256]{1,0:T(8,128)(2,1)S(1)}, bf16[512,256]{1,0:T(8,128)(2,1)S(1)}, u32[]{:S(2)}, u32[]{:S(2)}) collective-permute-start(bf16[512,256]{1,0:T(8,128)(2,1)S(1)} %get-tuple-element.109.refs_6_), channel_id=1, source_target_pairs={{0,16},{8,24},{16,0},{24,8},{1,17},{9,25},{17,1},{25,9},{2,18},{10... | collective-permute-start | bytes 786440 | tf_op jit(solution)/shard_map/ppermute | solution.py:464
  125.6 33.5 %collective-permute-start.17 = (bf16[512,256]{1,0:T(8,128)(2,1)S(1)}, bf16[512,256]{1,0:T(8,128)(2,1)S(1)}, u32[]{:S(2)}, u32[]{:S(2)}) collective-permute-start(bf16[512,256]{1,0:T(8,128)(2,1)S(1)} %get-tuple-element.100.refs_1_), channel_id=1, source_target_pairs={{0,4},{4,0},{1,5},{5,1},{2,6},{6,2},{3,7},{7,3},{8,12},{12,8},{9,1... | collective-permute-start | bytes 786440 | tf_op jit(solution)/shard_map/ppermute | solution.py:470
  126.2 77.2 %collective-permute-start.26 = (bf16[512,256]{1,0:T(8,128)(2,1)S(1)}, bf16[512,256]{1,0:T(8,128)(2,1)S(1)}, u32[]{:S(2)}, u32[]{:S(2)}) collective-permute-start(bf16[512,256]{1,0:T(8,128)(2,1)S(1)} %get-tuple-element.108.refs_5_.refs_1_), channel_id=1, source_target_pairs={{0,4},{4,0},{1,5},{5,1},{2,6},{6,2},{3,7},{7,3},{8,12},{12,8},{9,1... | collective-permute-start | bytes 786440 | tf_op jit(solution)/shard_map/ppermute | solution.py:470
  129.3 99.9 %collective-permute-start.4 = (bf16[512,256]{1,0:T(8,128)(2,1)S(1)}, bf16[512,256]{1,0:T(8,128)(2,1)S(1)}, u32[]{:S(2)}, u32[]{:S(2)}) collective-permute-start(bf16[512,256]{1,0:T(8,128)(2,1)S(1)} %add_convert_fusion.3.refs_1_.refs_5_), channel_id=1, source_target_pairs={{0,4},{4,0},{1,5},{5,1},{2,6},{6,2},{3,7},{7,3},{8,12},{12,8},{9,1... | collective-permute-start | bytes 786440 | tf_op jit(solution)/shard_map/ppermute | solution.py:470
  157.6 26.1 %collective-permute-start.12 = (bf16[512,128]{1,0:T(8,128)(2,1)S(1)}, bf16[512,128]{1,0:T(8,128)(2,1)S(1)}, u32[]{:S(2)}, u32[]{:S(2)}) collective-permute-start(bf16[512,128]{1,0:T(8,128)(2,1)S(1)} %get-tuple-element.55), channel_id=1, source_target_pairs={{0,4},{4,0},{1,5},{5,1},{2,6},{6,2},{3,7},{7,3},{8,12},{12,8},{9,1... | collective-permute-start | bytes 393224 | tf_op jit(solution)/shard_map/ppermute | solution.py:452
  201.1 57.3 %collective-permute-start.35 = (bf16[512,128]{1,0:T(8,128)(2,1)S(1)}, bf16[512,128]{1,0:T(8,128)(2,1)S(1)}, u32[]{:S(2)}, u32[]{:S(2)}) collective-permute-start(bf16[512,128]{1,0:T(8,128)(2,1)S(1)} %add_convert_fusion.20.refs_1_.refs_3_), channel_id=1, source_target_pairs={{0,4},{4,0},{1,5},{5,1},{2,6},{6,2},{3,7},{7,3},{8,12},{12,8},{9,1... | collective-permute-start | bytes 393224 | tf_op jit(solution)/shard_map/ppermute | solution.py:470
  202.5 79.5 %collective-permute-start.33 = (bf16[512,128]{1,0:T(8,128)(2,1)S(1)}, bf16[512,128]{1,0:T(8,128)(2,1)S(1)}, u32[]{:S(2)}, u32[]{:S(2)}) collective-permute-start(bf16[512,128]{1,0:T(8,128)(2,1)S(1)} %add_convert_fusion.21.refs_1_.refs_3_), channel_id=1, source_target_pairs={{0,4},{4,0},{1,5},{5,1},{2,6},{6,2},{3,7},{7,3},{8,12},{12,8},{9,1... | collective-permute-start | bytes 393224 | tf_op jit(solution)/shard_map/ppermute | solution.py:470
  227.9 26.1 %collective-permute-start.27 = (bf16[512,128]{1,0:T(8,128)(2,1)S(1)}, bf16[512,128]{1,0:T(8,128)(2,1)S(1)}, u32[]{:S(2)}, u32[]{:S(2)}) collective-permute-start(bf16[512,128]{1,0:T(8,128)(2,1)S(1)} %get-tuple-element.62), channel_id=1, source_target_pairs={{0,4},{4,0},{1,5},{5,1},{2,6},{6,2},{3,7},{7,3},{8,12},{12,8},{9,1... | collective-permute-start | bytes 393224 | tf_op jit(solution)/shard_map/ppermute | solution.py:452
  372.8 21.2 %collective-permute-start.46 = (bf16[512,128]{1,0:T(8,128)(2,1)S(1)}, bf16[512,128]{1,0:T(8,128)(2,1)S(1)}, u32[]{:S(2)}, u32[]{:S(2)}) collective-permute-start(bf16[512,128]{1,0:T(8,128)(2,1)S(1)} %get-tuple-element.78), channel_id=1, source_target_pairs={{0,4},{4,0},{1,5},{5,1},{2,6},{6,2},{3,7},{7,3},{8,12},{12,8},{9,1... | collective-permute-start | bytes 393224 | tf_op jit(solution)/shard_map/ppermute | solution.py:452
  374.7 21.1 %collective-permute-start.43 = (bf16[512,128]{1,0:T(8,128)(2,1)S(1)}, bf16[512,128]{1,0:T(8,128)(2,1)S(1)}, u32[]{:S(2)}, u32[]{:S(2)}) collective-permute-start(bf16[512,128]{1,0:T(8,128)(2,1)S(1)} %fusion.48.refs_1_), channel_id=1, source_target_pairs={{0,8},{8,0},{16,24},{24,16},{1,9},{9,1},{17,25},{25,17},{2,10},{10... | collective-permute-start | bytes 393224 | tf_op jit(solution)/shard_map/ppermute | solution.py:464
  407.4 24.4 %collective-permute-start.52 = (bf16[512,128]{1,0:T(8,128)(2,1)S(1)}, bf16[512,128]{1,0:T(8,128)(2,1)S(1)}, u32[]{:S(2)}, u32[]{:S(2)}) collective-permute-start(bf16[512,128]{1,0:T(8,128)(2,1)S(1)} %fusion.60.refs_6_), channel_id=1, source_target_pairs={{0,16},{8,24},{16,0},{24,8},{1,17},{9,25},{17,1},{25,9},{2,18},{10... | collective-permute-start | bytes 393224 | tf_op jit(solution)/shard_map/ppermute | solution.py:464
  408.7 24.4 %collective-permute-start.49 = (bf16[512,128]{1,0:T(8,128)(2,1)S(1)}, bf16[512,128]{1,0:T(8,128)(2,1)S(1)}, u32[]{:S(2)}, u32[]{:S(2)}) collective-permute-start(bf16[512,128]{1,0:T(8,128)(2,1)S(1)} %add_convert_fusion.17.refs_5_.refs_1_), channel_id=1, source_target_pairs={{0,4},{4,0},{1,5},{5,1},{2,6},{6,2},{3,7},{7,3},{8,12},{12,8},{9,1... | collective-permute-start | bytes 393224 | tf_op jit(solution)/shard_map/ppermute | solution.py:470
  452.6 28.4 %collective-permute-start.55 = (bf16[2048,128]{0,1:T(8,128)(2,1)}, bf16[2048,128]{0,1:T(8,128)(2,1)}, u32[]{:S(2)}, u32[]{:S(2)}) collective-permute-start(bf16[2048,128]{0,1:T(8,128)(2,1)} %get-tuple-element.107), channel_id=1, source_target_pairs={{0,1},{1,0},{2,3},{3,2},{4,5},{5,4},{6,7},{7,6},{8,9},{9,8},{10,11... | collective-permute-start | bytes 1572872 | tf_op jit(solution)/shard_map/ppermute | solution.py:437
  501.1 19.0 %collective-permute-start.62 = (bf16[448,256]{1,0:T(8,128)(2,1)}, bf16[448,256]{1,0:T(8,128)(2,1)}, u32[]{:S(2)}, u32[]{:S(2)}) collective-permute-start(bf16[448,256]{1,0:T(8,128)(2,1)} %get-tuple-element.91), channel_id=1, source_target_pairs={{0,4},{4,0},{1,5},{5,1},{2,6},{6,2},{3,7},{7,3},{8,12},{12,8},{9,1... | collective-permute-start | bytes 688136 | tf_op jit(solution)/shard_map/ppermute | solution.py:452
  507.6 75.4 %all-to-all-start.1 = ((bf16[8,256,256]{2,1,0:T(8,128)(2,1)}), bf16[8,256,256]{2,1,0:T(8,128)(2,1)}, u32[]{:S(2)}, u32[]{:S(2)}) async-start(bf16[8,256,256]{2,1,0:T(8,128)(2,1)} %broadcast_in_dim.2), calls=%async_computation.1 | async-start | bytes 2097152 | tf_op jit(solution)/shard_map/all_to_all | solution.py:514
  513.2 22.2 %collective-permute-start.59 = (bf16[448,256]{1,0:T(8,128)(2,1)S(1)}, bf16[448,256]{1,0:T(8,128)(2,1)S(1)}, u32[]{:S(2)}, u32[]{:S(2)}) collective-permute-start(bf16[448,256]{1,0:T(8,128)(2,1)S(1)} %add_convert_fusion.15.refs_0_), channel_id=1, source_target_pairs={{0,8},{8,0},{16,24},{24,16},{1,9},{9,1},{17,25},{25,17},{2,10},{10... | collective-permute-start | bytes 688136 | tf_op jit(solution)/shard_map/ppermute | solution.py:464
  518.5 26.3 %collective-permute-start.66 = (bf16[448,256]{1,0:T(8,128)(2,1)S(1)}, bf16[448,256]{1,0:T(8,128)(2,1)S(1)}, u32[]{:S(2)}, u32[]{:S(2)}) collective-permute-start(bf16[448,256]{1,0:T(8,128)(2,1)S(1)} %get-tuple-element.93), channel_id=1, source_target_pairs={{0,4},{4,0},{1,5},{5,1},{2,6},{6,2},{3,7},{7,3},{8,12},{12,8},{9,1... | collective-permute-start | bytes 688136 | tf_op jit(solution)/shard_map/ppermute | solution.py:452
  521.1 24.4 %collective-permute-start.63 = (bf16[448,256]{1,0:T(8,128)(2,1)S(1)}, bf16[448,256]{1,0:T(8,128)(2,1)S(1)}, u32[]{:S(2)}, u32[]{:S(2)}) collective-permute-start(bf16[448,256]{1,0:T(8,128)(2,1)S(1)} %add_convert_fusion.12.refs_1_), channel_id=1, source_target_pairs={{0,8},{8,0},{16,24},{24,16},{1,9},{9,1},{17,25},{25,17},{2,10},{10... | collective-permute-start | bytes 688136 | tf_op jit(solution)/shard_map/ppermute | solution.py:464
  538.8 33.1 %collective-permute-start.60 = (bf16[448,256]{1,0:T(8,128)(2,1)S(1)}, bf16[448,256]{1,0:T(8,128)(2,1)S(1)}, u32[]{:S(2)}, u32[]{:S(2)}) collective-permute-start(bf16[448,256]{1,0:T(8,128)(2,1)S(1)} %add_convert_fusion.14.refs_0_), channel_id=1, source_target_pairs={{0,16},{8,24},{16,0},{24,8},{1,17},{9,25},{17,1},{25,9},{2,18},{10... | collective-permute-start | bytes 688136 | tf_op jit(solution)/shard_map/ppermute | solution.py:464
  545.5 24.7 %collective-permute-start.64 = (bf16[448,256]{1,0:T(8,128)(2,1)S(1)}, bf16[448,256]{1,0:T(8,128)(2,1)S(1)}, u32[]{:S(2)}, u32[]{:S(2)}) collective-permute-start(bf16[448,256]{1,0:T(8,128)(2,1)S(1)} %add_convert_fusion.11), channel_id=1, source_target_pairs={{0,16},{8,24},{16,0},{24,8},{1,17},{9,25},{17,1},{25,9},{2,18},{10... | collective-permute-start | bytes 688136 | tf_op jit(solution)/shard_map/ppermute | solution.py:464
  549.5 23.1 %collective-permute-start.71 = (bf16[448,256]{1,0:T(8,128)(2,1)S(1)}, bf16[448,256]{1,0:T(8,128)(2,1)S(1)}, u32[]{:S(2)}, u32[]{:S(2)}) collective-permute-start(bf16[448,256]{1,0:T(8,128)(2,1)S(1)} %add_convert_fusion.6), channel_id=1, source_target_pairs={{0,8},{8,0},{16,24},{24,16},{1,9},{9,1},{17,25},{25,17},{2,10},{10... | collective-permute-start | bytes 688136 | tf_op jit(solution)/shard_map/ppermute | solution.py:464
  570.3 21.2 %collective-permute-start.65 = (bf16[448,256]{1,0:T(8,128)(2,1)S(1)}, bf16[448,256]{1,0:T(8,128)(2,1)S(1)}, u32[]{:S(2)}, u32[]{:S(2)}) collective-permute-start(bf16[448,256]{1,0:T(8,128)(2,1)S(1)} %add_convert_fusion.10.refs_3_), channel_id=1, source_target_pairs={{0,4},{4,0},{1,5},{5,1},{2,6},{6,2},{3,7},{7,3},{8,12},{12,8},{9,1... | collective-permute-start | bytes 688136 | tf_op jit(solution)/shard_map/ppermute | solution.py:470
  571.9 19.6 %collective-permute-start.61 = (bf16[448,256]{1,0:T(8,128)(2,1)S(1)}, bf16[448,256]{1,0:T(8,128)(2,1)S(1)}, u32[]{:S(2)}, u32[]{:S(2)}) collective-permute-start(bf16[448,256]{1,0:T(8,128)(2,1)S(1)} %add_convert_fusion.13.refs_1_), channel_id=1, source_target_pairs={{0,4},{4,0},{1,5},{5,1},{2,6},{6,2},{3,7},{7,3},{8,12},{12,8},{9,1... | collective-permute-start | bytes 688136 | tf_op jit(solution)/shard_map/ppermute | solution.py:470
  583.0 18.8 %all-to-all-start.2 = ((bf16[4,512,256]{2,1,0:T(8,128)(2,1)}), bf16[4,512,256]{2,1,0:T(8,128)(2,1)}, u32[]{:S(2)}, u32[]{:S(2)}) async-start(bf16[4,512,256]{2,1,0:T(8,128)(2,1)} %bitcast.20), calls=%async_computation.2 | async-start | bytes 2097152 | tf_op jit(solution)/shard_map/all_to_all | solution.py:624
  (55 other events, 1177.3 us)

commit v5 on v4

--- a/solution.py
+++ b/solution.py
@@ -97,7 +97,9 @@
             span = slice(begin, begin + width)
             block = jnp.dot(own, right[:, span], preferred_element_type=f32)
             rotated_ref[at, :, span] = (block * weight[:, span]).astype(bf16)
-    add_images(image_of(rotated_ref, basis_ref), first, rows, image)
+        product = jnp.dot(rotated_ref[at], basis_ref[...], preferred_element_type=f32)
+        lane = lax.broadcasted_iota(jnp.int32, (rows, COLS), 1) // RANK
+        image[...] = jnp.where(lane == query, product, image[...])
     write_image(image, send_ref, keep_ref)
 
 
@@ -246,108 +248,234 @@
     )(*images, rotated, *([] if first else before), *ties)
 
 
-def rotate_in_kernel(place_ref, query_ref, eigen_ref, theirs_ref, mine_ref):
+def rotate_out_kernel(n_dp, place_ref, query_ref, eigen_ref, *refs):
+    turned = refs[-1]
+    width = eigen_ref.shape[1]
+    rows = width // (PIECES * n_dp)
+    for side, index in ((0, place_ref[1]), (1, 1 - place_ref[1])):
+        queries = query_ref[pl.ds(pl.multiple_of(index * TOKS, TOKS), TOKS), :]
+        for begin, count in chunks(width):
+            product = jnp.dot(
+                queries, eigen_ref[:, begin : begin + count], preferred_element_type=f32
+            )
+            turned[begin : begin + count, :] = product.T
+        for piece in range(PIECES):
+            send_ref, keep_ref = refs[2 * (side * PIECES + piece) :][:2]
+            for part in range(n_dp):
+                at = piece * n_dp + lax.rem(place_ref[0] + 1 + part, n_dp)
+                taken = turned[pl.ds(pl.multiple_of(at * rows, rows), rows), :]
+                if part < n_dp - 1:
+                    send_ref[part * rows : (part + 1) * rows, :] = taken.astype(bf16)
+                else:
+                    keep_ref[...] = taken.astype(keep_ref.dtype)
+
+
+def rotate_out(place, query_out, eigen_out, n_dp):
+    width = eigen_out.shape[1]
+    rows = width // (PIECES * n_dp)
+    shapes = []
+    for kind in (f32, bf16):
+        for _ in range(PIECES):
+            shapes.append(jax.ShapeDtypeStruct(((n_dp - 1) * rows, TOKS), bf16))
+            shapes.append(jax.ShapeDtypeStruct((rows, TOKS), kind))
+    vmem = pl.BlockSpec(memory_space=pltpu.VMEM)
+    return pl.pallas_call(
+        functools.partial(rotate_out_kernel, n_dp),
+        in_specs=[pl.BlockSpec(memory_space=pltpu.SMEM), vmem, vmem],
+        out_specs=[vmem] * len(shapes),
+        out_shape=shapes,
+        scratch_shapes=[pltpu.VMEM((width, TOKS), f32)],
+        compiler_params=params(),
+        name="rotate_out",
+    )(place, query_out, eigen_out)
+
+
+def rotate_in_kernel(n_ties, place_ref, query_ref, eigen_ref, *refs):
+    theirs_ref, mine_ref, product = refs[n_ties:]
+    product[...] = jnp.dot(query_ref[...], eigen_ref[...], preferred_element_type=f32)
     for out_ref, index in ((theirs_ref, 1 - place_ref[1]), (mine_ref, place_ref[1])):
-        rows = pl.ds(pl.multiple_of(index * TOKS, TOKS), TOKS)
-        out_ref[...] = jnp.dot(query_ref[rows, :], eigen_ref[...], preferred_element_type=f32)
-
-
-def rotate_in(place, query_in, eigen_in):
+        out_ref[...] = product[pl.ds(pl.multiple_of(index * TOKS, TOKS), TOKS), :]
+
+
+def rotate_in(place, query_in, eigen_in, ties):
     depth, cols = eigen_in.shape
     width = LANES if cols % LANES == 0 else cols
     out = jax.ShapeDtypeStruct((TOKS, cols), f32)
     return pl.pallas_call(
-        rotate_in_kernel,
+        functools.partial(rotate_in_kernel, len(ties)),
         grid_spec=pltpu.PrefetchScalarGridSpec(
             num_scalar_prefetch=1,
             grid=(cols // width,),
             in_specs=[
                 pl.BlockSpec(query_in.shape, lambda at, _: (0, 0)),
                 pl.BlockSpec((depth, width), lambda at, _: (0, at)),
-            ],
+            ]
+            + tied(ties),
             out_specs=[pl.BlockSpec((TOKS, width), lambda at, _: (0, at))] * 2,
+            scratch_shapes=[pltpu.VMEM((CORES * TOKS, width), f32)],
         ),
         out_shape=[out, out],
         compiler_params=params(),
+        cost_estimate=pl.CostEstimate(
+            flops=2 * depth * cols * CORES * TOKS, bytes_accessed=2 * depth * cols, transcendentals=0
+        ),
         name="rotate_in",
-    )(place, query_in, eigen_in)
-
-
-def factor_kernel(n_ties, place_ref, eigen_ref, cols_ref, *refs):
-    send_ref, keep_ref = refs[n_ties:]
-    part, parts = pl.program_id(0), pl.num_programs(0)
-    product = jnp.dot(eigen_ref[...], cols_ref[...], preferred_element_type=f32)
-
-    @pl.when(part < parts - 1)
+    )(place, query_in, eigen_in, *ties)
+
+
+def side_by_side(place_ref, mine, theirs):
+    return jnp.where(
+        place_ref[1] == 0,
+        jnp.concatenate([mine, theirs], axis=1),
+        jnp.concatenate([theirs, mine], axis=1),
+    )
+
+
+def factor_kernel(n_dp, place_ref, eigen_ref, mine_ref, theirs_ref, *refs):
+    *out_refs, cols = refs
+    step = pl.program_id(0)
+    rows = eigen_ref.shape[0]
+
+    @pl.when(step == 0)
     def _():
-        send_ref[...] = product.astype(bf16)
-
-    @pl.when(part == parts - 1)
-    def _():
-        keep_ref[...] = product
-
-
-def factor_piece(place, eigen_in, in_cols, piece, pieces, n_dp, ties):
+        cols[...] = side_by_side(place_ref, mine_ref[...], theirs_ref[...])
+
+    product = jnp.dot(eigen_ref[...], cols[...], preferred_element_type=f32)
+    for piece in range(FACTOR_PIECES):
+        send_ref, keep_ref = out_refs[2 * piece : 2 * piece + 2]
+        for part in range(n_dp):
+
+            @pl.when(step == piece * n_dp + part)
+            def _(part=part, send_ref=send_ref, keep_ref=keep_ref):
+                if part < n_dp - 1:
+                    send_ref[part * rows : (part + 1) * rows, :] = product.astype(bf16)
+                else:
+                    keep_ref[...] = product
+
+
+def factor_in(place, eigen_in, mine, theirs, n_dp):
     rows, depth = eigen_in.shape
-    rows = rows // (pieces * n_dp)
-    width = in_cols.shape[1]
-    return pl.pallas_call(
-        functools.partial(factor_kernel, len(ties)),
+    rows = rows // (FACTOR_PIECES * n_dp)
+    width = CORES * COLS
+    fixed = pl.BlockSpec((depth, COLS), lambda at, _: (0, 0))
+
+    def eigen_block(at, place_ref):
+        return at // n_dp * n_dp + lax.rem(place_ref[0] + 1 + at % n_dp, n_dp), 0
+
+    shapes = [
+        jax.ShapeDtypeStruct(((n_dp - 1) * rows, width), bf16),
+        jax.ShapeDtypeStruct((rows, width), f32),
+    ] * FACTOR_PIECES
+    return pl.pallas_call(
+        functools.partial(factor_kernel, n_dp),
         grid_spec=pltpu.PrefetchScalarGridSpec(
             num_scalar_prefetch=1,
-            grid=(n_dp,),
-            in_specs=[
-                pl.BlockSpec(
-                    (rows, depth),
-                    lambda part, place_ref: (
-                        piece * n_dp + lax.rem(place_ref[0] + 1 + part, n_dp),
-                        0,
-                    ),
-                ),
-                pl.BlockSpec((depth, width), lambda part, _: (0, 0)),
-            ]
-            + tied(ties),
-            out_specs=[
-                pl.BlockSpec((rows, width), lambda part, _: (jnp.minimum(part, n_dp - 2), 0)),
-                pl.BlockSpec((rows, width), lambda part, _: (0, 0)),
-            ],
+            grid=(FACTOR_PIECES * n_dp,),
+            in_specs=[pl.BlockSpec((rows, depth), eigen_block), fixed, fixed],
+            out_specs=[pl.BlockSpec(each.shape, lambda at, _: (0, 0)) for each in shapes],
+            scratch_shapes=[pltpu.VMEM((depth, width), bf16)],
         ),
-        out_shape=[
-            jax.ShapeDtypeStruct(((n_dp - 1) * rows, width), bf16),
-            jax.ShapeDtypeStruct((rows, width), f32),
-        ],
-        compiler_params=params(),
-        name="factor",
-    )(place, eigen_in, in_cols, *ties)
-
-
-def project_kernel(n_dp, place_ref, hidden_ref, *refs):
-    *part_refs, factor_ref, proj_ref = refs
+        out_shape=shapes,
+        compiler_params=params(),
+        name="factor_in",
+    )(place, eigen_in, mine, theirs)
+
+
+def write_shares(place_ref, total, keep_ref, send_refs):
+    rows = keep_ref.shape[0]
+    for step in range(len(send_refs) + 1):
+        other = place_ref[2] ^ step
+        share = total[pl.ds(pl.multiple_of(other * rows, rows), rows), :]
+        if step == 0:
+            keep_ref[...] = share
+        else:
+            send_refs[step - 1][...] = share.astype(bf16)
+
+
+def factor_out_kernel(place_ref, eigen_ref, mine_ref, theirs_ref, keep_ref, *refs):
+    *send_refs, total = refs
+    total[...] = jnp.dot(
+        eigen_ref[...],
+        side_by_side(place_ref, mine_ref[...], theirs_ref[...]),
+        preferred_element_type=f32,
+    )
+    write_shares(place_ref, total, keep_ref, send_refs)
+
+
+def shares(rows, width, n_width):
+    shape = (rows // n_width, width)
+    return [jax.ShapeDtypeStruct(shape, f32)] + [jax.ShapeDtypeStruct(shape, bf16)] * (n_width - 1)
+
+
+def factor_out(place, eigen_out, mine, theirs, n_width):
+    rows = eigen_out.shape[0]
+    width = CORES * COLS
+    vmem = pl.BlockSpec(memory_space=pltpu.VMEM)
+    return pl.pallas_call(
+        factor_out_kernel,
+        in_specs=[pl.BlockSpec(memory_space=pltpu.SMEM)] + [vmem] * 3,
+        out_specs=[vmem] * n_width,
+        out_shape=shares(rows, width, n_width),
+        scratch_shapes=[pltpu.VMEM((rows, width), f32)],
+        compiler_params=params(),
+        name="factor_out",
+    )(place, eigen_out, mine, theirs)
+
+
+def project_kernel(n_dp, n_parts, place_ref, hidden_ref, *refs):
+    part_refs = refs[:n_parts]
+    factor_ref, keep_ref, *send_refs, total = refs[n_parts:]
     rows = part_refs[0].shape[0]
     for at, ref in enumerate(part_refs):
         owner = lax.rem(place_ref[0] + 1 + at % n_dp, n_dp)
         begin = (at // n_dp * n_dp + owner) * rows
         factor_ref[pl.ds(pl.multiple_of(begin, 8), rows), :] = ref[...]
-    proj_ref[...] = jnp.dot(
-        hidden_ref[...], factor_ref[...], preferred_element_type=f32
-    ).astype(bf16)
-
-
-def project(place, hidden, parts, n_dp):
+    total[...] = jnp.dot(hidden_ref[...], factor_ref[...], preferred_element_type=f32)
+    write_shares(place_ref, total, keep_ref, send_refs)
+
+
+def project(place, hidden, parts, n_dp, n_width):
     tokens, depth = hidden.shape
     width = parts[0].shape[1]
     vmem = pl.BlockSpec(memory_space=pltpu.VMEM)
     return pl.pallas_call(
-        functools.partial(project_kernel, n_dp),
+        functools.partial(project_kernel, n_dp, len(parts)),
         in_specs=[pl.BlockSpec(memory_space=pltpu.SMEM)] + [vmem] * (1 + len(parts)),
-        out_specs=[vmem, vmem],
-        out_shape=[
-            jax.ShapeDtypeStruct((depth, width), bf16),
-            jax.ShapeDtypeStruct((tokens, width), bf16),
-        ],
+        out_specs=[vmem] * (1 + n_width),
+        out_shape=[jax.ShapeDtypeStruct((depth, width), bf16)] + shares(tokens, width, n_width),
+        scratch_shapes=[pltpu.VMEM((tokens, width), f32)],
         compiler_params=params(),
         name="project",
     )(place, hidden, *parts)
+
+
+def turn_kernel(n_dp, place_ref, inverse_ref, *refs):
+    *image_refs, mine_ref, theirs_ref = refs
+    rows = image_refs[0].shape[0]
+    for at, ref in enumerate(image_refs):
+        out_ref = mine_ref if at < PIECES * n_dp else theirs_ref
+        owner = lax.rem(place_ref[0] + 1 + at % n_dp, n_dp)
+        begin = (at // n_dp % PIECES * n_dp + owner) * rows
+        out_ref[pl.ds(pl.multiple_of(begin, rows), rows), :] = lax.dot_general(
+            ref[...].astype(f32),
+            inverse_ref[...],
+            (((1,), (1,)), ((), ())),
+            precision=lax.Precision.HIGHEST,
+            preferred_element_type=f32,
+        ).astype(bf16)
+
+
+def turn(place, inverse, images, n_dp):
+    out = jax.ShapeDtypeStruct((PIECES * n_dp * images[0].shape[0], COLS), bf16)
+    vmem = pl.BlockSpec(memory_space=pltpu.VMEM)
+    return pl.pallas_call(
+        functools.partial(turn_kernel, n_dp),
+        in_specs=[pl.BlockSpec(memory_space=pltpu.SMEM)] + [vmem] * (1 + len(images)),
+        out_specs=[vmem, vmem],
+        out_shape=[out, out],
+        compiler_params=params(),
+        name="turn",
+    )(place, inverse, *images)
 
 
 def gram_kernel(*refs):
@@ -405,7 +533,8 @@
     )(gram, gram_got)
 
 
-def normalize_kernel(total_ref, got_ref, inverse_ref, basis_ref):
+def normalize_kernel(total_ref, got_ref, inverse_ref, *refs):
+    basis_ref = refs[-1]
     total = total_ref[...] + got_ref[...].astype(f32)
     basis_ref[...] = lax.dot_general(
         total,
@@ -416,13 +545,16 @@
     ).astype(bf16)
 
 
-def normalize(total, got, inverse):
+def normalize(total, got, inverse, ties):
+    vmem = pl.BlockSpec(memory_space=pltpu.VMEM)
     return pl.pallas_call(
         normalize_kernel,
+        in_specs=[vmem] * 3 + tied(ties),
+        out_specs=vmem,
         out_shape=jax.ShapeDtypeStruct((total.shape[1], COLS), bf16),
         compiler_params=params(),
         name="normalize",
-    )(total, got, inverse)
+    )(total, got, inverse, *ties)
 
 
 def turned_by(count, step):
@@ -439,7 +571,7 @@
 
 class Reduction:
     def __init__(self, sends, keep, n_grp, n_dp, even=False):
-        self.parts = None
+        self.parts = self.own = None
         self.steps = self.run(sends, keep, n_grp, n_dp, even)
         next(self.steps)
 
@@ -465,7 +597,7 @@
             yield [sent]
             total = (sent.astype(f32) if even else total) + got.astype(f32)
             step *= 2
-        own = total.astype(bf16)
+        own = self.own = total.astype(bf16)
         others = [
             lax.ppermute(own, "dp", turned_by(n_dp, n_dp - 1 - at)) for at in range(n_dp - 1)
         ]
@@ -488,19 +620,15 @@
     return ties
 
 
-def unrolled(parts, dp):
-    whole = jnp.stack(parts)
-    whole = jnp.roll(whole, dp + 1, axis=0)
-    return whole.reshape((-1,) + whole.shape[2:])
-
-
-def split_parts(part, dp, n_dp, piece, pieces):
-    rows = part.shape[0] // (pieces * n_dp)
-    taken = [
-        lax.dynamic_slice_in_dim(part, piece * n_dp * rows + (dp + 1 + at) % n_dp * rows, rows, 0)
-        for at in range(n_dp)
-    ]
-    return jnp.concatenate(taken[:-1], axis=0).astype(bf16), taken[-1].astype(f32)
+def after(array, others):
+    return lax.optimization_barrier((array, *others))[0] if others else array
+
+
+def sum_shares(keep, sends, n_width):
+    total = keep
+    for at, send in enumerate(sends):
+        total = total + lax.ppermute(send, "width", crossed(n_width, at + 1)).astype(f32)
+    return total
 
 
 def sum_scatter(part, axes, count):
@@ -522,46 +650,51 @@
         query_out, query_in, eigen_out, eigen_in, eigvals, start, grads_out, gate_pre, up_pre
     ):
         dp = lax.axis_index("dp")
-        core = lax.axis_index("width") % CORES
-        place = jnp.stack([dp, core]).astype(jnp.int32)
+        along = lax.axis_index("width")
+        core = along % CORES
+        place = jnp.stack([dp, core, along]).astype(jnp.int32)
         scale = 1.0 / (eigen_out.shape[0] * n_gd)
         rows_out = eigvals.shape[0]
 
-        def rows_of(array, index):
-            return lax.dynamic_slice_in_dim(array, index * TOKS, TOKS, 0)
-
-        def rotate_out(queries):
-            return lax.dot_general(
-                eigen_out, queries, (((0,), (1,)), ((), ())), preferred_element_type=f32
-            )
-
         def reduction(sends, keep, even=False):
             return Reduction(sends, keep, n_grp, n_dp, even)
 
-        theirs_in, mine_in = rotate_in(place, query_in, eigen_in)
-        total_in = mine_in + swap_cores(theirs_in, n_width)
-        mine_out = rotate_out(rows_of(query_out, core))
-        theirs_out = rotate_out(rows_of(query_out, 1 - core)).astype(bf16)
-        theirs_out = swap_cores(theirs_out, n_width)
-        step = 2
-        while step < n_width:
-            got = lax.ppermute(total_in.astype(bf16), "width", crossed(n_width, step))
-            total_in = total_in + got.astype(f32)
-            step *= 2
-        rot_in = total_in.astype(bf16)
-        eig_sent, _, _ = lax.optimization_barrier((eigvals, theirs_out, total_in))
-        eig_theirs = swap_cores(eig_sent, n_width)
-
-        turning = []
-        for part in (mine_out, theirs_out):
-            for piece in range(PIECES):
-                advance_all(turning)
-                turning.append(reduction(*split_parts(part, dp, n_dp, piece, PIECES)))
+        def sum_gram(parts):
+            gram = gram_of(parts)
+            total = gram
+            for step in range(1, n_dp):
+                total = total + lax.ppermute(gram, "dp", turned_by(n_dp, step))
+            return sum_but_last(total, f32)
+
+        def sum_but_last(total, kind):
+            step = 2
+            while True:
+                got = lax.ppermute(total.astype(kind), "width", crossed(n_width, step))
+                step *= 2
+                if step >= n_width:
+                    return total, got
+                total = total + got.astype(f32)
+
+        pieces = list(rotate_out(place, query_out, eigen_out, n_dp))
+        own_pieces, their_pieces = pieces[: 2 * PIECES], pieces[2 * PIECES :]
+        theirs_in, mine_in = rotate_in(place, query_in, eigen_in, pieces[:1])
+        turning = [reduction(own_pieces[0], own_pieces[1])]
+        their_pieces = [swap_cores(each, n_width) for each in their_pieces]
+        theirs_in = swap_cores(theirs_in, n_width)
+        total_in, got = sum_but_last(mine_in + theirs_in, bf16)
+        rot_in = (total_in + got.astype(f32)).astype(bf16)
+        hops = []
+        count = CORES * PIECES
+        for at in range(1, count):
+            hops = advance_all(turning)
+            sends, keep = (own_pieces + their_pieces)[2 * at : 2 * at + 2]
+            turning.append(reduction(after(sends, hops[:1]), keep))
+        eig_theirs = swap_cores(after(eigvals, [theirs_in, their_pieces[-1], *hops[:1]]), n_width)
+        hidden = (jax.nn.silu(gate_pre.astype(f32)) * up_pre.astype(f32)).astype(bf16)
         basis = lax.dynamic_slice_in_dim(start, core * COLS, COLS, 1)
-        count = len(turning)
         rotated = []
         for iteration in range(ITERS):
-            summing, ties = [], []
+            summing, ties = [], [hidden] if iteration == 0 else []
             for at in range(count):
                 if iteration == 0:
                     finish(turning[at], turning)
@@ -576,49 +709,44 @@
                     ties = []
                 ties += advance_all(summing)
                 summing.append(reduction(sends, keep))
-            sums = None
+            sums = gram = None
             for at in range(count):
                 finish(summing[at], summing)
-                if at == count - 1:
-                    gram = gram_of([part for each in summing for part in each.parts])
-                    step = 2
-                    while step < n_width:
-                        gram_got = lax.ppermute(gram, "width", crossed(n_width, step))
-                        step *= 2
-                        if step < n_width:
-                            gram = gram + gram_got
-                    ties = [gram]
+                if gram is None and all(each.own is not None for each in summing):
+                    gram, gram_got = sum_gram([each.own for each in summing])
+                    ties = ties + [gram]
+                elif gram is not None and at == count - 1:
+                    inverse = inverse_of(gram, gram_got, scale)
+                    ties = ties + [inverse]
+                    if iteration == ITERS - 1:
+                        images = [part for each in summing for part in each.parts]
+                        mine_out, theirs_out = turn(place, inverse, images, n_dp)
+                        theirs_out = swap_cores(theirs_out, n_width)
+                        ties = ties + [mine_out]
                 sums = return_piece(summing[at].parts, rotated[at], sums, ties)
                 ties = advance_all(summing)
-            inverse = inverse_of(gram, gram_got, scale)
-            total = sums[0]
-            step = 2
-            while step < n_width:
-                got = lax.ppermute(total.astype(bf16), "width", crossed(n_width, step))
-                step *= 2
-                if step < n_width:
-                    total = total + got.astype(f32)
-            basis = normalize(total, got, inverse)
-
-        def columns(mine, theirs):
-            return jnp.where(
-                core == 0,
-                jnp.concatenate([mine, theirs], axis=1),
-                jnp.concatenate([theirs, mine], axis=1),
-            )
-
-        hidden = (jax.nn.silu(gate_pre.astype(f32)) * up_pre.astype(f32)).astype(bf16)
-        image = jnp.concatenate([unrolled(each.parts, dp) for each in summing], axis=0)
-        basis_out = lax.dot_general(
-            image.astype(f32),
-            inverse,
-            (((1,), (1,)), ((), ())),
-            precision=lax.Precision.HIGHEST,
-            preferred_element_type=f32,
-        ).astype(bf16)
-        out_cols = columns(basis_out[:rows_out], swap_cores(basis_out[rows_out:], n_width))
-        part_factor_out = jnp.dot(eigen_out, out_cols, preferred_element_type=f32)
-        share = sum_scatter(part_factor_out, "width", n_width).astype(bf16)
+            total, got = sum_but_last(sums[0], bf16)
+            ties = []
+            if iteration == ITERS - 1:
+                keep_out, *sends_out = factor_out(
+                    place, eigen_out, mine_out, after(theirs_out, [total]), n_width
+                )
+                ties = [keep_out]
+            basis = normalize(total, got, inverse, ties)
+
+        their_basis = swap_cores(basis, n_width)
+        pieces = factor_in(place, eigen_in, basis, their_basis, n_dp)
+        share = sum_shares(keep_out, sends_out, n_width).astype(bf16)
+        factors, hops = [], []
+        for at in range(FACTOR_PIECES):
+            sends, keep = pieces[2 * at : 2 * at + 2]
+            factors.append(reduction(after(sends, hops[:1]), keep, even=True))
+            hops = advance_all(factors)
+        for each in factors:
+            finish(each, factors)
+        parts = [part for each in factors for part in each.parts]
+        in_factor, keep_in, *sends_in = project(place, hidden, parts, n_dp, n_width)
+
         piece_rows = share.shape[0]
         gathered = gather_rows(share, GD, n_gd)
         mixed = lax.all_to_all(gathered, "width", 0, 0, tiled=True)
@@ -627,21 +755,9 @@
             .transpose(1, 0, 2, 3)
             .reshape(rows_out, NQ * RANK)
         )
-        in_cols = columns(basis, swap_cores(basis, n_width))
-        factors, ties = [], []
-        for piece in range(FACTOR_PIECES):
-            sends, keep = factor_piece(
-                place, eigen_in, in_cols, piece, FACTOR_PIECES, n_dp, ties
-            )
-            ties = advance_all(factors)
-            factors.append(reduction(sends, keep, even=True))
-        for each in factors:
-            finish(each, factors)
-        parts = [part for each in factors for part in each.parts]
-        in_factor, proj_in = project(place, hidden, parts, n_dp)
         proj_out = jnp.dot(grads_out, out_factor, preferred_element_type=f32)
         proj_out = sum_scatter(proj_out, "width", n_width)
-        proj_in = sum_scatter(proj_in, "width", n_width)
+        proj_in = sum_shares(keep_in, sends_in, n_width)
         scores = (proj_out * proj_in).reshape(proj_out.shape[0], NQ, RANK).sum(axis=2).T
         return (scores, out_factor, in_factor)
 

time: 629 us -> 584 us (0.928)
  waiting for transfers between devices: 183 us -> 153 us
  matrix products: 15.5 us -> 0.76 us
  starting transfers between devices: 104 us -> 113 us
  other arithmetic: 30.1 us -> 22 us
  Pallas kernels: 273 us -> 281 us
    ppermute x16, waiting for transfers between devices: 21.5 us -> 39.7 us  [run(): lax.ppermute(sends[at * rows:(at + 1) * rows], 'dp', turned_by(n_dp, at +...]
    ppermute x32, waiting for transfers between devices: 98.5 us -> 82.3 us  [run(): got = lax.ppermute(sent, 'grp', crossed(n_grp, step))]
    ppermute x5 -> x13, waiting for transfers between devices: 41 us -> 24.9 us  [the longest x5 20.7 us: sum_but_last(): got = lax.ppermute(total.astype(kind), 'width', crossed(n_width, step))]
    dot_general x4 -> x0, matrix products: 14.8 us -> none  [the longest x2 9.65 us: rotate_out(): lax.dot_general(eigen_out, queries, (((0,), (1,)), ((), ())), preferred_e...]
    ppermute x32, starting transfers between devices: 40.1 us -> 50.1 us  [run(): got = lax.ppermute(sent, 'grp', crossed(n_grp, step))]
    all_to_all x3 -> x1, waiting for transfers between devices: 9.02 us -> 0.01 us  [sum_scatter(): pieces = lax.all_to_all(part.astype(bf16), axes, 0, 0, tiled=True)]
    all_to_all x3 -> x1, starting transfers between devices: 10.9 us -> 4.03 us  [sum_scatter(): pieces = lax.all_to_all(part.astype(bf16), axes, 0, 0, tiled=True)]
    all_to_all x1, waiting for transfers between devices: 6.72 us -> 0.01 us  [per_device(): mixed = lax.all_to_all(gathered, 'width', 0, 0, tiled=True)]
  transfers between devices with their start and end apart: 79 -> 88, of which waited for: 36 -> 35; matrix products, arithmetic and copies ran while one was open for 8% -> 4% of each run, Pallas kernels for 36% -> 38%
where the time goes in v5:
time: 584 us; the launch traced here: 580 us
  Pallas kernels  281 us (48%)
  waiting for transfers between devices  153 us (26%)
  starting transfers between devices  113 us (19%)
  other arithmetic  22 us (4%)
  local copies, waits for them, and re-layouts  9.36 us (2%)
    pallas_call x4, Pallas kernels, form_piece(): pl.pallas_call(functools.partial(form_kernel, n_dp, len(ties)), grid_spec...  98.9 us
    pallas_call x8, Pallas kernels, return_piece(): pl.pallas_call(functools.partial(return_kernel, n_dp, first), grid=(n_dp,...  88.6 us
    ppermute x32, waiting for transfers between devices, run(): got = lax.ppermute(sent, 'grp', crossed(n_grp, step))  82.3 us
    pallas_call x4, Pallas kernels, image_piece(): pl.pallas_call(functools.partial(image_kernel, len(ties)), grid=(n_dp, NG...  51 us
    ppermute x32, starting transfers between devices, run(): got = lax.ppermute(sent, 'grp', crossed(n_grp, step))  50.1 us
    ppermute x16, waiting for transfers between devices, run(): lax.ppermute(sends[at * rows:(at + 1) * rows], 'dp', turned_by(n_dp, at +...  39.7 us
    ppermute x5, waiting for transfers between devices, sum_but_last(): got = lax.ppermute(total.astype(kind), 'width', crossed(n_width, step))  20.7 us
    ppermute x16, starting transfers between devices, run(): lax.ppermute(sends[at * rows:(at + 1) * rows], 'dp', turned_by(n_dp, at +...  19.2 us
  transfers between devices with their start and end apart: 88, of which 35 were waited for; matrix products, arithmetic and copies ran while one was open for 4% of the time, Pallas kernels for 38%

profile of v5, /device:TPU:0, one launch (start us, length us, event | category | flops | bytes accessed | tf_op | source)
XLA Modules:
  0.0 580.1 jit_solution(2061583848247349064)
XLA Ops:
  2.1 5.1 rotate_out.1
  7.2 13.0 %rotate_in.1 = (f32[256,1792]{1,0:T(8,128)S(1)}, f32[256,1792]{1,0:T(8,128)S(1)}) custom-call(s32[3]{0:T(128)S(1)} %pad_add_fusion.place_ref, bf16[512,3584]{1,0:T(8,128)(2,1)} %query_ref.3, bf16[3584,1792]{1,0:T(8,128)(2,1)} %eigen_ref.7, bf16[512,256]{1,0:T(8,128)(2,1)S(1)} %get-tuple-element.77.refs_0_), custom_call_target="tpu_custom_call" | custom-call | flops 6576668672 | bytes 12845056 | tf_op jit(solution)/shard_map/rotate_in/pallas_call | solution.py:304
  23.4 6.9 %collective-permute-done.2 = bf16[512,256]{1,0:T(8,128)(2,1)S(1)} collective-permute-done((bf16[512,256]{1,0:T(8,128)(2,1)S(1)}, bf16[512,256]{1,0:T(8,128)(2,1)S(1)}, u32[]{:S(2)}, u32[]{:S(2)}) %collective-permute-start.2) | collective-permute-done | bytes 262176 | tf_op jit(solution)/shard_map/ppermute | solution.py:584
  32.2 6.3 %collective-permute-done.3 = bf16[512,256]{1,0:T(8,128)(2,1)S(1)} collective-permute-done((bf16[512,256]{1,0:T(8,128)(2,1)S(1)}, bf16[512,256]{1,0:T(8,128)(2,1)S(1)}, u32[]{:S(2)}, u32[]{:S(2)}) %collective-permute-start.3) | collective-permute-done | bytes 262176 | tf_op jit(solution)/shard_map/ppermute | solution.py:596
  41.3 11.1 %collective-permute-done.4 = bf16[512,256]{1,0:T(8,128)(2,1)S(1)} collective-permute-done((bf16[512,256]{1,0:T(8,128)(2,1)S(1)}, bf16[512,256]{1,0:T(8,128)(2,1)S(1)}, u32[]{:S(2)}, u32[]{:S(2)}) %collective-permute-start.4) | collective-permute-done | bytes 262176 | tf_op jit(solution)/shard_map/ppermute | solution.py:596
  77.5 5.2 collective-permute-done.22
  86.0 8.9 %collective-permute-done.6 = bf16[512,256]{1,0:T(8,128)(2,1)S(1)} collective-permute-done((bf16[512,256]{1,0:T(8,128)(2,1)S(1)}, bf16[512,256]{1,0:T(8,128)(2,1)S(1)}, u32[]{:S(2)}, u32[]{:S(2)}) %collective-permute-start.6) | collective-permute-done | bytes 262176 | tf_op jit(solution)/shard_map/ppermute | solution.py:596
  96.5 6.3 %collective-permute-start.7 = (bf16[512,256]{1,0:T(8,128)(2,1)S(1)}, bf16[512,256]{1,0:T(8,128)(2,1)S(1)}, u32[]{:S(2)}, u32[]{:S(2)}) collective-permute-start(bf16[512,256]{1,0:T(8,128)(2,1)S(1)} %fusion.10.refs_6_), channel_id=1, source_target_pairs={{0,16},{8,24},{16,0},{24,8},{1,17},{9,25},{17,1},{25,9},{2,18},{10... | collective-permute-start | bytes 786440 | tf_op jit(solution)/shard_map/ppermute | solution.py:596
  115.9 24.6 %form.4 = (bf16[8,1024,1792]{2,1,0:T(8,128)(2,1)}, bf16[512,128]{1,0:T(8,128)(2,1)S(1)}, f32[512,128]{1,0:T(8,128)S(1)}) custom-call(s32[3]{0:T(128)S(1)} %pad_add_fusion.place_ref, bf16[512,256]{1,0:T(8,128)(2,1)S(1)} %collective-permute-done.12.refs_0_, bf16[512,256]{1,0:T(8,128)(2,1)S(1)} %add_convert_fusion.4.refs_1_, ...), custom_call_target="tpu_custom_call" | custom-call | flops 11744051200 | bytes 29360128 | tf_op jit(solution)/shard_map/form/pallas_call | solution.py:122
  142.5 24.8 %form.5 = (bf16[8,1024,1792]{2,1,0:T(8,128)(2,1)}, bf16[512,128]{1,0:T(8,128)(2,1)S(1)}, f32[512,128]{1,0:T(8,128)S(1)}) custom-call(s32[3]{0:T(128)S(1)} %pad_add_fusion.place_ref, bf16[512,256]{1,0:T(8,128)(2,1)S(1)} %collective-permute-done.18.refs_0_, bf16[512,256]{1,0:T(8,128)(2,1)S(1)} %add_convert_fusion.2.refs_1_, ...), custom_call_target="tpu_custom_call" | custom-call | flops 11744051200 | bytes 29360128 | tf_op jit(solution)/shard_map/form/pallas_call | solution.py:122
  187.5 24.6 %form.7 = (bf16[8,1024,1792]{2,1,0:T(8,128)(2,1)}, bf16[512,128]{1,0:T(8,128)(2,1)S(1)}, f32[512,128]{1,0:T(8,128)S(1)}) custom-call(s32[3]{0:T(128)S(1)} %pad_add_fusion.place_ref, bf16[512,256]{1,0:T(8,128)(2,1)S(1)} %collective-permute-done.29.refs_0_, bf16[512,256]{1,0:T(8,128)(2,1)S(1)} %add_convert_fusion.1.refs_5_.refs_1_, ...), custom_call_target="tpu_custom_call" | custom-call | flops 11744051200 | bytes 29360128 | tf_op jit(solution)/shard_map/form/pallas_call | solution.py:122
  214.0 25.0 %form.6 = (bf16[8,1024,1792]{2,1,0:T(8,128)(2,1)}, bf16[512,128]{1,0:T(8,128)(2,1)S(1)}, f32[512,128]{1,0:T(8,128)S(1)}) custom-call(s32[3]{0:T(128)S(1)} %pad_add_fusion.place_ref, bf16[512,256]{1,0:T(8,128)(2,1)S(1)} %collective-permute-done.8.refs_0_, bf16[512,256]{1,0:T(8,128)(2,1)S(1)} %add_convert_fusion.3.refs_1_.refs_5_, ...), custom_call_target="tpu_custom_call" | custom-call | flops 11744051200 | bytes 29360128 | tf_op jit(solution)/shard_map/form/pallas_call | solution.py:122
  239.2 4.8 collective-permute-done.25
  256.7 10.9 %returned.8 = (f32[128,1792]{1,0:T(8,128)S(1)}, f32[128,128]{1,0:T(8,128)S(1)}) custom-call(bf16[512,128]{1,0:T(8,128)(2,1)S(1)} %collective-permute-done.38.refs_0_, bf16[512,128]{1,0:T(8,128)(2,1)S(1)} %add_convert_fusion.22.refs_1_.refs_3_.refs_0_, bf16[8,1024,1792]{2,1,0:T(8,128)(2,1)} %get-tuple-element.99.refs_2_.rotated_ref, ...), custom_call_target="tpu_custom_call" | custom-call | flops 7516192768 | bytes 29360128 | tf_op jit(solution)/shard_map/returned/pallas_call | solution.py:232
  271.2 10.9 %returned.9 = (f32[128,1792]{1,0:T(8,128)S(1)}, f32[128,128]{1,0:T(8,128)S(1)}) custom-call(bf16[512,128]{1,0:T(8,128)(2,1)S(1)} %collective-permute-done.36.refs_0_, bf16[512,128]{1,0:T(8,128)(2,1)S(1)} %add_convert_fusion.23.refs_1_, bf16[8,1024,1792]{2,1,0:T(8,128)(2,1)} %get-tuple-element.98.refs_2_.rotated_ref, ...), custom_call_target="tpu_custom_call" | custom-call | flops 7516192768 | bytes 29360128 | tf_op jit(solution)/shard_map/returned/pallas_call | solution.py:232
  283.7 10.9 %returned.10 = (f32[128,1792]{1,0:T(8,128)S(1)}, f32[128,128]{1,0:T(8,128)S(1)}) custom-call(bf16[512,128]{1,0:T(8,128)(2,1)S(1)} %collective-permute-done.33.refs_0_, bf16[512,128]{1,0:T(8,128)(2,1)S(1)} %add_convert_fusion.24.refs_5_.refs_2_.refs_1_, bf16[8,1024,1792]{2,1,0:T(8,128)(2,1)} %get-tuple-element.97.refs_2_.rotated_ref, ...), custom_call_target="tpu_custom_call" | custom-call | flops 7516192768 | bytes 29360128 | tf_op jit(solution)/shard_map/returned/pallas_call | solution.py:232
  294.6 11.5 %returned.11 = (f32[128,1792]{1,0:T(8,128)S(1)}, f32[128,128]{1,0:T(8,128)}) custom-call(bf16[512,128]{1,0:T(8,128)(2,1)S(1)} %collective-permute-done.28.refs_0_, bf16[512,128]{1,0:T(8,128)(2,1)S(1)} %add_convert_fusion.25.refs_3_.refs_5_.refs_1_, bf16[8,1024,1792]{2,1,0:T(8,128)(2,1)} %get-tuple-element.94.refs_2_.rotated_ref, ...), custom_call_target="tpu_custom_call" | custom-call | flops 7516192768 | bytes 29360128 | tf_op jit(solution)/shard_map/returned/pallas_call | solution.py:232
  306.8 8.0 %collective-permute-done.41.got_ref = bf16[128,1792]{1,0:T(8,128)(2,1)S(1)} collective-permute-done((bf16[128,1792]{1,0:T(8,128)(2,1)S(1)}, bf16[128,1792]{1,0:T(8,128)(2,1)S(1)}, u32[]{:S(2)}, u32[]{:S(2)}) %collective-permute-start.41) | collective-permute-done | bytes 458784 | tf_op jit(solution)/shard_map/ppermute | solution.py:672
  315.6 12.8 %image.4 = (bf16[512,128]{1,0:T(8,128)(2,1)S(1)}, f32[512,128]{1,0:T(8,128)S(1)}) custom-call(bf16[1792,128]{1,0:T(8,128)(2,1)S(1)} %normalize.2.basis_ref, bf16[8,1024,1792]{2,1,0:T(8,128)(2,1)} %get-tuple-element.99.refs_2_.rotated_ref), custom_call_target="tpu_custom_call" | custom-call | flops 7516192768 | bytes 29360128 | tf_op jit(solution)/shard_map/image/pallas_call | solution.py:168
  330.1 12.7 %image.5 = (bf16[512,128]{1,0:T(8,128)(2,1)S(1)}, f32[512,128]{1,0:T(8,128)S(1)}) custom-call(bf16[1792,128]{1,0:T(8,128)(2,1)S(1)} %normalize.2.basis_ref, bf16[8,1024,1792]{2,1,0:T(8,128)(2,1)} %get-tuple-element.98.refs_2_.rotated_ref), custom_call_target="tpu_custom_call" | custom-call | flops 7516192768 | bytes 29360128 | tf_op jit(solution)/shard_map/image/pallas_call | solution.py:168
  343.4 12.8 %image.6 = (bf16[512,128]{1,0:T(8,128)(2,1)S(1)}, f32[512,128]{1,0:T(8,128)S(1)}) custom-call(bf16[1792,128]{1,0:T(8,128)(2,1)S(1)} %normalize.2.basis_ref, bf16[8,1024,1792]{2,1,0:T(8,128)(2,1)} %get-tuple-element.97.refs_2_.rotated_ref, bf16[512,128]{1,0:T(8,128)(2,1)S(1)} %fusion.18.refs_0_), custom_call_target="tpu_custom_call" | custom-call | flops 7516192768 | bytes 29360128 | tf_op jit(solution)/shard_map/image/pallas_call | solution.py:168
  362.5 12.7 %image.7 = (bf16[512,128]{1,0:T(8,128)(2,1)S(1)}, f32[512,128]{1,0:T(8,128)S(1)}) custom-call(bf16[1792,128]{1,0:T(8,128)(2,1)S(1)} %normalize.2.basis_ref, bf16[8,1024,1792]{2,1,0:T(8,128)(2,1)} %get-tuple-element.94.refs_2_.rotated_ref, bf16[512,128]{1,0:T(8,128)(2,1)S(1)} %fusion.26.refs_0_, bf16[512,128]{1,0:T(8,128)(2,1)S(1)} %fusion.19.refs_1_), custom_call_target="tpu_custom_call" | custom-call | flops 7516192768 | bytes 29360128 | tf_op jit(solution)/shard_map/image/pallas_call | solution.py:168
  390.7 10.9 %returned.12 = (f32[128,1792]{1,0:T(8,128)S(1)}, f32[128,128]{1,0:T(8,128)S(1)}) custom-call(bf16[512,128]{1,0:T(8,128)(2,1)S(1)} %collective-permute-done.56.refs_0_, bf16[512,128]{1,0:T(8,128)(2,1)S(1)} %add_convert_fusion.21.refs_0_.refs_1_.refs_3_, bf16[8,1024,1792]{2,1,0:T(8,128)(2,1)} %get-tuple-element.99.refs_2_.rotated_ref, ...), custom_call_target="tpu_custom_call" | custom-call | flops 7516192768 | bytes 29360128 | tf_op jit(solution)/shard_map/returned/pallas_call | solution.py:232
  403.3 11.1 %returned.13 = (f32[128,1792]{1,0:T(8,128)S(1)}, f32[128,128]{1,0:T(8,128)S(1)}) custom-call(bf16[512,128]{1,0:T(8,128)(2,1)S(1)} %collective-permute-done.57.refs_2_.refs_0_, bf16[512,128]{1,0:T(8,128)(2,1)S(1)} %add_convert_fusion.20.refs_1_.refs_3_, bf16[8,1024,1792]{2,1,0:T(8,128)(2,1)} %get-tuple-element.98.refs_2_.rotated_ref, ...), custom_call_target="tpu_custom_call" | custom-call | flops 7516192768 | bytes 29360128 | tf_op jit(solution)/shard_map/returned/pallas_call | solution.py:232
  415.8 10.9 %returned.14 = (f32[128,1792]{1,0:T(8,128)S(1)}, f32[128,128]{1,0:T(8,128)S(1)}) custom-call(bf16[512,128]{1,0:T(8,128)(2,1)S(1)} %collective-permute-done.58.refs_4_.refs_0_, bf16[512,128]{1,0:T(8,128)(2,1)S(1)} %add_convert_fusion.19.refs_2_.refs_5_.refs_1_, bf16[8,1024,1792]{2,1,0:T(8,128)(2,1)} %get-tuple-element.97.refs_2_.rotated_ref, ...), custom_call_target="tpu_custom_call" | custom-call | flops 7516192768 | bytes 29360128 | tf_op jit(solution)/shard_map/returned/pallas_call | solution.py:232
  430.7 11.5 %returned.15 = (f32[128,1792]{1,0:T(8,128)S(1)}, f32[128,128]{1,0:T(8,128)}) custom-call(bf16[512,128]{1,0:T(8,128)(2,1)S(1)} %collective-permute-done.59.refs_6_.refs_0_, bf16[512,128]{1,0:T(8,128)(2,1)S(1)} %add_convert_fusion.18.refs_3_.refs_7_.refs_5_.refs_1_, bf16[8,1024,1792]{2,1,0:T(8,128)(2,1)} %get-tuple-element.94.refs_2_.rotated_ref, ...), custom_call_target="tpu_custom_call" | custom-call | flops 7516192768 | bytes 29360128 | tf_op jit(solution)/shard_map/returned/pallas_call | solution.py:232
  445.7 9.5 %collective-permute-done.64.got_ref = bf16[128,1792]{1,0:T(8,128)(2,1)S(1)} collective-permute-done((bf16[128,1792]{1,0:T(8,128)(2,1)S(1)}, bf16[128,1792]{1,0:T(8,128)(2,1)S(1)}, u32[]{:S(2)}, u32[]{:S(2)}) %collective-permute-start.64) | collective-permute-done | bytes 458784 | tf_op jit(solution)/shard_map/ppermute | solution.py:672
  458.1 10.7 %factor_in.1 = (bf16[448,256]{1,0:T(8,128)(2,1)S(1)}, f32[448,256]{1,0:T(8,128)S(1)}, bf16[448,256]{1,0:T(8,128)(2,1)S(1)}, f32[448,256]{1,0:T(8,128)S(1)}, bf16...) custom-call(s32[3]{0:T(128)S(1)} %pad_add_fusion.place_ref, ...), custom_call_target="tpu_custom_call" | custom-call | tf_op jit(solution)/shard_map/factor_in/pallas_call | solution.py:369
  489.7 11.6 %collective-permute-done.70 = bf16[448,256]{1,0:T(8,128)(2,1)S(1)} collective-permute-done((bf16[448,256]{1,0:T(8,128)(2,1)S(1)}, bf16[448,256]{1,0:T(8,128)(2,1)S(1)}, u32[]{:S(2)}, u32[]{:S(2)}) %collective-permute-start.70) | collective-permute-done | bytes 229408 | tf_op jit(solution)/shard_map/ppermute | solution.py:584
  504.4 15.4 %collective-permute-done.68 = bf16[448,256]{1,0:T(8,128)(2,1)S(1)} collective-permute-done((bf16[448,256]{1,0:T(8,128)(2,1)S(1)}, bf16[448,256]{1,0:T(8,128)(2,1)S(1)}, u32[]{:S(2)}, u32[]{:S(2)}) %collective-permute-start.68) | collective-permute-done | bytes 229408 | tf_op jit(solution)/shard_map/ppermute | solution.py:596
  525.2 6.6 %collective-permute-done.78 = bf16[448,256]{1,0:T(8,128)(2,1)S(1)} collective-permute-done((bf16[448,256]{1,0:T(8,128)(2,1)}, bf16[448,256]{1,0:T(8,128)(2,1)S(1)}, u32[]{:S(2)}, u32[]{:S(2)}) %collective-permute-start.78) | collective-permute-done | bytes 229408 | tf_op jit(solution)/shard_map/ppermute | solution.py:584
  548.9 8.0 %collective-permute-done.80 = bf16[448,256]{1,0:T(8,128)(2,1)S(1)} collective-permute-done((bf16[448,256]{1,0:T(8,128)(2,1)S(1)}, bf16[448,256]{1,0:T(8,128)(2,1)S(1)}, u32[]{:S(2)}, u32[]{:S(2)}) %collective-permute-start.80) | collective-permute-done | bytes 229408 | tf_op jit(solution)/shard_map/ppermute | solution.py:596
  (273 shorter events, 202.5 us)
Async XLA Ops:
  20.3 32.2 %collective-permute-start.9 = (f32[256,1792]{1,0:T(8,128)S(1)}, f32[256,1792]{1,0:T(8,128)S(1)}, u32[]{:S(2)}, u32[]{:S(2)}) collective-permute-start(f32[256,1792]{1,0:T(8,128)S(1)} %get-tuple-element.80), channel_id=1, source_target_pairs={{0,1},{1,0},{2,3},{3,2},{4,5},{5,4},{6,7},{7,6},{8,9},{9,8},{10,11... | collective-permute-start | bytes 5505032 | tf_op jit(solution)/shard_map/ppermute | solution.py:569
  52.5 134.9 %collective-permute-start.11 = (f32[2048,1792]{1,0:T(8,128)}, f32[2048,1792]{1,0:T(8,128)}, u32[]{:S(2)}, u32[]{:S(2)}) collective-permute-start(f32[2048,1792]{1,0:T(8,128)} %refs_3_.3), channel_id=1, source_target_pairs={{0,1},{1,0},{2,3},{3,2},{4,5},{5,4},{6,7},{7,6},{8,9},{9,8},{10,11... | collective-permute-start | bytes 44040200 | tf_op jit(solution)/shard_map/ppermute | solution.py:569
  53.2 19.2 %collective-permute-start.1 = (bf16[512,256]{1,0:T(8,128)(2,1)S(1)}, bf16[512,256]{1,0:T(8,128)(2,1)}, u32[]{:S(2)}, u32[]{:S(2)}) collective-permute-start(bf16[512,256]{1,0:T(8,128)(2,1)S(1)} %get-tuple-element.75), channel_id=1, source_target_pairs={{0,1},{1,0},{2,3},{3,2},{4,5},{5,4},{6,7},{7,6},{8,9},{9,8},{10,11... | collective-permute-start | bytes 786440 | tf_op jit(solution)/shard_map/ppermute | solution.py:569
  70.8 45.1 %collective-permute-start.12 = (bf16[512,256]{1,0:T(8,128)(2,1)S(1)}, bf16[512,256]{1,0:T(8,128)(2,1)S(1)}, u32[]{:S(2)}, u32[]{:S(2)}) collective-permute-start(bf16[512,256]{1,0:T(8,128)(2,1)S(1)} %add_convert_fusion.4.refs_1_), channel_id=1, source_target_pairs={{0,4},{4,0},{1,5},{5,1},{2,6},{6,2},{3,7},{7,3},{8,12},{12,8},{9,1... | collective-permute-start | bytes 786440 | tf_op jit(solution)/shard_map/ppermute | solution.py:602
  75.5 20.9 %collective-permute-start.17 = (bf16[512,256]{1,0:T(8,128)(2,1)S(1)}, bf16[512,256]{1,0:T(8,128)(2,1)S(1)}, u32[]{:S(2)}, u32[]{:S(2)}) collective-permute-start(bf16[512,256]{1,0:T(8,128)(2,1)S(1)} %fusion.13), channel_id=1, source_target_pairs={{0,16},{8,24},{16,0},{24,8},{1,17},{9,25},{17,1},{25,9},{2,18},{10... | collective-permute-start | bytes 786440 | tf_op jit(solution)/shard_map/ppermute | solution.py:596
  83.9 20.0 %collective-permute-start.23 = (bf16[512,256]{1,0:T(8,128)(2,1)S(1)}, bf16[512,256]{1,0:T(8,128)(2,1)S(1)}, u32[]{:S(2)}, u32[]{:S(2)}) collective-permute-start(bf16[512,256]{1,0:T(8,128)(2,1)S(1)} %fusion.11), channel_id=1, source_target_pairs={{0,16},{8,24},{16,0},{24,8},{1,17},{9,25},{17,1},{25,9},{2,18},{10... | collective-permute-start | bytes 786440 | tf_op jit(solution)/shard_map/ppermute | solution.py:596
  94.8 20.9 %collective-permute-start.10 = (bf16[256,1792]{1,0:T(8,128)(2,1)S(1)}, bf16[256,1792]{1,0:T(8,128)(2,1)S(1)}, u32[]{:S(2)}, u32[]{:S(2)}) collective-permute-start(bf16[256,1792]{1,0:T(8,128)(2,1)S(1)} %get-tuple-element.145), channel_id=1, source_target_pairs={{0,2},{1,3},{2,0},{3,1},{4,6},{5,7},{6,4},{7,5},{8,10},{9,11},{10,... | collective-permute-start | bytes 2752520 | tf_op jit(solution)/shard_map/ppermute | solution.py:672
  103.9 38.6 %collective-permute-start.18 = (bf16[512,256]{1,0:T(8,128)(2,1)S(1)}, bf16[512,256]{1,0:T(8,128)(2,1)S(1)}, u32[]{:S(2)}, u32[]{:S(2)}) collective-permute-start(bf16[512,256]{1,0:T(8,128)(2,1)S(1)} %add_convert_fusion.2.refs_1_), channel_id=1, source_target_pairs={{0,4},{4,0},{1,5},{5,1},{2,6},{6,2},{3,7},{7,3},{8,12},{12,8},{9,1... | collective-permute-start | bytes 786440 | tf_op jit(solution)/shard_map/ppermute | solution.py:602
  111.2 76.2 %collective-permute-start.29 = (bf16[512,256]{1,0:T(8,128)(2,1)S(1)}, bf16[512,256]{1,0:T(8,128)(2,1)S(1)}, u32[]{:S(2)}, u32[]{:S(2)}) collective-permute-start(bf16[512,256]{1,0:T(8,128)(2,1)S(1)} %add_convert_fusion.1.refs_5_.refs_1_), channel_id=1, source_target_pairs={{0,4},{4,0},{1,5},{5,1},{2,6},{6,2},{3,7},{7,3},{8,12},{12,8},{9,1... | collective-permute-start | bytes 786440 | tf_op jit(solution)/shard_map/ppermute | solution.py:602
  115.8 98.3 %collective-permute-start.8 = (bf16[512,256]{1,0:T(8,128)(2,1)S(1)}, bf16[512,256]{1,0:T(8,128)(2,1)S(1)}, u32[]{:S(2)}, u32[]{:S(2)}) collective-permute-start(bf16[512,256]{1,0:T(8,128)(2,1)S(1)} %add_convert_fusion.3.refs_1_.refs_5_), channel_id=1, source_target_pairs={{0,4},{4,0},{1,5},{5,1},{2,6},{6,2},{3,7},{7,3},{8,12},{12,8},{9,1... | collective-permute-start | bytes 786440 | tf_op jit(solution)/shard_map/ppermute | solution.py:602
  140.5 26.8 %collective-permute-start.13 = (bf16[512,128]{1,0:T(8,128)(2,1)S(1)}, bf16[512,128]{1,0:T(8,128)(2,1)S(1)}, u32[]{:S(2)}, u32[]{:S(2)}) collective-permute-start(bf16[512,128]{1,0:T(8,128)(2,1)S(1)} %get-tuple-element.83), channel_id=1, source_target_pairs={{0,4},{4,0},{1,5},{5,1},{2,6},{6,2},{3,7},{7,3},{8,12},{12,8},{9,1... | collective-permute-start | bytes 393224 | tf_op jit(solution)/shard_map/ppermute | solution.py:584
  183.0 73.7 %collective-permute-start.38 = (bf16[512,128]{1,0:T(8,128)(2,1)S(1)}, bf16[512,128]{1,0:T(8,128)(2,1)S(1)}, u32[]{:S(2)}, u32[]{:S(2)}) collective-permute-start(bf16[512,128]{1,0:T(8,128)(2,1)S(1)} %add_convert_fusion.22.refs_1_.refs_3_.refs_0_), channel_id=1, source_target_pairs={{0,4},{4,0},{1,5},{5,1},{2,6},{6,2},{3,7},{7,3},{8,12},{12,8},{9,1... | collective-permute-start | bytes 393224 | tf_op jit(solution)/shard_map/ppermute | solution.py:602
  187.4 83.9 %collective-permute-start.36 = (bf16[512,128]{1,0:T(8,128)(2,1)S(1)}, bf16[512,128]{1,0:T(8,128)(2,1)S(1)}, u32[]{:S(2)}, u32[]{:S(2)}) collective-permute-start(bf16[512,128]{1,0:T(8,128)(2,1)S(1)} %add_convert_fusion.23.refs_1_), channel_id=1, source_target_pairs={{0,4},{4,0},{1,5},{5,1},{2,6},{6,2},{3,7},{7,3},{8,12},{12,8},{9,1... | collective-permute-start | bytes 393224 | tf_op jit(solution)/shard_map/ppermute | solution.py:602
  212.1 27.0 %collective-permute-start.30 = (bf16[512,128]{1,0:T(8,128)(2,1)S(1)}, bf16[512,128]{1,0:T(8,128)(2,1)S(1)}, u32[]{:S(2)}, u32[]{:S(2)}) collective-permute-start(bf16[512,128]{1,0:T(8,128)(2,1)S(1)} %get-tuple-element.96), channel_id=1, source_target_pairs={{0,4},{4,0},{1,5},{5,1},{2,6},{6,2},{3,7},{7,3},{8,12},{12,8},{9,1... | collective-permute-start | bytes 393224 | tf_op jit(solution)/shard_map/ppermute | solution.py:584
  267.6 16.1 %collective-permute-start.33 = (bf16[512,128]{1,0:T(8,128)(2,1)S(1)}, bf16[512,128]{1,0:T(8,128)(2,1)S(1)}, u32[]{:S(2)}, u32[]{:S(2)}) collective-permute-start(bf16[512,128]{1,0:T(8,128)(2,1)S(1)} %add_convert_fusion.24.refs_5_.refs_2_.refs_1_), channel_id=1, source_target_pairs={{0,4},{4,0},{1,5},{5,1},{2,6},{6,2},{3,7},{7,3},{8,12},{12,8},{9,1... | collective-permute-start | bytes 393224 | tf_op jit(solution)/shard_map/ppermute | solution.py:602
  269.3 25.3 %collective-permute-start.28 = (bf16[512,128]{1,0:T(8,128)(2,1)S(1)}, bf16[512,128]{1,0:T(8,128)(2,1)S(1)}, u32[]{:S(2)}, u32[]{:S(2)}) collective-permute-start(bf16[512,128]{1,0:T(8,128)(2,1)S(1)} %add_convert_fusion.25.refs_3_.refs_5_.refs_1_), channel_id=1, source_target_pairs={{0,4},{4,0},{1,5},{5,1},{2,6},{6,2},{3,7},{7,3},{8,12},{12,8},{9,1... | collective-permute-start | bytes 393224 | tf_op jit(solution)/shard_map/ppermute | solution.py:602
  342.9 15.0 %collective-permute-start.45 = (bf16[512,128]{1,0:T(8,128)(2,1)S(1)}, bf16[512,128]{1,0:T(8,128)(2,1)S(1)}, u32[]{:S(2)}, u32[]{:S(2)}) collective-permute-start(bf16[512,128]{1,0:T(8,128)(2,1)S(1)} %get-tuple-element.110), channel_id=1, source_target_pairs={{0,4},{4,0},{1,5},{5,1},{2,6},{6,2},{3,7},{7,3},{8,12},{12,8},{9,1... | collective-permute-start | bytes 393224 | tf_op jit(solution)/shard_map/ppermute | solution.py:584
  356.2 20.2 %collective-permute-start.48 = (bf16[512,128]{1,0:T(8,128)(2,1)S(1)}, bf16[512,128]{1,0:T(8,128)(2,1)S(1)}, u32[]{:S(2)}, u32[]{:S(2)}) collective-permute-start(bf16[512,128]{1,0:T(8,128)(2,1)S(1)} %get-tuple-element.112), channel_id=1, source_target_pairs={{0,4},{4,0},{1,5},{5,1},{2,6},{6,2},{3,7},{7,3},{8,12},{12,8},{9,1... | collective-permute-start | bytes 393224 | tf_op jit(solution)/shard_map/ppermute | solution.py:584
  358.0 19.6 %collective-permute-start.46 = (bf16[512,128]{1,0:T(8,128)(2,1)S(1)}, bf16[512,128]{1,0:T(8,128)(2,1)S(1)}, u32[]{:S(2)}, u32[]{:S(2)}) collective-permute-start(bf16[512,128]{1,0:T(8,128)(2,1)S(1)} %fusion.19.refs_1_), channel_id=1, source_target_pairs={{0,8},{8,0},{16,24},{24,16},{1,9},{9,1},{17,25},{25,17},{2,10},{10... | collective-permute-start | bytes 393224 | tf_op jit(solution)/shard_map/ppermute | solution.py:596
  361.2 17.7 %collective-permute-start.44 = (bf16[512,128]{1,0:T(8,128)(2,1)S(1)}, bf16[512,128]{1,0:T(8,128)(2,1)S(1)}, u32[]{:S(2)}, u32[]{:S(2)}) collective-permute-start(bf16[512,128]{1,0:T(8,128)(2,1)S(1)} %fusion.26.refs_0_), channel_id=1, source_target_pairs={{0,16},{8,24},{16,0},{24,8},{1,17},{9,25},{17,1},{25,9},{2,18},{10... | collective-permute-start | bytes 393224 | tf_op jit(solution)/shard_map/ppermute | solution.py:596
  385.1 18.3 %collective-permute-start.57 = (bf16[512,128]{1,0:T(8,128)(2,1)S(1)}, bf16[512,128]{1,0:T(8,128)(2,1)S(1)}, u32[]{:S(2)}, u32[]{:S(2)}) collective-permute-start(bf16[512,128]{1,0:T(8,128)(2,1)S(1)} %add_convert_fusion.20.refs_1_.refs_3_), channel_id=1, source_target_pairs={{0,4},{4,0},{1,5},{5,1},{2,6},{6,2},{3,7},{7,3},{8,12},{12,8},{9,1... | collective-permute-start | bytes 393224 | tf_op jit(solution)/shard_map/ppermute | solution.py:602
  389.9 25.9 %collective-permute-start.58 = (bf16[512,128]{1,0:T(8,128)(2,1)S(1)}, bf16[512,128]{1,0:T(8,128)(2,1)S(1)}, u32[]{:S(2)}, u32[]{:S(2)}) collective-permute-start(bf16[512,128]{1,0:T(8,128)(2,1)S(1)} %add_convert_fusion.19.refs_2_.refs_5_.refs_1_), channel_id=1, source_target_pairs={{0,4},{4,0},{1,5},{5,1},{2,6},{6,2},{3,7},{7,3},{8,12},{12,8},{9,1... | collective-permute-start | bytes 393224 | tf_op jit(solution)/shard_map/ppermute | solution.py:602
  479.5 56.7 %all-to-all-start = ((bf16[8,256,256]{2,1,0:T(8,128)(2,1)}), bf16[8,256,256]{2,1,0:T(8,128)(2,1)}, u32[]{:S(2)}, u32[]{:S(2)}) async-start(bf16[8,256,256]{2,1,0:T(8,128)(2,1)} %broadcast_in_dim.2), calls=%async_computation | async-start | bytes 2097152 | tf_op jit(solution)/shard_map/all_to_all | solution.py:642
  483.7 17.6 %collective-permute-start.70 = (bf16[448,256]{1,0:T(8,128)(2,1)S(1)}, bf16[448,256]{1,0:T(8,128)(2,1)S(1)}, u32[]{:S(2)}, u32[]{:S(2)}) collective-permute-start(bf16[448,256]{1,0:T(8,128)(2,1)S(1)} %get-tuple-element.133), channel_id=1, source_target_pairs={{0,4},{4,0},{1,5},{5,1},{2,6},{6,2},{3,7},{7,3},{8,12},{12,8},{9,1... | collective-permute-start | bytes 688136 | tf_op jit(solution)/shard_map/ppermute | solution.py:584
  486.7 33.1 %collective-permute-start.68 = (bf16[448,256]{1,0:T(8,128)(2,1)S(1)}, bf16[448,256]{1,0:T(8,128)(2,1)S(1)}, u32[]{:S(2)}, u32[]{:S(2)}) collective-permute-start(bf16[448,256]{1,0:T(8,128)(2,1)S(1)} %add_convert_fusion.15), channel_id=1, source_target_pairs={{0,16},{8,24},{16,0},{24,8},{1,17},{9,25},{17,1},{25,9},{2,18},{10... | collective-permute-start | bytes 688136 | tf_op jit(solution)/shard_map/ppermute | solution.py:596
  489.2 32.8 %collective-permute-start.74 = (bf16[448,256]{1,0:T(8,128)(2,1)}, bf16[448,256]{1,0:T(8,128)(2,1)S(1)}, u32[]{:S(2)}, u32[]{:S(2)}) collective-permute-start(bf16[448,256]{1,0:T(8,128)(2,1)} %get-tuple-element.136), channel_id=1, source_target_pairs={{0,4},{4,0},{1,5},{5,1},{2,6},{6,2},{3,7},{7,3},{8,12},{12,8},{9,1... | collective-permute-start | bytes 688136 | tf_op jit(solution)/shard_map/ppermute | solution.py:584
  502.4 19.7 %collective-permute-start.71 = (bf16[448,256]{1,0:T(8,128)(2,1)S(1)}, bf16[448,256]{1,0:T(8,128)(2,1)S(1)}, u32[]{:S(2)}, u32[]{:S(2)}) collective-permute-start(bf16[448,256]{1,0:T(8,128)(2,1)S(1)} %add_convert_fusion.13), channel_id=1, source_target_pairs={{0,8},{8,0},{16,24},{24,16},{1,9},{9,1},{17,25},{25,17},{2,10},{10... | collective-permute-start | bytes 688136 | tf_op jit(solution)/shard_map/ppermute | solution.py:596
  519.9 45.9 %collective-permute-start.69 = (bf16[448,256]{1,0:T(8,128)(2,1)S(1)}, bf16[448,256]{1,0:T(8,128)(2,1)S(1)}, u32[]{:S(2)}, u32[]{:S(2)}) collective-permute-start(bf16[448,256]{1,0:T(8,128)(2,1)S(1)} %add_convert_fusion.14.refs_1_), channel_id=1, source_target_pairs={{0,4},{4,0},{1,5},{5,1},{2,6},{6,2},{3,7},{7,3},{8,12},{12,8},{9,1... | collective-permute-start | bytes 688136 | tf_op jit(solution)/shard_map/ppermute | solution.py:602
  522.2 18.5 %collective-permute-start.72 = (bf16[448,256]{1,0:T(8,128)(2,1)S(1)}, bf16[448,256]{1,0:T(8,128)(2,1)}, u32[]{:S(2)}, u32[]{:S(2)}) collective-permute-start(bf16[448,256]{1,0:T(8,128)(2,1)S(1)} %add_convert_fusion.12), channel_id=1, source_target_pairs={{0,16},{8,24},{16,0},{24,8},{1,17},{9,25},{17,1},{25,9},{2,18},{10... | collective-permute-start | bytes 688136 | tf_op jit(solution)/shard_map/ppermute | solution.py:596
  536.2 21.8 %all-to-all-start.1 = ((bf16[4,512,256]{2,1,0:T(8,128)(2,1)}), bf16[4,512,256]{2,1,0:T(8,128)(2,1)}, u32[]{:S(2)}, u32[]{:S(2)}) async-start(bf16[4,512,256]{2,1,0:T(8,128)(2,1)} %bitcast.3), calls=%async_computation.1 | async-start | bytes 2097152 | tf_op jit(solution)/shard_map/all_to_all | solution.py:752
  541.7 24.1 %collective-permute-start.73 = (bf16[448,256]{1,0:T(8,128)(2,1)S(1)}, bf16[448,256]{1,0:T(8,128)(2,1)S(1)}, u32[]{:S(2)}, u32[]{:S(2)}) collective-permute-start(bf16[448,256]{1,0:T(8,128)(2,1)S(1)} %add_convert_fusion.11.refs_3_), channel_id=1, source_target_pairs={{0,4},{4,0},{1,5},{5,1},{2,6},{6,2},{3,7},{7,3},{8,12},{12,8},{9,1... | collective-permute-start | bytes 688136 | tf_op jit(solution)/shard_map/ppermute | solution.py:602
  547.3 18.6 %collective-permute-start.77 = (bf16[448,256]{1,0:T(8,128)(2,1)S(1)}, bf16[448,256]{1,0:T(8,128)(2,1)}, u32[]{:S(2)}, u32[]{:S(2)}) collective-permute-start(bf16[448,256]{1,0:T(8,128)(2,1)S(1)} %add_convert_fusion.8.refs_5_), channel_id=1, source_target_pairs={{0,4},{4,0},{1,5},{5,1},{2,6},{6,2},{3,7},{7,3},{8,12},{12,8},{9,1... | collective-permute-start | bytes 688136 | tf_op jit(solution)/shard_map/ppermute | solution.py:602
  (73 other events, 1375.6 us)

commit v6 on v5

--- a/solution.py
+++ b/solution.py
@@ -43,14 +43,6 @@
     )
 
 
-def add_images(product, first, rows, image):
-    lane = lax.broadcasted_iota(jnp.int32, (rows, COLS), 1) // RANK
-    for at in range(BLOCK):
-        image[...] = jnp.where(
-            lane == first + at, product[at * rows : (at + 1) * rows], image[...]
-        )
-
-
 def write_image(image, send_ref, keep_ref):
     part, parts = pl.program_id(0), pl.num_programs(0)
     last = pl.program_id(1) == pl.num_programs(1) - 1
@@ -62,13 +54,6 @@
     @pl.when(last & (part == parts - 1))
     def _():
         keep_ref[...] = image[...]
-
-
-def image_of(rotated_ref, basis_ref):
-    _, rows, cols = rotated_ref.shape
-    return jnp.dot(
-        rotated_ref[...].reshape(BLOCK * rows, cols), basis_ref[...], preferred_element_type=f32
-    )
 
 
 def form_kernel(n_dp, n_ties, place_ref, *refs):
@@ -155,97 +140,120 @@
     )(place, *out_parts, rot_in, eigvals, basis, *ties)
 
 
-def image_kernel(n_ties, basis_ref, rotated_ref, *refs):
-    send_ref, keep_ref, image = refs[n_ties:]
+def stream(rotated_ref, buffers, sems, parts, begin, body):
+    rows = buffers.shape[1]
+    sets = NG // BLOCK
+
+    def copy(turn, slot):
+        part, query = turn // sets, lax.rem(turn, sets) * BLOCK + slot
+        return pltpu.make_async_copy(
+            rotated_ref.at[query, pl.ds(pl.multiple_of(part * rows, rows), rows), :],
+            buffers.at[slot],
+            sems.at[slot],
+        )
+
+    for slot in range(BLOCK):
+        copy(0, slot).start()
+
+    @pl.loop(0, parts * sets)
+    def _(turn):
+        part, first = turn // sets, lax.rem(turn, sets) * BLOCK
+
+        @pl.when(first == 0)
+        def _():
+            begin(part)
+
+        for slot in range(BLOCK):
+            copy(turn, slot).wait()
+            body(part, first + slot, buffers[slot])
+
+            @pl.when(turn + 1 < parts * sets)
+            def _(slot=slot):
+                copy(turn + 1, slot).start()
+
+
+def stream_scratch(rows, cols):
+    return [pltpu.VMEM((BLOCK, rows, cols), bf16), pltpu.SemaphoreType.DMA((BLOCK,))]
+
+
+def image_kernel(n_dp, n_ties, basis_ref, rotated_ref, *refs):
+    send_ref, keep_ref, buffers, sems, image = refs[n_ties:]
     rows = image.shape[0]
-    add_images(image_of(rotated_ref, basis_ref), pl.program_id(1) * BLOCK, rows, image)
-    write_image(image, send_ref, keep_ref)
+    lane = lax.broadcasted_iota(jnp.int32, (rows, COLS), 1) // RANK
+
+    def body(part, query, block):
+        product = jnp.dot(block, basis_ref[...], preferred_element_type=f32)
+        image[...] = jnp.where(lane == query, product, image[...])
+
+        @pl.when((query == NG - 1) & (part < n_dp - 1))
+        def _():
+            send_ref[pl.ds(pl.multiple_of(part * rows, rows), rows), :] = image[...].astype(bf16)
+
+        @pl.when((query == NG - 1) & (part == n_dp - 1))
+        def _():
+            keep_ref[...] = image[...]
+
+    stream(rotated_ref, buffers, sems, n_dp, lambda part: None, body)
 
 
 def image_piece(basis, rotated, n_dp, ties):
     _, rows, cols = rotated.shape
     rows = rows // n_dp
-    return pl.pallas_call(
-        functools.partial(image_kernel, len(ties)),
-        grid=(n_dp, NG // BLOCK),
-        in_specs=[
-            pl.BlockSpec((cols, COLS), lambda part, query: (0, 0)),
-            pl.BlockSpec((BLOCK, rows, cols), lambda part, query: (query, part, 0)),
-        ]
-        + tied(ties),
-        out_specs=[
-            pl.BlockSpec((rows, COLS), lambda part, query: (jnp.minimum(part, n_dp - 2), 0)),
-            pl.BlockSpec((rows, COLS), lambda part, query: (0, 0)),
-        ],
+    vmem = pl.BlockSpec(memory_space=pltpu.VMEM)
+    return pl.pallas_call(
+        functools.partial(image_kernel, n_dp, len(ties)),
+        in_specs=[vmem] + tied([rotated, *ties]),
+        out_specs=[vmem, vmem],
         out_shape=[
             jax.ShapeDtypeStruct(((n_dp - 1) * rows, COLS), bf16),
             jax.ShapeDtypeStruct((rows, COLS), f32),
         ],
-        scratch_shapes=[pltpu.VMEM((rows, COLS), f32)],
+        scratch_shapes=stream_scratch(rows, cols) + [pltpu.VMEM((rows, COLS), f32)],
         compiler_params=params(),
         cost_estimate=cost(rotated.shape, 256),
         name="image",
     )(basis, rotated, *ties)
 
 
-def return_kernel(n_dp, first, *refs):
+def return_kernel(n_dp, first, n_ties, *refs):
     image_refs, rotated_ref = refs[:n_dp], refs[n_dp]
-    total_ref, gram_ref, turned = refs[-3:]
-    part, step = pl.program_id(0), pl.program_id(1)
-
-    @pl.when((part == 0) & (step == 0))
-    def _():
-        if first:
-            total_ref[...] = jnp.zeros_like(total_ref)
-            gram_ref[...] = jnp.zeros_like(gram_ref)
-        else:
-            total_ref[...] = refs[n_dp + 1][...]
-            gram_ref[...] = refs[n_dp + 2][...]
-
-    for at in range(n_dp):
-
-        @pl.when((step == 0) & (part == at))
-        def _(at=at):
-            image = image_refs[at][...]
-            turned[...] = image.astype(f32).T.astype(bf16)
-            gram_ref[...] += lax.dot_general(
-                image, image, (((0,), (0,)), ((), ())), preferred_element_type=f32
-            )
-
-    for at in range(BLOCK):
-        own = pl.ds(pl.multiple_of((step * BLOCK + at) * RANK, RANK), RANK)
-        total_ref[own, :] += jnp.dot(
-            turned[own, :], rotated_ref[at], preferred_element_type=f32
-        )
+    total_ref, rounded_ref, buffers, sems, turned = refs[-5:]
+    total_ref[...] = jnp.zeros_like(total_ref) if first else refs[n_dp + 1][...]
+
+    def begin(part):
+        for at in range(n_dp):
+
+            @pl.when(part == at)
+            def _(at=at):
+                turned[...] = image_refs[at][...].astype(f32).T.astype(bf16)
+
+    def body(part, query, block):
+        own = pl.ds(pl.multiple_of(query * RANK, RANK), RANK)
+        total_ref[own, :] += jnp.dot(turned[own, :], block, preferred_element_type=f32)
+
+    stream(rotated_ref, buffers, sems, n_dp, begin, body)
+    rounded_ref[...] = total_ref[...].astype(bf16)
 
 
 def return_piece(images, rotated, before, ties):
     n_dp = len(images)
     _, rows, cols = rotated.shape
     rows = rows // n_dp
-    first = before is None
-
-    def fixed(shape):
-        return pl.BlockSpec(shape, lambda part, query: (0, 0))
-
-    sums = [fixed((COLS, cols)), fixed((COLS, COLS))]
-    return pl.pallas_call(
-        functools.partial(return_kernel, n_dp, first),
-        grid=(n_dp, NG // BLOCK),
-        in_specs=[fixed((rows, COLS))] * n_dp
-        + [pl.BlockSpec((BLOCK, rows, cols), lambda part, query: (query, part, 0))]
-        + ([] if first else sums)
-        + tied(ties),
-        out_specs=sums,
+    vmem = pl.BlockSpec(memory_space=pltpu.VMEM)
+    before = [] if before is None else [before]
+    return pl.pallas_call(
+        functools.partial(return_kernel, n_dp, not before, len(ties)),
+        in_specs=[vmem] * n_dp + tied([rotated]) + [vmem] * len(before) + tied(ties),
+        out_specs=[vmem, vmem],
         out_shape=[
             jax.ShapeDtypeStruct((COLS, cols), f32),
-            jax.ShapeDtypeStruct((COLS, COLS), f32),
+            jax.ShapeDtypeStruct((COLS, cols), bf16),
         ],
-        scratch_shapes=[pltpu.VMEM((COLS, rows), bf16)],
+        scratch_shapes=stream_scratch(rows, cols) + [pltpu.VMEM((COLS, rows), bf16)],
         compiler_params=params(),
         cost_estimate=cost(rotated.shape, 256),
         name="returned",
-    )(*images, rotated, *([] if first else before), *ties)
+    )(*images, rotated, *before, *ties)
 
 
 def rotate_out_kernel(n_dp, place_ref, query_ref, eigen_ref, *refs):
@@ -290,19 +298,17 @@
     )(place, query_out, eigen_out)
 
 
-def rotate_in_kernel(n_ties, place_ref, query_ref, eigen_ref, *refs):
-    theirs_ref, mine_ref, product = refs[n_ties:]
-    product[...] = jnp.dot(query_ref[...], eigen_ref[...], preferred_element_type=f32)
-    for out_ref, index in ((theirs_ref, 1 - place_ref[1]), (mine_ref, place_ref[1])):
-        out_ref[...] = product[pl.ds(pl.multiple_of(index * TOKS, TOKS), TOKS), :]
-
-
-def rotate_in(place, query_in, eigen_in, ties):
+def rotate_in_kernel(other, place_ref, query_ref, eigen_ref, *refs):
+    index = 1 - place_ref[1] if other else place_ref[1]
+    rows = pl.ds(pl.multiple_of(index * TOKS, TOKS), TOKS)
+    refs[-1][...] = jnp.dot(query_ref[rows, :], eigen_ref[...], preferred_element_type=f32)
+
+
+def rotate_in(place, query_in, eigen_in, other, ties):
     depth, cols = eigen_in.shape
     width = LANES if cols % LANES == 0 else cols
-    out = jax.ShapeDtypeStruct((TOKS, cols), f32)
-    return pl.pallas_call(
-        functools.partial(rotate_in_kernel, len(ties)),
+    return pl.pallas_call(
+        functools.partial(rotate_in_kernel, other),
         grid_spec=pltpu.PrefetchScalarGridSpec(
             num_scalar_prefetch=1,
             grid=(cols // width,),
@@ -311,13 +317,12 @@
                 pl.BlockSpec((depth, width), lambda at, _: (0, at)),
             ]
             + tied(ties),
-            out_specs=[pl.BlockSpec((TOKS, width), lambda at, _: (0, at))] * 2,
-            scratch_shapes=[pltpu.VMEM((CORES * TOKS, width), f32)],
+            out_specs=pl.BlockSpec((TOKS, width), lambda at, _: (0, at)),
         ),
-        out_shape=[out, out],
+        out_shape=jax.ShapeDtypeStruct((TOKS, cols), f32),
         compiler_params=params(),
         cost_estimate=pl.CostEstimate(
-            flops=2 * depth * cols * CORES * TOKS, bytes_accessed=2 * depth * cols, transcendentals=0
+            flops=2 * depth * cols * TOKS, bytes_accessed=2 * depth * cols, transcendentals=0
         ),
         name="rotate_in",
     )(place, query_in, eigen_in, *ties)
@@ -331,8 +336,8 @@
     )
 
 
-def factor_kernel(n_dp, place_ref, eigen_ref, mine_ref, theirs_ref, *refs):
-    *out_refs, cols = refs
+def factor_kernel(n_dp, n_ties, place_ref, eigen_ref, mine_ref, theirs_ref, *refs):
+    *out_refs, cols = refs[n_ties:]
     step = pl.program_id(0)
     rows = eigen_ref.shape[0]
 
@@ -353,7 +358,7 @@
                     keep_ref[...] = product
 
 
-def factor_in(place, eigen_in, mine, theirs, n_dp):
+def factor_in(place, eigen_in, mine, theirs, n_dp, ties):
     rows, depth = eigen_in.shape
     rows = rows // (FACTOR_PIECES * n_dp)
     width = CORES * COLS
@@ -367,18 +372,18 @@
         jax.ShapeDtypeStruct((rows, width), f32),
     ] * FACTOR_PIECES
     return pl.pallas_call(
-        functools.partial(factor_kernel, n_dp),
+        functools.partial(factor_kernel, n_dp, len(ties)),
         grid_spec=pltpu.PrefetchScalarGridSpec(
             num_scalar_prefetch=1,
             grid=(FACTOR_PIECES * n_dp,),
-            in_specs=[pl.BlockSpec((rows, depth), eigen_block), fixed, fixed],
+            in_specs=[pl.BlockSpec((rows, depth), eigen_block), fixed, fixed] + tied(ties),
             out_specs=[pl.BlockSpec(each.shape, lambda at, _: (0, 0)) for each in shapes],
             scratch_shapes=[pltpu.VMEM((depth, width), bf16)],
         ),
         out_shape=shapes,
         compiler_params=params(),
         name="factor_in",
-    )(place, eigen_in, mine, theirs)
+    )(place, eigen_in, mine, theirs, *ties)
 
 
 def write_shares(place_ref, total, keep_ref, send_refs):
@@ -590,14 +595,22 @@
         total = keep
         for part in got:
             total = total + part.astype(f32)
-        step = 1
+        step, odd = 1, lax.axis_index("grp") % 2
         while step < n_grp:
+            if even and step == 2:
+                total = lax.dynamic_slice_in_dim(total, odd * (rows // 2), rows // 2, 0)
             sent = total.astype(bf16)
             got = lax.ppermute(sent, "grp", crossed(n_grp, step))
             yield [sent]
             total = (sent.astype(f32) if even else total) + got.astype(f32)
             step *= 2
         own = self.own = total.astype(bf16)
+        if even and n_grp > 2:
+            got = lax.ppermute(own, "grp", crossed(n_grp, 1))
+            yield [own]
+            own = jnp.where(
+                odd == 0, jnp.concatenate([own, got]), jnp.concatenate([got, own])
+            )
         others = [
             lax.ppermute(own, "dp", turned_by(n_dp, n_dp - 1 - at)) for at in range(n_dp - 1)
         ]
@@ -664,32 +677,42 @@
             total = gram
             for step in range(1, n_dp):
                 total = total + lax.ppermute(gram, "dp", turned_by(n_dp, step))
-            return sum_but_last(total, f32)
-
-        def sum_but_last(total, kind):
             step = 2
             while True:
-                got = lax.ppermute(total.astype(kind), "width", crossed(n_width, step))
+                got = lax.ppermute(total, "width", crossed(n_width, step))
                 step *= 2
                 if step >= n_width:
                     return total, got
-                total = total + got.astype(f32)
+                total = total + got
+
+        def sum_but_last(total, sent=None):
+            step = 2
+            while True:
+                sent = total.astype(bf16) if sent is None else sent
+                got = lax.ppermute(sent, "width", crossed(n_width, step))
+                step *= 2
+                if step >= n_width:
+                    return total, sent, got
+                total, sent = total + got.astype(f32), None
 
         pieces = list(rotate_out(place, query_out, eigen_out, n_dp))
         own_pieces, their_pieces = pieces[: 2 * PIECES], pieces[2 * PIECES :]
-        theirs_in, mine_in = rotate_in(place, query_in, eigen_in, pieces[:1])
-        turning = [reduction(own_pieces[0], own_pieces[1])]
+        theirs_in = rotate_in(place, query_in, eigen_in, True, pieces[:1])
+        mine_in = rotate_in(place, query_in, eigen_in, False, [theirs_in])
+        theirs_in = swap_cores(theirs_in, n_width)
+        total_in, sent_in, got = sum_but_last(mine_in + theirs_in)
+        rot_in = (total_in + got.astype(f32)).astype(bf16)
+        turning = [reduction(own_pieces[0], after(own_pieces[1], [sent_in]))]
         their_pieces = [swap_cores(each, n_width) for each in their_pieces]
-        theirs_in = swap_cores(theirs_in, n_width)
-        total_in, got = sum_but_last(mine_in + theirs_in, bf16)
-        rot_in = (total_in + got.astype(f32)).astype(bf16)
         hops = []
         count = CORES * PIECES
         for at in range(1, count):
             hops = advance_all(turning)
             sends, keep = (own_pieces + their_pieces)[2 * at : 2 * at + 2]
             turning.append(reduction(after(sends, hops[:1]), keep))
-        eig_theirs = swap_cores(after(eigvals, [theirs_in, their_pieces[-1], *hops[:1]]), n_width)
+        finish(turning[0], turning)
+        eig_sent = after(eigvals, [rot_in, *turning[0].parts])
+        eig_theirs = swap_cores(eig_sent, n_width)
         hidden = (jax.nn.silu(gate_pre.astype(f32)) * up_pre.astype(f32)).astype(bf16)
         basis = lax.dynamic_slice_in_dim(start, core * COLS, COLS, 1)
         rotated = []
@@ -709,7 +732,7 @@
                     ties = []
                 ties += advance_all(summing)
                 summing.append(reduction(sends, keep))
-            sums = gram = None
+            total = gram = None
             for at in range(count):
                 finish(summing[at], summing)
                 if gram is None and all(each.own is not None for each in summing):
@@ -723,20 +746,20 @@
                         mine_out, theirs_out = turn(place, inverse, images, n_dp)
                         theirs_out = swap_cores(theirs_out, n_width)
                         ties = ties + [mine_out]
-                sums = return_piece(summing[at].parts, rotated[at], sums, ties)
+                total, sent = return_piece(summing[at].parts, rotated[at], total, ties)
                 ties = advance_all(summing)
-            total, got = sum_but_last(sums[0], bf16)
+            total, sent, got = sum_but_last(total, sent)
             ties = []
             if iteration == ITERS - 1:
                 keep_out, *sends_out = factor_out(
-                    place, eigen_out, mine_out, after(theirs_out, [total]), n_width
+                    place, eigen_out, mine_out, after(theirs_out, [sent]), n_width
                 )
                 ties = [keep_out]
             basis = normalize(total, got, inverse, ties)
 
         their_basis = swap_cores(basis, n_width)
-        pieces = factor_in(place, eigen_in, basis, their_basis, n_dp)
         share = sum_shares(keep_out, sends_out, n_width).astype(bf16)
+        pieces = factor_in(place, eigen_in, basis, their_basis, n_dp, [share])
         factors, hops = [], []
         for at in range(FACTOR_PIECES):
             sends, keep = pieces[2 * at : 2 * at + 2]

time: 584 us -> 623 us (1.067)
  Pallas kernels: 281 us -> 312 us
    pallas_call x14 -> x15, Pallas kernels: 163 us -> 194 us  [the longest x8 86.2 us: return_piece(): pl.pallas_call(functools.partial(return_kernel, n_dp, not before, len(tie...]
    ppermute x16, waiting for transfers between devices: 39.7 us -> 27.1 us  [run(): lax.ppermute(sends[at * rows:(at + 1) * rows], 'dp', turned_by(n_dp, at +...]
    ppermute x32, starting transfers between devices: 50.1 us -> 38.4 us  [run(): got = lax.ppermute(sent, 'grp', crossed(n_grp, step))]
    ppermute x5 -> x9, waiting for transfers between devices: 20.7 us -> 27.8 us  [the longest x3 19 us: sum_but_last(): got = lax.ppermute(sent, 'width', crossed(n_width, step))]
    ppermute x8, waiting for transfers between devices: 6.14 us -> 12.7 us  [swap_cores(): return lax.ppermute(part, 'width', crossed(n_width, 1))]
  transfers between devices with their start and end apart: 88 -> 92, of which waited for: 35 -> 36; matrix products, arithmetic and copies ran while one was open for 4% -> 4% of each run, Pallas kernels for 38% -> 41%
where the time goes in v6:
time: 623 us; the launch traced here: 619 us
  Pallas kernels  312 us (50%)
  waiting for transfers between devices  159 us (26%)
  starting transfers between devices  111 us (18%)
  other arithmetic  22.3 us (4%)
  local copies, waits for them, and re-layouts  12.4 us (2%)
    pallas_call x4, Pallas kernels, form_piece(): pl.pallas_call(functools.partial(form_kernel, n_dp, len(ties)), grid_spec...  99 us
    pallas_call x8, Pallas kernels, return_piece(): pl.pallas_call(functools.partial(return_kernel, n_dp, not before, len(tie...  86.2 us
    ppermute x32, waiting for transfers between devices, run(): got = lax.ppermute(sent, 'grp', crossed(n_grp, step))  77.1 us
    pallas_call x4, Pallas kernels, image_piece(): pl.pallas_call(functools.partial(image_kernel, n_dp, len(ties)), in_specs...  76.7 us
    ppermute x32, starting transfers between devices, run(): got = lax.ppermute(sent, 'grp', crossed(n_grp, step))  38.4 us
    ppermute x16, waiting for transfers between devices, run(): lax.ppermute(sends[at * rows:(at + 1) * rows], 'dp', turned_by(n_dp, at +...  27.1 us
    ppermute x16, starting transfers between devices, run(): lax.ppermute(own, 'dp', turned_by(n_dp, n_dp - 1 - at))  22.3 us
    pallas_call x2, Pallas kernels, rotate_in(): pl.pallas_call(functools.partial(rotate_in_kernel, other), grid_spec=pltp...  19.9 us
  transfers between devices with their start and end apart: 92, of which 36 were waited for; matrix products, arithmetic and copies ran while one was open for 4% of the time, Pallas kernels for 41%

profile of v6, /device:TPU:0, one launch (start us, length us, event | category | flops | bytes accessed | tf_op | source)
XLA Modules:
  0.0 619.1 jit_solution(12651954680423415425)
XLA Ops:
  2.2 5.9 rotate_out.1
  8.0 9.5 %rotate_in.2.refs_0_ = f32[256,1792]{1,0:T(8,128)S(1)} custom-call(s32[3]{0:T(128)S(1)} %pad_add_fusion.place_ref, bf16[512,3584]{1,0:T(8,128)(2,1)S(1)} %copy-done.4, bf16[3584,1792]{1,0:T(8,128)(2,1)} %eigen_ref.9, bf16[512,256]{1,0:T(8,128)(2,1)S(1)} %get-tuple-element.72.refs_0_), custom_call_target="tpu_custom_call" | custom-call | flops 3288334336 | bytes 12845056 | tf_op jit(solution)/shard_map/rotate_in/pallas_call | solution.py:310
  20.7 10.4 %rotate_in.3 = f32[256,1792]{1,0:T(8,128)S(1)} custom-call(s32[3]{0:T(128)S(1)} %pad_add_fusion.place_ref, bf16[512,3584]{1,0:T(8,128)(2,1)} %query_ref.5, bf16[3584,1792]{1,0:T(8,128)(2,1)} %eigen_ref.9, f32[256,1792]{1,0:T(8,128)S(1)} %rotate_in.2.refs_0_), custom_call_target="tpu_custom_call" | custom-call | flops 3288334336 | bytes 12845056 | tf_op jit(solution)/shard_map/rotate_in/pallas_call | solution.py:310
  34.6 5.3 collective-permute-done.4
  42.6 11.5 %collective-permute-done.5 = bf16[512,256]{1,0:T(8,128)(2,1)S(1)} collective-permute-done((bf16[512,256]{1,0:T(8,128)(2,1)S(1)}, bf16[512,256]{1,0:T(8,128)(2,1)S(1)}, u32[]{:S(2)}, u32[]{:S(2)}) %collective-permute-start.5) | collective-permute-done | bytes 262176 | tf_op jit(solution)/shard_map/ppermute | solution.py:603
  55.9 5.6 collective-permute-done.11.refs_0_
  77.6 7.8 %collective-permute-done.19 = bf16[512,256]{1,0:T(8,128)(2,1)} collective-permute-done((bf16[512,256]{1,0:T(8,128)(2,1)}, bf16[512,256]{1,0:T(8,128)(2,1)}, u32[]{:S(2)}, u32[]{:S(2)}) %collective-permute-start.19) | collective-permute-done | bytes 262176 | tf_op jit(solution)/shard_map/ppermute | solution.py:574
  101.7 9.8 %collective-permute-done.17 = bf16[512,256]{1,0:T(8,128)(2,1)S(1)} collective-permute-done((bf16[512,256]{1,0:T(8,128)(2,1)S(1)}, bf16[512,256]{1,0:T(8,128)(2,1)S(1)}, u32[]{:S(2)}, u32[]{:S(2)}) %collective-permute-start.17) | collective-permute-done | bytes 262176 | tf_op jit(solution)/shard_map/ppermute | solution.py:603
  113.4 24.6 %form.4 = (bf16[8,1024,1792]{2,1,0:T(8,128)(2,1)}, bf16[512,128]{1,0:T(8,128)(2,1)S(1)}, f32[512,128]{1,0:T(8,128)S(1)}) custom-call(s32[3]{0:T(128)S(1)} %pad_add_fusion.place_ref, bf16[512,256]{1,0:T(8,128)(2,1)S(1)} %copy-done.12, bf16[512,256]{1,0:T(8,128)(2,1)S(1)} %copy-done.8, bf16[256,1792]{1,0:T(8,128)(2,1)S(1)} %add_convert_fusion.refs_2_, ...), custom_call_target="tpu_custom_call" | custom-call | flops 11744051200 | bytes 29360128 | tf_op jit(solution)/shard_map/form/pallas_call | solution.py:107
  144.3 25.1 %form.5 = (bf16[8,1024,1792]{2,1,0:T(8,128)(2,1)}, bf16[512,128]{1,0:T(8,128)(2,1)S(1)}, f32[512,128]{1,0:T(8,128)S(1)}) custom-call(s32[3]{0:T(128)S(1)} %pad_add_fusion.place_ref, bf16[512,256]{1,0:T(8,128)(2,1)S(1)} %collective-permute-done.18.refs_0_, bf16[512,256]{1,0:T(8,128)(2,1)S(1)} %add_convert_fusion.2.refs_1_, ...), custom_call_target="tpu_custom_call" | custom-call | flops 11744051200 | bytes 29360128 | tf_op jit(solution)/shard_map/form/pallas_call | solution.py:107
  190.3 24.6 %form.7 = (bf16[8,1024,1792]{2,1,0:T(8,128)(2,1)}, bf16[512,128]{1,0:T(8,128)(2,1)S(1)}, f32[512,128]{1,0:T(8,128)S(1)}) custom-call(s32[3]{0:T(128)S(1)} %pad_add_fusion.place_ref, bf16[512,256]{1,0:T(8,128)(2,1)S(1)} %collective-permute-done.29.refs_0_, bf16[512,256]{1,0:T(8,128)(2,1)S(1)} %add_convert_fusion.1.refs_5_.refs_1_, ...), custom_call_target="tpu_custom_call" | custom-call | flops 11744051200 | bytes 29360128 | tf_op jit(solution)/shard_map/form/pallas_call | solution.py:107
  215.6 24.7 %form.6 = (bf16[8,1024,1792]{2,1,0:T(8,128)(2,1)}, bf16[512,128]{1,0:T(8,128)(2,1)S(1)}, f32[512,128]{1,0:T(8,128)S(1)}) custom-call(s32[3]{0:T(128)S(1)} %pad_add_fusion.place_ref, bf16[512,256]{1,0:T(8,128)(2,1)S(1)} %collective-permute-done.9.refs_0_, bf16[512,256]{1,0:T(8,128)(2,1)S(1)} %add_convert_fusion.3.refs_1_.refs_5_, ...), custom_call_target="tpu_custom_call" | custom-call | flops 11744051200 | bytes 29360128 | tf_op jit(solution)/shard_map/form/pallas_call | solution.py:107
  251.6 5.6 collective-permute-done.32
  262.2 10.9 %returned.8 = (f32[128,1792]{1,0:T(8,128)S(1)}, bf16[128,1792]{1,0:T(8,128)(2,1)}) custom-call(bf16[512,128]{1,0:T(8,128)(2,1)S(1)} %collective-permute-done.38.refs_0_, bf16[512,128]{1,0:T(8,128)(2,1)S(1)} %add_convert_fusion.14.refs_1_.refs_3_.refs_0_, bf16[8,1024,1792]{2,1,0:T(8,128)(2,1)} %get-tuple-element.93.refs_2_.rotated_ref, ...), custom_call_target="tpu_custom_call" | custom-call | flops 7516192768 | bytes 29360128 | tf_op jit(solution)/shard_map/returned/pallas_call | solution.py:244
  276.7 10.9 %returned.9 = (f32[128,1792]{1,0:T(8,128)S(1)}, bf16[128,1792]{1,0:T(8,128)(2,1)}) custom-call(bf16[512,128]{1,0:T(8,128)(2,1)S(1)} %collective-permute-done.36.refs_0_, bf16[512,128]{1,0:T(8,128)(2,1)S(1)} %add_convert_fusion.15.refs_1_, bf16[8,1024,1792]{2,1,0:T(8,128)(2,1)} %get-tuple-element.92.refs_2_.rotated_ref, ...), custom_call_target="tpu_custom_call" | custom-call | flops 7516192768 | bytes 29360128 | tf_op jit(solution)/shard_map/returned/pallas_call | solution.py:244
  289.2 10.9 %returned.10 = (f32[128,1792]{1,0:T(8,128)S(1)}, bf16[128,1792]{1,0:T(8,128)(2,1)}) custom-call(bf16[512,128]{1,0:T(8,128)(2,1)S(1)} %collective-permute-done.33.refs_0_, bf16[512,128]{1,0:T(8,128)(2,1)S(1)} %add_convert_fusion.16.refs_4_.refs_2_.refs_1_, bf16[8,1024,1792]{2,1,0:T(8,128)(2,1)} %get-tuple-element.91.refs_2_.rotated_ref, ...), custom_call_target="tpu_custom_call" | custom-call | flops 7516192768 | bytes 29360128 | tf_op jit(solution)/shard_map/returned/pallas_call | solution.py:244
  300.1 10.3 %returned.11 = (f32[128,1792]{1,0:T(8,128)S(1)}, bf16[128,1792]{1,0:T(8,128)(2,1)S(1)}) custom-call(bf16[512,128]{1,0:T(8,128)(2,1)S(1)} %collective-permute-done.28.refs_0_, bf16[512,128]{1,0:T(8,128)(2,1)S(1)} %add_convert_fusion.17.refs_3_.refs_4_.refs_1_, bf16[8,1024,1792]{2,1,0:T(8,128)(2,1)} %get-tuple-element.88.refs_2_.rotated_ref, ...), custom_call_target="tpu_custom_call" | custom-call | flops 7516192768 | bytes 29360128 | tf_op jit(solution)/shard_map/returned/pallas_call | solution.py:244
  311.0 9.4 %collective-permute-done.41.got_ref = bf16[128,1792]{1,0:T(8,128)(2,1)S(1)} collective-permute-done((bf16[128,1792]{1,0:T(8,128)(2,1)S(1)}, bf16[128,1792]{1,0:T(8,128)(2,1)S(1)}, u32[]{:S(2)}, u32[]{:S(2)}) %collective-permute-start.41) | collective-permute-done | bytes 458784 | tf_op jit(solution)/shard_map/ppermute | solution.py:692
  321.3 19.2 %image.4 = (bf16[512,128]{1,0:T(8,128)(2,1)S(1)}, f32[512,128]{1,0:T(8,128)S(1)}) custom-call(bf16[1792,128]{1,0:T(8,128)(2,1)S(1)} %normalize.2.basis_ref, bf16[8,1024,1792]{2,1,0:T(8,128)(2,1)} %get-tuple-element.93.refs_2_.rotated_ref), custom_call_target="tpu_custom_call" | custom-call | flops 7516192768 | bytes 29360128 | tf_op jit(solution)/shard_map/image/pallas_call | solution.py:203
  340.9 19.2 %image.5 = (bf16[512,128]{1,0:T(8,128)(2,1)S(1)}, f32[512,128]{1,0:T(8,128)S(1)}) custom-call(bf16[1792,128]{1,0:T(8,128)(2,1)S(1)} %normalize.2.basis_ref, bf16[8,1024,1792]{2,1,0:T(8,128)(2,1)} %get-tuple-element.92.refs_2_.rotated_ref), custom_call_target="tpu_custom_call" | custom-call | flops 7516192768 | bytes 29360128 | tf_op jit(solution)/shard_map/image/pallas_call | solution.py:203
  361.8 19.2 %image.6 = (bf16[512,128]{1,0:T(8,128)(2,1)S(1)}, f32[512,128]{1,0:T(8,128)S(1)}) custom-call(bf16[1792,128]{1,0:T(8,128)(2,1)S(1)} %normalize.2.basis_ref, bf16[8,1024,1792]{2,1,0:T(8,128)(2,1)} %get-tuple-element.91.refs_2_.rotated_ref, bf16[512,128]{1,0:T(8,128)(2,1)S(1)} %fusion.18.refs_0_), custom_call_target="tpu_custom_call" | custom-call | flops 7516192768 | bytes 29360128 | tf_op jit(solution)/shard_map/image/pallas_call | solution.py:203
  387.8 19.2 %image.7 = (bf16[512,128]{1,0:T(8,128)(2,1)S(1)}, f32[512,128]{1,0:T(8,128)S(1)}) custom-call(bf16[1792,128]{1,0:T(8,128)(2,1)S(1)} %normalize.2.basis_ref, bf16[8,1024,1792]{2,1,0:T(8,128)(2,1)} %get-tuple-element.88.refs_2_.rotated_ref, bf16[512,128]{1,0:T(8,128)(2,1)S(1)} %fusion.26.refs_0_, bf16[512,128]{1,0:T(8,128)(2,1)S(1)} %fusion.19.refs_1_), custom_call_target="tpu_custom_call" | custom-call | flops 7516192768 | bytes 29360128 | tf_op jit(solution)/shard_map/image/pallas_call | solution.py:203
  423.3 11.3 %returned.12 = (f32[128,1792]{1,0:T(8,128)S(1)}, bf16[128,1792]{1,0:T(8,128)(2,1)}) custom-call(bf16[512,128]{1,0:T(8,128)(2,1)S(1)} %collective-permute-done.56.refs_0_, bf16[512,128]{1,0:T(8,128)(2,1)S(1)} %add_convert_fusion.13.refs_0_.refs_1_.refs_3_, bf16[8,1024,1792]{2,1,0:T(8,128)(2,1)} %get-tuple-element.93.refs_2_.rotated_ref, ...), custom_call_target="tpu_custom_call" | custom-call | flops 7516192768 | bytes 29360128 | tf_op jit(solution)/shard_map/returned/pallas_call | solution.py:244
  435.8 10.9 %returned.13 = (f32[128,1792]{1,0:T(8,128)S(1)}, bf16[128,1792]{1,0:T(8,128)(2,1)}) custom-call(bf16[512,128]{1,0:T(8,128)(2,1)S(1)} %collective-permute-done.57.refs_2_.refs_0_, bf16[512,128]{1,0:T(8,128)(2,1)S(1)} %add_convert_fusion.12.refs_1_.refs_3_, bf16[8,1024,1792]{2,1,0:T(8,128)(2,1)} %get-tuple-element.92.refs_2_.rotated_ref, ...), custom_call_target="tpu_custom_call" | custom-call | flops 7516192768 | bytes 29360128 | tf_op jit(solution)/shard_map/returned/pallas_call | solution.py:244
  448.7 10.9 %returned.14 = (f32[128,1792]{1,0:T(8,128)S(1)}, bf16[128,1792]{1,0:T(8,128)(2,1)}) custom-call(bf16[512,128]{1,0:T(8,128)(2,1)S(1)} %collective-permute-done.58.refs_4_.refs_0_, bf16[512,128]{1,0:T(8,128)(2,1)S(1)} %add_convert_fusion.11.refs_2_.refs_5_.refs_4_.refs_1_, bf16[8,1024,1792]{2,1,0:T(8,128)(2,1)} %get-tuple-element.91.refs_2_.rotated_ref, ...), custom_call_target="tpu_custom_call" | custom-call | flops 7516192768 | bytes 29360128 | tf_op jit(solution)/shard_map/returned/pallas_call | solution.py:244
  463.6 10.3 %returned.15 = (f32[128,1792]{1,0:T(8,128)S(1)}, bf16[128,1792]{1,0:T(8,128)(2,1)S(1)}) custom-call(bf16[512,128]{1,0:T(8,128)(2,1)S(1)} %collective-permute-done.59.refs_6_.refs_0_, bf16[512,128]{1,0:T(8,128)(2,1)S(1)} %add_convert_fusion.10.refs_3_.refs_7_.refs_4_.refs_1_, bf16[8,1024,1792]{2,1,0:T(8,128)(2,1)} %get-tuple-element.88.refs_2_.rotated_ref, ...), custom_call_target="tpu_custom_call" | custom-call | flops 7516192768 | bytes 29360128 | tf_op jit(solution)/shard_map/returned/pallas_call | solution.py:244
  477.2 9.6 %collective-permute-done.64.got_ref = bf16[128,1792]{1,0:T(8,128)(2,1)S(1)} collective-permute-done((bf16[128,1792]{1,0:T(8,128)(2,1)S(1)}, bf16[128,1792]{1,0:T(8,128)(2,1)S(1)}, u32[]{:S(2)}, u32[]{:S(2)}) %collective-permute-start.64) | collective-permute-done | bytes 458784 | tf_op jit(solution)/shard_map/ppermute | solution.py:692
  495.8 10.8 %factor_in.1 = (bf16[448,256]{1,0:T(8,128)(2,1)S(1)}, f32[448,256]{1,0:T(8,128)S(1)}, bf16[448,256]{1,0:T(8,128)(2,1)S(1)}, f32[448,256]{1,0:T(8,128)S(1)}, bf16...) custom-call(s32[3]{0:T(128)S(1)} %pad_add_fusion.place_ref, ...), custom_call_target="tpu_custom_call" | custom-call | tf_op jit(solution)/shard_map/factor_in/pallas_call | solution.py:374
  508.1 7.5 %collective-permute-done.66 = bf16[448,256]{1,0:T(8,128)(2,1)S(1)} collective-permute-done((bf16[448,256]{1,0:T(8,128)(2,1)S(1)}, bf16[448,256]{1,0:T(8,128)(2,1)S(1)}, u32[]{:S(2)}, u32[]{:S(2)}) %collective-permute-start.66) | collective-permute-done | bytes 229408 | tf_op jit(solution)/shard_map/ppermute | solution.py:589
  517.1 6.9 %collective-permute-done.67 = bf16[448,256]{1,0:T(8,128)(2,1)} collective-permute-done((bf16[448,256]{1,0:T(8,128)(2,1)}, bf16[448,256]{1,0:T(8,128)(2,1)}, u32[]{:S(2)}, u32[]{:S(2)}) %collective-permute-start.67) | collective-permute-done | bytes 229408 | tf_op jit(solution)/shard_map/ppermute | solution.py:603
  536.5 11.5 %collective-permute-done.71 = bf16[448,256]{1,0:T(8,128)(2,1)S(1)} collective-permute-done((bf16[448,256]{1,0:T(8,128)(2,1)S(1)}, bf16[448,256]{1,0:T(8,128)(2,1)S(1)}, u32[]{:S(2)}, u32[]{:S(2)}) %collective-permute-start.71) | collective-permute-done | bytes 229408 | tf_op jit(solution)/shard_map/ppermute | solution.py:589
  584.9 6.0 collective-permute-done.83
  (284 shorter events, 222.5 us)
Async XLA Ops:
  33.1 22.6 %collective-permute-start.10 = (bf16[256,1792]{1,0:T(8,128)(2,1)S(1)}, bf16[256,1792]{1,0:T(8,128)(2,1)S(1)}, u32[]{:S(2)}, u32[]{:S(2)}) collective-permute-start(bf16[256,1792]{1,0:T(8,128)(2,1)S(1)} %get-tuple-element.135), channel_id=1, source_target_pairs={{0,2},{1,3},{2,0},{3,1},{4,6},{5,7},{6,4},{7,5},{8,10},{9,11},{10,... | collective-permute-start | bytes 2752520 | tf_op jit(solution)/shard_map/ppermute | solution.py:692
  62.2 128.1 %collective-permute-start.12 = (f32[2048,1792]{1,0:T(8,128)}, f32[2048,1792]{1,0:T(8,128)}, u32[]{:S(2)}, u32[]{:S(2)}) collective-permute-start(f32[2048,1792]{1,0:T(8,128)} %refs_3_.3), channel_id=1, source_target_pairs={{0,1},{1,0},{2,3},{3,2},{4,5},{5,4},{6,7},{7,6},{8,9},{9,8},{10,11... | collective-permute-start | bytes 44040200 | tf_op jit(solution)/shard_map/ppermute | solution.py:574
  63.6 21.9 %collective-permute-start.19 = (bf16[512,256]{1,0:T(8,128)(2,1)}, bf16[512,256]{1,0:T(8,128)(2,1)}, u32[]{:S(2)}, u32[]{:S(2)}) collective-permute-start(bf16[512,256]{1,0:T(8,128)(2,1)} %get-tuple-element.81), channel_id=1, source_target_pairs={{0,1},{1,0},{2,3},{3,2},{4,5},{5,4},{6,7},{7,6},{8,9},{9,8},{10,11... | collective-permute-start | bytes 786440 | tf_op jit(solution)/shard_map/ppermute | solution.py:574
  63.6 30.6 %collective-permute-start.1 = (bf16[512,256]{1,0:T(8,128)(2,1)}, bf16[512,256]{1,0:T(8,128)(2,1)}, u32[]{:S(2)}, u32[]{:S(2)}) collective-permute-start(bf16[512,256]{1,0:T(8,128)(2,1)} %get-tuple-element.70), channel_id=1, source_target_pairs={{0,1},{1,0},{2,3},{3,2},{4,5},{5,4},{6,7},{7,6},{8,9},{9,8},{10,11... | collective-permute-start | bytes 786440 | tf_op jit(solution)/shard_map/ppermute | solution.py:574
  68.9 16.6 %collective-permute-start.21 = (bf16[512,256]{1,0:T(8,128)(2,1)}, bf16[512,256]{1,0:T(8,128)(2,1)}, u32[]{:S(2)}, u32[]{:S(2)}) collective-permute-start(bf16[512,256]{1,0:T(8,128)(2,1)} %collective-permute-done.20), channel_id=1, source_target_pairs={{0,4},{4,0},{1,5},{5,1},{2,6},{6,2},{3,7},{7,3},{8,12},{12,8},{9,1... | collective-permute-start | bytes 786440 | tf_op jit(solution)/shard_map/ppermute | solution.py:589
  72.4 16.1 %collective-permute-start.16 = (bf16[512,256]{1,0:T(8,128)(2,1)}, bf16[512,256]{1,0:T(8,128)(2,1)}, u32[]{:S(2)}, u32[]{:S(2)}) collective-permute-start(bf16[512,256]{1,0:T(8,128)(2,1)} %fusion.9), channel_id=1, source_target_pairs={{0,8},{8,0},{16,24},{24,16},{1,9},{9,1},{17,25},{25,17},{2,10},{10... | collective-permute-start | bytes 786440 | tf_op jit(solution)/shard_map/ppermute | solution.py:603
  85.4 27.8 %collective-permute-start = (bf16[512,256]{1,0:T(8,128)(2,1)}, bf16[512,256]{1,0:T(8,128)(2,1)S(1)}, u32[]{:S(2)}, u32[]{:S(2)}) collective-permute-start(bf16[512,256]{1,0:T(8,128)(2,1)} %copy-done.10), channel_id=1, source_target_pairs={{0,1},{1,0},{2,3},{3,2},{4,5},{5,4},{6,7},{7,6},{8,9},{9,8},{10,11... | collective-permute-start | bytes 786440 | tf_op jit(solution)/shard_map/ppermute | solution.py:574
  89.6 21.8 %collective-permute-start.17 = (bf16[512,256]{1,0:T(8,128)(2,1)S(1)}, bf16[512,256]{1,0:T(8,128)(2,1)S(1)}, u32[]{:S(2)}, u32[]{:S(2)}) collective-permute-start(bf16[512,256]{1,0:T(8,128)(2,1)S(1)} %fusion.13), channel_id=1, source_target_pairs={{0,16},{8,24},{16,0},{24,8},{1,17},{9,25},{17,1},{25,9},{2,18},{10... | collective-permute-start | bytes 786440 | tf_op jit(solution)/shard_map/ppermute | solution.py:603
  94.2 19.1 %collective-permute-start.6 = (bf16[512,256]{1,0:T(8,128)(2,1)}, bf16[512,256]{1,0:T(8,128)(2,1)S(1)}, u32[]{:S(2)}, u32[]{:S(2)}) collective-permute-start(bf16[512,256]{1,0:T(8,128)(2,1)} %collective-permute-done.1), channel_id=1, source_target_pairs={{0,4},{4,0},{1,5},{5,1},{2,6},{6,2},{3,7},{7,3},{8,12},{12,8},{9,1... | collective-permute-start | bytes 786440 | tf_op jit(solution)/shard_map/ppermute | solution.py:589
  100.6 38.8 %collective-permute-start.23 = (bf16[512,256]{1,0:T(8,128)(2,1)S(1)}, bf16[512,256]{1,0:T(8,128)(2,1)S(1)}, u32[]{:S(2)}, u32[]{:S(2)}) collective-permute-start(bf16[512,256]{1,0:T(8,128)(2,1)S(1)} %fusion.11), channel_id=1, source_target_pairs={{0,16},{8,24},{16,0},{24,8},{1,17},{9,25},{17,1},{25,9},{2,18},{10... | collective-permute-start | bytes 786440 | tf_op jit(solution)/shard_map/ppermute | solution.py:603
  112.6 31.7 %collective-permute-start.18 = (bf16[512,256]{1,0:T(8,128)(2,1)S(1)}, bf16[512,256]{1,0:T(8,128)(2,1)S(1)}, u32[]{:S(2)}, u32[]{:S(2)}) collective-permute-start(bf16[512,256]{1,0:T(8,128)(2,1)S(1)} %add_convert_fusion.2.refs_1_), channel_id=1, source_target_pairs={{0,4},{4,0},{1,5},{5,1},{2,6},{6,2},{3,7},{7,3},{8,12},{12,8},{9,1... | collective-permute-start | bytes 786440 | tf_op jit(solution)/shard_map/ppermute | solution.py:615
  113.3 27.9 %collective-permute-start.7 = (bf16[512,256]{1,0:T(8,128)(2,1)S(1)}, bf16[512,256]{1,0:T(8,128)(2,1)S(1)}, u32[]{:S(2)}, u32[]{:S(2)}) collective-permute-start(bf16[512,256]{1,0:T(8,128)(2,1)S(1)} %fusion.6), channel_id=1, source_target_pairs={{0,8},{8,0},{16,24},{24,16},{1,9},{9,1},{17,25},{25,17},{2,10},{10... | collective-permute-start | bytes 786440 | tf_op jit(solution)/shard_map/ppermute | solution.py:603
  138.0 33.0 %collective-permute-start.13 = (bf16[512,128]{1,0:T(8,128)(2,1)S(1)}, bf16[512,128]{1,0:T(8,128)(2,1)S(1)}, u32[]{:S(2)}, u32[]{:S(2)}) collective-permute-start(bf16[512,128]{1,0:T(8,128)(2,1)S(1)} %get-tuple-element.77), channel_id=1, source_target_pairs={{0,4},{4,0},{1,5},{5,1},{2,6},{6,2},{3,7},{7,3},{8,12},{12,8},{9,1... | collective-permute-start | bytes 393224 | tf_op jit(solution)/shard_map/ppermute | solution.py:589
  140.7 49.6 %collective-permute-start.29 = (bf16[512,256]{1,0:T(8,128)(2,1)S(1)}, bf16[512,256]{1,0:T(8,128)(2,1)S(1)}, u32[]{:S(2)}, u32[]{:S(2)}) collective-permute-start(bf16[512,256]{1,0:T(8,128)(2,1)S(1)} %add_convert_fusion.1.refs_5_.refs_1_), channel_id=1, source_target_pairs={{0,4},{4,0},{1,5},{5,1},{2,6},{6,2},{3,7},{7,3},{8,12},{12,8},{9,1... | collective-permute-start | bytes 786440 | tf_op jit(solution)/shard_map/ppermute | solution.py:615
  141.3 35.7 %collective-permute-start.8 = (bf16[512,256]{1,0:T(8,128)(2,1)S(1)}, bf16[512,256]{1,0:T(8,128)(2,1)S(1)}, u32[]{:S(2)}, u32[]{:S(2)}) collective-permute-start(bf16[512,256]{1,0:T(8,128)(2,1)S(1)} %fusion.10.refs_6_), channel_id=1, source_target_pairs={{0,16},{8,24},{16,0},{24,8},{1,17},{9,25},{17,1},{25,9},{2,18},{10... | collective-permute-start | bytes 786440 | tf_op jit(solution)/shard_map/ppermute | solution.py:603
  177.2 38.5 %collective-permute-start.9 = (bf16[512,256]{1,0:T(8,128)(2,1)S(1)}, bf16[512,256]{1,0:T(8,128)(2,1)S(1)}, u32[]{:S(2)}, u32[]{:S(2)}) collective-permute-start(bf16[512,256]{1,0:T(8,128)(2,1)S(1)} %add_convert_fusion.3.refs_1_.refs_5_), channel_id=1, source_target_pairs={{0,4},{4,0},{1,5},{5,1},{2,6},{6,2},{3,7},{7,3},{8,12},{12,8},{9,1... | collective-permute-start | bytes 786440 | tf_op jit(solution)/shard_map/ppermute | solution.py:615
  184.7 77.5 %collective-permute-start.38 = (bf16[512,128]{1,0:T(8,128)(2,1)S(1)}, bf16[512,128]{1,0:T(8,128)(2,1)S(1)}, u32[]{:S(2)}, u32[]{:S(2)}) collective-permute-start(bf16[512,128]{1,0:T(8,128)(2,1)S(1)} %add_convert_fusion.14.refs_1_.refs_3_.refs_0_), channel_id=1, source_target_pairs={{0,4},{4,0},{1,5},{5,1},{2,6},{6,2},{3,7},{7,3},{8,12},{12,8},{9,1... | collective-permute-start | bytes 393224 | tf_op jit(solution)/shard_map/ppermute | solution.py:615
  189.0 87.8 %collective-permute-start.36 = (bf16[512,128]{1,0:T(8,128)(2,1)S(1)}, bf16[512,128]{1,0:T(8,128)(2,1)S(1)}, u32[]{:S(2)}, u32[]{:S(2)}) collective-permute-start(bf16[512,128]{1,0:T(8,128)(2,1)S(1)} %add_convert_fusion.15.refs_1_), channel_id=1, source_target_pairs={{0,4},{4,0},{1,5},{5,1},{2,6},{6,2},{3,7},{7,3},{8,12},{12,8},{9,1... | collective-permute-start | bytes 393224 | tf_op jit(solution)/shard_map/ppermute | solution.py:615
  214.9 26.7 %collective-permute-start.30 = (bf16[512,128]{1,0:T(8,128)(2,1)S(1)}, bf16[512,128]{1,0:T(8,128)(2,1)S(1)}, u32[]{:S(2)}, u32[]{:S(2)}) collective-permute-start(bf16[512,128]{1,0:T(8,128)(2,1)S(1)} %get-tuple-element.90), channel_id=1, source_target_pairs={{0,4},{4,0},{1,5},{5,1},{2,6},{6,2},{3,7},{7,3},{8,12},{12,8},{9,1... | collective-permute-start | bytes 393224 | tf_op jit(solution)/shard_map/ppermute | solution.py:589
  273.2 26.9 %collective-permute-start.28 = (bf16[512,128]{1,0:T(8,128)(2,1)S(1)}, bf16[512,128]{1,0:T(8,128)(2,1)S(1)}, u32[]{:S(2)}, u32[]{:S(2)}) collective-permute-start(bf16[512,128]{1,0:T(8,128)(2,1)S(1)} %add_convert_fusion.17.refs_3_.refs_4_.refs_1_), channel_id=1, source_target_pairs={{0,4},{4,0},{1,5},{5,1},{2,6},{6,2},{3,7},{7,3},{8,12},{12,8},{9,1... | collective-permute-start | bytes 393224 | tf_op jit(solution)/shard_map/ppermute | solution.py:615
  340.5 21.3 %collective-permute-start.42 = (bf16[512,128]{1,0:T(8,128)(2,1)S(1)}, bf16[512,128]{1,0:T(8,128)(2,1)S(1)}, u32[]{:S(2)}, u32[]{:S(2)}) collective-permute-start(bf16[512,128]{1,0:T(8,128)(2,1)S(1)} %get-tuple-element.100), channel_id=1, source_target_pairs={{0,4},{4,0},{1,5},{5,1},{2,6},{6,2},{3,7},{7,3},{8,12},{12,8},{9,1... | collective-permute-start | bytes 393224 | tf_op jit(solution)/shard_map/ppermute | solution.py:589
  360.1 21.5 %collective-permute-start.45 = (bf16[512,128]{1,0:T(8,128)(2,1)S(1)}, bf16[512,128]{1,0:T(8,128)(2,1)S(1)}, u32[]{:S(2)}, u32[]{:S(2)}) collective-permute-start(bf16[512,128]{1,0:T(8,128)(2,1)S(1)} %get-tuple-element.102), channel_id=1, source_target_pairs={{0,4},{4,0},{1,5},{5,1},{2,6},{6,2},{3,7},{7,3},{8,12},{12,8},{9,1... | collective-permute-start | bytes 393224 | tf_op jit(solution)/shard_map/ppermute | solution.py:589
  381.1 26.4 %collective-permute-start.48 = (bf16[512,128]{1,0:T(8,128)(2,1)S(1)}, bf16[512,128]{1,0:T(8,128)(2,1)S(1)}, u32[]{:S(2)}, u32[]{:S(2)}) collective-permute-start(bf16[512,128]{1,0:T(8,128)(2,1)S(1)} %get-tuple-element.104), channel_id=1, source_target_pairs={{0,4},{4,0},{1,5},{5,1},{2,6},{6,2},{3,7},{7,3},{8,12},{12,8},{9,1... | collective-permute-start | bytes 393224 | tf_op jit(solution)/shard_map/ppermute | solution.py:589
  381.6 27.9 %collective-permute-start.46 = (bf16[512,128]{1,0:T(8,128)(2,1)S(1)}, bf16[512,128]{1,0:T(8,128)(2,1)S(1)}, u32[]{:S(2)}, u32[]{:S(2)}) collective-permute-start(bf16[512,128]{1,0:T(8,128)(2,1)S(1)} %fusion.19.refs_1_), channel_id=1, source_target_pairs={{0,8},{8,0},{16,24},{24,16},{1,9},{9,1},{17,25},{25,17},{2,10},{10... | collective-permute-start | bytes 393224 | tf_op jit(solution)/shard_map/ppermute | solution.py:603
  387.5 22.8 %collective-permute-start.44 = (bf16[512,128]{1,0:T(8,128)(2,1)S(1)}, bf16[512,128]{1,0:T(8,128)(2,1)S(1)}, u32[]{:S(2)}, u32[]{:S(2)}) collective-permute-start(bf16[512,128]{1,0:T(8,128)(2,1)S(1)} %fusion.26.refs_0_), channel_id=1, source_target_pairs={{0,16},{8,24},{16,0},{24,8},{1,17},{9,25},{17,1},{25,9},{2,18},{10... | collective-permute-start | bytes 393224 | tf_op jit(solution)/shard_map/ppermute | solution.py:603
  419.1 16.7 %collective-permute-start.57 = (bf16[512,128]{1,0:T(8,128)(2,1)S(1)}, bf16[512,128]{1,0:T(8,128)(2,1)S(1)}, u32[]{:S(2)}, u32[]{:S(2)}) collective-permute-start(bf16[512,128]{1,0:T(8,128)(2,1)S(1)} %add_convert_fusion.12.refs_1_.refs_3_), channel_id=1, source_target_pairs={{0,4},{4,0},{1,5},{5,1},{2,6},{6,2},{3,7},{7,3},{8,12},{12,8},{9,1... | collective-permute-start | bytes 393224 | tf_op jit(solution)/shard_map/ppermute | solution.py:615
  421.9 26.7 %collective-permute-start.58 = (bf16[512,128]{1,0:T(8,128)(2,1)S(1)}, bf16[512,128]{1,0:T(8,128)(2,1)S(1)}, u32[]{:S(2)}, u32[]{:S(2)}) collective-permute-start(bf16[512,128]{1,0:T(8,128)(2,1)S(1)} %add_convert_fusion.11.refs_2_.refs_5_.refs_4_.refs_1_), channel_id=1, source_target_pairs={{0,4},{4,0},{1,5},{5,1},{2,6},{6,2},{3,7},{7,3},{8,12},{12,8},{9,1... | collective-permute-start | bytes 393224 | tf_op jit(solution)/shard_map/ppermute | solution.py:615
  527.8 48.7 %all-to-all-start = ((bf16[8,256,256]{2,1,0:T(8,128)(2,1)}), bf16[8,256,256]{2,1,0:T(8,128)(2,1)}, u32[]{:S(2)}, u32[]{:S(2)}) async-start(bf16[8,256,256]{2,1,0:T(8,128)(2,1)} %broadcast_in_dim.2), calls=%async_computation | async-start | bytes 2097152 | tf_op jit(solution)/shard_map/all_to_all | solution.py:655
  535.0 17.8 %collective-permute-start.69 = (bf16[224,256]{1,0:T(8,128)(2,1)S(1)}, bf16[224,256]{1,0:T(8,128)(2,1)S(1)}, u32[]{:S(2)}, u32[]{:S(2)}) collective-permute-start(bf16[224,256]{1,0:T(8,128)(2,1)S(1)} %add_convert_fusion.24), channel_id=1, source_target_pairs={{0,8},{8,0},{16,24},{24,16},{1,9},{9,1},{17,25},{25,17},{2,10},{10... | collective-permute-start | bytes 344072 | tf_op jit(solution)/shard_map/ppermute | solution.py:609
  552.8 52.0 %collective-permute-start.70 = (bf16[448,256]{1,0:T(8,128)(2,1)S(1)}, bf16[448,256]{1,0:T(8,128)(2,1)S(1)}, u32[]{:S(2)}, u32[]{:S(2)}) collective-permute-start(bf16[448,256]{1,0:T(8,128)(2,1)S(1)} %maximum_select_fusion.refs_1_), channel_id=1, source_target_pairs={{0,4},{4,0},{1,5},{5,1},{2,6},{6,2},{3,7},{7,3},{8,12},{12,8},{9,1... | collective-permute-start | bytes 688136 | tf_op jit(solution)/shard_map/ppermute | solution.py:615
  573.7 31.1 %collective-permute-start.75 = (bf16[448,256]{1,0:T(8,128)(2,1)S(1)}, bf16[448,256]{1,0:T(8,128)(2,1)S(1)}, u32[]{:S(2)}, u32[]{:S(2)}) collective-permute-start(bf16[448,256]{1,0:T(8,128)(2,1)S(1)} %maximum_select_fusion.1.refs_3_), channel_id=1, source_target_pairs={{0,4},{4,0},{1,5},{5,1},{2,6},{6,2},{3,7},{7,3},{8,12},{12,8},{9,1... | collective-permute-start | bytes 688136 | tf_op jit(solution)/shard_map/ppermute | solution.py:615
  576.5 20.5 %all-to-all-start.1 = ((bf16[4,512,256]{2,1,0:T(8,128)(2,1)}), bf16[4,512,256]{2,1,0:T(8,128)(2,1)}, u32[]{:S(2)}, u32[]{:S(2)}) async-start(bf16[4,512,256]{2,1,0:T(8,128)(2,1)} %bitcast.3), calls=%async_computation.1 | async-start | bytes 2097152 | tf_op jit(solution)/shard_map/all_to_all | solution.py:775
  (77 other events, 1384.5 us)

commit v7 on v6

--- a/solution.py
+++ b/solution.py
@@ -18,6 +18,7 @@
 LANES = 256
 PIECES = 2
 BLOCK = 4
+IMAGE_BLOCK = 2
 FACTOR_PIECES = 4
 
 damping = 0.01
@@ -43,23 +44,14 @@
     )
 
 
-def write_image(image, send_ref, keep_ref):
-    part, parts = pl.program_id(0), pl.num_programs(0)
-    last = pl.program_id(1) == pl.num_programs(1) - 1
-
-    @pl.when(last & (part < parts - 1))
-    def _():
-        send_ref[...] = image[...].astype(bf16)
-
-    @pl.when(last & (part == parts - 1))
-    def _():
-        keep_ref[...] = image[...]
-
-
-def form_kernel(n_dp, n_ties, place_ref, *refs):
-    out_refs = refs[:n_dp]
-    in_ref, eig_ref, basis_ref = refs[n_dp : n_dp + 3]
-    rotated_ref, send_ref, keep_ref, weight, left, image = refs[n_dp + 3 + n_ties :]
+def tied(ties):
+    return [pl.BlockSpec(memory_space=pl.ANY)] * len(ties)
+
+
+def form_kernel(n_parts, n_ties, place_ref, *refs):
+    out_refs = refs[:n_parts]
+    in_ref, eig_ref, basis_ref = refs[n_parts : n_parts + 3]
+    rotated_ref, image_ref, weight, left, image = refs[n_parts + 3 + n_ties :]
     part, first = pl.program_id(0), pl.program_id(1) * BLOCK
     rows, cols = eig_ref.shape
 
@@ -67,13 +59,14 @@
     def _():
         weight[...] = 1.0 / (eig_ref[...] + damping)
 
-    for at in range(n_dp):
+    for at in range(n_parts):
 
         @pl.when((first == 0) & (part == at))
         def _(at=at):
             for query in range(NG):
                 left[query] = out_refs[at][:, query * QTOK : (query + 1) * QTOK]
 
+    lane = lax.broadcasted_iota(jnp.int32, (rows, COLS), 1) // RANK
     for at in range(BLOCK):
         query = first + at
         own = left[query]
@@ -83,33 +76,31 @@
             block = jnp.dot(own, right[:, span], preferred_element_type=f32)
             rotated_ref[at, :, span] = (block * weight[:, span]).astype(bf16)
         product = jnp.dot(rotated_ref[at], basis_ref[...], preferred_element_type=f32)
-        lane = lax.broadcasted_iota(jnp.int32, (rows, COLS), 1) // RANK
         image[...] = jnp.where(lane == query, product, image[...])
-    write_image(image, send_ref, keep_ref)
-
-
-def tied(ties):
-    return [pl.BlockSpec(memory_space=pl.ANY)] * len(ties)
-
-
-def form_piece(place, out_parts, rot_in, eigvals, basis, piece, ties):
-    n_dp = len(out_parts)
+
+    @pl.when(first == NG - BLOCK)
+    def _():
+        image_ref[...] = image[...].astype(image_ref.dtype)
+
+
+def form_parts(place, out_parts, rot_in, eigvals, basis, at, n_dp, kind, ties):
+    n_parts = len(out_parts)
     rows = out_parts[0].shape[0]
     cols = rot_in.shape[1]
 
     def eig_block(part, query, place_ref):
-        return piece * n_dp + lax.rem(place_ref[0] + 1 + part, n_dp), 0
+        return at // n_dp * n_dp + lax.rem(place_ref[0] + 1 + at % n_dp + part, n_dp), 0
 
     def fixed(shape):
         return pl.BlockSpec(shape, lambda part, query, _: (0, 0))
 
-    shape = (NG, n_dp * rows, cols)
-    return pl.pallas_call(
-        functools.partial(form_kernel, n_dp, len(ties)),
+    shape = (NG, n_parts * rows, cols)
+    return pl.pallas_call(
+        functools.partial(form_kernel, n_parts, len(ties)),
         grid_spec=pltpu.PrefetchScalarGridSpec(
             num_scalar_prefetch=1,
-            grid=(n_dp, NG // BLOCK),
-            in_specs=[fixed((rows, TOKS))] * n_dp
+            grid=(n_parts, NG // BLOCK),
+            in_specs=[fixed((rows, TOKS))] * n_parts
             + [
                 fixed((TOKS, cols)),
                 pl.BlockSpec((rows, cols), eig_block),
@@ -118,10 +109,7 @@
             + tied(ties),
             out_specs=[
                 pl.BlockSpec((BLOCK, rows, cols), lambda part, query, _: (query, part, 0)),
-                pl.BlockSpec(
-                    (rows, COLS), lambda part, query, _: (jnp.minimum(part, n_dp - 2), 0)
-                ),
-                fixed((rows, COLS)),
+                pl.BlockSpec((rows, COLS), lambda part, query, _: (part, 0)),
             ],
             scratch_shapes=[
                 pltpu.VMEM((rows, cols), f32),
@@ -131,8 +119,7 @@
         ),
         out_shape=[
             jax.ShapeDtypeStruct(shape, bf16),
-            jax.ShapeDtypeStruct(((n_dp - 1) * rows, COLS), bf16),
-            jax.ShapeDtypeStruct((rows, COLS), f32),
+            jax.ShapeDtypeStruct((n_parts * rows, COLS), kind),
         ],
         compiler_params=params(),
         cost_estimate=cost(shape, 400),
@@ -176,52 +163,50 @@
     return [pltpu.VMEM((BLOCK, rows, cols), bf16), pltpu.SemaphoreType.DMA((BLOCK,))]
 
 
-def image_kernel(n_dp, n_ties, basis_ref, rotated_ref, *refs):
-    send_ref, keep_ref, buffers, sems, image = refs[n_ties:]
-    rows = image.shape[0]
+def image_kernel(n_ties, basis_ref, rotated_ref, *refs):
+    image_ref, image = refs[n_ties:]
+    count, rows, cols = rotated_ref.shape
+    first = pl.program_id(1) * count
+    product = jnp.dot(
+        rotated_ref[...].reshape(count * rows, cols), basis_ref[...], preferred_element_type=f32
+    )
     lane = lax.broadcasted_iota(jnp.int32, (rows, COLS), 1) // RANK
-
-    def body(part, query, block):
-        product = jnp.dot(block, basis_ref[...], preferred_element_type=f32)
-        image[...] = jnp.where(lane == query, product, image[...])
-
-        @pl.when((query == NG - 1) & (part < n_dp - 1))
-        def _():
-            send_ref[pl.ds(pl.multiple_of(part * rows, rows), rows), :] = image[...].astype(bf16)
-
-        @pl.when((query == NG - 1) & (part == n_dp - 1))
-        def _():
-            keep_ref[...] = image[...]
-
-    stream(rotated_ref, buffers, sems, n_dp, lambda part: None, body)
-
-
-def image_piece(basis, rotated, n_dp, ties):
-    _, rows, cols = rotated.shape
-    rows = rows // n_dp
-    vmem = pl.BlockSpec(memory_space=pltpu.VMEM)
-    return pl.pallas_call(
-        functools.partial(image_kernel, n_dp, len(ties)),
-        in_specs=[vmem] + tied([rotated, *ties]),
-        out_specs=[vmem, vmem],
-        out_shape=[
-            jax.ShapeDtypeStruct(((n_dp - 1) * rows, COLS), bf16),
-            jax.ShapeDtypeStruct((rows, COLS), f32),
-        ],
-        scratch_shapes=stream_scratch(rows, cols) + [pltpu.VMEM((rows, COLS), f32)],
+    for at in range(count):
+        image[...] = jnp.where(
+            lane == first + at, product[at * rows : (at + 1) * rows], image[...]
+        )
+
+    @pl.when(first == NG - count)
+    def _():
+        image_ref[...] = image[...].astype(image_ref.dtype)
+
+
+def image_parts(basis, rotated, rows, kind, ties):
+    _, total, cols = rotated.shape
+    return pl.pallas_call(
+        functools.partial(image_kernel, len(ties)),
+        grid=(total // rows, NG // IMAGE_BLOCK),
+        in_specs=[
+            pl.BlockSpec((cols, COLS), lambda part, query: (0, 0)),
+            pl.BlockSpec((IMAGE_BLOCK, rows, cols), lambda part, query: (query, part, 0)),
+        ]
+        + tied(ties),
+        out_specs=pl.BlockSpec((rows, COLS), lambda part, query: (part, 0)),
+        out_shape=jax.ShapeDtypeStruct((total, COLS), kind),
+        scratch_shapes=[pltpu.VMEM((rows, COLS), f32)],
         compiler_params=params(),
         cost_estimate=cost(rotated.shape, 256),
         name="image",
     )(basis, rotated, *ties)
 
 
-def return_kernel(n_dp, first, n_ties, *refs):
-    image_refs, rotated_ref = refs[:n_dp], refs[n_dp]
+def return_kernel(n_parts, first, *refs):
+    image_refs, rotated_ref = refs[:n_parts], refs[n_parts]
     total_ref, rounded_ref, buffers, sems, turned = refs[-5:]
-    total_ref[...] = jnp.zeros_like(total_ref) if first else refs[n_dp + 1][...]
+    total_ref[...] = jnp.zeros_like(total_ref) if first else refs[n_parts + 1][...]
 
     def begin(part):
-        for at in range(n_dp):
+        for at in range(n_parts):
 
             @pl.when(part == at)
             def _(at=at):
@@ -231,19 +216,19 @@
         own = pl.ds(pl.multiple_of(query * RANK, RANK), RANK)
         total_ref[own, :] += jnp.dot(turned[own, :], block, preferred_element_type=f32)
 
-    stream(rotated_ref, buffers, sems, n_dp, begin, body)
+    stream(rotated_ref, buffers, sems, n_parts, begin, body)
     rounded_ref[...] = total_ref[...].astype(bf16)
 
 
-def return_piece(images, rotated, before, ties):
-    n_dp = len(images)
+def return_parts(images, rotated, before, ties):
+    n_parts = len(images)
     _, rows, cols = rotated.shape
-    rows = rows // n_dp
+    rows = rows // n_parts
     vmem = pl.BlockSpec(memory_space=pltpu.VMEM)
     before = [] if before is None else [before]
     return pl.pallas_call(
-        functools.partial(return_kernel, n_dp, not before, len(ties)),
-        in_specs=[vmem] * n_dp + tied([rotated]) + [vmem] * len(before) + tied(ties),
+        functools.partial(return_kernel, n_parts, not before),
+        in_specs=[vmem] * n_parts + tied([rotated]) + [vmem] * len(before) + tied(ties),
         out_specs=[vmem, vmem],
         out_shape=[
             jax.ShapeDtypeStruct((COLS, cols), f32),
@@ -298,17 +283,19 @@
     )(place, query_out, eigen_out)
 
 
-def rotate_in_kernel(other, place_ref, query_ref, eigen_ref, *refs):
-    index = 1 - place_ref[1] if other else place_ref[1]
-    rows = pl.ds(pl.multiple_of(index * TOKS, TOKS), TOKS)
-    refs[-1][...] = jnp.dot(query_ref[rows, :], eigen_ref[...], preferred_element_type=f32)
-
-
-def rotate_in(place, query_in, eigen_in, other, ties):
+def rotate_in_kernel(n_ties, place_ref, query_ref, eigen_ref, *refs):
+    theirs_ref, mine_ref, product = refs[n_ties:]
+    product[...] = jnp.dot(query_ref[...], eigen_ref[...], preferred_element_type=f32)
+    for out_ref, index in ((theirs_ref, 1 - place_ref[1]), (mine_ref, place_ref[1])):
+        out_ref[...] = product[pl.ds(pl.multiple_of(index * TOKS, TOKS), TOKS), :]
+
+
+def rotate_in(place, query_in, eigen_in, ties):
     depth, cols = eigen_in.shape
     width = LANES if cols % LANES == 0 else cols
-    return pl.pallas_call(
-        functools.partial(rotate_in_kernel, other),
+    out = jax.ShapeDtypeStruct((TOKS, cols), f32)
+    return pl.pallas_call(
+        functools.partial(rotate_in_kernel, len(ties)),
         grid_spec=pltpu.PrefetchScalarGridSpec(
             num_scalar_prefetch=1,
             grid=(cols // width,),
@@ -317,12 +304,13 @@
                 pl.BlockSpec((depth, width), lambda at, _: (0, at)),
             ]
             + tied(ties),
-            out_specs=pl.BlockSpec((TOKS, width), lambda at, _: (0, at)),
+            out_specs=[pl.BlockSpec((TOKS, width), lambda at, _: (0, at))] * 2,
+            scratch_shapes=[pltpu.VMEM((CORES * TOKS, width), f32)],
         ),
-        out_shape=jax.ShapeDtypeStruct((TOKS, cols), f32),
+        out_shape=[out, out],
         compiler_params=params(),
         cost_estimate=pl.CostEstimate(
-            flops=2 * depth * cols * TOKS, bytes_accessed=2 * depth * cols, transcendentals=0
+            flops=2 * depth * cols * CORES * TOKS, bytes_accessed=2 * depth * cols, transcendentals=0
         ),
         name="rotate_in",
     )(place, query_in, eigen_in, *ties)
@@ -574,25 +562,31 @@
     return lax.ppermute(part, "width", crossed(n_width, 1))
 
 
+def after(array, others):
+    return lax.optimization_barrier((array, *others))[0] if others else array
+
+
 class Reduction:
-    def __init__(self, sends, keep, n_grp, n_dp, even=False):
+    def __init__(self, sends, n_grp, n_dp, even=False, keep=None):
         self.parts = self.own = None
-        self.steps = self.run(sends, keep, n_grp, n_dp, even)
+        self.keep = keep
+        self.steps = self.run(sends, n_grp, n_dp, even)
         next(self.steps)
 
-    def advance(self):
-        return next(self.steps, None) or []
-
-    def run(self, sends, keep, n_grp, n_dp, even):
-        rows = keep.shape[0]
+    def advance(self, others):
+        try:
+            return self.steps.send(others)
+        except StopIteration:
+            return []
+
+    def run(self, sends, n_grp, n_dp, even):
+        rows = sends.shape[0] // (n_dp - 1)
         got = [
-            lax.ppermute(
-                sends[at * rows : (at + 1) * rows], "dp", turned_by(n_dp, at + 1)
-            )
+            lax.ppermute(sends[at * rows : (at + 1) * rows], "dp", turned_by(n_dp, at + 1))
             for at in range(n_dp - 1)
         ]
-        yield []
-        total = keep
+        others = yield []
+        total = after(self.keep, others)
         for part in got:
             total = total + part.astype(f32)
         step, odd = 1, lax.axis_index("grp") % 2
@@ -601,40 +595,45 @@
                 total = lax.dynamic_slice_in_dim(total, odd * (rows // 2), rows // 2, 0)
             sent = total.astype(bf16)
             got = lax.ppermute(sent, "grp", crossed(n_grp, step))
-            yield [sent]
-            total = (sent.astype(f32) if even else total) + got.astype(f32)
+            others = yield [sent]
+            total = (sent.astype(f32) if even else total) + after(got, others).astype(f32)
             step *= 2
-        own = self.own = total.astype(bf16)
+        own = total.astype(bf16)
         if even and n_grp > 2:
             got = lax.ppermute(own, "grp", crossed(n_grp, 1))
-            yield [own]
+            others = yield [own]
+            got = after(got, others)
             own = jnp.where(
                 odd == 0, jnp.concatenate([own, got]), jnp.concatenate([got, own])
             )
-        others = [
+        self.own = own
+        parts = [
             lax.ppermute(own, "dp", turned_by(n_dp, n_dp - 1 - at)) for at in range(n_dp - 1)
         ]
         yield [own]
-        self.parts = others + [own]
-
-
-def advance_all(reductions):
+        self.parts = parts + [own]
+
+
+class Steps:
+    def __init__(self, steps):
+        self.steps, self.count = steps, 0
+
+    def advance(self, others):
+        self.count += 1
+        try:
+            return self.steps.send(others if self.count > 1 else None)
+        except StopIteration:
+            return []
+
+
+def boundary(others, reductions):
     ties = []
     for reduction in reductions:
-        if reduction.parts is None:
-            ties += reduction.advance()
+        if reduction.parts is None and reduction.keep is not None:
+            hop = reduction.advance(others)
+            ties += hop
+            others = hop or others
     return ties
-
-
-def finish(reduction, reductions):
-    ties = []
-    while reduction.parts is None:
-        ties = advance_all(reductions)
-    return ties
-
-
-def after(array, others):
-    return lax.optimization_barrier((array, *others))[0] if others else array
 
 
 def sum_shares(keep, sends, n_width):
@@ -669,23 +668,7 @@
         scale = 1.0 / (eigen_out.shape[0] * n_gd)
         rows_out = eigvals.shape[0]
 
-        def reduction(sends, keep, even=False):
-            return Reduction(sends, keep, n_grp, n_dp, even)
-
-        def sum_gram(parts):
-            gram = gram_of(parts)
-            total = gram
-            for step in range(1, n_dp):
-                total = total + lax.ppermute(gram, "dp", turned_by(n_dp, step))
-            step = 2
-            while True:
-                got = lax.ppermute(total, "width", crossed(n_width, step))
-                step *= 2
-                if step >= n_width:
-                    return total, got
-                total = total + got
-
-        def sum_but_last(total, sent=None):
+        def last_hop(total, sent=None):
             step = 2
             while True:
                 sent = total.astype(bf16) if sent is None else sent
@@ -695,94 +678,145 @@
                     return total, sent, got
                 total, sent = total + got.astype(f32), None
 
+        def output_side(summing, last):
+            gram = gram_of([each.own for each in summing])
+            got = [lax.ppermute(gram, "dp", turned_by(n_dp, at)) for at in range(1, n_dp)]
+            others = yield [gram]
+            gram = after(gram, others)
+            for each in got:
+                gram = gram + each
+            step = 2
+            while True:
+                got = lax.ppermute(gram, "width", crossed(n_width, step))
+                step *= 2
+                if step >= n_width:
+                    break
+                gram = gram + got
+            others = yield [gram]
+            inverse = found["inverse"] = inverse_of(after(gram, others), got, scale)
+            if not last:
+                return
+            images = [part for each in summing for part in each.parts]
+            mine, theirs = turn(place, inverse, images, n_dp)
+            theirs = swap_cores(theirs, n_width)
+            others = yield [mine]
+            keep, *sends = factor_out(place, eigen_out, after(mine, others), theirs, n_width)
+            sends = [
+                lax.ppermute(send, "width", crossed(n_width, at + 1))
+                for at, send in enumerate(sends)
+            ]
+            others = yield [keep]
+            share = after(keep, others)
+            for send in sends:
+                share = share + send.astype(f32)
+            share = share.astype(bf16)
+            piece_rows = share.shape[0]
+            gathered = gather_rows(share, GD, n_gd)
+            others = yield [share]
+            mixed = lax.all_to_all(after(gathered, others), "width", 0, 0, tiled=True)
+            others = yield [gathered]
+            out_factor = found["out_factor"] = (
+                after(mixed, others)
+                .reshape(n_width, n_gd // n_width, piece_rows, NQ * RANK)
+                .transpose(1, 0, 2, 3)
+                .reshape(rows_out, NQ * RANK)
+            )
+            proj_out = jnp.dot(grads_out, out_factor, preferred_element_type=f32)
+            found["proj_out"] = sum_scatter(proj_out, "width", n_width)
+
+        found = {}
+        count = CORES * PIECES
         pieces = list(rotate_out(place, query_out, eigen_out, n_dp))
         own_pieces, their_pieces = pieces[: 2 * PIECES], pieces[2 * PIECES :]
-        theirs_in = rotate_in(place, query_in, eigen_in, True, pieces[:1])
-        mine_in = rotate_in(place, query_in, eigen_in, False, [theirs_in])
+        turning = [Reduction(own_pieces[0], n_grp, n_dp, keep=own_pieces[1])]
+        theirs_in, mine_in = rotate_in(place, query_in, eigen_in, pieces[:1])
         theirs_in = swap_cores(theirs_in, n_width)
-        total_in, sent_in, got = sum_but_last(mine_in + theirs_in)
-        rot_in = (total_in + got.astype(f32)).astype(bf16)
-        turning = [reduction(own_pieces[0], after(own_pieces[1], [sent_in]))]
         their_pieces = [swap_cores(each, n_width) for each in their_pieces]
-        hops = []
-        count = CORES * PIECES
+        hops = boundary([mine_in], turning)
+        total_in, sent_in, got_in = last_hop(after(mine_in, hops) + theirs_in)
+        last = [sent_in]
         for at in range(1, count):
-            hops = advance_all(turning)
             sends, keep = (own_pieces + their_pieces)[2 * at : 2 * at + 2]
-            turning.append(reduction(after(sends, hops[:1]), keep))
-        finish(turning[0], turning)
-        eig_sent = after(eigvals, [rot_in, *turning[0].parts])
-        eig_theirs = swap_cores(eig_sent, n_width)
+            turning.append(Reduction(after(sends, last), n_grp, n_dp, keep=keep))
+            last = boundary(last, turning)[:1] or last
         hidden = (jax.nn.silu(gate_pre.astype(f32)) * up_pre.astype(f32)).astype(bf16)
+        rot_in = (total_in + got_in.astype(f32)).astype(bf16)
         basis = lax.dynamic_slice_in_dim(start, core * COLS, COLS, 1)
-        rotated = []
+        rotated, eig_theirs, ties = [], None, [hidden]
         for iteration in range(ITERS):
-            summing, ties = [], [hidden] if iteration == 0 else []
+            summing = []
+            found.clear()
             for at in range(count):
                 if iteration == 0:
-                    finish(turning[at], turning)
-                    eig = eigvals if at < PIECES else eig_theirs
-                    block, sends, keep = form_piece(
-                        place, turning[at].parts, rot_in, eig, basis, at % PIECES, ties
+                    while turning[at].parts is None:
+                        last = boundary(last, turning) or last
+                    if eig_theirs is None:
+                        eig_sent = after(eigvals, [rot_in, *turning[0].parts])
+                        eig_theirs = swap_cores(eig_sent, n_width)
+                    rotated.append([None, None])
+                for side, kind in ((0, bf16), (1, f32)):
+                    if iteration == 0:
+                        parts = turning[at].parts
+                        block, image = form_parts(
+                            place,
+                            parts[-1:] if side else parts[:-1],
+                            rot_in,
+                            eigvals if at < PIECES else eig_theirs,
+                            basis,
+                            at % PIECES * n_dp + side * (n_dp - 1),
+                            n_dp,
+                            kind,
+                            ties,
+                        )
+                        rotated[at][side] = block
+                    else:
+                        rows = rotated[at][1].shape[1]
+                        image = image_parts(basis, rotated[at][side], rows, kind, ties)
+                    if side:
+                        summing[at].keep = image
+                    last = [image]
+                    ties = boundary(last, turning + summing)
+                    if not side:
+                        summing.append(Reduction(image, n_grp, n_dp))
+            total = path = None
+            for at in range(count):
+                while summing[at].parts is None:
+                    last = boundary(last, summing) or last
+                for side in range(2):
+                    parts = summing[at].parts
+                    total, sent = return_parts(
+                        parts[-1:] if side else parts[:-1], rotated[at][side], total, ties
                     )
-                    rotated.append(block)
-                    ties = advance_all(turning)
-                else:
-                    sends, keep = image_piece(basis, rotated[at], n_dp, ties)
-                    ties = []
-                ties += advance_all(summing)
-                summing.append(reduction(sends, keep))
-            total = gram = None
-            for at in range(count):
-                finish(summing[at], summing)
-                if gram is None and all(each.own is not None for each in summing):
-                    gram, gram_got = sum_gram([each.own for each in summing])
-                    ties = ties + [gram]
-                elif gram is not None and at == count - 1:
-                    inverse = inverse_of(gram, gram_got, scale)
-                    ties = ties + [inverse]
-                    if iteration == ITERS - 1:
-                        images = [part for each in summing for part in each.parts]
-                        mine_out, theirs_out = turn(place, inverse, images, n_dp)
-                        theirs_out = swap_cores(theirs_out, n_width)
-                        ties = ties + [mine_out]
-                total, sent = return_piece(summing[at].parts, rotated[at], total, ties)
-                ties = advance_all(summing)
-            total, sent, got = sum_but_last(total, sent)
+                    last = [sent]
+                    ties = boundary(last, summing)
+                    if path is None and all(each.own is not None for each in summing):
+                        path = Steps(output_side(summing, iteration == ITERS - 1))
+                    if path is not None and path.count < 5:
+                        ties += path.advance(last)
+            while "inverse" not in found:
+                path.advance([])
+            total, sent, got = last_hop(total, sent)
+            basis = normalize(total, got, found["inverse"], ties)
             ties = []
-            if iteration == ITERS - 1:
-                keep_out, *sends_out = factor_out(
-                    place, eigen_out, mine_out, after(theirs_out, [sent]), n_width
-                )
-                ties = [keep_out]
-            basis = normalize(total, got, inverse, ties)
 
         their_basis = swap_cores(basis, n_width)
-        share = sum_shares(keep_out, sends_out, n_width).astype(bf16)
-        pieces = factor_in(place, eigen_in, basis, their_basis, n_dp, [share])
-        factors, hops = [], []
+        pieces = factor_in(place, eigen_in, basis, their_basis, n_dp, [])
+        factors, last = [], [pieces[0]]
         for at in range(FACTOR_PIECES):
             sends, keep = pieces[2 * at : 2 * at + 2]
-            factors.append(reduction(after(sends, hops[:1]), keep, even=True))
-            hops = advance_all(factors)
-        for each in factors:
-            finish(each, factors)
+            factors.append(Reduction(after(sends, last[:1]), n_grp, n_dp, True, keep))
+            last = boundary(last, factors)
+            if at % 2:
+                path.advance(last)
+        while any(each.parts is None for each in factors):
+            last = boundary(last, factors) or last
         parts = [part for each in factors for part in each.parts]
         in_factor, keep_in, *sends_in = project(place, hidden, parts, n_dp, n_width)
-
-        piece_rows = share.shape[0]
-        gathered = gather_rows(share, GD, n_gd)
-        mixed = lax.all_to_all(gathered, "width", 0, 0, tiled=True)
-        out_factor = (
-            mixed.reshape(n_width, n_gd // n_width, piece_rows, NQ * RANK)
-            .transpose(1, 0, 2, 3)
-            .reshape(rows_out, NQ * RANK)
-        )
-        proj_out = jnp.dot(grads_out, out_factor, preferred_element_type=f32)
-        proj_out = sum_scatter(proj_out, "width", n_width)
+        while "proj_out" not in found:
+            path.advance([])
         proj_in = sum_shares(keep_in, sends_in, n_width)
-        scores = (proj_out * proj_in).reshape(proj_out.shape[0], NQ, RANK).sum(axis=2).T
-        return (scores, out_factor, in_factor)
+        scores = (found["proj_out"] * proj_in).reshape(proj_in.shape[0], NQ, RANK).sum(axis=2).T
+        return (scores, found["out_factor"], in_factor)
 
     return per_device
 

time: 623 us -> 609 us (0.978)
  waiting for transfers between devices: 159 us -> 134 us
  Pallas kernels: 312 us -> 329 us
    ppermute x32, waiting for transfers between devices: 77.1 us -> 42.2 us  [run(): got = lax.ppermute(sent, 'grp', crossed(n_grp, step))]
    pallas_call x18 -> x33, Pallas kernels: 282 us -> 300 us  [the longest x8 120 us: form_parts(): pl.pallas_call(functools.partial(form_kernel, n_parts, len(ties)), grid_s...]
    ppermute x16, waiting for transfers between devices: 27.1 us -> 38.2 us  [run(): lax.ppermute(sends[at * rows:(at + 1) * rows], 'dp', turned_by(n_dp, at +...]
    ppermute x16, waiting for transfers between devices: 5.62 us -> 14.7 us  [run(): lax.ppermute(own, 'dp', turned_by(n_dp, n_dp - 1 - at))]
    ppermute x32, starting transfers between devices: 38.4 us -> 46.3 us  [run(): got = lax.ppermute(sent, 'grp', crossed(n_grp, step))]
    ppermute x16, starting transfers between devices: 22.3 us -> 14.8 us  [run(): lax.ppermute(own, 'dp', turned_by(n_dp, n_dp - 1 - at))]
    ppermute x7 -> x10, waiting for transfers between devices: 19 us -> 19.4 us  [the longest x3 12.3 us: last_hop(): got = lax.ppermute(sent, 'width', crossed(n_width, step))]
  transfers between devices with their start and end apart: 92 -> 92, of which waited for: 36 -> 28; matrix products, arithmetic and copies ran while one was open for 4% -> 3% of each run, Pallas kernels for 41% -> 43%
where the time goes in v7:
time: 609 us; the launch traced here: 605 us
  Pallas kernels  329 us (54%)
  waiting for transfers between devices  134 us (22%)
  starting transfers between devices  108 us (18%)
  other arithmetic  17.8 us (3%)
  local copies, waits for them, and re-layouts  12.2 us (2%)
    pallas_call x8, Pallas kernels, form_parts(): pl.pallas_call(functools.partial(form_kernel, n_parts, len(ties)), grid_s...  120 us
    pallas_call x16, Pallas kernels, return_parts(): pl.pallas_call(functools.partial(return_kernel, n_parts, not before), in_...  106 us
    pallas_call x8, Pallas kernels, image_parts(): pl.pallas_call(functools.partial(image_kernel, len(ties)), grid=(total //...  61.9 us
    ppermute x32, starting transfers between devices, run(): got = lax.ppermute(sent, 'grp', crossed(n_grp, step))  46.3 us
    ppermute x32, waiting for transfers between devices, run(): got = lax.ppermute(sent, 'grp', crossed(n_grp, step))  42.2 us
    ppermute x16, waiting for transfers between devices, run(): lax.ppermute(sends[at * rows:(at + 1) * rows], 'dp', turned_by(n_dp, at +...  38.2 us
    ppermute x16, starting transfers between devices, run(): lax.ppermute(sends[at * rows:(at + 1) * rows], 'dp', turned_by(n_dp, at +...  19.8 us
    ppermute x16, starting transfers between devices, run(): lax.ppermute(own, 'dp', turned_by(n_dp, n_dp - 1 - at))  14.8 us
  transfers between devices with their start and end apart: 92, of which 28 were waited for; matrix products, arithmetic and copies ran while one was open for 3% of the time, Pallas kernels for 43%

profile of v7, /device:TPU:0, one launch (start us, length us, event | category | flops | bytes accessed | tf_op | source)
XLA Modules:
  0.0 604.6 jit_solution(6047673268687638217)
XLA Ops:
  8.6 12.8 %rotate_in.1 = (f32[256,1792]{1,0:T(8,128)S(1)}, f32[256,1792]{1,0:T(8,128)S(1)}) custom-call(s32[3]{0:T(128)S(1)} %pad_add_fusion.place_ref, bf16[512,3584]{1,0:T(8,128)(2,1)} %query_ref.3, bf16[3584,1792]{1,0:T(8,128)(2,1)} %eigen_ref.7, bf16[512,256]{1,0:T(8,128)(2,1)S(1)} %get-tuple-element.128.refs_0_), custom_call_target="tpu_custom_call" | custom-call | flops 6576668672 | bytes 12845056 | tf_op jit(solution)/shard_map/rotate_in/pallas_call | solution.py:297
  24.5 6.9 %collective-permute-done.2 = bf16[512,256]{1,0:T(8,128)(2,1)S(1)} collective-permute-done((bf16[512,256]{1,0:T(8,128)(2,1)S(1)}, bf16[512,256]{1,0:T(8,128)(2,1)S(1)}, u32[]{:S(2)}, u32[]{:S(2)}) %collective-permute-start.2) | collective-permute-done | bytes 262176 | tf_op jit(solution)/shard_map/ppermute | solution.py:585
  42.4 11.1 %collective-permute-done.7 = bf16[512,256]{1,0:T(8,128)(2,1)S(1)} collective-permute-done((bf16[512,256]{1,0:T(8,128)(2,1)S(1)}, bf16[512,256]{1,0:T(8,128)(2,1)S(1)}, u32[]{:S(2)}, u32[]{:S(2)}) %collective-permute-start.7) | collective-permute-done | bytes 262176 | tf_op jit(solution)/shard_map/ppermute | solution.py:597
  63.6 6.8 %collective-permute-done.5 = bf16[512,256]{1,0:T(8,128)(2,1)S(1)} collective-permute-done((bf16[512,256]{1,0:T(8,128)(2,1)S(1)}, bf16[512,256]{1,0:T(8,128)(2,1)S(1)}, u32[]{:S(2)}, u32[]{:S(2)}) %collective-permute-start.5) | collective-permute-done | bytes 262176 | tf_op jit(solution)/shard_map/ppermute | solution.py:585
  76.7 8.2 %collective-permute-done.8 = bf16[512,256]{1,0:T(8,128)(2,1)} collective-permute-done((bf16[512,256]{1,0:T(8,128)(2,1)}, bf16[512,256]{1,0:T(8,128)(2,1)}, u32[]{:S(2)}, u32[]{:S(2)}) %collective-permute-start.8) | collective-permute-done | bytes 262176 | tf_op jit(solution)/shard_map/ppermute | solution.py:562
  110.5 14.8 %form.8 = (bf16[8,512,1792]{2,1,0:T(8,128)(2,1)}, bf16[512,128]{1,0:T(8,128)(2,1)S(1)}) custom-call(s32[3]{0:T(128)S(1)} %pad_add_fusion.place_ref, bf16[512,256]{1,0:T(8,128)(2,1)S(1)} %copy-done.10, bf16[256,1792]{1,0:T(8,128)(2,1)S(1)} %add_convert_fusion.refs_1_, f32[2048,1792]{1,0:T(8,128)} %refs_2_.7, ...), custom_call_target="tpu_custom_call" | custom-call | flops 5872025600 | bytes 14680064 | tf_op jit(solution)/shard_map/form/pallas_call | solution.py:98
  127.7 15.2 %form.9 = (bf16[8,512,1792]{2,1,0:T(8,128)(2,1)}, f32[512,128]{1,0:T(8,128)S(1)}) custom-call(s32[3]{0:T(128)S(1)} %pad_add_fusion.place_ref, bf16[512,256]{1,0:T(8,128)(2,1)S(1)} %copy-done.6, bf16[256,1792]{1,0:T(8,128)(2,1)S(1)} %add_convert_fusion.refs_1_, f32[2048,1792]{1,0:T(8,128)} %refs_2_.7, ...), custom_call_target="tpu_custom_call" | custom-call | flops 5872025600 | bytes 14680064 | tf_op jit(solution)/shard_map/form/pallas_call | solution.py:98
  147.2 14.7 %form.10 = (bf16[8,512,1792]{2,1,0:T(8,128)(2,1)}, bf16[512,128]{1,0:T(8,128)(2,1)S(1)}) custom-call(s32[3]{0:T(128)S(1)} %pad_add_fusion.place_ref, bf16[512,256]{1,0:T(8,128)(2,1)S(1)} %collective-permute-done.22.refs_0_, bf16[256,1792]{1,0:T(8,128)(2,1)S(1)} %add_convert_fusion.refs_1_, f32[2048,1792]{1,0:T(8,128)} %refs_2_.7, ...), custom_call_target="tpu_custom_call" | custom-call | flops 5872025600 | bytes 14680064 | tf_op jit(solution)/shard_map/form/pallas_call | solution.py:98
  164.1 15.0 %form.11 = (bf16[8,512,1792]{2,1,0:T(8,128)(2,1)}, f32[512,128]{1,0:T(8,128)S(1)}) custom-call(s32[3]{0:T(128)S(1)} %pad_add_fusion.place_ref, bf16[512,256]{1,0:T(8,128)(2,1)S(1)} %add_convert_fusion.3.refs_0_, bf16[256,1792]{1,0:T(8,128)(2,1)S(1)} %add_convert_fusion.refs_1_, f32[2048,1792]{1,0:T(8,128)} %refs_2_.7, ...), custom_call_target="tpu_custom_call" | custom-call | flops 5872025600 | bytes 14680064 | tf_op jit(solution)/shard_map/form/pallas_call | solution.py:98
  182.2 14.8 %form.12 = (bf16[8,512,1792]{2,1,0:T(8,128)(2,1)}, bf16[512,128]{1,0:T(8,128)(2,1)S(1)}) custom-call(s32[3]{0:T(128)S(1)} %pad_add_fusion.place_ref, bf16[512,256]{1,0:T(8,128)(2,1)S(1)} %collective-permute-done.26.refs_0_, bf16[256,1792]{1,0:T(8,128)(2,1)S(1)} %add_convert_fusion.refs_1_, f32[2048,1792]{1,0:T(8,128)} %collective-permute-done.19.refs_2_, ...), custom_call_target="tpu_custom_call" | custom-call | flops 5872025600 | bytes 14680064 | tf_op jit(solution)/shard_map/form/pallas_call | solution.py:98
  198.3 15.1 %form.13 = (bf16[8,512,1792]{2,1,0:T(8,128)(2,1)}, f32[512,128]{1,0:T(8,128)S(1)}) custom-call(s32[3]{0:T(128)S(1)} %pad_add_fusion.place_ref, bf16[512,256]{1,0:T(8,128)(2,1)S(1)} %add_convert_fusion.2.refs_4_.refs_0_, bf16[256,1792]{1,0:T(8,128)(2,1)S(1)} %add_convert_fusion.refs_1_, f32[2048,1792]{1,0:T(8,128)} %collective-permute-done.19.refs_2_, ...), custom_call_target="tpu_custom_call" | custom-call | flops 5872025600 | bytes 14680064 | tf_op jit(solution)/shard_map/form/pallas_call | solution.py:98
  216.5 14.7 %form.14 = (bf16[8,512,1792]{2,1,0:T(8,128)(2,1)}, bf16[512,128]{1,0:T(8,128)(2,1)S(1)}) custom-call(s32[3]{0:T(128)S(1)} %pad_add_fusion.place_ref, bf16[512,256]{1,0:T(8,128)(2,1)S(1)} %collective-permute-done.30.refs_0_, bf16[256,1792]{1,0:T(8,128)(2,1)S(1)} %add_convert_fusion.refs_1_, f32[2048,1792]{1,0:T(8,128)} %collective-permute-done.19.refs_2_, ...), custom_call_target="tpu_custom_call" | custom-call | flops 5872025600 | bytes 14680064 | tf_op jit(solution)/shard_map/form/pallas_call | solution.py:98
  233.4 15.2 %form.15 = (bf16[8,512,1792]{2,1,0:T(8,128)(2,1)}, f32[512,128]{1,0:T(8,128)S(1)}) custom-call(s32[3]{0:T(128)S(1)} %pad_add_fusion.place_ref, bf16[512,256]{1,0:T(8,128)(2,1)S(1)} %add_convert_fusion.1.refs_4_.refs_0_, bf16[256,1792]{1,0:T(8,128)(2,1)S(1)} %add_convert_fusion.refs_1_, f32[2048,1792]{1,0:T(8,128)} %collective-permute-done.19.refs_2_, ...), custom_call_target="tpu_custom_call" | custom-call | flops 5872025600 | bytes 14680064 | tf_op jit(solution)/shard_map/form/pallas_call | solution.py:98
  274.7 6.7 %returned.19 = (f32[128,1792]{1,0:T(8,128)S(1)}, bf16[128,1792]{1,0:T(8,128)(2,1)}) custom-call(bf16[512,128]{1,0:T(8,128)(2,1)S(1)} %add_convert_fusion.16.refs_4_.refs_1_.refs_0_, bf16[8,512,1792]{2,1,0:T(8,128)(2,1)} %get-tuple-element.173.refs_1_.rotated_ref, f32[128,1792]{1,0:T(8,128)S(1)} %get-tuple-element.179.refs_2_, ...), custom_call_target="tpu_custom_call" | custom-call | flops 3758096384 | bytes 14680064 | tf_op jit(solution)/shard_map/returned/pallas_call | solution.py:229
  281.4 6.7 %returned.20 = (f32[128,1792]{1,0:T(8,128)S(1)}, bf16[128,1792]{1,0:T(8,128)(2,1)}) custom-call(bf16[512,128]{1,0:T(8,128)(2,1)S(1)} %collective-permute-done.36.refs_0_, bf16[8,512,1792]{2,1,0:T(8,128)(2,1)} %get-tuple-element.172.refs_1_.rotated_ref, f32[128,1792]{1,0:T(8,128)S(1)} %get-tuple-element.180.refs_2_), custom_call_target="tpu_custom_call" | custom-call | flops 3758096384 | bytes 14680064 | tf_op jit(solution)/shard_map/returned/pallas_call | solution.py:229
  288.1 6.7 %returned.21 = (f32[128,1792]{1,0:T(8,128)S(1)}, bf16[128,1792]{1,0:T(8,128)(2,1)}) custom-call(bf16[512,128]{1,0:T(8,128)(2,1)S(1)} %add_convert_fusion.15.refs_2_.refs_0_, bf16[8,512,1792]{2,1,0:T(8,128)(2,1)} %get-tuple-element.171.refs_1_.rotated_ref, f32[128,1792]{1,0:T(8,128)S(1)} %get-tuple-element.181.refs_2_), custom_call_target="tpu_custom_call" | custom-call | flops 3758096384 | bytes 14680064 | tf_op jit(solution)/shard_map/returned/pallas_call | solution.py:229
  294.8 6.7 %returned.22 = (f32[128,1792]{1,0:T(8,128)S(1)}, bf16[128,1792]{1,0:T(8,128)(2,1)}) custom-call(bf16[512,128]{1,0:T(8,128)(2,1)S(1)} %collective-permute-done.35.refs_0_, bf16[8,512,1792]{2,1,0:T(8,128)(2,1)} %get-tuple-element.170.refs_1_.rotated_ref, f32[128,1792]{1,0:T(8,128)S(1)} %get-tuple-element.182.refs_2_), custom_call_target="tpu_custom_call" | custom-call | flops 3758096384 | bytes 14680064 | tf_op jit(solution)/shard_map/returned/pallas_call | solution.py:229
  309.6 7.2 %collective-permute-done.41.gram_got_ref = f32[128,128]{1,0:T(8,128)S(1)} collective-permute-done((f32[128,128]{1,0:T(8,128)S(1)}, f32[128,128]{1,0:T(8,128)S(1)}, u32[]{:S(2)}, u32[]{:S(2)}) %collective-permute-start.41) | collective-permute-done | bytes 65568 | tf_op jit(solution)/shard_map/ppermute | solution.py:690
  319.2 7.7 %image.9 = bf16[512,128]{1,0:T(8,128)(2,1)S(1)} custom-call(bf16[1792,128]{1,0:T(8,128)(2,1)S(1)} %normalize.2.basis_ref, bf16[8,512,1792]{2,1,0:T(8,128)(2,1)} %get-tuple-element.176.refs_1_.rotated_ref), custom_call_target="tpu_custom_call" | custom-call | flops 3758096384 | bytes 14680064 | tf_op jit(solution)/shard_map/image/pallas_call | solution.py:186
  328.1 7.7 %image.8 = f32[512,128]{1,0:T(8,128)S(1)} custom-call(bf16[1792,128]{1,0:T(8,128)(2,1)S(1)} %normalize.2.basis_ref, bf16[8,512,1792]{2,1,0:T(8,128)(2,1)} %get-tuple-element.175.refs_1_.rotated_ref), custom_call_target="tpu_custom_call" | custom-call | flops 3758096384 | bytes 14680064 | tf_op jit(solution)/shard_map/image/pallas_call | solution.py:186
  337.2 7.7 %image.10 = bf16[512,128]{1,0:T(8,128)(2,1)S(1)} custom-call(bf16[1792,128]{1,0:T(8,128)(2,1)S(1)} %normalize.2.basis_ref, bf16[8,512,1792]{2,1,0:T(8,128)(2,1)} %get-tuple-element.174.refs_1_.rotated_ref, bf16[512,128]{1,0:T(8,128)(2,1)S(1)} %fusion.18.refs_0_), custom_call_target="tpu_custom_call" | custom-call | flops 3758096384 | bytes 14680064 | tf_op jit(solution)/shard_map/image/pallas_call | solution.py:186
  347.6 7.7 %image.11 = f32[512,128]{1,0:T(8,128)S(1)} custom-call(bf16[1792,128]{1,0:T(8,128)(2,1)S(1)} %normalize.2.basis_ref, bf16[8,512,1792]{2,1,0:T(8,128)(2,1)} %get-tuple-element.173.refs_1_.rotated_ref, bf16[512,128]{1,0:T(8,128)(2,1)S(1)} %fusion.26.refs_0_), custom_call_target="tpu_custom_call" | custom-call | flops 3758096384 | bytes 14680064 | tf_op jit(solution)/shard_map/image/pallas_call | solution.py:186
  357.5 7.7 %image.12 = bf16[512,128]{1,0:T(8,128)(2,1)S(1)} custom-call(bf16[1792,128]{1,0:T(8,128)(2,1)S(1)} %normalize.2.basis_ref, bf16[8,512,1792]{2,1,0:T(8,128)(2,1)} %get-tuple-element.172.refs_1_.rotated_ref, bf16[512,128]{1,0:T(8,128)(2,1)S(1)} %add_convert_fusion.13.refs_0_.refs_1_, bf16[512,128]{1,0:T(8,128)(2,1)S(1)} %fusion.19.refs_1_), custom_call_target="tpu_custom_call" | custom-call | flops 3758096384 | bytes 14680064 | tf_op jit(solution)/shard_map/image/pallas_call | solution.py:186
  366.6 7.7 %image.13 = f32[512,128]{1,0:T(8,128)S(1)} custom-call(bf16[1792,128]{1,0:T(8,128)(2,1)S(1)} %normalize.2.basis_ref, bf16[8,512,1792]{2,1,0:T(8,128)(2,1)} %get-tuple-element.171.refs_1_.rotated_ref, bf16[512,128]{1,0:T(8,128)(2,1)S(1)} %fusion.27.refs_0_), custom_call_target="tpu_custom_call" | custom-call | flops 3758096384 | bytes 14680064 | tf_op jit(solution)/shard_map/image/pallas_call | solution.py:186
  375.8 7.7 %image.14 = bf16[512,128]{1,0:T(8,128)(2,1)S(1)} custom-call(bf16[1792,128]{1,0:T(8,128)(2,1)S(1)} %normalize.2.basis_ref, bf16[8,512,1792]{2,1,0:T(8,128)(2,1)} %get-tuple-element.170.refs_1_.rotated_ref, bf16[512,128]{1,0:T(8,128)(2,1)S(1)} %add_convert_fusion.12.refs_0_.refs_1_.refs_3_, bf16[512,128]{1,0:T(8,128)(2,1)S(1)} %fusion.20.refs_1_), custom_call_target="tpu_custom_call" | custom-call | flops 3758096384 | bytes 14680064 | tf_op jit(solution)/shard_map/image/pallas_call | solution.py:186
  386.2 7.9 %image.15 = f32[512,128]{1,0:T(8,128)S(1)} custom-call(bf16[1792,128]{1,0:T(8,128)(2,1)S(1)} %normalize.2.basis_ref, bf16[8,512,1792]{2,1,0:T(8,128)(2,1)} %get-tuple-element.169.refs_1_.rotated_ref, bf16[512,128]{1,0:T(8,128)(2,1)S(1)} %fusion.28.refs_0_), custom_call_target="tpu_custom_call" | custom-call | flops 3758096384 | bytes 14680064 | tf_op jit(solution)/shard_map/image/pallas_call | solution.py:186
  436.7 6.9 %returned.28 = (f32[128,1792]{1,0:T(8,128)S(1)}, bf16[128,1792]{1,0:T(8,128)(2,1)}) custom-call(bf16[512,128]{1,0:T(8,128)(2,1)S(1)} %collective-permute-done.58.refs_4_.refs_0_, bf16[8,512,1792]{2,1,0:T(8,128)(2,1)} %get-tuple-element.172.refs_1_.rotated_ref, f32[128,1792]{1,0:T(8,128)S(1)} %get-tuple-element.204.refs_2_, ...), custom_call_target="tpu_custom_call" | custom-call | flops 3758096384 | bytes 14680064 | tf_op jit(solution)/shard_map/returned/pallas_call | solution.py:229
  454.3 6.7 %returned.30 = (f32[128,1792]{1,0:T(8,128)S(1)}, bf16[128,1792]{1,0:T(8,128)(2,1)}) custom-call(bf16[512,128]{1,0:T(8,128)(2,1)S(1)} %collective-permute-done.59.refs_6_.refs_0_, bf16[8,512,1792]{2,1,0:T(8,128)(2,1)} %get-tuple-element.170.refs_1_.rotated_ref, f32[128,1792]{1,0:T(8,128)S(1)} %get-tuple-element.206.refs_2_, ...), custom_call_target="tpu_custom_call" | custom-call | flops 3758096384 | bytes 14680064 | tf_op jit(solution)/shard_map/returned/pallas_call | solution.py:229
  467.9 12.3 %collective-permute-done.64.got_ref = bf16[128,1792]{1,0:T(8,128)(2,1)S(1)} collective-permute-done((bf16[128,1792]{1,0:T(8,128)(2,1)S(1)}, bf16[128,1792]{1,0:T(8,128)(2,1)S(1)}, u32[]{:S(2)}, u32[]{:S(2)}) %collective-permute-start.64) | collective-permute-done | bytes 458784 | tf_op jit(solution)/shard_map/ppermute | solution.py:675
  483.0 10.0 %factor_in.1 = (bf16[448,256]{1,0:T(8,128)(2,1)S(1)}, f32[448,256]{1,0:T(8,128)S(1)}, bf16[448,256]{1,0:T(8,128)(2,1)S(1)}, f32[448,256]{1,0:T(8,128)S(1)}, bf16...) custom-call(s32[3]{0:T(128)S(1)} %pad_add_fusion.place_ref, ...), custom_call_target="tpu_custom_call" | custom-call | tf_op jit(solution)/shard_map/factor_in/pallas_call | solution.py:362
  513.5 13.4 %collective-permute-done.68 = bf16[448,256]{1,0:T(8,128)(2,1)} collective-permute-done((bf16[448,256]{1,0:T(8,128)(2,1)}, bf16[448,256]{1,0:T(8,128)(2,1)}, u32[]{:S(2)}, u32[]{:S(2)}) %collective-permute-start.68) | collective-permute-done | bytes 229408 | tf_op jit(solution)/shard_map/ppermute | solution.py:585
  528.4 9.7 %collective-permute-done.69 = bf16[224,256]{1,0:T(8,128)(2,1)S(1)} collective-permute-done((bf16[224,256]{1,0:T(8,128)(2,1)S(1)}, bf16[224,256]{1,0:T(8,128)(2,1)S(1)}, u32[]{:S(2)}, u32[]{:S(2)}) %collective-permute-start.69) | collective-permute-done | bytes 114720 | tf_op jit(solution)/shard_map/ppermute | solution.py:597
  (301 shorter events, 282.6 us)
Async XLA Ops:
  33.6 22.1 %collective-permute-start.17 = (bf16[256,1792]{1,0:T(8,128)(2,1)S(1)}, bf16[256,1792]{1,0:T(8,128)(2,1)S(1)}, u32[]{:S(2)}, u32[]{:S(2)}) collective-permute-start(bf16[256,1792]{1,0:T(8,128)(2,1)S(1)} %get-tuple-element.245), channel_id=1, source_target_pairs={{0,2},{1,3},{2,0},{3,1},{4,6},{5,7},{6,4},{7,5},{8,10},{9,11},{10,... | collective-permute-start | bytes 2752520 | tf_op jit(solution)/shard_map/ppermute | solution.py:675
  61.7 120.5 %collective-permute-start.19 = (f32[2048,1792]{1,0:T(8,128)}, f32[2048,1792]{1,0:T(8,128)}, u32[]{:S(2)}, u32[]{:S(2)}) collective-permute-start(f32[2048,1792]{1,0:T(8,128)} %refs_2_.7), channel_id=1, source_target_pairs={{0,1},{1,0},{2,3},{3,2},{4,5},{5,4},{6,7},{7,6},{8,9},{9,8},{10,11... | collective-permute-start | bytes 44040200 | tf_op jit(solution)/shard_map/ppermute | solution.py:562
  62.9 25.6 %collective-permute-start.1 = (bf16[512,256]{1,0:T(8,128)(2,1)}, bf16[512,256]{1,0:T(8,128)(2,1)}, u32[]{:S(2)}, u32[]{:S(2)}) collective-permute-start(bf16[512,256]{1,0:T(8,128)(2,1)} %get-tuple-element.125), channel_id=1, source_target_pairs={{0,1},{1,0},{2,3},{3,2},{4,5},{5,4},{6,7},{7,6},{8,9},{9,8},{10,11... | collective-permute-start | bytes 786440 | tf_op jit(solution)/shard_map/ppermute | solution.py:562
  63.1 21.8 %collective-permute-start.8 = (bf16[512,256]{1,0:T(8,128)(2,1)}, bf16[512,256]{1,0:T(8,128)(2,1)}, u32[]{:S(2)}, u32[]{:S(2)}) collective-permute-start(bf16[512,256]{1,0:T(8,128)(2,1)} %get-tuple-element.140), channel_id=1, source_target_pairs={{0,1},{1,0},{2,3},{3,2},{4,5},{5,4},{6,7},{7,6},{8,9},{9,8},{10,11... | collective-permute-start | bytes 786440 | tf_op jit(solution)/shard_map/ppermute | solution.py:562
  63.4 25.0 %collective-permute-start.12 = (bf16[512,256]{1,0:T(8,128)(2,1)}, bf16[512,256]{1,0:T(8,128)(2,1)}, u32[]{:S(2)}, u32[]{:S(2)}) collective-permute-start(bf16[512,256]{1,0:T(8,128)(2,1)} %get-tuple-element.145), channel_id=1, source_target_pairs={{0,1},{1,0},{2,3},{3,2},{4,5},{5,4},{6,7},{7,6},{8,9},{9,8},{10,11... | collective-permute-start | bytes 786440 | tf_op jit(solution)/shard_map/ppermute | solution.py:562
  88.4 19.5 %collective-permute-start = (bf16[512,256]{1,0:T(8,128)(2,1)}, bf16[512,256]{1,0:T(8,128)(2,1)S(1)}, u32[]{:S(2)}, u32[]{:S(2)}) collective-permute-start(bf16[512,256]{1,0:T(8,128)(2,1)} %copy-done.8), channel_id=1, source_target_pairs={{0,1},{1,0},{2,3},{3,2},{4,5},{5,4},{6,7},{7,6},{8,9},{9,8},{10,11... | collective-permute-start | bytes 786440 | tf_op jit(solution)/shard_map/ppermute | solution.py:562
  88.5 19.4 %collective-permute-start.13 = (bf16[512,256]{1,0:T(8,128)(2,1)}, bf16[512,256]{1,0:T(8,128)(2,1)S(1)}, u32[]{:S(2)}, u32[]{:S(2)}) collective-permute-start(bf16[512,256]{1,0:T(8,128)(2,1)} %collective-permute-done.12), channel_id=1, source_target_pairs={{0,4},{4,0},{1,5},{5,1},{2,6},{6,2},{3,7},{7,3},{8,12},{12,8},{9,1... | collective-permute-start | bytes 786440 | tf_op jit(solution)/shard_map/ppermute | solution.py:585
  103.2 44.1 %collective-permute-start.22 = (bf16[512,256]{1,0:T(8,128)(2,1)S(1)}, bf16[512,256]{1,0:T(8,128)(2,1)S(1)}, u32[]{:S(2)}, u32[]{:S(2)}) collective-permute-start(bf16[512,256]{1,0:T(8,128)(2,1)S(1)} %add_convert_fusion.3.refs_0_), channel_id=1, source_target_pairs={{0,4},{4,0},{1,5},{5,1},{2,6},{6,2},{3,7},{7,3},{8,12},{12,8},{9,1... | collective-permute-start | bytes 786440 | tf_op jit(solution)/shard_map/ppermute | solution.py:611
  106.7 19.5 %collective-permute-start.15 = (bf16[512,256]{1,0:T(8,128)(2,1)S(1)}, bf16[512,256]{1,0:T(8,128)(2,1)S(1)}, u32[]{:S(2)}, u32[]{:S(2)}) collective-permute-start(bf16[512,256]{1,0:T(8,128)(2,1)S(1)} %fusion.10), channel_id=1, source_target_pairs={{0,16},{8,24},{16,0},{24,8},{1,17},{9,25},{17,1},{25,9},{2,18},{10... | collective-permute-start | bytes 786440 | tf_op jit(solution)/shard_map/ppermute | solution.py:597
  108.0 19.3 %collective-permute-start.14 = (bf16[512,256]{1,0:T(8,128)(2,1)S(1)}, bf16[512,256]{1,0:T(8,128)(2,1)S(1)}, u32[]{:S(2)}, u32[]{:S(2)}) collective-permute-start(bf16[512,256]{1,0:T(8,128)(2,1)S(1)} %fusion.7), channel_id=1, source_target_pairs={{0,8},{8,0},{16,24},{24,16},{1,9},{9,1},{17,25},{25,17},{2,10},{10... | collective-permute-start | bytes 786440 | tf_op jit(solution)/shard_map/ppermute | solution.py:597
  125.4 19.8 %collective-permute-start.20 = (bf16[512,128]{1,0:T(8,128)(2,1)S(1)}, bf16[512,128]{1,0:T(8,128)(2,1)S(1)}, u32[]{:S(2)}, u32[]{:S(2)}) collective-permute-start(bf16[512,128]{1,0:T(8,128)(2,1)S(1)} %get-tuple-element.147), channel_id=1, source_target_pairs={{0,4},{4,0},{1,5},{5,1},{2,6},{6,2},{3,7},{7,3},{8,12},{12,8},{9,1... | collective-permute-start | bytes 393224 | tf_op jit(solution)/shard_map/ppermute | solution.py:585
  142.9 39.3 %collective-permute-start.26 = (bf16[512,256]{1,0:T(8,128)(2,1)S(1)}, bf16[512,256]{1,0:T(8,128)(2,1)S(1)}, u32[]{:S(2)}, u32[]{:S(2)}) collective-permute-start(bf16[512,256]{1,0:T(8,128)(2,1)S(1)} %add_convert_fusion.2.refs_4_.refs_0_), channel_id=1, source_target_pairs={{0,4},{4,0},{1,5},{5,1},{2,6},{6,2},{3,7},{7,3},{8,12},{12,8},{9,1... | collective-permute-start | bytes 786440 | tf_op jit(solution)/shard_map/ppermute | solution.py:611
  144.1 72.5 %collective-permute-start.30 = (bf16[512,256]{1,0:T(8,128)(2,1)S(1)}, bf16[512,256]{1,0:T(8,128)(2,1)S(1)}, u32[]{:S(2)}, u32[]{:S(2)}) collective-permute-start(bf16[512,256]{1,0:T(8,128)(2,1)S(1)} %add_convert_fusion.1.refs_4_.refs_0_), channel_id=1, source_target_pairs={{0,4},{4,0},{1,5},{5,1},{2,6},{6,2},{3,7},{7,3},{8,12},{12,8},{9,1... | collective-permute-start | bytes 786440 | tf_op jit(solution)/shard_map/ppermute | solution.py:611
  145.2 17.2 %collective-permute-start.21 = (bf16[512,128]{1,0:T(8,128)(2,1)S(1)}, bf16[512,128]{1,0:T(8,128)(2,1)S(1)}, u32[]{:S(2)}, u32[]{:S(2)}) collective-permute-start(bf16[512,128]{1,0:T(8,128)(2,1)S(1)} %fusion.14.refs_5_), channel_id=1, source_target_pairs={{0,8},{8,0},{16,24},{24,16},{1,9},{9,1},{17,25},{25,17},{2,10},{10... | collective-permute-start | bytes 393224 | tf_op jit(solution)/shard_map/ppermute | solution.py:597
  162.0 18.1 %collective-permute-start.24 = (bf16[512,128]{1,0:T(8,128)(2,1)S(1)}, bf16[512,128]{1,0:T(8,128)(2,1)S(1)}, u32[]{:S(2)}, u32[]{:S(2)}) collective-permute-start(bf16[512,128]{1,0:T(8,128)(2,1)S(1)} %get-tuple-element.154), channel_id=1, source_target_pairs={{0,4},{4,0},{1,5},{5,1},{2,6},{6,2},{3,7},{7,3},{8,12},{12,8},{9,1... | collective-permute-start | bytes 393224 | tf_op jit(solution)/shard_map/ppermute | solution.py:585
  179.2 72.5 %collective-permute-start.38 = (bf16[512,128]{1,0:T(8,128)(2,1)S(1)}, bf16[512,128]{1,0:T(8,128)(2,1)S(1)}, u32[]{:S(2)}, u32[]{:S(2)}) collective-permute-start(bf16[512,128]{1,0:T(8,128)(2,1)S(1)} %add_convert_fusion.17.refs_4_.refs_0_), channel_id=1, source_target_pairs={{0,4},{4,0},{1,5},{5,1},{2,6},{6,2},{3,7},{7,3},{8,12},{12,8},{9,1... | collective-permute-start | bytes 393224 | tf_op jit(solution)/shard_map/ppermute | solution.py:611
  180.1 18.0 %collective-permute-start.25 = (bf16[512,128]{1,0:T(8,128)(2,1)S(1)}, bf16[512,128]{1,0:T(8,128)(2,1)S(1)}, u32[]{:S(2)}, u32[]{:S(2)}) collective-permute-start(bf16[512,128]{1,0:T(8,128)(2,1)S(1)} %fusion.15.refs_5_), channel_id=1, source_target_pairs={{0,8},{8,0},{16,24},{24,16},{1,9},{9,1},{17,25},{25,17},{2,10},{10... | collective-permute-start | bytes 393224 | tf_op jit(solution)/shard_map/ppermute | solution.py:597
  196.9 17.5 %collective-permute-start.28 = (bf16[512,128]{1,0:T(8,128)(2,1)S(1)}, bf16[512,128]{1,0:T(8,128)(2,1)S(1)}, u32[]{:S(2)}, u32[]{:S(2)}) collective-permute-start(bf16[512,128]{1,0:T(8,128)(2,1)S(1)} %get-tuple-element.159), channel_id=1, source_target_pairs={{0,4},{4,0},{1,5},{5,1},{2,6},{6,2},{3,7},{7,3},{8,12},{12,8},{9,1... | collective-permute-start | bytes 393224 | tf_op jit(solution)/shard_map/ppermute | solution.py:585
  213.4 54.5 %collective-permute-start.37 = (bf16[512,128]{1,0:T(8,128)(2,1)S(1)}, bf16[512,128]{1,0:T(8,128)(2,1)S(1)}, u32[]{:S(2)}, u32[]{:S(2)}) collective-permute-start(bf16[512,128]{1,0:T(8,128)(2,1)S(1)} %add_convert_fusion.16.refs_4_.refs_1_.refs_0_), channel_id=1, source_target_pairs={{0,4},{4,0},{1,5},{5,1},{2,6},{6,2},{3,7},{7,3},{8,12},{12,8},{9,1... | collective-permute-start | bytes 393224 | tf_op jit(solution)/shard_map/ppermute | solution.py:611
  214.5 17.2 %collective-permute-start.29 = (bf16[512,128]{1,0:T(8,128)(2,1)S(1)}, bf16[512,128]{1,0:T(8,128)(2,1)S(1)}, u32[]{:S(2)}, u32[]{:S(2)}) collective-permute-start(bf16[512,128]{1,0:T(8,128)(2,1)S(1)} %fusion.16.refs_5_), channel_id=1, source_target_pairs={{0,8},{8,0},{16,24},{24,16},{1,9},{9,1},{17,25},{25,17},{2,10},{10... | collective-permute-start | bytes 393224 | tf_op jit(solution)/shard_map/ppermute | solution.py:597
  231.3 18.2 %collective-permute-start.32 = (bf16[512,128]{1,0:T(8,128)(2,1)S(1)}, bf16[512,128]{1,0:T(8,128)(2,1)S(1)}, u32[]{:S(2)}, u32[]{:S(2)}) collective-permute-start(bf16[512,128]{1,0:T(8,128)(2,1)S(1)} %get-tuple-element.164), channel_id=1, source_target_pairs={{0,4},{4,0},{1,5},{5,1},{2,6},{6,2},{3,7},{7,3},{8,12},{12,8},{9,1... | collective-permute-start | bytes 393224 | tf_op jit(solution)/shard_map/ppermute | solution.py:585
  248.6 32.8 %collective-permute-start.36 = (bf16[512,128]{1,0:T(8,128)(2,1)S(1)}, bf16[512,128]{1,0:T(8,128)(2,1)S(1)}, u32[]{:S(2)}, u32[]{:S(2)}) collective-permute-start(bf16[512,128]{1,0:T(8,128)(2,1)S(1)} %add_convert_fusion.15.refs_2_.refs_0_), channel_id=1, source_target_pairs={{0,4},{4,0},{1,5},{5,1},{2,6},{6,2},{3,7},{7,3},{8,12},{12,8},{9,1... | collective-permute-start | bytes 393224 | tf_op jit(solution)/shard_map/ppermute | solution.py:611
  265.8 29.0 %collective-permute-start.35 = (bf16[512,128]{1,0:T(8,128)(2,1)S(1)}, bf16[512,128]{1,0:T(8,128)(2,1)S(1)}, u32[]{:S(2)}, u32[]{:S(2)}) collective-permute-start(bf16[512,128]{1,0:T(8,128)(2,1)S(1)} %add_convert_fusion.14.refs_3_.refs_0_), channel_id=1, source_target_pairs={{0,4},{4,0},{1,5},{5,1},{2,6},{6,2},{3,7},{7,3},{8,12},{12,8},{9,1... | collective-permute-start | bytes 393224 | tf_op jit(solution)/shard_map/ppermute | solution.py:611
  397.5 21.8 %collective-permute-start.57 = (bf16[512,128]{1,0:T(8,128)(2,1)S(1)}, bf16[512,128]{1,0:T(8,128)(2,1)S(1)}, u32[]{:S(2)}, u32[]{:S(2)}) collective-permute-start(bf16[512,128]{1,0:T(8,128)(2,1)S(1)} %add_convert_fusion.12.refs_0_.refs_1_.refs_3_), channel_id=1, source_target_pairs={{0,4},{4,0},{1,5},{5,1},{2,6},{6,2},{3,7},{7,3},{8,12},{12,8},{9,1... | collective-permute-start | bytes 393224 | tf_op jit(solution)/shard_map/ppermute | solution.py:611
  398.3 29.2 %collective-permute-start.58 = (bf16[512,128]{1,0:T(8,128)(2,1)S(1)}, bf16[512,128]{1,0:T(8,128)(2,1)S(1)}, u32[]{:S(2)}, u32[]{:S(2)}) collective-permute-start(bf16[512,128]{1,0:T(8,128)(2,1)S(1)} %add_convert_fusion.11.refs_2_.refs_5_.refs_0_), channel_id=1, source_target_pairs={{0,4},{4,0},{1,5},{5,1},{2,6},{6,2},{3,7},{7,3},{8,12},{12,8},{9,1... | collective-permute-start | bytes 393224 | tf_op jit(solution)/shard_map/ppermute | solution.py:611
  503.3 51.6 %all-to-all-start = ((bf16[8,256,256]{2,1,0:T(8,128)(2,1)}), bf16[8,256,256]{2,1,0:T(8,128)(2,1)}, u32[]{:S(2)}, u32[]{:S(2)}) async-start(bf16[8,256,256]{2,1,0:T(8,128)(2,1)} %broadcast_in_dim.2), calls=%async_computation | async-start | bytes 2097152 | tf_op jit(solution)/shard_map/all_to_all | solution.py:654
  507.6 19.4 %collective-permute-start.68 = (bf16[448,256]{1,0:T(8,128)(2,1)}, bf16[448,256]{1,0:T(8,128)(2,1)}, u32[]{:S(2)}, u32[]{:S(2)}) collective-permute-start(bf16[448,256]{1,0:T(8,128)(2,1)} %copy-done.13), channel_id=1, source_target_pairs={{0,4},{4,0},{1,5},{5,1},{2,6},{6,2},{3,7},{7,3},{8,12},{12,8},{9,1... | collective-permute-start | bytes 688136 | tf_op jit(solution)/shard_map/ppermute | solution.py:585
  510.5 27.5 %collective-permute-start.69 = (bf16[224,256]{1,0:T(8,128)(2,1)S(1)}, bf16[224,256]{1,0:T(8,128)(2,1)S(1)}, u32[]{:S(2)}, u32[]{:S(2)}) collective-permute-start(bf16[224,256]{1,0:T(8,128)(2,1)S(1)} %add_convert_fusion.25), channel_id=1, source_target_pairs={{0,16},{8,24},{16,0},{24,8},{1,17},{9,25},{17,1},{25,9},{2,18},{10... | collective-permute-start | bytes 344072 | tf_op jit(solution)/shard_map/ppermute | solution.py:597
  513.0 29.2 %collective-permute-start.72 = (bf16[448,256]{1,0:T(8,128)(2,1)}, bf16[448,256]{1,0:T(8,128)(2,1)S(1)}, u32[]{:S(2)}, u32[]{:S(2)}) collective-permute-start(bf16[448,256]{1,0:T(8,128)(2,1)} %copy-done.12), channel_id=1, source_target_pairs={{0,4},{4,0},{1,5},{5,1},{2,6},{6,2},{3,7},{7,3},{8,12},{12,8},{9,1... | collective-permute-start | bytes 688136 | tf_op jit(solution)/shard_map/ppermute | solution.py:585
  554.9 19.0 %all-to-all-start.1 = ((bf16[4,512,256]{2,1,0:T(8,128)(2,1)}), bf16[4,512,256]{2,1,0:T(8,128)(2,1)}, u32[]{:S(2)}, u32[]{:S(2)}) async-start(bf16[4,512,256]{2,1,0:T(8,128)(2,1)} %bitcast.4), calls=%async_computation.1 | async-start | bytes 2097152 | tf_op jit(solution)/shard_map/all_to_all | solution.py:716
  573.6 17.3 %collective-permute-start.85 = (bf16[448,256]{1,0:T(8,128)(2,1)S(1)}, bf16[448,256]{1,0:T(8,128)(2,1)}, u32[]{:S(2)}, u32[]{:S(2)}) collective-permute-start(bf16[448,256]{1,0:T(8,128)(2,1)S(1)} %maximum_select_fusion.3.refs_7_), channel_id=1, source_target_pairs={{0,4},{4,0},{1,5},{5,1},{2,6},{6,2},{3,7},{7,3},{8,12},{12,8},{9,1... | collective-permute-start | bytes 688136 | tf_op jit(solution)/shard_map/ppermute | solution.py:611
  577.7 21.1 %all-to-all-start.2 = ((bf16[4,128,256]{1,2,0:T(8,128)(2,1)}), bf16[4,128,256]{1,2,0:T(8,128)(2,1)}, u32[]{:S(2)}, u32[]{:S(2)}) async-start(bf16[4,128,256]{1,2,0:T(8,128)(2,1)} %bitcast.23), calls=%async_computation.2 | async-start | bytes 524288 | tf_op jit(solution)/shard_map/all_to_all | solution.py:647
  (78 other events, 1361.1 us)

commit v8 on v7

--- a/solution.py
+++ b/solution.py
@@ -18,8 +18,7 @@
 LANES = 256
 PIECES = 2
 BLOCK = 4
-IMAGE_BLOCK = 2
-FACTOR_PIECES = 4
+FACTOR_PIECES = 2
 
 damping = 0.01
 ridge_scale = 1e-06
@@ -48,10 +47,50 @@
     return [pl.BlockSpec(memory_space=pl.ANY)] * len(ties)
 
 
-def form_kernel(n_parts, n_ties, place_ref, *refs):
+def write_image(image, n_keep, refs):
+    part = pl.program_id(0)
+    done = pl.program_id(1) == pl.num_programs(1) - 1
+
+    if n_keep:
+
+        @pl.when(done & (part == 0))
+        def _():
+            refs[0][...] = image[...]
+
+    if len(refs) > n_keep:
+
+        @pl.when(done & (part >= n_keep))
+        def _():
+            refs[-1][...] = image[...].astype(bf16)
+
+
+def image_outputs(n_keep, n_send, rows):
+    shapes, specs = [], []
+    if n_keep:
+        shapes.append(jax.ShapeDtypeStruct((rows, COLS), f32))
+        specs.append(pl.BlockSpec((rows, COLS), lambda part, query, *_: (0, 0)))
+    if n_send:
+        shapes.append(jax.ShapeDtypeStruct((n_send * rows, COLS), bf16))
+        specs.append(
+            pl.BlockSpec(
+                (rows, COLS), lambda part, query, *_: (jnp.maximum(part - n_keep, 0), 0)
+            )
+        )
+    return shapes, specs
+
+
+def add_images(product, first, rows, image):
+    lane = lax.broadcasted_iota(jnp.int32, (rows, COLS), 1) // RANK
+    for at in range(BLOCK):
+        image[...] = jnp.where(
+            lane == first + at, product[at * rows : (at + 1) * rows], image[...]
+        )
+
+
+def form_kernel(n_keep, n_parts, n_ties, place_ref, *refs):
     out_refs = refs[:n_parts]
     in_ref, eig_ref, basis_ref = refs[n_parts : n_parts + 3]
-    rotated_ref, image_ref, weight, left, image = refs[n_parts + 3 + n_ties :]
+    rotated_ref, *image_refs, weight, left, image = refs[n_parts + 3 + n_ties :]
     part, first = pl.program_id(0), pl.program_id(1) * BLOCK
     rows, cols = eig_ref.shape
 
@@ -66,7 +105,6 @@
             for query in range(NG):
                 left[query] = out_refs[at][:, query * QTOK : (query + 1) * QTOK]
 
-    lane = lax.broadcasted_iota(jnp.int32, (rows, COLS), 1) // RANK
     for at in range(BLOCK):
         query = first + at
         own = left[query]
@@ -75,28 +113,30 @@
             span = slice(begin, begin + width)
             block = jnp.dot(own, right[:, span], preferred_element_type=f32)
             rotated_ref[at, :, span] = (block * weight[:, span]).astype(bf16)
-        product = jnp.dot(rotated_ref[at], basis_ref[...], preferred_element_type=f32)
-        image[...] = jnp.where(lane == query, product, image[...])
-
-    @pl.when(first == NG - BLOCK)
-    def _():
-        image_ref[...] = image[...].astype(image_ref.dtype)
-
-
-def form_parts(place, out_parts, rot_in, eigvals, basis, at, n_dp, kind, ties):
-    n_parts = len(out_parts)
-    rows = out_parts[0].shape[0]
+    product = jnp.dot(
+        rotated_ref[...].reshape(BLOCK * rows, cols), basis_ref[...], preferred_element_type=f32
+    )
+    add_images(product, first, rows, image)
+    write_image(image, n_keep, image_refs)
+
+
+def form_parts(place, kept, sent, pieces, rot_in, eigvals, basis, n_dp, ties):
+    n_keep, n_parts = len(kept), len(kept) + len(sent)
+    rows = (kept + sent)[0].shape[0]
     cols = rot_in.shape[1]
+    keep_piece, send_piece = pieces
 
     def eig_block(part, query, place_ref):
-        return at // n_dp * n_dp + lax.rem(place_ref[0] + 1 + at % n_dp + part, n_dp), 0
+        at = send_piece * n_dp + lax.rem(place_ref[0] + 1 + part + n_dp - n_keep, n_dp)
+        return jnp.where(part < n_keep, keep_piece * n_dp + place_ref[0], at), 0
 
     def fixed(shape):
         return pl.BlockSpec(shape, lambda part, query, _: (0, 0))
 
     shape = (NG, n_parts * rows, cols)
-    return pl.pallas_call(
-        functools.partial(form_kernel, n_parts, len(ties)),
+    shapes, specs = image_outputs(n_keep, len(sent), rows)
+    return pl.pallas_call(
+        functools.partial(form_kernel, n_keep, n_parts, len(ties)),
         grid_spec=pltpu.PrefetchScalarGridSpec(
             num_scalar_prefetch=1,
             grid=(n_parts, NG // BLOCK),
@@ -108,23 +148,20 @@
             ]
             + tied(ties),
             out_specs=[
-                pl.BlockSpec((BLOCK, rows, cols), lambda part, query, _: (query, part, 0)),
-                pl.BlockSpec((rows, COLS), lambda part, query, _: (part, 0)),
-            ],
+                pl.BlockSpec((BLOCK, rows, cols), lambda part, query, _: (query, part, 0))
+            ]
+            + specs,
             scratch_shapes=[
                 pltpu.VMEM((rows, cols), f32),
                 pltpu.VMEM((NG, rows, QTOK), bf16),
                 pltpu.VMEM((rows, COLS), f32),
             ],
         ),
-        out_shape=[
-            jax.ShapeDtypeStruct(shape, bf16),
-            jax.ShapeDtypeStruct((n_parts * rows, COLS), kind),
-        ],
+        out_shape=[jax.ShapeDtypeStruct(shape, bf16)] + shapes,
         compiler_params=params(),
         cost_estimate=cost(shape, 400),
         name="form",
-    )(place, *out_parts, rot_in, eigvals, basis, *ties)
+    )(place, *kept, *sent, rot_in, eigvals, basis, *ties)
 
 
 def stream(rotated_ref, buffers, sems, parts, begin, body):
@@ -163,36 +200,30 @@
     return [pltpu.VMEM((BLOCK, rows, cols), bf16), pltpu.SemaphoreType.DMA((BLOCK,))]
 
 
-def image_kernel(n_ties, basis_ref, rotated_ref, *refs):
-    image_ref, image = refs[n_ties:]
-    count, rows, cols = rotated_ref.shape
-    first = pl.program_id(1) * count
+def image_kernel(n_keep, n_ties, basis_ref, rotated_ref, *refs):
+    *image_refs, image = refs[n_ties:]
+    _, rows, cols = rotated_ref.shape
     product = jnp.dot(
-        rotated_ref[...].reshape(count * rows, cols), basis_ref[...], preferred_element_type=f32
+        rotated_ref[...].reshape(BLOCK * rows, cols), basis_ref[...], preferred_element_type=f32
     )
-    lane = lax.broadcasted_iota(jnp.int32, (rows, COLS), 1) // RANK
-    for at in range(count):
-        image[...] = jnp.where(
-            lane == first + at, product[at * rows : (at + 1) * rows], image[...]
-        )
-
-    @pl.when(first == NG - count)
-    def _():
-        image_ref[...] = image[...].astype(image_ref.dtype)
-
-
-def image_parts(basis, rotated, rows, kind, ties):
-    _, total, cols = rotated.shape
-    return pl.pallas_call(
-        functools.partial(image_kernel, len(ties)),
-        grid=(total // rows, NG // IMAGE_BLOCK),
+    add_images(product, pl.program_id(1) * BLOCK, rows, image)
+    write_image(image, n_keep, image_refs)
+
+
+def image_parts(basis, rotated, n_keep, n_send, ties):
+    _, rows, cols = rotated.shape
+    rows = rows // (n_keep + n_send)
+    shapes, specs = image_outputs(n_keep, n_send, rows)
+    return pl.pallas_call(
+        functools.partial(image_kernel, n_keep, len(ties)),
+        grid=(n_keep + n_send, NG // BLOCK),
         in_specs=[
             pl.BlockSpec((cols, COLS), lambda part, query: (0, 0)),
-            pl.BlockSpec((IMAGE_BLOCK, rows, cols), lambda part, query: (query, part, 0)),
+            pl.BlockSpec((BLOCK, rows, cols), lambda part, query: (query, part, 0)),
         ]
         + tied(ties),
-        out_specs=pl.BlockSpec((rows, COLS), lambda part, query: (part, 0)),
-        out_shape=jax.ShapeDtypeStruct((total, COLS), kind),
+        out_specs=specs,
+        out_shape=shapes,
         scratch_shapes=[pltpu.VMEM((rows, COLS), f32)],
         compiler_params=params(),
         cost_estimate=cost(rotated.shape, 256),
@@ -324,54 +355,52 @@
     )
 
 
-def factor_kernel(n_dp, n_ties, place_ref, eigen_ref, mine_ref, theirs_ref, *refs):
-    *out_refs, cols = refs[n_ties:]
-    step = pl.program_id(0)
-    rows = eigen_ref.shape[0]
-
-    @pl.when(step == 0)
+def factor_kernel(place_ref, eigen_ref, mine_ref, theirs_ref, send_ref, keep_ref, cols):
+    part, parts = pl.program_id(0), pl.num_programs(0)
+
+    @pl.when(part == 0)
     def _():
         cols[...] = side_by_side(place_ref, mine_ref[...], theirs_ref[...])
 
     product = jnp.dot(eigen_ref[...], cols[...], preferred_element_type=f32)
-    for piece in range(FACTOR_PIECES):
-        send_ref, keep_ref = out_refs[2 * piece : 2 * piece + 2]
-        for part in range(n_dp):
-
-            @pl.when(step == piece * n_dp + part)
-            def _(part=part, send_ref=send_ref, keep_ref=keep_ref):
-                if part < n_dp - 1:
-                    send_ref[part * rows : (part + 1) * rows, :] = product.astype(bf16)
-                else:
-                    keep_ref[...] = product
-
-
-def factor_in(place, eigen_in, mine, theirs, n_dp, ties):
+
+    @pl.when(part < parts - 1)
+    def _():
+        send_ref[...] = product.astype(bf16)
+
+    @pl.when(part == parts - 1)
+    def _():
+        keep_ref[...] = product
+
+
+def factor_piece(place, eigen_in, mine, theirs, piece, n_dp):
     rows, depth = eigen_in.shape
     rows = rows // (FACTOR_PIECES * n_dp)
     width = CORES * COLS
-    fixed = pl.BlockSpec((depth, COLS), lambda at, _: (0, 0))
-
-    def eigen_block(at, place_ref):
-        return at // n_dp * n_dp + lax.rem(place_ref[0] + 1 + at % n_dp, n_dp), 0
-
-    shapes = [
-        jax.ShapeDtypeStruct(((n_dp - 1) * rows, width), bf16),
-        jax.ShapeDtypeStruct((rows, width), f32),
-    ] * FACTOR_PIECES
-    return pl.pallas_call(
-        functools.partial(factor_kernel, n_dp, len(ties)),
+    fixed = pl.BlockSpec((depth, COLS), lambda part, _: (0, 0))
+
+    def eigen_block(part, place_ref):
+        return piece * n_dp + lax.rem(place_ref[0] + 1 + part, n_dp), 0
+
+    return pl.pallas_call(
+        factor_kernel,
         grid_spec=pltpu.PrefetchScalarGridSpec(
             num_scalar_prefetch=1,
-            grid=(FACTOR_PIECES * n_dp,),
-            in_specs=[pl.BlockSpec((rows, depth), eigen_block), fixed, fixed] + tied(ties),
-            out_specs=[pl.BlockSpec(each.shape, lambda at, _: (0, 0)) for each in shapes],
+            grid=(n_dp,),
+            in_specs=[pl.BlockSpec((rows, depth), eigen_block), fixed, fixed],
+            out_specs=[
+                pl.BlockSpec((rows, width), lambda part, _: (jnp.minimum(part, n_dp - 2), 0)),
+                pl.BlockSpec((rows, width), lambda part, _: (0, 0)),
+            ],
             scratch_shapes=[pltpu.VMEM((depth, width), bf16)],
         ),
-        out_shape=shapes,
-        compiler_params=params(),
-        name="factor_in",
-    )(place, eigen_in, mine, theirs, *ties)
+        out_shape=[
+            jax.ShapeDtypeStruct(((n_dp - 1) * rows, width), bf16),
+            jax.ShapeDtypeStruct((rows, width), f32),
+        ],
+        compiler_params=params(),
+        name="factor",
+    )(place, eigen_in, mine, theirs)
 
 
 def write_shares(place_ref, total, keep_ref, send_refs):
@@ -589,29 +618,18 @@
         total = after(self.keep, others)
         for part in got:
             total = total + part.astype(f32)
-        step, odd = 1, lax.axis_index("grp") % 2
+        step = 1
         while step < n_grp:
-            if even and step == 2:
-                total = lax.dynamic_slice_in_dim(total, odd * (rows // 2), rows // 2, 0)
             sent = total.astype(bf16)
             got = lax.ppermute(sent, "grp", crossed(n_grp, step))
             others = yield [sent]
             total = (sent.astype(f32) if even else total) + after(got, others).astype(f32)
             step *= 2
-        own = total.astype(bf16)
-        if even and n_grp > 2:
-            got = lax.ppermute(own, "grp", crossed(n_grp, 1))
-            others = yield [own]
-            got = after(got, others)
-            own = jnp.where(
-                odd == 0, jnp.concatenate([own, got]), jnp.concatenate([got, own])
-            )
-        self.own = own
-        parts = [
+        own = self.own = total.astype(bf16)
+        self.parts = [
             lax.ppermute(own, "dp", turned_by(n_dp, n_dp - 1 - at)) for at in range(n_dp - 1)
-        ]
+        ] + [own]
         yield [own]
-        self.parts = parts + [own]
 
 
 class Steps:
@@ -628,10 +646,10 @@
 
 def boundary(others, reductions):
     ties = []
-    for reduction in reductions:
+    for reduction in reversed(reductions):
         if reduction.parts is None and reduction.keep is not None:
             hop = reduction.advance(others)
-            ties += hop
+            ties = hop + ties
             others = hop or others
     return ties
 
@@ -738,78 +756,78 @@
         for at in range(1, count):
             sends, keep = (own_pieces + their_pieces)[2 * at : 2 * at + 2]
             turning.append(Reduction(after(sends, last), n_grp, n_dp, keep=keep))
-            last = boundary(last, turning)[:1] or last
+            if turning[0].parts is None:
+                last = boundary(last, turning)[:1]
         hidden = (jax.nn.silu(gate_pre.astype(f32)) * up_pre.astype(f32)).astype(bf16)
         rot_in = (total_in + got_in.astype(f32)).astype(bf16)
+        eig_sent = after(eigvals, [rot_in, *turning[0].parts])
+        eig_theirs = swap_cores(eig_sent, n_width)
         basis = lax.dynamic_slice_in_dim(start, core * COLS, COLS, 1)
-        rotated, eig_theirs, ties = [], None, [hidden]
+        calls = []
+        for begin in range(0, count, PIECES):
+            span = list(range(begin, begin + PIECES))
+            calls += zip([None] + span, span + [None])
+        rotated, ties = [None] * len(calls), [hidden]
+
+        def parts_of(reductions, pieces):
+            for piece in pieces:
+                while piece is not None and reductions[piece].parts is None:
+                    boundary([], reductions)
+            keep, send = pieces
+            return (
+                [] if keep is None else reductions[keep].parts[-1:],
+                [] if send is None else reductions[send].parts[:-1],
+            )
+
         for iteration in range(ITERS):
             summing = []
             found.clear()
-            for at in range(count):
+            for at, (keep, send) in enumerate(calls):
+                n_keep, n_send = int(keep is not None), (n_dp - 1) * int(send is not None)
                 if iteration == 0:
-                    while turning[at].parts is None:
-                        last = boundary(last, turning) or last
-                    if eig_theirs is None:
-                        eig_sent = after(eigvals, [rot_in, *turning[0].parts])
-                        eig_theirs = swap_cores(eig_sent, n_width)
-                    rotated.append([None, None])
-                for side, kind in ((0, bf16), (1, f32)):
-                    if iteration == 0:
-                        parts = turning[at].parts
-                        block, image = form_parts(
-                            place,
-                            parts[-1:] if side else parts[:-1],
-                            rot_in,
-                            eigvals if at < PIECES else eig_theirs,
-                            basis,
-                            at % PIECES * n_dp + side * (n_dp - 1),
-                            n_dp,
-                            kind,
-                            ties,
-                        )
-                        rotated[at][side] = block
-                    else:
-                        rows = rotated[at][1].shape[1]
-                        image = image_parts(basis, rotated[at][side], rows, kind, ties)
-                    if side:
-                        summing[at].keep = image
-                    last = [image]
-                    ties = boundary(last, turning + summing)
-                    if not side:
-                        summing.append(Reduction(image, n_grp, n_dp))
+                    ours = (keep if send is None else send) < PIECES
+                    rotated[at], *images = form_parts(
+                        place,
+                        *parts_of(turning, (keep, send)),
+                        [0 if each is None else each % PIECES for each in (keep, send)],
+                        rot_in,
+                        eigvals if ours else eig_theirs,
+                        basis,
+                        n_dp,
+                        ties,
+                    )
+                else:
+                    images = image_parts(basis, rotated[at], n_keep, n_send, ties)
+                if n_keep:
+                    summing[keep].keep = images[0]
+                ties = boundary(images[:1], summing + turning)
+                if n_send:
+                    summing.append(Reduction(images[-1], n_grp, n_dp))
             total = path = None
-            for at in range(count):
-                while summing[at].parts is None:
-                    last = boundary(last, summing) or last
-                for side in range(2):
-                    parts = summing[at].parts
-                    total, sent = return_parts(
-                        parts[-1:] if side else parts[:-1], rotated[at][side], total, ties
-                    )
-                    last = [sent]
-                    ties = boundary(last, summing)
-                    if path is None and all(each.own is not None for each in summing):
-                        path = Steps(output_side(summing, iteration == ITERS - 1))
-                    if path is not None and path.count < 5:
-                        ties += path.advance(last)
+            for at, pieces in enumerate(calls):
+                kept, sent = parts_of(summing, pieces)
+                total, rounded = return_parts(kept + sent, rotated[at], total, ties)
+                ties = boundary([rounded], summing)
+                if path is None and all(each.own is not None for each in summing):
+                    path = Steps(output_side(summing, iteration == ITERS - 1))
+                if path is not None and path.count < 5:
+                    ties = ties + path.advance([rounded])
             while "inverse" not in found:
                 path.advance([])
-            total, sent, got = last_hop(total, sent)
+            total, sent, got = last_hop(total, rounded)
             basis = normalize(total, got, found["inverse"], ties)
             ties = []
 
         their_basis = swap_cores(basis, n_width)
-        pieces = factor_in(place, eigen_in, basis, their_basis, n_dp, [])
-        factors, last = [], [pieces[0]]
-        for at in range(FACTOR_PIECES):
-            sends, keep = pieces[2 * at : 2 * at + 2]
-            factors.append(Reduction(after(sends, last[:1]), n_grp, n_dp, True, keep))
-            last = boundary(last, factors)
-            if at % 2:
-                path.advance(last)
+        factors, last = [], []
+        for piece in range(FACTOR_PIECES):
+            sends, keep = factor_piece(place, eigen_in, basis, their_basis, piece, n_dp)
+            if piece:
+                last = boundary([keep], factors)
+            factors.append(Reduction(sends, n_grp, n_dp, True, keep))
+        path.advance(last)
         while any(each.parts is None for each in factors):
-            last = boundary(last, factors) or last
+            last = boundary(last, factors)[:1]
         parts = [part for each in factors for part in each.parts]
         in_factor, keep_in, *sends_in = project(place, hidden, parts, n_dp, n_width)
         while "proj_out" not in found:

time: 609 us -> 583 us (0.957)
  Pallas kernels: 329 us -> 299 us
  waiting for transfers between devices: 134 us -> 151 us
  starting transfers between devices: 108 us -> 96.7 us
    pallas_call x17 -> x14, Pallas kernels: 191 us -> 172 us  [the longest x6 107 us: form_parts(): pl.pallas_call(functools.partial(form_kernel, n_keep, n_parts, len(ties))...]
    ppermute x32 -> x28, waiting for transfers between devices: 42.2 us -> 59 us  [run(): got = lax.ppermute(sent, 'grp', crossed(n_grp, step))]
    ppermute x3, waiting for transfers between devices: 0.01 us -> 14.7 us  [output_side(): lax.ppermute(send, 'width', crossed(n_width, at + 1))]
    pallas_call x16 -> x12, Pallas kernels: 106 us -> 96 us  [return_parts(): pl.pallas_call(functools.partial(return_kernel, n_parts, not before), in_...]
    ppermute x3, waiting for transfers between devices: 12.3 us -> 2.71 us  [last_hop(): got = lax.ppermute(sent, 'width', crossed(n_width, step))]
    ppermute x4 -> x0, waiting for transfers between devices: 6.85 us -> none  [run(): got = lax.ppermute(own, 'grp', crossed(n_grp, 1))]
    ppermute x32 -> x28, starting transfers between devices: 46.3 us -> 39.6 us  [run(): got = lax.ppermute(sent, 'grp', crossed(n_grp, step))]
    ppermute x16 -> x14, starting transfers between devices: 19.8 us -> 15.2 us  [run(): lax.ppermute(sends[at * rows:(at + 1) * rows], 'dp', turned_by(n_dp, at +...]
  transfers between devices with their start and end apart: 92 -> 80, of which waited for: 28 -> 25; matrix products, arithmetic and copies ran while one was open for 3% -> 3% of each run, Pallas kernels for 43% -> 42%
where the time goes in v8:
time: 583 us; the launch traced here: 579 us
  Pallas kernels  299 us (51%)
  waiting for transfers between devices  151 us (26%)
  starting transfers between devices  96.7 us (17%)
  other arithmetic  14.9 us (3%)
  local copies, waits for them, and re-layouts  13.9 us (2%)
    pallas_call x6, Pallas kernels, form_parts(): pl.pallas_call(functools.partial(form_kernel, n_keep, n_parts, len(ties))...  107 us
    pallas_call x12, Pallas kernels, return_parts(): pl.pallas_call(functools.partial(return_kernel, n_parts, not before), in_...  96 us
    ppermute x28, waiting for transfers between devices, run(): got = lax.ppermute(sent, 'grp', crossed(n_grp, step))  59 us
    pallas_call x6, Pallas kernels, image_parts(): pl.pallas_call(functools.partial(image_kernel, n_keep, len(ties)), grid=(...  55.1 us
    ppermute x14, waiting for transfers between devices, run(): lax.ppermute(sends[at * rows:(at + 1) * rows], 'dp', turned_by(n_dp, at +...  39.9 us
    ppermute x28, starting transfers between devices, run(): got = lax.ppermute(sent, 'grp', crossed(n_grp, step))  39.6 us
    ppermute x14, starting transfers between devices, run(): lax.ppermute(sends[at * rows:(at + 1) * rows], 'dp', turned_by(n_dp, at +...  15.2 us
    ppermute x8, waiting for transfers between devices, swap_cores(): return lax.ppermute(part, 'width', crossed(n_width, 1))  15 us
  transfers between devices with their start and end apart: 80, of which 25 were waited for; matrix products, arithmetic and copies ran while one was open for 3% of the time, Pallas kernels for 42%

profile of v8, /device:TPU:0, one launch (start us, length us, event | category | flops | bytes accessed | tf_op | source)
XLA Modules:
  0.0 578.8 jit_solution(16209393109689519144)
XLA Ops:
  8.0 12.7 %rotate_in.1 = (f32[256,1792]{1,0:T(8,128)S(1)}, f32[256,1792]{1,0:T(8,128)S(1)}) custom-call(s32[3]{0:T(128)S(1)} %pad_add_fusion.place_ref, bf16[512,3584]{1,0:T(8,128)(2,1)} %query_ref.3, bf16[3584,1792]{1,0:T(8,128)(2,1)} %eigen_ref.9, bf16[512,256]{1,0:T(8,128)(2,1)S(1)} %get-tuple-element.101.refs_0_), custom_call_target="tpu_custom_call" | custom-call | flops 6576668672 | bytes 12845056 | tf_op jit(solution)/shard_map/rotate_in/pallas_call | solution.py:328
  23.8 6.9 %collective-permute-done.1 = bf16[512,256]{1,0:T(8,128)(2,1)S(1)} collective-permute-done((bf16[512,256]{1,0:T(8,128)(2,1)S(1)}, bf16[512,256]{1,0:T(8,128)(2,1)S(1)}, u32[]{:S(2)}, u32[]{:S(2)}) %collective-permute-start.1) | collective-permute-done | bytes 262176 | tf_op jit(solution)/shard_map/ppermute | solution.py:614
  72.3 15.0 %collective-permute-done.12 = bf16[512,256]{1,0:T(8,128)(2,1)} collective-permute-done((bf16[512,256]{1,0:T(8,128)(2,1)}, bf16[512,256]{1,0:T(8,128)(2,1)}, u32[]{:S(2)}, u32[]{:S(2)}) %collective-permute-start.12) | collective-permute-done | bytes 262176 | tf_op jit(solution)/shard_map/ppermute | solution.py:591
  91.6 14.6 %form.6 = (bf16[8,512,1792]{2,1,0:T(8,128)(2,1)}, bf16[512,128]{1,0:T(8,128)(2,1)S(1)}) custom-call(s32[3]{0:T(128)S(1)} %pad_add_fusion.place_ref, bf16[512,256]{1,0:T(8,128)(2,1)S(1)} %copy-done.9, bf16[256,1792]{1,0:T(8,128)(2,1)S(1)} %add_convert_fusion.refs_1_.refs_2_, f32[2048,1792]{1,0:T(8,128)} %refs_2_.3, ...), custom_call_target="tpu_custom_call" | custom-call | flops 5872025600 | bytes 14680064 | tf_op jit(solution)/shard_map/form/pallas_call | solution.py:138
  116.8 24.4 %form.7 = (bf16[8,1024,1792]{2,1,0:T(8,128)(2,1)}, f32[512,128]{1,0:T(8,128)S(1)}, bf16[512,128]{1,0:T(8,128)(2,1)S(1)}) custom-call(s32[3]{0:T(128)S(1)} %pad_add_fusion.place_ref, bf16[512,256]{1,0:T(8,128)(2,1)S(1)} %copy-done.6, bf16[512,256]{1,0:T(8,128)(2,1)S(1)} %collective-permute-done.17.refs_1_, ...), custom_call_target="tpu_custom_call" | custom-call | flops 11744051200 | bytes 29360128 | tf_op jit(solution)/shard_map/form/pallas_call | solution.py:138
  143.7 14.5 %form.8 = (bf16[8,512,1792]{2,1,0:T(8,128)(2,1)}, f32[512,128]{1,0:T(8,128)S(1)}) custom-call(s32[3]{0:T(128)S(1)} %pad_add_fusion.place_ref, bf16[512,256]{1,0:T(8,128)(2,1)S(1)} %add_convert_fusion.9.refs_5_.refs_0_, bf16[256,1792]{1,0:T(8,128)(2,1)S(1)} %add_convert_fusion.refs_1_.refs_2_, f32[2048,1792]{1,0:T(8,128)} %refs_2_.3, ...), custom_call_target="tpu_custom_call" | custom-call | flops 5872025600 | bytes 14680064 | tf_op jit(solution)/shard_map/form/pallas_call | solution.py:138
  163.9 7.3 %collective-permute-done.22 = bf16[512,128]{1,0:T(8,128)(2,1)S(1)} collective-permute-done((bf16[512,128]{1,0:T(8,128)(2,1)S(1)}, bf16[512,128]{1,0:T(8,128)(2,1)S(1)}, u32[]{:S(2)}, u32[]{:S(2)}) %collective-permute-start.22) | collective-permute-done | bytes 131104 | tf_op jit(solution)/shard_map/ppermute | solution.py:614
  173.3 14.9 %form.9 = (bf16[8,512,1792]{2,1,0:T(8,128)(2,1)}, bf16[512,128]{1,0:T(8,128)(2,1)S(1)}) custom-call(s32[3]{0:T(128)S(1)} %pad_add_fusion.place_ref, bf16[512,256]{1,0:T(8,128)(2,1)S(1)} %collective-permute-done.24.refs_0_, bf16[256,1792]{1,0:T(8,128)(2,1)S(1)} %add_convert_fusion.refs_1_.refs_2_, f32[2048,1792]{1,0:T(8,128)} %collective-permute-done.21.refs_2_.refs_3_, ...), custom_call_target="tpu_custom_call" | custom-call | flops 5872025600 | bytes 14680064 | tf_op jit(solution)/shard_map/form/pallas_call | solution.py:138
  191.8 24.2 %form.10 = (bf16[8,1024,1792]{2,1,0:T(8,128)(2,1)}, f32[512,128]{1,0:T(8,128)S(1)}, bf16[512,128]{1,0:T(8,128)(2,1)S(1)}) custom-call(s32[3]{0:T(128)S(1)} %pad_add_fusion.place_ref, bf16[512,256]{1,0:T(8,128)(2,1)S(1)} %add_convert_fusion.8.refs_5_.refs_0_, bf16[512,256]{1,0:T(8,128)(2,1)S(1)} %collective-permute-done.27.refs_1_, ...), custom_call_target="tpu_custom_call" | custom-call | flops 11744051200 | bytes 29360128 | tf_op jit(solution)/shard_map/form/pallas_call | solution.py:138
  220.0 14.6 %form.11 = (bf16[8,512,1792]{2,1,0:T(8,128)(2,1)}, f32[512,128]{1,0:T(8,128)S(1)}) custom-call(s32[3]{0:T(128)S(1)} %pad_add_fusion.place_ref, bf16[512,256]{1,0:T(8,128)(2,1)S(1)} %add_convert_fusion.7.refs_6_.refs_0_, bf16[256,1792]{1,0:T(8,128)(2,1)S(1)} %add_convert_fusion.refs_1_.refs_2_, f32[2048,1792]{1,0:T(8,128)} %collective-permute-done.21.refs_2_.refs_3_, ...), custom_call_target="tpu_custom_call" | custom-call | flops 5872025600 | bytes 14680064 | tf_op jit(solution)/shard_map/form/pallas_call | solution.py:138
  241.1 6.7 %returned.12 = (f32[128,1792]{1,0:T(8,128)S(1)}, bf16[128,1792]{1,0:T(8,128)(2,1)}) custom-call(bf16[512,128]{1,0:T(8,128)(2,1)S(1)} %collective-permute-done.38.refs_0_, bf16[8,512,1792]{2,1,0:T(8,128)(2,1)} %get-tuple-element.147.refs_1_.rotated_ref, bf16[512,128]{1,0:T(8,128)(2,1)S(1)} %fusion.25.refs_2_, bf16[512,128]{1,0:T(8,128)(2,1)S(1)} %fusion.17.refs_3_), custom_call_target="tpu_custom_call" | custom-call | flops 3758096384 | bytes 14680064 | tf_op jit(solution)/shard_map/returned/pallas_call | solution.py:260
  251.1 10.9 %returned.13 = (f32[128,1792]{1,0:T(8,128)S(1)}, bf16[128,1792]{1,0:T(8,128)(2,1)}) custom-call(bf16[512,128]{1,0:T(8,128)(2,1)S(1)} %add_convert_fusion.19.refs_5_.refs_0_, bf16[512,128]{1,0:T(8,128)(2,1)S(1)} %collective-permute-done.37.refs_1_, bf16[8,1024,1792]{2,1,0:T(8,128)(2,1)} %get-tuple-element.146.refs_2_.rotated_ref, ...), custom_call_target="tpu_custom_call" | custom-call | flops 7516192768 | bytes 29360128 | tf_op jit(solution)/shard_map/returned/pallas_call | solution.py:260
  262.0 6.7 %returned.14 = (f32[128,1792]{1,0:T(8,128)S(1)}, bf16[128,1792]{1,0:T(8,128)(2,1)}) custom-call(bf16[512,128]{1,0:T(8,128)(2,1)S(1)} %add_convert_fusion.18.refs_4_.refs_1_.refs_0_, bf16[8,512,1792]{2,1,0:T(8,128)(2,1)} %get-tuple-element.145.refs_1_.rotated_ref, f32[128,1792]{1,0:T(8,128)S(1)} %get-tuple-element.149.refs_2_, ...), custom_call_target="tpu_custom_call" | custom-call | flops 3758096384 | bytes 14680064 | tf_op jit(solution)/shard_map/returned/pallas_call | solution.py:260
  268.7 6.7 %returned.15 = (f32[128,1792]{1,0:T(8,128)S(1)}, bf16[128,1792]{1,0:T(8,128)(2,1)}) custom-call(bf16[512,128]{1,0:T(8,128)(2,1)S(1)} %collective-permute-done.36.refs_0_, bf16[8,512,1792]{2,1,0:T(8,128)(2,1)} %get-tuple-element.144.refs_1_.rotated_ref, f32[128,1792]{1,0:T(8,128)S(1)} %get-tuple-element.150.refs_2_, f32[128,128]{1,0:T(8,128)S(1)} %add.196.refs_3_.gram_ref), custom_call_target="tpu_custom_call" | custom-call | flops 3758096384 | bytes 14680064 | tf_op jit(solution)/shard_map/returned/pallas_call | solution.py:260
  275.5 10.9 %returned.16 = (f32[128,1792]{1,0:T(8,128)S(1)}, bf16[128,1792]{1,0:T(8,128)(2,1)}) custom-call(bf16[512,128]{1,0:T(8,128)(2,1)S(1)} %add_convert_fusion.16.refs_4_.refs_2_.refs_0_, bf16[512,128]{1,0:T(8,128)(2,1)S(1)} %collective-permute-done.35.refs_1_, bf16[8,1024,1792]{2,1,0:T(8,128)(2,1)} %get-tuple-element.143.refs_2_.rotated_ref, ...), custom_call_target="tpu_custom_call" | custom-call | flops 7516192768 | bytes 29360128 | tf_op jit(solution)/shard_map/returned/pallas_call | solution.py:260
  294.4 7.2 %collective-permute-done.41.gram_got_ref = f32[128,128]{1,0:T(8,128)S(1)} collective-permute-done((f32[128,128]{1,0:T(8,128)S(1)}, f32[128,128]{1,0:T(8,128)S(1)}, u32[]{:S(2)}, u32[]{:S(2)}) %collective-permute-start.41) | collective-permute-done | bytes 65568 | tf_op jit(solution)/shard_map/ppermute | solution.py:708
  304.0 7.3 %image.7 = bf16[512,128]{1,0:T(8,128)(2,1)S(1)} custom-call(bf16[1792,128]{1,0:T(8,128)(2,1)S(1)} %normalize.2.basis_ref, bf16[8,512,1792]{2,1,0:T(8,128)(2,1)} %get-tuple-element.147.refs_1_.rotated_ref), custom_call_target="tpu_custom_call" | custom-call | flops 3758096384 | bytes 14680064 | tf_op jit(solution)/shard_map/image/pallas_call | solution.py:217
  312.8 12.7 %image.6 = (f32[512,128]{1,0:T(8,128)S(1)}, bf16[512,128]{1,0:T(8,128)(2,1)S(1)}) custom-call(bf16[1792,128]{1,0:T(8,128)(2,1)S(1)} %normalize.2.basis_ref, bf16[8,1024,1792]{2,1,0:T(8,128)(2,1)} %get-tuple-element.146.refs_2_.rotated_ref), custom_call_target="tpu_custom_call" | custom-call | flops 7516192768 | bytes 29360128 | tf_op jit(solution)/shard_map/image/pallas_call | solution.py:217
  326.3 7.3 %image.8 = f32[512,128]{1,0:T(8,128)S(1)} custom-call(bf16[1792,128]{1,0:T(8,128)(2,1)S(1)} %normalize.2.basis_ref, bf16[8,512,1792]{2,1,0:T(8,128)(2,1)} %get-tuple-element.145.refs_1_.rotated_ref, bf16[512,128]{1,0:T(8,128)(2,1)S(1)} %fusion.18.refs_0_), custom_call_target="tpu_custom_call" | custom-call | flops 3758096384 | bytes 14680064 | tf_op jit(solution)/shard_map/image/pallas_call | solution.py:217
  339.0 7.3 %image.9 = bf16[512,128]{1,0:T(8,128)(2,1)S(1)} custom-call(bf16[1792,128]{1,0:T(8,128)(2,1)S(1)} %normalize.2.basis_ref, bf16[8,512,1792]{2,1,0:T(8,128)(2,1)} %get-tuple-element.144.refs_1_.rotated_ref, bf16[512,128]{1,0:T(8,128)(2,1)S(1)} %fusion.26.refs_0_, bf16[512,128]{1,0:T(8,128)(2,1)S(1)} %fusion.19.refs_1_), custom_call_target="tpu_custom_call" | custom-call | flops 3758096384 | bytes 14680064 | tf_op jit(solution)/shard_map/image/pallas_call | solution.py:217
  354.4 13.2 %image.10 = (f32[512,128]{1,0:T(8,128)S(1)}, bf16[512,128]{1,0:T(8,128)(2,1)S(1)}) custom-call(bf16[1792,128]{1,0:T(8,128)(2,1)S(1)} %normalize.2.basis_ref, bf16[8,1024,1792]{2,1,0:T(8,128)(2,1)} %get-tuple-element.143.refs_2_.rotated_ref, bf16[512,128]{1,0:T(8,128)(2,1)S(1)} %add_convert_fusion.15.refs_0_.refs_1_, bf16[512,128]{1,0:T(8,128)(2,1)S(1)} %fusion.27.refs_1_), custom_call_target="tpu_custom_call" | custom-call | flops 7516192768 | bytes 29360128 | tf_op jit(solution)/shard_map/image/pallas_call | solution.py:217
  370.3 7.3 %image.11 = f32[512,128]{1,0:T(8,128)S(1)} custom-call(bf16[1792,128]{1,0:T(8,128)(2,1)S(1)} %normalize.2.basis_ref, bf16[8,512,1792]{2,1,0:T(8,128)(2,1)} %get-tuple-element.140.refs_1_.rotated_ref, bf16[512,128]{1,0:T(8,128)(2,1)S(1)} %add_convert_fusion.14.refs_0_.refs_1_.refs_3_, bf16[512,128]{1,0:T(8,128)(2,1)S(1)} %fusion.20.refs_1_), custom_call_target="tpu_custom_call" | custom-call | flops 3758096384 | bytes 14680064 | tf_op jit(solution)/shard_map/image/pallas_call | solution.py:217
  383.5 6.7 %returned.18 = (f32[128,1792]{1,0:T(8,128)S(1)}, bf16[128,1792]{1,0:T(8,128)(2,1)}) custom-call(bf16[512,128]{1,0:T(8,128)(2,1)S(1)} %collective-permute-done.56.refs_0_, bf16[8,512,1792]{2,1,0:T(8,128)(2,1)} %get-tuple-element.147.refs_1_.rotated_ref, bf16[512,128]{1,0:T(8,128)(2,1)S(1)} %fusion.28.refs_2_, bf16[512,128]{1,0:T(8,128)(2,1)S(1)} %fusion.21.refs_3_), custom_call_target="tpu_custom_call" | custom-call | flops 3758096384 | bytes 14680064 | tf_op jit(solution)/shard_map/returned/pallas_call | solution.py:260
  391.4 10.9 %returned.19 = (f32[128,1792]{1,0:T(8,128)S(1)}, bf16[128,1792]{1,0:T(8,128)(2,1)}) custom-call(bf16[512,128]{1,0:T(8,128)(2,1)S(1)} %add_convert_fusion.15.refs_0_.refs_1_, bf16[512,128]{1,0:T(8,128)(2,1)S(1)} %collective-permute-done.57.refs_2_.refs_1_, bf16[8,1024,1792]{2,1,0:T(8,128)(2,1)} %get-tuple-element.146.refs_2_.rotated_ref, ...), custom_call_target="tpu_custom_call" | custom-call | flops 7516192768 | bytes 29360128 | tf_op jit(solution)/shard_map/returned/pallas_call | solution.py:260
  412.1 6.9 %returned.21 = (f32[128,1792]{1,0:T(8,128)S(1)}, bf16[128,1792]{1,0:T(8,128)(2,1)}) custom-call(bf16[512,128]{1,0:T(8,128)(2,1)S(1)} %collective-permute-done.58.refs_4_.refs_0_, bf16[8,512,1792]{2,1,0:T(8,128)(2,1)} %get-tuple-element.144.refs_1_.rotated_ref, f32[128,1792]{1,0:T(8,128)S(1)} %get-tuple-element.170.refs_2_, f32[128,128]{1,0:T(8,128)S(1)} %add.209.gram_ref.refs_3_), custom_call_target="tpu_custom_call" | custom-call | flops 3758096384 | bytes 14680064 | tf_op jit(solution)/shard_map/returned/pallas_call | solution.py:260
  423.0 11.0 %returned.22 = (f32[128,1792]{1,0:T(8,128)S(1)}, bf16[128,1792]{1,0:T(8,128)(2,1)}) custom-call(bf16[512,128]{1,0:T(8,128)(2,1)S(1)} %add_convert_fusion.13.refs_2_.refs_5_.refs_4_.refs_0_, bf16[512,128]{1,0:T(8,128)(2,1)S(1)} %collective-permute-done.59.refs_6_.refs_1_, bf16[8,1024,1792]{2,1,0:T(8,128)(2,1)} %get-tuple-element.143.refs_2_.rotated_ref, ...), custom_call_target="tpu_custom_call" | custom-call | flops 7516192768 | bytes 29360128 | tf_op jit(solution)/shard_map/returned/pallas_call | solution.py:260
  445.4 12.7 %collective-permute-done.62 = bf16[256,256]{1,0:T(8,128)(2,1)S(1)} collective-permute-done((bf16[256,256]{1,0:T(8,128)(2,1)S(1)}, bf16[256,256]{1,0:T(8,128)(2,1)S(1)}, u32[]{:S(2)}, u32[]{:S(2)}) %collective-permute-start.62) | collective-permute-done | bytes 131104 | tf_op jit(solution)/shard_map/ppermute | solution.py:723
  462.4 6.8 %all-to-all-start = ((bf16[8,256,256]{2,1,0:T(8,128)(2,1)}), bf16[8,256,256]{2,1,0:T(8,128)(2,1)}, u32[]{:S(2)}, u32[]{:S(2)}) async-start(bf16[8,256,256]{2,1,0:T(8,128)(2,1)} %broadcast_in_dim.2), calls=%async_computation | async-start | bytes 2097152 | tf_op jit(solution)/shard_map/all_to_all | solution.py:672
  480.8 12.9 %collective-permute-done.66 = bf16[896,256]{1,0:T(8,128)(2,1)S(1)} collective-permute-done((bf16[896,256]{1,0:T(8,128)(2,1)S(1)}, bf16[896,256]{1,0:T(8,128)(2,1)S(1)}, u32[]{:S(2)}, u32[]{:S(2)}) %collective-permute-start.66) | collective-permute-done | bytes 458784 | tf_op jit(solution)/shard_map/ppermute | solution.py:614
  495.2 8.0 %collective-permute-done.68 = bf16[896,256]{1,0:T(8,128)(2,1)S(1)} collective-permute-done((bf16[896,256]{1,0:T(8,128)(2,1)S(1)}, bf16[896,256]{1,0:T(8,128)(2,1)S(1)}, u32[]{:S(2)}, u32[]{:S(2)}) %collective-permute-start.68) | collective-permute-done | bytes 458784 | tf_op jit(solution)/shard_map/ppermute | solution.py:614
  509.0 16.3 %collective-permute-done.70 = bf16[896,256]{1,0:T(8,128)(2,1)S(1)} collective-permute-done((bf16[896,256]{1,0:T(8,128)(2,1)S(1)}, bf16[896,256]{1,0:T(8,128)(2,1)S(1)}, u32[]{:S(2)}, u32[]{:S(2)}) %collective-permute-start.70) | collective-permute-done | bytes 458784 | tf_op jit(solution)/shard_map/ppermute | solution.py:624
  530.9 21.4 %collective-permute-done.72 = bf16[896,256]{1,0:T(8,128)(2,1)S(1)} collective-permute-done((bf16[896,256]{1,0:T(8,128)(2,1)S(1)}, bf16[896,256]{1,0:T(8,128)(2,1)S(1)}, u32[]{:S(2)}, u32[]{:S(2)}) %collective-permute-start.72) | collective-permute-done | bytes 458784 | tf_op jit(solution)/shard_map/ppermute | solution.py:624
  (266 shorter events, 210.3 us)
Async XLA Ops:
  41.1 20.6 %collective-permute-start.11 = (bf16[256,1792]{1,0:T(8,128)(2,1)S(1)}, bf16[256,1792]{1,0:T(8,128)(2,1)S(1)}, u32[]{:S(2)}, u32[]{:S(2)}) collective-permute-start(bf16[256,1792]{1,0:T(8,128)(2,1)S(1)} %get-tuple-element.195), channel_id=1, source_target_pairs={{0,2},{1,3},{2,0},{3,1},{4,6},{5,7},{6,4},{7,5},{8,10},{9,11},{10,... | collective-permute-start | bytes 2752520 | tf_op jit(solution)/shard_map/ppermute | solution.py:693
  64.0 109.2 %collective-permute-start.21 = (f32[2048,1792]{1,0:T(8,128)}, f32[2048,1792]{1,0:T(8,128)}, u32[]{:S(2)}, u32[]{:S(2)}) collective-permute-start(f32[2048,1792]{1,0:T(8,128)} %refs_2_.3), channel_id=1, source_target_pairs={{0,1},{1,0},{2,3},{3,2},{4,5},{5,4},{6,7},{7,6},{8,9},{9,8},{10,11... | collective-permute-start | bytes 44040200 | tf_op jit(solution)/shard_map/ppermute | solution.py:591
  64.0 42.2 %collective-permute-start = (bf16[512,256]{1,0:T(8,128)(2,1)}, bf16[512,256]{1,0:T(8,128)(2,1)}, u32[]{:S(2)}, u32[]{:S(2)}) collective-permute-start(bf16[512,256]{1,0:T(8,128)(2,1)} %get-tuple-element.99), channel_id=1, source_target_pairs={{0,1},{1,0},{2,3},{3,2},{4,5},{5,4},{6,7},{7,6},{8,9},{9,8},{10,11... | collective-permute-start | bytes 786440 | tf_op jit(solution)/shard_map/ppermute | solution.py:591
  64.5 22.7 %collective-permute-start.12 = (bf16[512,256]{1,0:T(8,128)(2,1)}, bf16[512,256]{1,0:T(8,128)(2,1)}, u32[]{:S(2)}, u32[]{:S(2)}) collective-permute-start(bf16[512,256]{1,0:T(8,128)(2,1)} %get-tuple-element.119), channel_id=1, source_target_pairs={{0,1},{1,0},{2,3},{3,2},{4,5},{5,4},{6,7},{7,6},{8,9},{9,8},{10,11... | collective-permute-start | bytes 786440 | tf_op jit(solution)/shard_map/ppermute | solution.py:591
  69.1 38.1 %collective-permute-start.16 = (bf16[512,256]{1,0:T(8,128)(2,1)}, bf16[512,256]{1,0:T(8,128)(2,1)S(1)}, u32[]{:S(2)}, u32[]{:S(2)}) collective-permute-start(bf16[512,256]{1,0:T(8,128)(2,1)} %fusion.6), channel_id=1, source_target_pairs={{0,8},{8,0},{16,24},{24,16},{1,9},{9,1},{17,25},{25,17},{2,10},{10... | collective-permute-start | bytes 786440 | tf_op jit(solution)/shard_map/ppermute | solution.py:624
  69.6 37.8 %collective-permute-start.15 = (bf16[512,256]{1,0:T(8,128)(2,1)}, bf16[512,256]{1,0:T(8,128)(2,1)S(1)}, u32[]{:S(2)}, u32[]{:S(2)}) collective-permute-start(bf16[512,256]{1,0:T(8,128)(2,1)} %fusion.13), channel_id=1, source_target_pairs={{0,16},{8,24},{16,0},{24,8},{1,17},{9,25},{17,1},{25,9},{2,18},{10... | collective-permute-start | bytes 786440 | tf_op jit(solution)/shard_map/ppermute | solution.py:624
  87.3 18.9 %collective-permute-start.13 = (bf16[512,256]{1,0:T(8,128)(2,1)}, bf16[512,256]{1,0:T(8,128)(2,1)S(1)}, u32[]{:S(2)}, u32[]{:S(2)}) collective-permute-start(bf16[512,256]{1,0:T(8,128)(2,1)} %collective-permute-done.12), channel_id=1, source_target_pairs={{0,4},{4,0},{1,5},{5,1},{2,6},{6,2},{3,7},{7,3},{8,12},{12,8},{9,1... | collective-permute-start | bytes 786440 | tf_op jit(solution)/shard_map/ppermute | solution.py:614
  108.2 33.0 %collective-permute-start.14 = (bf16[512,256]{1,0:T(8,128)(2,1)S(1)}, bf16[512,256]{1,0:T(8,128)(2,1)S(1)}, u32[]{:S(2)}, u32[]{:S(2)}) collective-permute-start(bf16[512,256]{1,0:T(8,128)(2,1)S(1)} %fusion.7.refs_7_), channel_id=1, source_target_pairs={{0,8},{8,0},{16,24},{24,16},{1,9},{9,1},{17,25},{25,17},{2,10},{10... | collective-permute-start | bytes 786440 | tf_op jit(solution)/shard_map/ppermute | solution.py:624
  108.6 34.9 %collective-permute-start.19 = (bf16[512,256]{1,0:T(8,128)(2,1)S(1)}, bf16[512,256]{1,0:T(8,128)(2,1)S(1)}, u32[]{:S(2)}, u32[]{:S(2)}) collective-permute-start(bf16[512,256]{1,0:T(8,128)(2,1)S(1)} %fusion.10.refs_6_), channel_id=1, source_target_pairs={{0,16},{8,24},{16,0},{24,8},{1,17},{9,25},{17,1},{25,9},{2,18},{10... | collective-permute-start | bytes 786440 | tf_op jit(solution)/shard_map/ppermute | solution.py:624
  111.3 32.4 %collective-permute-start.20 = (bf16[512,128]{1,0:T(8,128)(2,1)S(1)}, bf16[512,128]{1,0:T(8,128)(2,1)S(1)}, u32[]{:S(2)}, u32[]{:S(2)}) collective-permute-start(bf16[512,128]{1,0:T(8,128)(2,1)S(1)} %get-tuple-element.117), channel_id=1, source_target_pairs={{0,4},{4,0},{1,5},{5,1},{2,6},{6,2},{3,7},{7,3},{8,12},{12,8},{9,1... | collective-permute-start | bytes 393224 | tf_op jit(solution)/shard_map/ppermute | solution.py:614
  142.2 19.8 %collective-permute-start.18 = (bf16[512,256]{1,0:T(8,128)(2,1)S(1)}, bf16[512,256]{1,0:T(8,128)(2,1)S(1)}, u32[]{:S(2)}, u32[]{:S(2)}) collective-permute-start(bf16[512,256]{1,0:T(8,128)(2,1)S(1)} %fusion.11.refs_6_), channel_id=1, source_target_pairs={{0,16},{8,24},{16,0},{24,8},{1,17},{9,25},{17,1},{25,9},{2,18},{10... | collective-permute-start | bytes 786440 | tf_op jit(solution)/shard_map/ppermute | solution.py:624
  163.1 28.7 %collective-permute-start.27 = (bf16[512,256]{1,0:T(8,128)(2,1)S(1)}, bf16[512,256]{1,0:T(8,128)(2,1)S(1)}, u32[]{:S(2)}, u32[]{:S(2)}) collective-permute-start(bf16[512,256]{1,0:T(8,128)(2,1)S(1)} %add_convert_fusion.7.refs_6_.refs_0_), channel_id=1, source_target_pairs={{0,4},{4,0},{1,5},{5,1},{2,6},{6,2},{3,7},{7,3},{8,12},{12,8},{9,1... | collective-permute-start | bytes 786440 | tf_op jit(solution)/shard_map/ppermute | solution.py:630
  171.6 18.7 %collective-permute-start.28 = (bf16[512,128]{1,0:T(8,128)(2,1)S(1)}, bf16[512,128]{1,0:T(8,128)(2,1)S(1)}, u32[]{:S(2)}, u32[]{:S(2)}) collective-permute-start(bf16[512,128]{1,0:T(8,128)(2,1)S(1)} %fusion.22.refs_4_), channel_id=1, source_target_pairs={{0,16},{8,24},{16,0},{24,8},{1,17},{9,25},{17,1},{25,9},{2,18},{10... | collective-permute-start | bytes 393224 | tf_op jit(solution)/shard_map/ppermute | solution.py:624
  188.2 28.4 %collective-permute-start.29 = (bf16[512,128]{1,0:T(8,128)(2,1)S(1)}, bf16[512,128]{1,0:T(8,128)(2,1)S(1)}, u32[]{:S(2)}, u32[]{:S(2)}) collective-permute-start(bf16[512,128]{1,0:T(8,128)(2,1)S(1)} %get-tuple-element.133), channel_id=1, source_target_pairs={{0,4},{4,0},{1,5},{5,1},{2,6},{6,2},{3,7},{7,3},{8,12},{12,8},{9,1... | collective-permute-start | bytes 393224 | tf_op jit(solution)/shard_map/ppermute | solution.py:614
  188.9 29.6 %collective-permute-start.26 = (bf16[512,128]{1,0:T(8,128)(2,1)S(1)}, bf16[512,128]{1,0:T(8,128)(2,1)S(1)}, u32[]{:S(2)}, u32[]{:S(2)}) collective-permute-start(bf16[512,128]{1,0:T(8,128)(2,1)S(1)} %fusion.23.refs_6_), channel_id=1, source_target_pairs={{0,16},{8,24},{16,0},{24,8},{1,17},{9,25},{17,1},{25,9},{2,18},{10... | collective-permute-start | bytes 393224 | tf_op jit(solution)/shard_map/ppermute | solution.py:624
  190.3 50.7 %collective-permute-start.38 = (bf16[512,128]{1,0:T(8,128)(2,1)S(1)}, bf16[512,128]{1,0:T(8,128)(2,1)S(1)}, u32[]{:S(2)}, u32[]{:S(2)}) collective-permute-start(bf16[512,128]{1,0:T(8,128)(2,1)S(1)} %add_convert_fusion.19.refs_5_.refs_0_), channel_id=1, source_target_pairs={{0,4},{4,0},{1,5},{5,1},{2,6},{6,2},{3,7},{7,3},{8,12},{12,8},{9,1... | collective-permute-start | bytes 393224 | tf_op jit(solution)/shard_map/ppermute | solution.py:630
  216.0 18.6 %collective-permute-start.30 = (bf16[512,128]{1,0:T(8,128)(2,1)S(1)}, bf16[512,128]{1,0:T(8,128)(2,1)S(1)}, u32[]{:S(2)}, u32[]{:S(2)}) collective-permute-start(bf16[512,128]{1,0:T(8,128)(2,1)S(1)} %get-tuple-element.139), channel_id=1, source_target_pairs={{0,4},{4,0},{1,5},{5,1},{2,6},{6,2},{3,7},{7,3},{8,12},{12,8},{9,1... | collective-permute-start | bytes 393224 | tf_op jit(solution)/shard_map/ppermute | solution.py:614
  216.7 18.3 %collective-permute-start.33 = (bf16[512,128]{1,0:T(8,128)(2,1)S(1)}, bf16[512,128]{1,0:T(8,128)(2,1)S(1)}, u32[]{:S(2)}, u32[]{:S(2)}) collective-permute-start(bf16[512,128]{1,0:T(8,128)(2,1)S(1)} %fusion.16.refs_5_), channel_id=1, source_target_pairs={{0,8},{8,0},{16,24},{24,16},{1,9},{9,1},{17,25},{25,17},{2,10},{10... | collective-permute-start | bytes 393224 | tf_op jit(solution)/shard_map/ppermute | solution.py:624
  218.6 32.5 %collective-permute-start.37 = (bf16[512,128]{1,0:T(8,128)(2,1)S(1)}, bf16[512,128]{1,0:T(8,128)(2,1)S(1)}, u32[]{:S(2)}, u32[]{:S(2)}) collective-permute-start(bf16[512,128]{1,0:T(8,128)(2,1)S(1)} %add_convert_fusion.18.refs_4_.refs_1_.refs_0_), channel_id=1, source_target_pairs={{0,4},{4,0},{1,5},{5,1},{2,6},{6,2},{3,7},{7,3},{8,12},{12,8},{9,1... | collective-permute-start | bytes 393224 | tf_op jit(solution)/shard_map/ppermute | solution.py:630
  247.9 20.9 %collective-permute-start.36 = (bf16[512,128]{1,0:T(8,128)(2,1)S(1)}, bf16[512,128]{1,0:T(8,128)(2,1)S(1)}, u32[]{:S(2)}, u32[]{:S(2)}) collective-permute-start(bf16[512,128]{1,0:T(8,128)(2,1)S(1)} %add_convert_fusion.16.refs_4_.refs_2_.refs_0_), channel_id=1, source_target_pairs={{0,4},{4,0},{1,5},{5,1},{2,6},{6,2},{3,7},{7,3},{8,12},{12,8},{9,1... | collective-permute-start | bytes 393224 | tf_op jit(solution)/shard_map/ppermute | solution.py:630
  249.0 26.5 %collective-permute-start.35 = (bf16[512,128]{1,0:T(8,128)(2,1)S(1)}, bf16[512,128]{1,0:T(8,128)(2,1)S(1)}, u32[]{:S(2)}, u32[]{:S(2)}) collective-permute-start(bf16[512,128]{1,0:T(8,128)(2,1)S(1)} %add_convert_fusion.17.refs_3_.refs_0_), channel_id=1, source_target_pairs={{0,4},{4,0},{1,5},{5,1},{2,6},{6,2},{3,7},{7,3},{8,12},{12,8},{9,1... | collective-permute-start | bytes 393224 | tf_op jit(solution)/shard_map/ppermute | solution.py:630
  350.6 19.6 %collective-permute-start.47 = (bf16[512,128]{1,0:T(8,128)(2,1)S(1)}, bf16[512,128]{1,0:T(8,128)(2,1)S(1)}, u32[]{:S(2)}, u32[]{:S(2)}) collective-permute-start(bf16[512,128]{1,0:T(8,128)(2,1)S(1)} %fusion.27.refs_1_), channel_id=1, source_target_pairs={{0,16},{8,24},{16,0},{24,8},{1,17},{9,25},{17,1},{25,9},{2,18},{10... | collective-permute-start | bytes 393224 | tf_op jit(solution)/shard_map/ppermute | solution.py:624
  390.4 21.7 %collective-permute-start.58 = (bf16[512,128]{1,0:T(8,128)(2,1)S(1)}, bf16[512,128]{1,0:T(8,128)(2,1)S(1)}, u32[]{:S(2)}, u32[]{:S(2)}) collective-permute-start(bf16[512,128]{1,0:T(8,128)(2,1)S(1)} %add_convert_fusion.13.refs_2_.refs_5_.refs_4_.refs_0_), channel_id=1, source_target_pairs={{0,4},{4,0},{1,5},{5,1},{2,6},{6,2},{3,7},{7,3},{8,12},{12,8},{9,1... | collective-permute-start | bytes 393224 | tf_op jit(solution)/shard_map/ppermute | solution.py:630
  441.9 18.3 %collective-permute-start.64 = (bf16[128,1792]{1,0:T(8,128)(2,1)S(1)}, bf16[128,1792]{1,0:T(8,128)(2,1)S(1)}, u32[]{:S(2)}, u32[]{:S(2)}) collective-permute-start(bf16[128,1792]{1,0:T(8,128)(2,1)S(1)} %get-tuple-element.173), channel_id=1, source_target_pairs={{0,2},{1,3},{2,0},{3,1},{4,6},{5,7},{6,4},{7,5},{8,10},{9,11},{10,... | collective-permute-start | bytes 1376264 | tf_op jit(solution)/shard_map/ppermute | solution.py:693
  462.4 62.8 %all-to-all-start = ((bf16[8,256,256]{2,1,0:T(8,128)(2,1)}), bf16[8,256,256]{2,1,0:T(8,128)(2,1)}, u32[]{:S(2)}, u32[]{:S(2)}) async-start(bf16[8,256,256]{2,1,0:T(8,128)(2,1)} %broadcast_in_dim.2), calls=%async_computation | async-start | bytes 2097152 | tf_op jit(solution)/shard_map/all_to_all | solution.py:672
  473.9 19.8 %collective-permute-start.66 = (bf16[896,256]{1,0:T(8,128)(2,1)S(1)}, bf16[896,256]{1,0:T(8,128)(2,1)S(1)}, u32[]{:S(2)}, u32[]{:S(2)}) collective-permute-start(bf16[896,256]{1,0:T(8,128)(2,1)S(1)} %get-tuple-element.182), channel_id=1, source_target_pairs={{0,4},{4,0},{1,5},{5,1},{2,6},{6,2},{3,7},{7,3},{8,12},{12,8},{9,1... | collective-permute-start | bytes 1376264 | tf_op jit(solution)/shard_map/ppermute | solution.py:614
  480.7 22.6 %collective-permute-start.68 = (bf16[896,256]{1,0:T(8,128)(2,1)S(1)}, bf16[896,256]{1,0:T(8,128)(2,1)S(1)}, u32[]{:S(2)}, u32[]{:S(2)}) collective-permute-start(bf16[896,256]{1,0:T(8,128)(2,1)S(1)} %get-tuple-element.185), channel_id=1, source_target_pairs={{0,4},{4,0},{1,5},{5,1},{2,6},{6,2},{3,7},{7,3},{8,12},{12,8},{9,1... | collective-permute-start | bytes 1376264 | tf_op jit(solution)/shard_map/ppermute | solution.py:614
  503.4 21.8 %collective-permute-start.70 = (bf16[896,256]{1,0:T(8,128)(2,1)S(1)}, bf16[896,256]{1,0:T(8,128)(2,1)S(1)}, u32[]{:S(2)}, u32[]{:S(2)}) collective-permute-start(bf16[896,256]{1,0:T(8,128)(2,1)S(1)} %add_convert_fusion.5), channel_id=1, source_target_pairs={{0,8},{8,0},{16,24},{24,16},{1,9},{9,1},{17,25},{25,17},{2,10},{10... | collective-permute-start | bytes 1376264 | tf_op jit(solution)/shard_map/ppermute | solution.py:624
  506.0 23.7 %collective-permute-start.69 = (bf16[896,256]{1,0:T(8,128)(2,1)S(1)}, bf16[896,256]{1,0:T(8,128)(2,1)}, u32[]{:S(2)}, u32[]{:S(2)}) collective-permute-start(bf16[896,256]{1,0:T(8,128)(2,1)S(1)} %add_convert_fusion.4), channel_id=1, source_target_pairs={{0,16},{8,24},{16,0},{24,8},{1,17},{9,25},{17,1},{25,9},{2,18},{10... | collective-permute-start | bytes 1376264 | tf_op jit(solution)/shard_map/ppermute | solution.py:624
  525.2 27.4 %all-to-all-start.1 = ((bf16[4,512,256]{2,1,0:T(8,128)(2,1)}), bf16[4,512,256]{2,1,0:T(8,128)(2,1)}, u32[]{:S(2)}, u32[]{:S(2)}) async-start(bf16[4,512,256]{2,1,0:T(8,128)(2,1)} %bitcast.4), calls=%async_computation.1 | async-start | bytes 2097152 | tf_op jit(solution)/shard_map/all_to_all | solution.py:734
  529.6 22.7 %collective-permute-start.72 = (bf16[896,256]{1,0:T(8,128)(2,1)S(1)}, bf16[896,256]{1,0:T(8,128)(2,1)S(1)}, u32[]{:S(2)}, u32[]{:S(2)}) collective-permute-start(bf16[896,256]{1,0:T(8,128)(2,1)S(1)} %add_convert_fusion.3), channel_id=1, source_target_pairs={{0,16},{8,24},{16,0},{24,8},{1,17},{9,25},{17,1},{25,9},{2,18},{10... | collective-permute-start | bytes 1376264 | tf_op jit(solution)/shard_map/ppermute | solution.py:624
  530.9 34.2 %collective-permute-start.71 = (bf16[896,256]{1,0:T(8,128)(2,1)S(1)}, bf16[896,256]{1,0:T(8,128)(2,1)S(1)}, u32[]{:S(2)}, u32[]{:S(2)}) collective-permute-start(bf16[896,256]{1,0:T(8,128)(2,1)S(1)} %add_convert_fusion.2.refs_1_), channel_id=1, source_target_pairs={{0,4},{4,0},{1,5},{5,1},{2,6},{6,2},{3,7},{7,3},{8,12},{12,8},{9,1... | collective-permute-start | bytes 1376264 | tf_op jit(solution)/shard_map/ppermute | solution.py:630
  (69 other events, 1350.3 us)

commit v9 on v8

--- a/solution.py
+++ b/solution.py
@@ -414,8 +414,8 @@
             send_refs[step - 1][...] = share.astype(bf16)
 
 
-def factor_out_kernel(place_ref, eigen_ref, mine_ref, theirs_ref, keep_ref, *refs):
-    *send_refs, total = refs
+def factor_out_kernel(n_ties, place_ref, eigen_ref, mine_ref, theirs_ref, *refs):
+    keep_ref, *send_refs, total = refs[n_ties:]
     total[...] = jnp.dot(
         eigen_ref[...],
         side_by_side(place_ref, mine_ref[...], theirs_ref[...]),
@@ -429,19 +429,19 @@
     return [jax.ShapeDtypeStruct(shape, f32)] + [jax.ShapeDtypeStruct(shape, bf16)] * (n_width - 1)
 
 
-def factor_out(place, eigen_out, mine, theirs, n_width):
+def factor_out(place, eigen_out, mine, theirs, n_width, ties):
     rows = eigen_out.shape[0]
     width = CORES * COLS
     vmem = pl.BlockSpec(memory_space=pltpu.VMEM)
     return pl.pallas_call(
-        factor_out_kernel,
-        in_specs=[pl.BlockSpec(memory_space=pltpu.SMEM)] + [vmem] * 3,
+        functools.partial(factor_out_kernel, len(ties)),
+        in_specs=[pl.BlockSpec(memory_space=pltpu.SMEM)] + [vmem] * 3 + tied(ties),
         out_specs=[vmem] * n_width,
         out_shape=shares(rows, width, n_width),
         scratch_shapes=[pltpu.VMEM((rows, width), f32)],
         compiler_params=params(),
         name="factor_out",
-    )(place, eigen_out, mine, theirs)
+    )(place, eigen_out, mine, theirs, *ties)
 
 
 def project_kernel(n_dp, n_parts, place_ref, hidden_ref, *refs):
@@ -542,17 +542,20 @@
     return (right * lax.rsqrt(diagonal)).reshape(COLS, COLS)
 
 
-def inverse_kernel(scale, gram_ref, gram_got_ref, inverse_ref):
-    inverse_ref[...] = lower_inverse((gram_ref[...] + gram_got_ref[...]) * scale)
-
-
-def inverse_of(gram, gram_got, scale):
+def inverse_kernel(scale, gram_ref, gram_got_ref, *refs):
+    refs[-1][...] = lower_inverse((gram_ref[...] + gram_got_ref[...]) * scale)
+
+
+def inverse_of(gram, gram_got, scale, ties):
+    vmem = pl.BlockSpec(memory_space=pltpu.VMEM)
     return pl.pallas_call(
         functools.partial(inverse_kernel, scale),
+        in_specs=[vmem, vmem] + tied(ties),
+        out_specs=vmem,
         out_shape=jax.ShapeDtypeStruct((COLS, COLS), f32),
         compiler_params=params(),
         name="inverse",
-    )(gram, gram_got)
+    )(gram, gram_got, *ties)
 
 
 def normalize_kernel(total_ref, got_ref, inverse_ref, *refs):
@@ -595,6 +598,30 @@
     return lax.optimization_barrier((array, *others))[0] if others else array
 
 
+def hop_kernel(n_got, n_ties, total_ref, *refs):
+    total = total_ref[...]
+    for ref in refs[:n_got]:
+        total = total + ref[...].astype(f32)
+    rounded_ref, *total_refs = refs[n_got + n_ties :]
+    rounded_ref[...] = total.astype(bf16)
+    for ref in total_refs:
+        ref[...] = total
+
+
+def hop_sum(total, got, others, last):
+    vmem = pl.BlockSpec(memory_space=pltpu.VMEM)
+    shapes = [jax.ShapeDtypeStruct(total.shape, bf16), jax.ShapeDtypeStruct(total.shape, f32)]
+    shapes = shapes[:1] if last else shapes
+    return pl.pallas_call(
+        functools.partial(hop_kernel, len(got), len(others)),
+        in_specs=[vmem] * (1 + len(got)) + tied(others),
+        out_specs=[vmem] * len(shapes),
+        out_shape=shapes,
+        compiler_params=params(),
+        name="hop",
+    )(total, *got, *others)
+
+
 class Reduction:
     def __init__(self, sends, n_grp, n_dp, even=False, keep=None):
         self.parts = self.own = None
@@ -615,17 +642,33 @@
             for at in range(n_dp - 1)
         ]
         others = yield []
-        total = after(self.keep, others)
-        for part in got:
-            total = total + part.astype(f32)
-        step = 1
-        while step < n_grp:
-            sent = total.astype(bf16)
-            got = lax.ppermute(sent, "grp", crossed(n_grp, step))
+        total, step, odd = self.keep, 1, lax.axis_index("grp") % 2
+        while True:
+            last = step >= n_grp
+            if even:
+                total = after(total, others)
+                for part in got:
+                    total = total + part.astype(f32)
+                if step == 2:
+                    total = lax.dynamic_slice_in_dim(total, odd * (rows // 2), rows // 2, 0)
+                own = sent = total.astype(bf16)
+                total = sent.astype(f32)
+            else:
+                sent, *totals = hop_sum(total, got, others, last)
+                own, total = sent, totals[0] if totals else None
+            if last:
+                break
+            got = [lax.ppermute(sent, "grp", crossed(n_grp, step))]
             others = yield [sent]
-            total = (sent.astype(f32) if even else total) + after(got, others).astype(f32)
             step *= 2
-        own = self.own = total.astype(bf16)
+        if even and n_grp > 2:
+            got = lax.ppermute(own, "grp", crossed(n_grp, 1))
+            others = yield [own]
+            got = after(got, others)
+            own = jnp.where(
+                odd == 0, jnp.concatenate([own, got]), jnp.concatenate([got, own])
+            )
+        self.own = own
         self.parts = [
             lax.ppermute(own, "dp", turned_by(n_dp, n_dp - 1 - at)) for at in range(n_dp - 1)
         ] + [own]
@@ -665,12 +708,6 @@
     pieces = lax.all_to_all(part.astype(bf16), axes, 0, 0, tiled=True)
     pieces = pieces.reshape((count, part.shape[0] // count) + part.shape[1:])
     return jnp.sum(pieces.astype(f32), axis=0)
-
-
-def gather_rows(piece, axes, count):
-    copies = jnp.broadcast_to(piece[None], (count,) + piece.shape)
-    whole = lax.all_to_all(copies, axes, 0, 0, tiled=True)
-    return whole.reshape((count * piece.shape[0],) + piece.shape[1:])
 
 
 def make_per_device(n_grp, n_dp, n_width):
@@ -699,8 +736,6 @@
         def output_side(summing, last):
             gram = gram_of([each.own for each in summing])
             got = [lax.ppermute(gram, "dp", turned_by(n_dp, at)) for at in range(1, n_dp)]
-            others = yield [gram]
-            gram = after(gram, others)
             for each in got:
                 gram = gram + each
             step = 2
@@ -711,14 +746,14 @@
                     break
                 gram = gram + got
             others = yield [gram]
-            inverse = found["inverse"] = inverse_of(after(gram, others), got, scale)
+            inverse = found["inverse"] = inverse_of(gram, got, scale, others)
             if not last:
                 return
             images = [part for each in summing for part in each.parts]
             mine, theirs = turn(place, inverse, images, n_dp)
             theirs = swap_cores(theirs, n_width)
             others = yield [mine]
-            keep, *sends = factor_out(place, eigen_out, after(mine, others), theirs, n_width)
+            keep, *sends = factor_out(place, eigen_out, mine, theirs, n_width, others)
             sends = [
                 lax.ppermute(send, "width", crossed(n_width, at + 1))
                 for at, send in enumerate(sends)
@@ -729,8 +764,11 @@
                 share = share + send.astype(f32)
             share = share.astype(bf16)
             piece_rows = share.shape[0]
-            gathered = gather_rows(share, GD, n_gd)
             others = yield [share]
+            copies = jnp.broadcast_to(after(share, others)[None], (n_gd,) + share.shape)
+            gathered = lax.all_to_all(copies, GD, 0, 0, tiled=True)
+            gathered = gathered.reshape(n_gd * piece_rows, -1)
+            others = yield [copies]
             mixed = lax.all_to_all(after(gathered, others), "width", 0, 0, tiled=True)
             others = yield [gathered]
             out_factor = found["out_factor"] = (
@@ -750,6 +788,7 @@
         theirs_in, mine_in = rotate_in(place, query_in, eigen_in, pieces[:1])
         theirs_in = swap_cores(theirs_in, n_width)
         their_pieces = [swap_cores(each, n_width) for each in their_pieces]
+        hidden = (jax.nn.silu(gate_pre.astype(f32)) * up_pre.astype(f32)).astype(bf16)
         hops = boundary([mine_in], turning)
         total_in, sent_in, got_in = last_hop(after(mine_in, hops) + theirs_in)
         last = [sent_in]
@@ -757,10 +796,9 @@
             sends, keep = (own_pieces + their_pieces)[2 * at : 2 * at + 2]
             turning.append(Reduction(after(sends, last), n_grp, n_dp, keep=keep))
             if turning[0].parts is None:
-                last = boundary(last, turning)[:1]
-        hidden = (jax.nn.silu(gate_pre.astype(f32)) * up_pre.astype(f32)).astype(bf16)
+                last = boundary(last + [hidden] if at == 2 else last, turning)[:1]
         rot_in = (total_in + got_in.astype(f32)).astype(bf16)
-        eig_sent = after(eigvals, [rot_in, *turning[0].parts])
+        eig_sent = after(eigvals, [rot_in, *turning[0].parts, *their_pieces])
         eig_theirs = swap_cores(eig_sent, n_width)
         basis = lax.dynamic_slice_in_dim(start, core * COLS, COLS, 1)
         calls = []
@@ -827,7 +865,7 @@
             factors.append(Reduction(sends, n_grp, n_dp, True, keep))
         path.advance(last)
         while any(each.parts is None for each in factors):
-            last = boundary(last, factors)[:1]
+            last = boundary(last, factors[::-1])[:1]
         parts = [part for each in factors for part in each.parts]
         in_factor, keep_in, *sends_in = project(place, hidden, parts, n_dp, n_width)
         while "proj_out" not in found:

time: 583 us -> 533 us (0.914)
  waiting for transfers between devices: 151 us -> 94.4 us
    ppermute x28 -> x30, waiting for transfers between devices: 59 us -> 33.5 us  [the longest x28 29.1 us: run(): got = [lax.ppermute(sent, 'grp', crossed(n_grp, step))]]
    ppermute x14, waiting for transfers between devices: 39.9 us -> 19.5 us  [run(): lax.ppermute(sends[at * rows:(at + 1) * rows], 'dp', turned_by(n_dp, at +...]
    ppermute x3, waiting for transfers between devices: 14.7 us -> 0.01 us  [output_side(): lax.ppermute(send, 'width', crossed(n_width, at + 1))]
    ppermute x8, waiting for transfers between devices: 15 us -> 1.82 us  [swap_cores(): return lax.ppermute(part, 'width', crossed(n_width, 1))]
    ppermute x3, waiting for transfers between devices: 2.71 us -> 13.1 us  [last_hop(): got = lax.ppermute(sent, 'width', crossed(n_width, step))]
    unnamed x42 -> x50, local copies, waits for them, and re-layouts: 9.49 us -> 12.9 us
    ppermute x28 -> x30, starting transfers between devices: 39.6 us -> 40.3 us  [the longest x28 39.5 us: run(): got = [lax.ppermute(sent, 'grp', crossed(n_grp, step))]]
  transfers between devices with their start and end apart: 80 -> 82, of which waited for: 25 -> 23; matrix products, arithmetic and copies ran while one was open for 3% -> 4% of each run, Pallas kernels for 42% -> 44%
where the time goes in v9:
time: 533 us; the launch traced here: 529 us
  Pallas kernels  297 us (56%)
  starting transfers between devices  97.3 us (18%)
  waiting for transfers between devices  94.4 us (18%)
  other arithmetic  20.5 us (4%)
  local copies, waits for them, and re-layouts  17.3 us (3%)
    pallas_call x6, Pallas kernels, form_parts(): pl.pallas_call(functools.partial(form_kernel, n_keep, n_parts, len(ties))...  107 us
    pallas_call x12, Pallas kernels, return_parts(): pl.pallas_call(functools.partial(return_kernel, n_parts, not before), in_...  90.4 us
    pallas_call x6, Pallas kernels, image_parts(): pl.pallas_call(functools.partial(image_kernel, n_keep, len(ties)), grid=(...  54.8 us
    ppermute x28, starting transfers between devices, run(): got = [lax.ppermute(sent, 'grp', crossed(n_grp, step))]  39.5 us
    ppermute x28, waiting for transfers between devices, run(): got = [lax.ppermute(sent, 'grp', crossed(n_grp, step))]  29.1 us
    ppermute x14, waiting for transfers between devices, run(): lax.ppermute(sends[at * rows:(at + 1) * rows], 'dp', turned_by(n_dp, at +...  19.5 us
    ppermute x14, starting transfers between devices, run(): lax.ppermute(sends[at * rows:(at + 1) * rows], 'dp', turned_by(n_dp, at +...  17.1 us
    ppermute x14, starting transfers between devices, run(): lax.ppermute(own, 'dp', turned_by(n_dp, n_dp - 1 - at))  15.2 us
  transfers between devices with their start and end apart: 82, of which 23 were waited for; matrix products, arithmetic and copies ran while one was open for 4% of the time, Pallas kernels for 44%

profile of v9, /device:TPU:0, one launch (start us, length us, event | category | flops | bytes accessed | tf_op | source)
XLA Modules:
  0.0 528.9 jit_solution(7760589642925006734)
XLA Ops:
  7.2 13.0 %rotate_in.1 = (f32[256,1792]{1,0:T(8,128)S(1)}, f32[256,1792]{1,0:T(8,128)S(1)}) custom-call(s32[3]{0:T(128)S(1)} %pad_add_fusion.place_ref, bf16[512,3584]{1,0:T(8,128)(2,1)} %query_ref.3, bf16[3584,1792]{1,0:T(8,128)(2,1)} %eigen_ref.9, bf16[512,256]{1,0:T(8,128)(2,1)S(1)} %get-tuple-element.133.refs_0_), custom_call_target="tpu_custom_call" | custom-call | flops 6576668672 | bytes 12845056 | tf_op jit(solution)/shard_map/rotate_in/pallas_call | solution.py:328
  23.3 6.9 %collective-permute-done.2.refs_0_ = bf16[512,256]{1,0:T(8,128)(2,1)S(1)} collective-permute-done((bf16[512,256]{1,0:T(8,128)(2,1)S(1)}, bf16[512,256]{1,0:T(8,128)(2,1)S(1)}, u32[]{:S(2)}, u32[]{:S(2)}) %collective-permute-start.2) | collective-permute-done | bytes 262176 | tf_op jit(solution)/shard_map/ppermute | solution.py:641
  69.9 14.5 %form.6 = (bf16[8,512,1792]{2,1,0:T(8,128)(2,1)}, bf16[512,128]{1,0:T(8,128)(2,1)S(1)}) custom-call(s32[3]{0:T(128)S(1)} %pad_add_fusion.place_ref, bf16[512,256]{1,0:T(8,128)(2,1)S(1)} %copy-done.19, bf16[256,1792]{1,0:T(8,128)(2,1)S(1)} %add_convert_fusion.refs_1_.refs_2_, f32[2048,1792]{1,0:T(8,128)} %refs_2_.3, ...), custom_call_target="tpu_custom_call" | custom-call | flops 5872025600 | bytes 14680064 | tf_op jit(solution)/shard_map/form/pallas_call | solution.py:138
  93.9 24.4 %form.7 = (bf16[8,1024,1792]{2,1,0:T(8,128)(2,1)}, f32[512,128]{1,0:T(8,128)S(1)}, bf16[512,128]{1,0:T(8,128)(2,1)S(1)}) custom-call(s32[3]{0:T(128)S(1)} %pad_add_fusion.place_ref, bf16[512,256]{1,0:T(8,128)(2,1)S(1)} %copy-done.12, bf16[512,256]{1,0:T(8,128)(2,1)S(1)} %collective-permute-done.17.refs_1_, ...), custom_call_target="tpu_custom_call" | custom-call | flops 11744051200 | bytes 29360128 | tf_op jit(solution)/shard_map/form/pallas_call | solution.py:138
  122.7 14.5 %form.8 = (bf16[8,512,1792]{2,1,0:T(8,128)(2,1)}, f32[512,128]{1,0:T(8,128)S(1)}) custom-call(s32[3]{0:T(128)S(1)} %pad_add_fusion.place_ref, bf16[512,256]{1,0:T(8,128)(2,1)S(1)} %hop.44.refs_5_.refs_0_, bf16[256,1792]{1,0:T(8,128)(2,1)S(1)} %add_convert_fusion.refs_1_.refs_2_, f32[2048,1792]{1,0:T(8,128)} %refs_2_.3, ...), custom_call_target="tpu_custom_call" | custom-call | flops 5872025600 | bytes 14680064 | tf_op jit(solution)/shard_map/form/pallas_call | solution.py:138
  141.6 14.7 %form.9 = (bf16[8,512,1792]{2,1,0:T(8,128)(2,1)}, bf16[512,128]{1,0:T(8,128)(2,1)S(1)}) custom-call(s32[3]{0:T(128)S(1)} %pad_add_fusion.place_ref, bf16[512,256]{1,0:T(8,128)(2,1)S(1)} %collective-permute-done.24.refs_0_, bf16[256,1792]{1,0:T(8,128)(2,1)S(1)} %add_convert_fusion.refs_1_.refs_2_, f32[2048,1792]{1,0:T(8,128)} %collective-permute-done.21.refs_2_.refs_3_, ...), custom_call_target="tpu_custom_call" | custom-call | flops 5872025600 | bytes 14680064 | tf_op jit(solution)/shard_map/form/pallas_call | solution.py:138
  158.9 24.2 %form.10 = (bf16[8,1024,1792]{2,1,0:T(8,128)(2,1)}, f32[512,128]{1,0:T(8,128)S(1)}, bf16[512,128]{1,0:T(8,128)(2,1)S(1)}) custom-call(s32[3]{0:T(128)S(1)} %pad_add_fusion.place_ref, bf16[512,256]{1,0:T(8,128)(2,1)S(1)} %hop.46.refs_1_.refs_5_.refs_0_, bf16[512,256]{1,0:T(8,128)(2,1)S(1)} %collective-permute-done.27.refs_1_, ...), custom_call_target="tpu_custom_call" | custom-call | flops 11744051200 | bytes 29360128 | tf_op jit(solution)/shard_map/form/pallas_call | solution.py:138
  186.3 14.9 %form.11 = (bf16[8,512,1792]{2,1,0:T(8,128)(2,1)}, f32[512,128]{1,0:T(8,128)S(1)}) custom-call(s32[3]{0:T(128)S(1)} %pad_add_fusion.place_ref, bf16[512,256]{1,0:T(8,128)(2,1)S(1)} %hop.48.refs_1_.refs_6_.refs_0_, bf16[256,1792]{1,0:T(8,128)(2,1)S(1)} %add_convert_fusion.refs_1_.refs_2_, f32[2048,1792]{1,0:T(8,128)} %collective-permute-done.21.refs_2_.refs_3_, ...), custom_call_target="tpu_custom_call" | custom-call | flops 5872025600 | bytes 14680064 | tf_op jit(solution)/shard_map/form/pallas_call | solution.py:138
  205.0 5.9 %returned.12 = (f32[128,1792]{1,0:T(8,128)S(1)}, bf16[128,1792]{1,0:T(8,128)(2,1)S(1)}) custom-call(bf16[512,128]{1,0:T(8,128)(2,1)S(1)} %collective-permute-done.32.refs_0_, bf16[8,512,1792]{2,1,0:T(8,128)(2,1)} %get-tuple-element.180.refs_1_.rotated_ref, bf16[512,128]{1,0:T(8,128)(2,1)S(1)} %get-tuple-element.182.refs_2_, ...), custom_call_target="tpu_custom_call" | custom-call | flops 3758096384 | bytes 14680064 | tf_op jit(solution)/shard_map/returned/pallas_call | solution.py:260
  212.0 10.1 %returned.13 = (f32[128,1792]{1,0:T(8,128)S(1)}, bf16[128,1792]{1,0:T(8,128)(2,1)S(1)}) custom-call(bf16[512,128]{1,0:T(8,128)(2,1)S(1)} %hop.52.refs_5_.refs_0_, bf16[512,128]{1,0:T(8,128)(2,1)S(1)} %collective-permute-done.35.refs_1_, bf16[8,1024,1792]{2,1,0:T(8,128)(2,1)} %get-tuple-element.186.refs_2_.rotated_ref, ...), custom_call_target="tpu_custom_call" | custom-call | flops 7516192768 | bytes 29360128 | tf_op jit(solution)/shard_map/returned/pallas_call | solution.py:260
  226.9 6.0 %returned.14 = (f32[128,1792]{1,0:T(8,128)S(1)}, bf16[128,1792]{1,0:T(8,128)(2,1)S(1)}) custom-call(bf16[512,128]{1,0:T(8,128)(2,1)S(1)} %hop.54.refs_4_.refs_1_.refs_0_, bf16[8,512,1792]{2,1,0:T(8,128)(2,1)} %get-tuple-element.193.refs_1_.rotated_ref, f32[128,1792]{1,0:T(8,128)S(1)} %get-tuple-element.194.refs_2_, ...), custom_call_target="tpu_custom_call" | custom-call | flops 3758096384 | bytes 14680064 | tf_op jit(solution)/shard_map/returned/pallas_call | solution.py:260
  232.9 6.7 %returned.15 = (f32[128,1792]{1,0:T(8,128)S(1)}, bf16[128,1792]{1,0:T(8,128)(2,1)}) custom-call(bf16[512,128]{1,0:T(8,128)(2,1)S(1)} %collective-permute-done.38.refs_0_, bf16[8,512,1792]{2,1,0:T(8,128)(2,1)} %get-tuple-element.192.refs_1_.rotated_ref, f32[128,1792]{1,0:T(8,128)S(1)} %get-tuple-element.195.refs_2_), custom_call_target="tpu_custom_call" | custom-call | flops 3758096384 | bytes 14680064 | tf_op jit(solution)/shard_map/returned/pallas_call | solution.py:260
  239.6 10.9 %returned.16 = (f32[128,1792]{1,0:T(8,128)S(1)}, bf16[128,1792]{1,0:T(8,128)(2,1)}) custom-call(bf16[512,128]{1,0:T(8,128)(2,1)S(1)} %hop.58.refs_4_.refs_2_.refs_0_, bf16[512,128]{1,0:T(8,128)(2,1)S(1)} %collective-permute-done.37.refs_1_, bf16[8,1024,1792]{2,1,0:T(8,128)(2,1)} %get-tuple-element.191.refs_2_.rotated_ref, ...), custom_call_target="tpu_custom_call" | custom-call | flops 7516192768 | bytes 29360128 | tf_op jit(solution)/shard_map/returned/pallas_call | solution.py:260
  250.5 5.9 %returned.17 = (f32[128,1792]{1,0:T(8,128)S(1)}, bf16[128,1792]{1,0:T(8,128)(2,1)S(1)}) custom-call(bf16[512,128]{1,0:T(8,128)(2,1)S(1)} %hop.59.refs_3_.refs_0_, bf16[8,512,1792]{2,1,0:T(8,128)(2,1)} %get-tuple-element.190.refs_1_.rotated_ref, f32[128,1792]{1,0:T(8,128)S(1)} %get-tuple-element.197.refs_2_), custom_call_target="tpu_custom_call" | custom-call | flops 3758096384 | bytes 14680064 | tf_op jit(solution)/shard_map/returned/pallas_call | solution.py:260
  258.5 7.2 %collective-permute-done.41.gram_got_ref = f32[128,128]{1,0:T(8,128)S(1)} collective-permute-done((f32[128,128]{1,0:T(8,128)S(1)}, f32[128,128]{1,0:T(8,128)S(1)}, u32[]{:S(2)}, u32[]{:S(2)}) %collective-permute-start.41) | collective-permute-done | bytes 65568 | tf_op jit(solution)/shard_map/ppermute | solution.py:743
  268.2 7.3 %image.7 = bf16[512,128]{1,0:T(8,128)(2,1)S(1)} custom-call(bf16[1792,128]{1,0:T(8,128)(2,1)S(1)} %normalize.2.basis_ref, bf16[8,512,1792]{2,1,0:T(8,128)(2,1)} %get-tuple-element.180.refs_1_.rotated_ref), custom_call_target="tpu_custom_call" | custom-call | flops 3758096384 | bytes 14680064 | tf_op jit(solution)/shard_map/image/pallas_call | solution.py:217
  276.0 12.7 %image.6 = (f32[512,128]{1,0:T(8,128)S(1)}, bf16[512,128]{1,0:T(8,128)(2,1)S(1)}) custom-call(bf16[1792,128]{1,0:T(8,128)(2,1)S(1)} %normalize.2.basis_ref, bf16[8,1024,1792]{2,1,0:T(8,128)(2,1)} %get-tuple-element.186.refs_2_.rotated_ref), custom_call_target="tpu_custom_call" | custom-call | flops 7516192768 | bytes 29360128 | tf_op jit(solution)/shard_map/image/pallas_call | solution.py:217
  290.8 7.3 %image.8.total_ref.refs_1_ = f32[512,128]{1,0:T(8,128)S(1)} custom-call(bf16[1792,128]{1,0:T(8,128)(2,1)S(1)} %normalize.2.basis_ref, bf16[8,512,1792]{2,1,0:T(8,128)(2,1)} %get-tuple-element.193.refs_1_.rotated_ref, bf16[512,128]{1,0:T(8,128)(2,1)S(1)} %get-tuple-element.203.refs_0_), custom_call_target="tpu_custom_call" | custom-call | flops 3758096384 | bytes 14680064 | tf_op jit(solution)/shard_map/image/pallas_call | solution.py:217
  302.0 7.3 %image.9.refs_1_ = bf16[512,128]{1,0:T(8,128)(2,1)S(1)} custom-call(bf16[1792,128]{1,0:T(8,128)(2,1)S(1)} %normalize.2.basis_ref, bf16[8,512,1792]{2,1,0:T(8,128)(2,1)} %get-tuple-element.192.refs_1_.rotated_ref, bf16[512,128]{1,0:T(8,128)(2,1)S(1)} %get-tuple-element.207.refs_0_, bf16[512,128]{1,0:T(8,128)(2,1)S(1)} %get-tuple-element.205.refs_1_), custom_call_target="tpu_custom_call" | custom-call | flops 3758096384 | bytes 14680064 | tf_op jit(solution)/shard_map/image/pallas_call | solution.py:217
  310.9 13.0 %image.10 = (f32[512,128]{1,0:T(8,128)S(1)}, bf16[512,128]{1,0:T(8,128)(2,1)S(1)}) custom-call(bf16[1792,128]{1,0:T(8,128)(2,1)S(1)} %normalize.2.basis_ref, bf16[8,1024,1792]{2,1,0:T(8,128)(2,1)} %get-tuple-element.191.refs_2_.rotated_ref, bf16[512,128]{1,0:T(8,128)(2,1)S(1)} %hop.64.refs_0_.refs_1_, bf16[512,128]{1,0:T(8,128)(2,1)S(1)} %get-tuple-element.209.refs_1_), custom_call_target="tpu_custom_call" | custom-call | flops 7516192768 | bytes 29360128 | tf_op jit(solution)/shard_map/image/pallas_call | solution.py:217
  327.5 7.3 %image.11.total_ref.refs_1_ = f32[512,128]{1,0:T(8,128)S(1)} custom-call(bf16[1792,128]{1,0:T(8,128)(2,1)S(1)} %normalize.2.basis_ref, bf16[8,512,1792]{2,1,0:T(8,128)(2,1)} %get-tuple-element.190.refs_1_.rotated_ref, bf16[512,128]{1,0:T(8,128)(2,1)S(1)} %hop.66.refs_0_.refs_1_.refs_3_, bf16[512,128]{1,0:T(8,128)(2,1)S(1)} %get-tuple-element.212.refs_1_), custom_call_target="tpu_custom_call" | custom-call | flops 3758096384 | bytes 14680064 | tf_op jit(solution)/shard_map/image/pallas_call | solution.py:217
  339.2 5.9 %returned.18 = (f32[128,1792]{1,0:T(8,128)S(1)}, bf16[128,1792]{1,0:T(8,128)(2,1)S(1)}) custom-call(bf16[512,128]{1,0:T(8,128)(2,1)S(1)} %collective-permute-done.53.refs_0_, bf16[8,512,1792]{2,1,0:T(8,128)(2,1)} %get-tuple-element.180.refs_1_.rotated_ref, bf16[512,128]{1,0:T(8,128)(2,1)S(1)} %get-tuple-element.217.refs_2_, ...), custom_call_target="tpu_custom_call" | custom-call | flops 3758096384 | bytes 14680064 | tf_op jit(solution)/shard_map/returned/pallas_call | solution.py:260
  346.3 10.1 %returned.19 = (f32[128,1792]{1,0:T(8,128)S(1)}, bf16[128,1792]{1,0:T(8,128)(2,1)S(1)}) custom-call(bf16[512,128]{1,0:T(8,128)(2,1)S(1)} %hop.64.refs_0_.refs_1_, bf16[512,128]{1,0:T(8,128)(2,1)S(1)} %collective-permute-done.55.refs_1_.refs_2_, bf16[8,1024,1792]{2,1,0:T(8,128)(2,1)} %get-tuple-element.186.refs_2_.rotated_ref, ...), custom_call_target="tpu_custom_call" | custom-call | flops 7516192768 | bytes 29360128 | tf_op jit(solution)/shard_map/returned/pallas_call | solution.py:260
  372.6 5.9 %returned.21 = (f32[128,1792]{1,0:T(8,128)S(1)}, bf16[128,1792]{1,0:T(8,128)(2,1)S(1)}) custom-call(bf16[512,128]{1,0:T(8,128)(2,1)S(1)} %collective-permute-done.58.refs_4_.refs_0_, bf16[8,512,1792]{2,1,0:T(8,128)(2,1)} %get-tuple-element.192.refs_1_.rotated_ref, f32[128,1792]{1,0:T(8,128)S(1)} %get-tuple-element.228.refs_2_, ...), custom_call_target="tpu_custom_call" | custom-call | flops 3758096384 | bytes 14680064 | tf_op jit(solution)/shard_map/returned/pallas_call | solution.py:260
  384.1 10.9 %returned.22 = (f32[128,1792]{1,0:T(8,128)S(1)}, bf16[128,1792]{1,0:T(8,128)(2,1)}) custom-call(bf16[512,128]{1,0:T(8,128)(2,1)S(1)} %hop.70.refs_4_.refs_2_.refs_5_.refs_0_, bf16[512,128]{1,0:T(8,128)(2,1)S(1)} %collective-permute-done.59.refs_6_.refs_1_, bf16[8,1024,1792]{2,1,0:T(8,128)(2,1)} %get-tuple-element.191.refs_2_.rotated_ref, ...), custom_call_target="tpu_custom_call" | custom-call | flops 7516192768 | bytes 29360128 | tf_op jit(solution)/shard_map/returned/pallas_call | solution.py:260
  395.1 5.9 %returned.23 = (f32[128,1792]{1,0:T(8,128)S(1)}, bf16[128,1792]{1,0:T(8,128)(2,1)S(1)}) custom-call(bf16[512,128]{1,0:T(8,128)(2,1)S(1)} %hop.71.refs_3_.refs_7_.refs_0_, bf16[8,512,1792]{2,1,0:T(8,128)(2,1)} %get-tuple-element.190.refs_1_.rotated_ref, f32[128,1792]{1,0:T(8,128)S(1)} %get-tuple-element.235.refs_2_, ...), custom_call_target="tpu_custom_call" | custom-call | flops 3758096384 | bytes 14680064 | tf_op jit(solution)/shard_map/returned/pallas_call | solution.py:260
  401.7 12.5 %collective-permute-done.64.got_ref = bf16[128,1792]{1,0:T(8,128)(2,1)S(1)} collective-permute-done((bf16[128,1792]{1,0:T(8,128)(2,1)S(1)}, bf16[128,1792]{1,0:T(8,128)(2,1)S(1)}, u32[]{:S(2)}, u32[]{:S(2)}) %collective-permute-start.64) | collective-permute-done | bytes 458784 | tf_op jit(solution)/shard_map/ppermute | solution.py:730
  435.0 8.8 %collective-permute-done.66 = bf16[896,256]{1,0:T(8,128)(2,1)} collective-permute-done((bf16[896,256]{1,0:T(8,128)(2,1)}, bf16[896,256]{1,0:T(8,128)(2,1)}, u32[]{:S(2)}, u32[]{:S(2)}) %collective-permute-start.66) | collective-permute-done | bytes 458784 | tf_op jit(solution)/shard_map/ppermute | solution.py:641
  447.9 12.6 %collective-permute-done.67 = bf16[896,256]{1,0:T(8,128)(2,1)} collective-permute-done((bf16[896,256]{1,0:T(8,128)(2,1)}, bf16[896,256]{1,0:T(8,128)(2,1)}, u32[]{:S(2)}, u32[]{:S(2)}) %collective-permute-start.67) | collective-permute-done | bytes 458784 | tf_op jit(solution)/shard_map/ppermute | solution.py:661
  474.6 7.1 %collective-permute-done.71 = bf16[896,256]{1,0:T(8,128)(2,1)} collective-permute-done((bf16[896,256]{1,0:T(8,128)(2,1)}, bf16[896,256]{1,0:T(8,128)(2,1)}, u32[]{:S(2)}, u32[]{:S(2)}) %collective-permute-start.71) | collective-permute-done | bytes 458784 | tf_op jit(solution)/shard_map/ppermute | solution.py:661
  486.8 6.3 %collective-permute-done.73 = bf16[448,256]{1,0:T(8,128)(2,1)} collective-permute-done((bf16[448,256]{1,0:T(8,128)(2,1)S(1)}, bf16[448,256]{1,0:T(8,128)(2,1)}, u32[]{:S(2)}, u32[]{:S(2)}) %collective-permute-start.73) | collective-permute-done | bytes 229408 | tf_op jit(solution)/shard_map/ppermute | solution.py:661
  508.7 6.3 %collective-permute-done.75.refs_2_ = bf16[896,256]{1,0:T(8,128)(2,1)} collective-permute-done((bf16[896,256]{1,0:T(8,128)(2,1)S(1)}, bf16[896,256]{1,0:T(8,128)(2,1)}, u32[]{:S(2)}, u32[]{:S(2)}) %collective-permute-start.75) | collective-permute-done | bytes 458784 | tf_op jit(solution)/shard_map/ppermute | solution.py:673
  (280 shorter events, 199.9 us)
Async XLA Ops:
  34.5 22.4 %collective-permute-start.13 = (bf16[256,1792]{1,0:T(8,128)(2,1)S(1)}, bf16[256,1792]{1,0:T(8,128)(2,1)}, u32[]{:S(2)}, u32[]{:S(2)}) collective-permute-start(bf16[256,1792]{1,0:T(8,128)(2,1)S(1)} %get-tuple-element.265.refs_1_), channel_id=1, source_target_pairs={{0,2},{1,3},{2,0},{3,1},{4,6},{5,7},{6,4},{7,5},{8,10},{9,11},{10,... | collective-permute-start | bytes 2752520 | tf_op jit(solution)/shard_map/ppermute | solution.py:730
  61.2 80.5 %collective-permute-start.21 = (f32[2048,1792]{1,0:T(8,128)}, f32[2048,1792]{1,0:T(8,128)}, u32[]{:S(2)}, u32[]{:S(2)}) collective-permute-start(f32[2048,1792]{1,0:T(8,128)} %refs_2_.3), channel_id=1, source_target_pairs={{0,1},{1,0},{2,3},{3,2},{4,5},{5,4},{6,7},{7,6},{8,9},{9,8},{10,11... | collective-permute-start | bytes 44040200 | tf_op jit(solution)/shard_map/ppermute | solution.py:594
  62.3 22.2 %collective-permute-start.16 = (bf16[512,256]{1,0:T(8,128)(2,1)}, bf16[512,256]{1,0:T(8,128)(2,1)S(1)}, u32[]{:S(2)}, u32[]{:S(2)}) collective-permute-start(bf16[512,256]{1,0:T(8,128)(2,1)} %copy-done.16), channel_id=1, source_target_pairs={{0,8},{8,0},{16,24},{24,16},{1,9},{9,1},{17,25},{25,17},{2,10},{10... | collective-permute-start | bytes 786440 | tf_op jit(solution)/shard_map/ppermute | solution.py:661
  63.5 21.1 %collective-permute-start.15 = (bf16[512,256]{1,0:T(8,128)(2,1)}, bf16[512,256]{1,0:T(8,128)(2,1)S(1)}, u32[]{:S(2)}, u32[]{:S(2)}) collective-permute-start(bf16[512,256]{1,0:T(8,128)(2,1)} %copy-done.13), channel_id=1, source_target_pairs={{0,16},{8,24},{16,0},{24,8},{1,17},{9,25},{17,1},{25,9},{2,18},{10... | collective-permute-start | bytes 786440 | tf_op jit(solution)/shard_map/ppermute | solution.py:661
  66.1 18.4 %collective-permute-start.11 = (bf16[512,256]{1,0:T(8,128)(2,1)}, bf16[512,256]{1,0:T(8,128)(2,1)S(1)}, u32[]{:S(2)}, u32[]{:S(2)}) collective-permute-start(bf16[512,256]{1,0:T(8,128)(2,1)} %copy-done.24), channel_id=1, source_target_pairs={{0,4},{4,0},{1,5},{5,1},{2,6},{6,2},{3,7},{7,3},{8,12},{12,8},{9,1... | collective-permute-start | bytes 786440 | tf_op jit(solution)/shard_map/ppermute | solution.py:641
  85.9 32.5 %collective-permute-start.14 = (bf16[512,256]{1,0:T(8,128)(2,1)S(1)}, bf16[512,256]{1,0:T(8,128)(2,1)S(1)}, u32[]{:S(2)}, u32[]{:S(2)}) collective-permute-start(bf16[512,256]{1,0:T(8,128)(2,1)S(1)} %get-tuple-element.154.refs_1_.refs_7_), channel_id=1, source_target_pairs={{0,8},{8,0},{16,24},{24,16},{1,9},{9,1},{17,25},{25,17},{2,10},{10... | collective-permute-start | bytes 786440 | tf_op jit(solution)/shard_map/ppermute | solution.py:661
  86.0 34.0 %collective-permute-start.20 = (bf16[512,256]{1,0:T(8,128)(2,1)S(1)}, bf16[512,256]{1,0:T(8,128)(2,1)S(1)}, u32[]{:S(2)}, u32[]{:S(2)}) collective-permute-start(bf16[512,256]{1,0:T(8,128)(2,1)S(1)} %get-tuple-element.157.refs_1_.refs_6_), channel_id=1, source_target_pairs={{0,16},{8,24},{16,0},{24,8},{1,17},{9,25},{17,1},{25,9},{2,18},{10... | collective-permute-start | bytes 786440 | tf_op jit(solution)/shard_map/ppermute | solution.py:661
  87.2 33.8 %collective-permute-start.19 = (bf16[512,128]{1,0:T(8,128)(2,1)S(1)}, bf16[512,128]{1,0:T(8,128)(2,1)S(1)}, u32[]{:S(2)}, u32[]{:S(2)}) collective-permute-start(bf16[512,128]{1,0:T(8,128)(2,1)S(1)} %get-tuple-element.152.refs_1_), channel_id=1, source_target_pairs={{0,4},{4,0},{1,5},{5,1},{2,6},{6,2},{3,7},{7,3},{8,12},{12,8},{9,1... | collective-permute-start | bytes 393224 | tf_op jit(solution)/shard_map/ppermute | solution.py:641
  118.4 18.7 %collective-permute-start.18 = (bf16[512,256]{1,0:T(8,128)(2,1)S(1)}, bf16[512,256]{1,0:T(8,128)(2,1)S(1)}, u32[]{:S(2)}, u32[]{:S(2)}) collective-permute-start(bf16[512,256]{1,0:T(8,128)(2,1)S(1)} %get-tuple-element.160.refs_1_.refs_6_), channel_id=1, source_target_pairs={{0,16},{8,24},{16,0},{24,8},{1,17},{9,25},{17,1},{25,9},{2,18},{10... | collective-permute-start | bytes 786440 | tf_op jit(solution)/shard_map/ppermute | solution.py:661
  118.9 18.9 %collective-permute-start.22 = (bf16[512,128]{1,0:T(8,128)(2,1)S(1)}, bf16[512,128]{1,0:T(8,128)(2,1)S(1)}, u32[]{:S(2)}, u32[]{:S(2)}) collective-permute-start(bf16[512,128]{1,0:T(8,128)(2,1)S(1)} %get-tuple-element.165), channel_id=1, source_target_pairs={{0,4},{4,0},{1,5},{5,1},{2,6},{6,2},{3,7},{7,3},{8,12},{12,8},{9,1... | collective-permute-start | bytes 393224 | tf_op jit(solution)/shard_map/ppermute | solution.py:641
  120.1 21.6 %collective-permute-start.24 = (bf16[512,256]{1,0:T(8,128)(2,1)S(1)}, bf16[512,256]{1,0:T(8,128)(2,1)S(1)}, u32[]{:S(2)}, u32[]{:S(2)}) collective-permute-start(bf16[512,256]{1,0:T(8,128)(2,1)S(1)} %hop.46.refs_1_.refs_5_.refs_0_), channel_id=1, source_target_pairs={{0,4},{4,0},{1,5},{5,1},{2,6},{6,2},{3,7},{7,3},{8,12},{12,8},{9,1... | collective-permute-start | bytes 786440 | tf_op jit(solution)/shard_map/ppermute | solution.py:673
  121.0 17.9 %collective-permute-start.25 = (bf16[512,128]{1,0:T(8,128)(2,1)S(1)}, bf16[512,128]{1,0:T(8,128)(2,1)S(1)}, u32[]{:S(2)}, u32[]{:S(2)}) collective-permute-start(bf16[512,128]{1,0:T(8,128)(2,1)S(1)} %get-tuple-element.162.refs_4_), channel_id=1, source_target_pairs={{0,8},{8,0},{16,24},{24,16},{1,9},{9,1},{17,25},{25,17},{2,10},{10... | collective-permute-start | bytes 393224 | tf_op jit(solution)/shard_map/ppermute | solution.py:661
  137.2 21.7 %collective-permute-start.27 = (bf16[512,256]{1,0:T(8,128)(2,1)S(1)}, bf16[512,256]{1,0:T(8,128)(2,1)S(1)}, u32[]{:S(2)}, u32[]{:S(2)}) collective-permute-start(bf16[512,256]{1,0:T(8,128)(2,1)S(1)} %hop.48.refs_1_.refs_6_.refs_0_), channel_id=1, source_target_pairs={{0,4},{4,0},{1,5},{5,1},{2,6},{6,2},{3,7},{7,3},{8,12},{12,8},{9,1... | collective-permute-start | bytes 786440 | tf_op jit(solution)/shard_map/ppermute | solution.py:673
  137.8 19.4 %collective-permute-start.23 = (bf16[512,128]{1,0:T(8,128)(2,1)S(1)}, bf16[512,128]{1,0:T(8,128)(2,1)S(1)}, u32[]{:S(2)}, u32[]{:S(2)}) collective-permute-start(bf16[512,128]{1,0:T(8,128)(2,1)S(1)} %get-tuple-element.167.refs_1_.refs_5_), channel_id=1, source_target_pairs={{0,8},{8,0},{16,24},{24,16},{1,9},{9,1},{17,25},{25,17},{2,10},{10... | collective-permute-start | bytes 393224 | tf_op jit(solution)/shard_map/ppermute | solution.py:661
  139.0 18.7 %collective-permute-start.28 = (bf16[512,128]{1,0:T(8,128)(2,1)S(1)}, bf16[512,128]{1,0:T(8,128)(2,1)S(1)}, u32[]{:S(2)}, u32[]{:S(2)}) collective-permute-start(bf16[512,128]{1,0:T(8,128)(2,1)S(1)} %get-tuple-element.169.refs_4_), channel_id=1, source_target_pairs={{0,16},{8,24},{16,0},{24,8},{1,17},{9,25},{17,1},{25,9},{2,18},{10... | collective-permute-start | bytes 393224 | tf_op jit(solution)/shard_map/ppermute | solution.py:661
  156.3 27.6 %collective-permute-start.29 = (bf16[512,128]{1,0:T(8,128)(2,1)S(1)}, bf16[512,128]{1,0:T(8,128)(2,1)S(1)}, u32[]{:S(2)}, u32[]{:S(2)}) collective-permute-start(bf16[512,128]{1,0:T(8,128)(2,1)S(1)} %get-tuple-element.170.refs_1_), channel_id=1, source_target_pairs={{0,4},{4,0},{1,5},{5,1},{2,6},{6,2},{3,7},{7,3},{8,12},{12,8},{9,1... | collective-permute-start | bytes 393224 | tf_op jit(solution)/shard_map/ppermute | solution.py:641
  157.2 28.4 %collective-permute-start.26 = (bf16[512,128]{1,0:T(8,128)(2,1)S(1)}, bf16[512,128]{1,0:T(8,128)(2,1)S(1)}, u32[]{:S(2)}, u32[]{:S(2)}) collective-permute-start(bf16[512,128]{1,0:T(8,128)(2,1)S(1)} %get-tuple-element.172.refs_1_.refs_6_), channel_id=1, source_target_pairs={{0,16},{8,24},{16,0},{24,8},{1,17},{9,25},{17,1},{25,9},{2,18},{10... | collective-permute-start | bytes 393224 | tf_op jit(solution)/shard_map/ppermute | solution.py:661
  157.7 47.3 %collective-permute-start.32 = (bf16[512,128]{1,0:T(8,128)(2,1)S(1)}, bf16[512,128]{1,0:T(8,128)(2,1)S(1)}, u32[]{:S(2)}, u32[]{:S(2)}) collective-permute-start(bf16[512,128]{1,0:T(8,128)(2,1)S(1)} %hop.52.refs_5_.refs_0_), channel_id=1, source_target_pairs={{0,4},{4,0},{1,5},{5,1},{2,6},{6,2},{3,7},{7,3},{8,12},{12,8},{9,1... | collective-permute-start | bytes 393224 | tf_op jit(solution)/shard_map/ppermute | solution.py:673
  183.1 18.0 %collective-permute-start.30 = (bf16[512,128]{1,0:T(8,128)(2,1)S(1)}, bf16[512,128]{1,0:T(8,128)(2,1)S(1)}, u32[]{:S(2)}, u32[]{:S(2)}) collective-permute-start(bf16[512,128]{1,0:T(8,128)(2,1)S(1)} %get-tuple-element.177), channel_id=1, source_target_pairs={{0,4},{4,0},{1,5},{5,1},{2,6},{6,2},{3,7},{7,3},{8,12},{12,8},{9,1... | collective-permute-start | bytes 393224 | tf_op jit(solution)/shard_map/ppermute | solution.py:641
  184.0 18.3 %collective-permute-start.33 = (bf16[512,128]{1,0:T(8,128)(2,1)S(1)}, bf16[512,128]{1,0:T(8,128)(2,1)S(1)}, u32[]{:S(2)}, u32[]{:S(2)}) collective-permute-start(bf16[512,128]{1,0:T(8,128)(2,1)S(1)} %get-tuple-element.175.refs_1_.refs_5_), channel_id=1, source_target_pairs={{0,8},{8,0},{16,24},{24,16},{1,9},{9,1},{17,25},{25,17},{2,10},{10... | collective-permute-start | bytes 393224 | tf_op jit(solution)/shard_map/ppermute | solution.py:661
  185.7 26.3 %collective-permute-start.35 = (bf16[512,128]{1,0:T(8,128)(2,1)S(1)}, bf16[512,128]{1,0:T(8,128)(2,1)S(1)}, u32[]{:S(2)}, u32[]{:S(2)}) collective-permute-start(bf16[512,128]{1,0:T(8,128)(2,1)S(1)} %hop.54.refs_4_.refs_1_.refs_0_), channel_id=1, source_target_pairs={{0,4},{4,0},{1,5},{5,1},{2,6},{6,2},{3,7},{7,3},{8,12},{12,8},{9,1... | collective-permute-start | bytes 393224 | tf_op jit(solution)/shard_map/ppermute | solution.py:673
  224.6 14.9 %collective-permute-start.37 = (bf16[512,128]{1,0:T(8,128)(2,1)S(1)}, bf16[512,128]{1,0:T(8,128)(2,1)S(1)}, u32[]{:S(2)}, u32[]{:S(2)}) collective-permute-start(bf16[512,128]{1,0:T(8,128)(2,1)S(1)} %hop.59.refs_3_.refs_0_), channel_id=1, source_target_pairs={{0,4},{4,0},{1,5},{5,1},{2,6},{6,2},{3,7},{7,3},{8,12},{12,8},{9,1... | collective-permute-start | bytes 393224 | tf_op jit(solution)/shard_map/ppermute | solution.py:673
  275.5 14.9 %collective-permute-start.42 = (bf16[512,128]{1,0:T(8,128)(2,1)S(1)}, bf16[512,128]{1,0:T(8,128)(2,1)S(1)}, u32[]{:S(2)}, u32[]{:S(2)}) collective-permute-start(bf16[512,128]{1,0:T(8,128)(2,1)S(1)} %image.7), channel_id=1, source_target_pairs={{0,4},{4,0},{1,5},{5,1},{2,6},{6,2},{3,7},{7,3},{8,12},{12,8},{9,1... | collective-permute-start | bytes 393224 | tf_op jit(solution)/shard_map/ppermute | solution.py:641
  309.3 16.7 %collective-permute-start.48 = (bf16[512,128]{1,0:T(8,128)(2,1)S(1)}, bf16[512,128]{1,0:T(8,128)(2,1)S(1)}, u32[]{:S(2)}, u32[]{:S(2)}) collective-permute-start(bf16[512,128]{1,0:T(8,128)(2,1)S(1)} %image.9.refs_1_), channel_id=1, source_target_pairs={{0,4},{4,0},{1,5},{5,1},{2,6},{6,2},{3,7},{7,3},{8,12},{12,8},{9,1... | collective-permute-start | bytes 393224 | tf_op jit(solution)/shard_map/ppermute | solution.py:641
  310.2 17.2 %collective-permute-start.47 = (bf16[512,128]{1,0:T(8,128)(2,1)S(1)}, bf16[512,128]{1,0:T(8,128)(2,1)S(1)}, u32[]{:S(2)}, u32[]{:S(2)}) collective-permute-start(bf16[512,128]{1,0:T(8,128)(2,1)S(1)} %get-tuple-element.209.refs_1_), channel_id=1, source_target_pairs={{0,16},{8,24},{16,0},{24,8},{1,17},{9,25},{17,1},{25,9},{2,18},{10... | collective-permute-start | bytes 393224 | tf_op jit(solution)/shard_map/ppermute | solution.py:661
  323.9 15.4 %collective-permute-start.53 = (bf16[512,128]{1,0:T(8,128)(2,1)S(1)}, bf16[512,128]{1,0:T(8,128)(2,1)S(1)}, u32[]{:S(2)}, u32[]{:S(2)}) collective-permute-start(bf16[512,128]{1,0:T(8,128)(2,1)S(1)} %hop.64.refs_0_.refs_1_), channel_id=1, source_target_pairs={{0,4},{4,0},{1,5},{5,1},{2,6},{6,2},{3,7},{7,3},{8,12},{12,8},{9,1... | collective-permute-start | bytes 393224 | tf_op jit(solution)/shard_map/ppermute | solution.py:673
  424.5 19.3 %collective-permute-start.66 = (bf16[896,256]{1,0:T(8,128)(2,1)}, bf16[896,256]{1,0:T(8,128)(2,1)}, u32[]{:S(2)}, u32[]{:S(2)}) collective-permute-start(bf16[896,256]{1,0:T(8,128)(2,1)} %get-tuple-element.242), channel_id=1, source_target_pairs={{0,4},{4,0},{1,5},{5,1},{2,6},{6,2},{3,7},{7,3},{8,12},{12,8},{9,1... | collective-permute-start | bytes 1376264 | tf_op jit(solution)/shard_map/ppermute | solution.py:641
  425.0 43.5 %all-to-all-start = ((bf16[8,256,256]{2,1,0:T(8,128)(2,1)}), bf16[8,256,256]{2,1,0:T(8,128)(2,1)}, u32[]{:S(2)}, u32[]{:S(2)}) async-start(bf16[8,256,256]{2,1,0:T(8,128)(2,1)} %broadcast_in_dim.2.refs_0_), calls=%async_computation | async-start | bytes 2097152 | tf_op jit(solution)/shard_map/all_to_all | solution.py:769
  446.1 17.6 %collective-permute-start.68 = (bf16[896,256]{1,0:T(8,128)(2,1)S(1)}, bf16[896,256]{1,0:T(8,128)(2,1)}, u32[]{:S(2)}, u32[]{:S(2)}) collective-permute-start(bf16[896,256]{1,0:T(8,128)(2,1)S(1)} %get-tuple-element.246), channel_id=1, source_target_pairs={{0,4},{4,0},{1,5},{5,1},{2,6},{6,2},{3,7},{7,3},{8,12},{12,8},{9,1... | collective-permute-start | bytes 1376264 | tf_op jit(solution)/shard_map/ppermute | solution.py:641
  466.0 15.7 %collective-permute-start.71 = (bf16[896,256]{1,0:T(8,128)(2,1)}, bf16[896,256]{1,0:T(8,128)(2,1)}, u32[]{:S(2)}, u32[]{:S(2)}) collective-permute-start(bf16[896,256]{1,0:T(8,128)(2,1)} %get-tuple-element.260), channel_id=1, source_target_pairs={{0,8},{8,0},{16,24},{24,16},{1,9},{9,1},{17,25},{25,17},{2,10},{10... | collective-permute-start | bytes 1376264 | tf_op jit(solution)/shard_map/ppermute | solution.py:661
  468.5 27.2 %all-to-all-start.1 = ((bf16[4,512,256]{2,1,0:T(8,128)(2,1)}), bf16[4,512,256]{2,1,0:T(8,128)(2,1)}, u32[]{:S(2)}, u32[]{:S(2)}) async-start(bf16[4,512,256]{2,1,0:T(8,128)(2,1)} %bitcast.4), calls=%async_computation.1 | async-start | bytes 2097152 | tf_op jit(solution)/shard_map/all_to_all | solution.py:772
  504.7 18.3 %all-to-all-start.2 = ((bf16[4,128,256]{1,2,0:T(8,128)(2,1)}), bf16[4,128,256]{1,2,0:T(8,128)(2,1)}, u32[]{:S(2)}, u32[]{:S(2)}) async-start(bf16[4,128,256]{1,2,0:T(8,128)(2,1)} %bitcast.22), calls=%async_computation.2 | async-start | bytes 524288 | tf_op jit(solution)/shard_map/all_to_all | solution.py:708
  (75 other events, 1168.8 us)

commit v10 on v9

--- a/solution.py
+++ b/solution.py
@@ -272,7 +272,8 @@
     )(*images, rotated, *before, *ties)
 
 
-def rotate_out_kernel(n_dp, place_ref, query_ref, eigen_ref, *refs):
+def rotate_out_kernel(n_dp, n_ties, place_ref, query_ref, eigen_ref, *refs):
+    refs = refs[n_ties:]
     turned = refs[-1]
     width = eigen_ref.shape[1]
     rows = width // (PIECES * n_dp)
@@ -294,7 +295,7 @@
                     keep_ref[...] = taken.astype(keep_ref.dtype)
 
 
-def rotate_out(place, query_out, eigen_out, n_dp):
+def rotate_out(place, query_out, eigen_out, n_dp, ties):
     width = eigen_out.shape[1]
     rows = width // (PIECES * n_dp)
     shapes = []
@@ -304,37 +305,35 @@
             shapes.append(jax.ShapeDtypeStruct((rows, TOKS), kind))
     vmem = pl.BlockSpec(memory_space=pltpu.VMEM)
     return pl.pallas_call(
-        functools.partial(rotate_out_kernel, n_dp),
-        in_specs=[pl.BlockSpec(memory_space=pltpu.SMEM), vmem, vmem],
+        functools.partial(rotate_out_kernel, n_dp, len(ties)),
+        in_specs=[pl.BlockSpec(memory_space=pltpu.SMEM), vmem, vmem] + tied(ties),
         out_specs=[vmem] * len(shapes),
         out_shape=shapes,
         scratch_shapes=[pltpu.VMEM((width, TOKS), f32)],
         compiler_params=params(),
         name="rotate_out",
-    )(place, query_out, eigen_out)
-
-
-def rotate_in_kernel(n_ties, place_ref, query_ref, eigen_ref, *refs):
-    theirs_ref, mine_ref, product = refs[n_ties:]
+    )(place, query_out, eigen_out, *ties)
+
+
+def rotate_in_kernel(place_ref, query_ref, eigen_ref, theirs_ref, mine_ref, product):
     product[...] = jnp.dot(query_ref[...], eigen_ref[...], preferred_element_type=f32)
     for out_ref, index in ((theirs_ref, 1 - place_ref[1]), (mine_ref, place_ref[1])):
         out_ref[...] = product[pl.ds(pl.multiple_of(index * TOKS, TOKS), TOKS), :]
 
 
-def rotate_in(place, query_in, eigen_in, ties):
+def rotate_in(place, query_in, eigen_in):
     depth, cols = eigen_in.shape
     width = LANES if cols % LANES == 0 else cols
     out = jax.ShapeDtypeStruct((TOKS, cols), f32)
     return pl.pallas_call(
-        functools.partial(rotate_in_kernel, len(ties)),
+        rotate_in_kernel,
         grid_spec=pltpu.PrefetchScalarGridSpec(
             num_scalar_prefetch=1,
             grid=(cols // width,),
             in_specs=[
                 pl.BlockSpec(query_in.shape, lambda at, _: (0, 0)),
                 pl.BlockSpec((depth, width), lambda at, _: (0, at)),
-            ]
-            + tied(ties),
+            ],
             out_specs=[pl.BlockSpec((TOKS, width), lambda at, _: (0, at))] * 2,
             scratch_shapes=[pltpu.VMEM((CORES * TOKS, width), f32)],
         ),
@@ -344,7 +343,7 @@
             flops=2 * depth * cols * CORES * TOKS, bytes_accessed=2 * depth * cols, transcendentals=0
         ),
         name="rotate_in",
-    )(place, query_in, eigen_in, *ties)
+    )(place, query_in, eigen_in)
 
 
 def side_by_side(place_ref, mine, theirs):
@@ -355,7 +354,8 @@
     )
 
 
-def factor_kernel(place_ref, eigen_ref, mine_ref, theirs_ref, send_ref, keep_ref, cols):
+def factor_kernel(n_ties, place_ref, eigen_ref, mine_ref, theirs_ref, *refs):
+    send_ref, keep_ref, cols = refs[n_ties:]
     part, parts = pl.program_id(0), pl.num_programs(0)
 
     @pl.when(part == 0)
@@ -373,7 +373,7 @@
         keep_ref[...] = product
 
 
-def factor_piece(place, eigen_in, mine, theirs, piece, n_dp):
+def factor_piece(place, eigen_in, mine, theirs, piece, n_dp, ties):
     rows, depth = eigen_in.shape
     rows = rows // (FACTOR_PIECES * n_dp)
     width = CORES * COLS
@@ -383,11 +383,11 @@
         return piece * n_dp + lax.rem(place_ref[0] + 1 + part, n_dp), 0
 
     return pl.pallas_call(
-        factor_kernel,
+        functools.partial(factor_kernel, len(ties)),
         grid_spec=pltpu.PrefetchScalarGridSpec(
             num_scalar_prefetch=1,
             grid=(n_dp,),
-            in_specs=[pl.BlockSpec((rows, depth), eigen_block), fixed, fixed],
+            in_specs=[pl.BlockSpec((rows, depth), eigen_block), fixed, fixed] + tied(ties),
             out_specs=[
                 pl.BlockSpec((rows, width), lambda part, _: (jnp.minimum(part, n_dp - 2), 0)),
                 pl.BlockSpec((rows, width), lambda part, _: (0, 0)),
@@ -400,7 +400,7 @@
         ],
         compiler_params=params(),
         name="factor",
-    )(place, eigen_in, mine, theirs)
+    )(place, eigen_in, mine, theirs, *ties)
 
 
 def write_shares(place_ref, total, keep_ref, send_refs):
@@ -599,7 +599,7 @@
 
 
 def hop_kernel(n_got, n_ties, total_ref, *refs):
-    total = total_ref[...]
+    total = total_ref[...].astype(f32)
     for ref in refs[:n_got]:
         total = total + ref[...].astype(f32)
     rounded_ref, *total_refs = refs[n_got + n_ties :]
@@ -645,17 +645,13 @@
         total, step, odd = self.keep, 1, lax.axis_index("grp") % 2
         while True:
             last = step >= n_grp
-            if even:
-                total = after(total, others)
-                for part in got:
-                    total = total + part.astype(f32)
-                if step == 2:
-                    total = lax.dynamic_slice_in_dim(total, odd * (rows // 2), rows // 2, 0)
-                own = sent = total.astype(bf16)
-                total = sent.astype(f32)
+            if even and step == 2:
+                total = after(total, others).astype(f32) + got[0].astype(f32)
+                total = lax.dynamic_slice_in_dim(total, odd * (rows // 2), rows // 2, 0)
+                own = sent = total = total.astype(bf16)
             else:
-                sent, *totals = hop_sum(total, got, others, last)
-                own, total = sent, totals[0] if totals else None
+                sent, *totals = hop_sum(total, got, others, last or even)
+                own, total = sent, totals[0] if totals else sent
             if last:
                 break
             got = [lax.ppermute(sent, "grp", crossed(n_grp, step))]
@@ -764,8 +760,7 @@
                 share = share + send.astype(f32)
             share = share.astype(bf16)
             piece_rows = share.shape[0]
-            others = yield [share]
-            copies = jnp.broadcast_to(after(share, others)[None], (n_gd,) + share.shape)
+            copies = jnp.broadcast_to(share[None], (n_gd,) + share.shape)
             gathered = lax.all_to_all(copies, GD, 0, 0, tiled=True)
             gathered = gathered.reshape(n_gd * piece_rows, -1)
             others = yield [copies]
@@ -782,10 +777,10 @@
 
         found = {}
         count = CORES * PIECES
-        pieces = list(rotate_out(place, query_out, eigen_out, n_dp))
+        theirs_in, mine_in = rotate_in(place, query_in, eigen_in)
+        pieces = list(rotate_out(place, query_out, eigen_out, n_dp, [mine_in]))
         own_pieces, their_pieces = pieces[: 2 * PIECES], pieces[2 * PIECES :]
         turning = [Reduction(own_pieces[0], n_grp, n_dp, keep=own_pieces[1])]
-        theirs_in, mine_in = rotate_in(place, query_in, eigen_in, pieces[:1])
         theirs_in = swap_cores(theirs_in, n_width)
         their_pieces = [swap_cores(each, n_width) for each in their_pieces]
         hidden = (jax.nn.silu(gate_pre.astype(f32)) * up_pre.astype(f32)).astype(bf16)
@@ -848,7 +843,7 @@
                 ties = boundary([rounded], summing)
                 if path is None and all(each.own is not None for each in summing):
                     path = Steps(output_side(summing, iteration == ITERS - 1))
-                if path is not None and path.count < 5:
+                if path is not None and path.count < 4:
                     ties = ties + path.advance([rounded])
             while "inverse" not in found:
                 path.advance([])
@@ -859,7 +854,7 @@
         their_basis = swap_cores(basis, n_width)
         factors, last = [], []
         for piece in range(FACTOR_PIECES):
-            sends, keep = factor_piece(place, eigen_in, basis, their_basis, piece, n_dp)
+            sends, keep = factor_piece(place, eigen_in, basis, their_basis, piece, n_dp, [])
             if piece:
                 last = boundary([keep], factors)
             factors.append(Reduction(sends, n_grp, n_dp, True, keep))

time: 533 us -> 527 us (0.989); the launches traced: 529 us -> 517 us
  other arithmetic: 20.5 us -> 12.2 us
    convert_element_type x6 -> x2, other arithmetic: 9.8 us -> 2.68 us  [run(): own = sent = total = total.astype(bf16)]
    unnamed x50 -> x38, local copies, waits for them, and re-layouts: 12.9 us -> 9.7 us
  transfers between devices with their start and end apart: 82 -> 82, of which waited for: 23 -> 23; matrix products, arithmetic and copies ran while one was open for 4% -> 3% of each run, Pallas kernels for 44% -> 48%
where the time goes in v10:
time: 527 us; the launch traced here: 517 us
  Pallas kernels  299 us (57%)
  starting transfers between devices  96.9 us (18%)
  waiting for transfers between devices  92 us (17%)
  local copies, waits for them, and re-layouts  14.1 us (3%)
  other arithmetic  12.2 us (2%)
    pallas_call x6, Pallas kernels, form_parts(): pl.pallas_call(functools.partial(form_kernel, n_keep, n_parts, len(ties))...  107 us
    pallas_call x12, Pallas kernels, return_parts(): pl.pallas_call(functools.partial(return_kernel, n_parts, not before), in_...  91.1 us
    pallas_call x6, Pallas kernels, image_parts(): pl.pallas_call(functools.partial(image_kernel, n_keep, len(ties)), grid=(...  54.8 us
    ppermute x28, starting transfers between devices, run(): got = [lax.ppermute(sent, 'grp', crossed(n_grp, step))]  38.3 us
    ppermute x28, waiting for transfers between devices, run(): got = [lax.ppermute(sent, 'grp', crossed(n_grp, step))]  25.5 us
    ppermute x14, waiting for transfers between devices, run(): lax.ppermute(sends[at * rows:(at + 1) * rows], 'dp', turned_by(n_dp, at +...  18.8 us
    ppermute x14, starting transfers between devices, run(): lax.ppermute(sends[at * rows:(at + 1) * rows], 'dp', turned_by(n_dp, at +...  15.3 us
    ppermute x14, waiting for transfers between devices, run(): lax.ppermute(own, 'dp', turned_by(n_dp, n_dp - 1 - at))  14 us
  transfers between devices with their start and end apart: 82, of which 23 were waited for; matrix products, arithmetic and copies ran while one was open for 3% of the time, Pallas kernels for 48%

profile of v10, /device:TPU:0, one launch (start us, length us, event | category | flops | bytes accessed | tf_op | source)
XLA Modules:
  0.0 517.2 jit_solution(2471978676194861070)
XLA Ops:
  0.7 12.5 %rotate_in.1 = (f32[256,1792]{1,0:T(8,128)S(1)}, f32[256,1792]{1,0:T(8,128)S(1)}) custom-call(s32[3]{0:T(128)S(1)} %pad_add_fusion.place_ref, bf16[512,3584]{1,0:T(8,128)(2,1)} %query_ref.2, bf16[3584,1792]{1,0:T(8,128)(2,1)} %eigen_ref.9), custom_call_target="tpu_custom_call" | custom-call | flops 6576668672 | bytes 12845056 | tf_op jit(solution)/shard_map/rotate_in/pallas_call | solution.py:328
  21.5 7.0 %collective-permute-done.2.refs_0_ = bf16[512,256]{1,0:T(8,128)(2,1)S(1)} collective-permute-done((bf16[512,256]{1,0:T(8,128)(2,1)S(1)}, bf16[512,256]{1,0:T(8,128)(2,1)S(1)}, u32[]{:S(2)}, u32[]{:S(2)}) %collective-permute-start.2) | collective-permute-done | bytes 262176 | tf_op jit(solution)/shard_map/ppermute | solution.py:641
  68.2 14.7 %form.6 = (bf16[8,512,1792]{2,1,0:T(8,128)(2,1)}, bf16[512,128]{1,0:T(8,128)(2,1)S(1)}) custom-call(s32[3]{0:T(128)S(1)} %pad_add_fusion.place_ref, bf16[512,256]{1,0:T(8,128)(2,1)S(1)} %copy-done.15, bf16[256,1792]{1,0:T(8,128)(2,1)S(1)} %add_convert_fusion.refs_1_.refs_2_, f32[2048,1792]{1,0:T(8,128)} %refs_2_.3, ...), custom_call_target="tpu_custom_call" | custom-call | flops 5872025600 | bytes 14680064 | tf_op jit(solution)/shard_map/form/pallas_call | solution.py:138
  92.4 24.2 %form.7 = (bf16[8,1024,1792]{2,1,0:T(8,128)(2,1)}, f32[512,128]{1,0:T(8,128)S(1)}, bf16[512,128]{1,0:T(8,128)(2,1)S(1)}) custom-call(s32[3]{0:T(128)S(1)} %pad_add_fusion.place_ref, bf16[512,256]{1,0:T(8,128)(2,1)S(1)} %copy-done.8, bf16[512,256]{1,0:T(8,128)(2,1)S(1)} %collective-permute-done.17.refs_1_, ...), custom_call_target="tpu_custom_call" | custom-call | flops 11744051200 | bytes 29360128 | tf_op jit(solution)/shard_map/form/pallas_call | solution.py:138
  121.0 14.5 %form.8 = (bf16[8,512,1792]{2,1,0:T(8,128)(2,1)}, f32[512,128]{1,0:T(8,128)S(1)}) custom-call(s32[3]{0:T(128)S(1)} %pad_add_fusion.place_ref, bf16[512,256]{1,0:T(8,128)(2,1)S(1)} %hop.48.refs_5_.refs_0_, bf16[256,1792]{1,0:T(8,128)(2,1)S(1)} %add_convert_fusion.refs_1_.refs_2_, f32[2048,1792]{1,0:T(8,128)} %refs_2_.3, ...), custom_call_target="tpu_custom_call" | custom-call | flops 5872025600 | bytes 14680064 | tf_op jit(solution)/shard_map/form/pallas_call | solution.py:138
  139.9 14.7 %form.9 = (bf16[8,512,1792]{2,1,0:T(8,128)(2,1)}, bf16[512,128]{1,0:T(8,128)(2,1)S(1)}) custom-call(s32[3]{0:T(128)S(1)} %pad_add_fusion.place_ref, bf16[512,256]{1,0:T(8,128)(2,1)S(1)} %collective-permute-done.24.refs_0_, bf16[256,1792]{1,0:T(8,128)(2,1)S(1)} %add_convert_fusion.refs_1_.refs_2_, f32[2048,1792]{1,0:T(8,128)} %collective-permute-done.21.refs_2_.refs_3_, ...), custom_call_target="tpu_custom_call" | custom-call | flops 5872025600 | bytes 14680064 | tf_op jit(solution)/shard_map/form/pallas_call | solution.py:138
  157.2 24.2 %form.10 = (bf16[8,1024,1792]{2,1,0:T(8,128)(2,1)}, f32[512,128]{1,0:T(8,128)S(1)}, bf16[512,128]{1,0:T(8,128)(2,1)S(1)}) custom-call(s32[3]{0:T(128)S(1)} %pad_add_fusion.place_ref, bf16[512,256]{1,0:T(8,128)(2,1)S(1)} %hop.50.refs_1_.refs_5_.refs_0_, bf16[512,256]{1,0:T(8,128)(2,1)S(1)} %collective-permute-done.27.refs_1_, ...), custom_call_target="tpu_custom_call" | custom-call | flops 11744051200 | bytes 29360128 | tf_op jit(solution)/shard_map/form/pallas_call | solution.py:138
  184.7 14.8 %form.11 = (bf16[8,512,1792]{2,1,0:T(8,128)(2,1)}, f32[512,128]{1,0:T(8,128)S(1)}) custom-call(s32[3]{0:T(128)S(1)} %pad_add_fusion.place_ref, bf16[512,256]{1,0:T(8,128)(2,1)S(1)} %hop.52.refs_1_.refs_6_.refs_0_, bf16[256,1792]{1,0:T(8,128)(2,1)S(1)} %add_convert_fusion.refs_1_.refs_2_, f32[2048,1792]{1,0:T(8,128)} %collective-permute-done.21.refs_2_.refs_3_, ...), custom_call_target="tpu_custom_call" | custom-call | flops 5872025600 | bytes 14680064 | tf_op jit(solution)/shard_map/form/pallas_call | solution.py:138
  203.3 5.9 %returned.12 = (f32[128,1792]{1,0:T(8,128)S(1)}, bf16[128,1792]{1,0:T(8,128)(2,1)S(1)}) custom-call(bf16[512,128]{1,0:T(8,128)(2,1)S(1)} %collective-permute-done.32.refs_0_, bf16[8,512,1792]{2,1,0:T(8,128)(2,1)} %get-tuple-element.175.refs_1_.rotated_ref, bf16[512,128]{1,0:T(8,128)(2,1)S(1)} %get-tuple-element.177.refs_2_, ...), custom_call_target="tpu_custom_call" | custom-call | flops 3758096384 | bytes 14680064 | tf_op jit(solution)/shard_map/returned/pallas_call | solution.py:260
  210.4 10.1 %returned.13 = (f32[128,1792]{1,0:T(8,128)S(1)}, bf16[128,1792]{1,0:T(8,128)(2,1)S(1)}) custom-call(bf16[512,128]{1,0:T(8,128)(2,1)S(1)} %hop.56.refs_5_.refs_0_, bf16[512,128]{1,0:T(8,128)(2,1)S(1)} %collective-permute-done.35.refs_1_, bf16[8,1024,1792]{2,1,0:T(8,128)(2,1)} %get-tuple-element.181.refs_2_.rotated_ref, ...), custom_call_target="tpu_custom_call" | custom-call | flops 7516192768 | bytes 29360128 | tf_op jit(solution)/shard_map/returned/pallas_call | solution.py:260
  225.2 6.0 %returned.14 = (f32[128,1792]{1,0:T(8,128)S(1)}, bf16[128,1792]{1,0:T(8,128)(2,1)S(1)}) custom-call(bf16[512,128]{1,0:T(8,128)(2,1)S(1)} %hop.58.refs_4_.refs_1_.refs_0_, bf16[8,512,1792]{2,1,0:T(8,128)(2,1)} %get-tuple-element.188.refs_1_.rotated_ref, f32[128,1792]{1,0:T(8,128)S(1)} %get-tuple-element.189.refs_2_, ...), custom_call_target="tpu_custom_call" | custom-call | flops 3758096384 | bytes 14680064 | tf_op jit(solution)/shard_map/returned/pallas_call | solution.py:260
  231.2 6.7 %returned.15 = (f32[128,1792]{1,0:T(8,128)S(1)}, bf16[128,1792]{1,0:T(8,128)(2,1)}) custom-call(bf16[512,128]{1,0:T(8,128)(2,1)S(1)} %collective-permute-done.38.refs_0_, bf16[8,512,1792]{2,1,0:T(8,128)(2,1)} %get-tuple-element.187.refs_1_.rotated_ref, f32[128,1792]{1,0:T(8,128)S(1)} %get-tuple-element.190.refs_2_), custom_call_target="tpu_custom_call" | custom-call | flops 3758096384 | bytes 14680064 | tf_op jit(solution)/shard_map/returned/pallas_call | solution.py:260
  237.9 10.9 %returned.16 = (f32[128,1792]{1,0:T(8,128)S(1)}, bf16[128,1792]{1,0:T(8,128)(2,1)}) custom-call(bf16[512,128]{1,0:T(8,128)(2,1)S(1)} %hop.62.refs_4_.refs_2_.refs_0_, bf16[512,128]{1,0:T(8,128)(2,1)S(1)} %collective-permute-done.37.refs_1_, bf16[8,1024,1792]{2,1,0:T(8,128)(2,1)} %get-tuple-element.186.refs_2_.rotated_ref, ...), custom_call_target="tpu_custom_call" | custom-call | flops 7516192768 | bytes 29360128 | tf_op jit(solution)/shard_map/returned/pallas_call | solution.py:260
  248.8 5.9 %returned.17 = (f32[128,1792]{1,0:T(8,128)S(1)}, bf16[128,1792]{1,0:T(8,128)(2,1)S(1)}) custom-call(bf16[512,128]{1,0:T(8,128)(2,1)S(1)} %hop.63.refs_3_.refs_0_, bf16[8,512,1792]{2,1,0:T(8,128)(2,1)} %get-tuple-element.185.refs_1_.rotated_ref, f32[128,1792]{1,0:T(8,128)S(1)} %get-tuple-element.192.refs_2_), custom_call_target="tpu_custom_call" | custom-call | flops 3758096384 | bytes 14680064 | tf_op jit(solution)/shard_map/returned/pallas_call | solution.py:260
  256.9 7.2 %collective-permute-done.41.gram_got_ref = f32[128,128]{1,0:T(8,128)S(1)} collective-permute-done((f32[128,128]{1,0:T(8,128)S(1)}, f32[128,128]{1,0:T(8,128)S(1)}, u32[]{:S(2)}, u32[]{:S(2)}) %collective-permute-start.41) | collective-permute-done | bytes 65568 | tf_op jit(solution)/shard_map/ppermute | solution.py:739
  266.5 7.3 %image.7 = bf16[512,128]{1,0:T(8,128)(2,1)S(1)} custom-call(bf16[1792,128]{1,0:T(8,128)(2,1)S(1)} %normalize.2.basis_ref, bf16[8,512,1792]{2,1,0:T(8,128)(2,1)} %get-tuple-element.175.refs_1_.rotated_ref), custom_call_target="tpu_custom_call" | custom-call | flops 3758096384 | bytes 14680064 | tf_op jit(solution)/shard_map/image/pallas_call | solution.py:217
  274.4 12.7 %image.6 = (f32[512,128]{1,0:T(8,128)S(1)}, bf16[512,128]{1,0:T(8,128)(2,1)S(1)}) custom-call(bf16[1792,128]{1,0:T(8,128)(2,1)S(1)} %normalize.2.basis_ref, bf16[8,1024,1792]{2,1,0:T(8,128)(2,1)} %get-tuple-element.181.refs_2_.rotated_ref), custom_call_target="tpu_custom_call" | custom-call | flops 7516192768 | bytes 29360128 | tf_op jit(solution)/shard_map/image/pallas_call | solution.py:217
  289.2 7.3 %image.8.total_ref.refs_1_ = f32[512,128]{1,0:T(8,128)S(1)} custom-call(bf16[1792,128]{1,0:T(8,128)(2,1)S(1)} %normalize.2.basis_ref, bf16[8,512,1792]{2,1,0:T(8,128)(2,1)} %get-tuple-element.188.refs_1_.rotated_ref, bf16[512,128]{1,0:T(8,128)(2,1)S(1)} %get-tuple-element.198.refs_0_), custom_call_target="tpu_custom_call" | custom-call | flops 3758096384 | bytes 14680064 | tf_op jit(solution)/shard_map/image/pallas_call | solution.py:217
  300.3 7.3 %image.9.refs_1_ = bf16[512,128]{1,0:T(8,128)(2,1)S(1)} custom-call(bf16[1792,128]{1,0:T(8,128)(2,1)S(1)} %normalize.2.basis_ref, bf16[8,512,1792]{2,1,0:T(8,128)(2,1)} %get-tuple-element.187.refs_1_.rotated_ref, bf16[512,128]{1,0:T(8,128)(2,1)S(1)} %get-tuple-element.202.refs_0_, bf16[512,128]{1,0:T(8,128)(2,1)S(1)} %get-tuple-element.200.refs_1_), custom_call_target="tpu_custom_call" | custom-call | flops 3758096384 | bytes 14680064 | tf_op jit(solution)/shard_map/image/pallas_call | solution.py:217
  309.3 13.0 %image.10 = (f32[512,128]{1,0:T(8,128)S(1)}, bf16[512,128]{1,0:T(8,128)(2,1)S(1)}) custom-call(bf16[1792,128]{1,0:T(8,128)(2,1)S(1)} %normalize.2.basis_ref, bf16[8,1024,1792]{2,1,0:T(8,128)(2,1)} %get-tuple-element.186.refs_2_.rotated_ref, bf16[512,128]{1,0:T(8,128)(2,1)S(1)} %hop.68.refs_0_.refs_1_, bf16[512,128]{1,0:T(8,128)(2,1)S(1)} %get-tuple-element.204.refs_1_), custom_call_target="tpu_custom_call" | custom-call | flops 7516192768 | bytes 29360128 | tf_op jit(solution)/shard_map/image/pallas_call | solution.py:217
  325.8 7.3 %image.11.total_ref.refs_1_ = f32[512,128]{1,0:T(8,128)S(1)} custom-call(bf16[1792,128]{1,0:T(8,128)(2,1)S(1)} %normalize.2.basis_ref, bf16[8,512,1792]{2,1,0:T(8,128)(2,1)} %get-tuple-element.185.refs_1_.rotated_ref, bf16[512,128]{1,0:T(8,128)(2,1)S(1)} %hop.70.refs_0_.refs_1_.refs_3_, bf16[512,128]{1,0:T(8,128)(2,1)S(1)} %get-tuple-element.207.refs_1_), custom_call_target="tpu_custom_call" | custom-call | flops 3758096384 | bytes 14680064 | tf_op jit(solution)/shard_map/image/pallas_call | solution.py:217
  337.6 5.9 %returned.18 = (f32[128,1792]{1,0:T(8,128)S(1)}, bf16[128,1792]{1,0:T(8,128)(2,1)S(1)}) custom-call(bf16[512,128]{1,0:T(8,128)(2,1)S(1)} %collective-permute-done.53.refs_0_, bf16[8,512,1792]{2,1,0:T(8,128)(2,1)} %get-tuple-element.175.refs_1_.rotated_ref, bf16[512,128]{1,0:T(8,128)(2,1)S(1)} %get-tuple-element.212.refs_2_, ...), custom_call_target="tpu_custom_call" | custom-call | flops 3758096384 | bytes 14680064 | tf_op jit(solution)/shard_map/returned/pallas_call | solution.py:260
  344.6 10.1 %returned.19 = (f32[128,1792]{1,0:T(8,128)S(1)}, bf16[128,1792]{1,0:T(8,128)(2,1)S(1)}) custom-call(bf16[512,128]{1,0:T(8,128)(2,1)S(1)} %hop.68.refs_0_.refs_1_, bf16[512,128]{1,0:T(8,128)(2,1)S(1)} %collective-permute-done.55.refs_1_.refs_2_, bf16[8,1024,1792]{2,1,0:T(8,128)(2,1)} %get-tuple-element.181.refs_2_.rotated_ref, ...), custom_call_target="tpu_custom_call" | custom-call | flops 7516192768 | bytes 29360128 | tf_op jit(solution)/shard_map/returned/pallas_call | solution.py:260
  361.0 5.9 %returned.20 = (f32[128,1792]{1,0:T(8,128)S(1)}, bf16[128,1792]{1,0:T(8,128)(2,1)S(1)}) custom-call(bf16[512,128]{1,0:T(8,128)(2,1)S(1)} %hop.70.refs_0_.refs_1_.refs_3_, bf16[8,512,1792]{2,1,0:T(8,128)(2,1)} %get-tuple-element.188.refs_1_.rotated_ref, f32[128,1792]{1,0:T(8,128)S(1)} %get-tuple-element.219.refs_2_, ...), custom_call_target="tpu_custom_call" | custom-call | flops 3758096384 | bytes 14680064 | tf_op jit(solution)/shard_map/returned/pallas_call | solution.py:260
  371.0 5.9 %returned.21 = (f32[128,1792]{1,0:T(8,128)S(1)}, bf16[128,1792]{1,0:T(8,128)(2,1)S(1)}) custom-call(bf16[512,128]{1,0:T(8,128)(2,1)S(1)} %collective-permute-done.58.refs_4_.refs_0_, bf16[8,512,1792]{2,1,0:T(8,128)(2,1)} %get-tuple-element.187.refs_1_.rotated_ref, f32[128,1792]{1,0:T(8,128)S(1)} %get-tuple-element.223.refs_2_, ...), custom_call_target="tpu_custom_call" | custom-call | flops 3758096384 | bytes 14680064 | tf_op jit(solution)/shard_map/returned/pallas_call | solution.py:260
  382.5 10.9 %returned.22 = (f32[128,1792]{1,0:T(8,128)S(1)}, bf16[128,1792]{1,0:T(8,128)(2,1)}) custom-call(bf16[512,128]{1,0:T(8,128)(2,1)S(1)} %hop.74.refs_4_.refs_2_.refs_5_.refs_0_, bf16[512,128]{1,0:T(8,128)(2,1)S(1)} %collective-permute-done.59.refs_6_.refs_1_, bf16[8,1024,1792]{2,1,0:T(8,128)(2,1)} %get-tuple-element.186.refs_2_.rotated_ref, ...), custom_call_target="tpu_custom_call" | custom-call | flops 7516192768 | bytes 29360128 | tf_op jit(solution)/shard_map/returned/pallas_call | solution.py:260
  394.5 6.7 %returned.23 = (f32[128,1792]{1,0:T(8,128)S(1)}, bf16[128,1792]{1,0:T(8,128)(2,1)}) custom-call(bf16[512,128]{1,0:T(8,128)(2,1)S(1)} %hop.75.refs_3_.refs_7_.refs_0_, bf16[8,512,1792]{2,1,0:T(8,128)(2,1)} %get-tuple-element.185.refs_1_.rotated_ref, f32[128,1792]{1,0:T(8,128)S(1)} %get-tuple-element.230.refs_2_, bf16[8,256,256]{2,1,0:T(8,128)(2,1)} %broadcast_in_dim.2.refs_3_), custom_call_target="tpu_custom_call" | custom-call | flops 3758096384 | bytes 14680064 | tf_op jit(solution)/shard_map/returned/pallas_call | solution.py:260
  406.2 8.5 %collective-permute-done.64.got_ref = bf16[128,1792]{1,0:T(8,128)(2,1)S(1)} collective-permute-done((bf16[128,1792]{1,0:T(8,128)(2,1)}, bf16[128,1792]{1,0:T(8,128)(2,1)S(1)}, u32[]{:S(2)}, u32[]{:S(2)}) %collective-permute-start.64) | collective-permute-done | bytes 458784 | tf_op jit(solution)/shard_map/ppermute | solution.py:726
  428.2 7.8 %collective-permute-done.66.refs_0_ = bf16[896,256]{1,0:T(8,128)(2,1)S(1)} collective-permute-done((bf16[896,256]{1,0:T(8,128)(2,1)S(1)}, bf16[896,256]{1,0:T(8,128)(2,1)S(1)}, u32[]{:S(2)}, u32[]{:S(2)}) %collective-permute-start.66) | collective-permute-done | bytes 458784 | tf_op jit(solution)/shard_map/ppermute | solution.py:641
  437.4 11.3 %collective-permute-done.67 = bf16[896,256]{1,0:T(8,128)(2,1)} collective-permute-done((bf16[896,256]{1,0:T(8,128)(2,1)S(1)}, bf16[896,256]{1,0:T(8,128)(2,1)}, u32[]{:S(2)}, u32[]{:S(2)}) %collective-permute-start.67) | collective-permute-done | bytes 458784 | tf_op jit(solution)/shard_map/ppermute | solution.py:657
  458.5 7.8 %collective-permute-done.68.refs_0_ = bf16[448,256]{1,0:T(8,128)(2,1)S(1)} collective-permute-done((bf16[448,256]{1,0:T(8,128)(2,1)}, bf16[448,256]{1,0:T(8,128)(2,1)S(1)}, u32[]{:S(2)}, u32[]{:S(2)}) %collective-permute-start.68) | collective-permute-done | bytes 229408 | tf_op jit(solution)/shard_map/ppermute | solution.py:657
  496.0 6.2 %collective-permute-done.75.refs_2_ = bf16[896,256]{1,0:T(8,128)(2,1)S(1)} collective-permute-done((bf16[896,256]{1,0:T(8,128)(2,1)S(1)}, bf16[896,256]{1,0:T(8,128)(2,1)S(1)}, u32[]{:S(2)}, u32[]{:S(2)}) %collective-permute-start.75) | collective-permute-done | bytes 458784 | tf_op jit(solution)/shard_map/ppermute | solution.py:669
  (268 shorter events, 193.9 us)
Async XLA Ops:
  13.2 15.3 %collective-permute-start.4 = (f32[256,1792]{1,0:T(8,128)S(1)}, f32[256,1792]{1,0:T(8,128)S(1)}, u32[]{:S(2)}, u32[]{:S(2)}) collective-permute-start(f32[256,1792]{1,0:T(8,128)S(1)} %get-tuple-element.135), channel_id=1, source_target_pairs={{0,1},{1,0},{2,3},{3,2},{4,5},{5,4},{6,7},{7,6},{8,9},{9,8},{10,11... | collective-permute-start | bytes 5505032 | tf_op jit(solution)/shard_map/ppermute | solution.py:594
  32.1 14.6 %collective-permute-start.8 = (bf16[512,256]{1,0:T(8,128)(2,1)S(1)}, bf16[512,256]{1,0:T(8,128)(2,1)S(1)}, u32[]{:S(2)}, u32[]{:S(2)}) collective-permute-start(bf16[512,256]{1,0:T(8,128)(2,1)S(1)} %get-tuple-element.141), channel_id=1, source_target_pairs={{0,1},{1,0},{2,3},{3,2},{4,5},{5,4},{6,7},{7,6},{8,9},{9,8},{10,11... | collective-permute-start | bytes 786440 | tf_op jit(solution)/shard_map/ppermute | solution.py:594
  32.6 22.4 %collective-permute-start.13 = (bf16[256,1792]{1,0:T(8,128)(2,1)S(1)}, bf16[256,1792]{1,0:T(8,128)(2,1)}, u32[]{:S(2)}, u32[]{:S(2)}) collective-permute-start(bf16[256,1792]{1,0:T(8,128)(2,1)S(1)} %get-tuple-element.247.refs_1_), channel_id=1, source_target_pairs={{0,2},{1,3},{2,0},{3,1},{4,6},{5,7},{6,4},{7,5},{8,10},{9,11},{10,... | collective-permute-start | bytes 2752520 | tf_op jit(solution)/shard_map/ppermute | solution.py:726
  59.5 80.5 %collective-permute-start.21 = (f32[2048,1792]{1,0:T(8,128)}, f32[2048,1792]{1,0:T(8,128)}, u32[]{:S(2)}, u32[]{:S(2)}) collective-permute-start(f32[2048,1792]{1,0:T(8,128)} %refs_2_.3), channel_id=1, source_target_pairs={{0,1},{1,0},{2,3},{3,2},{4,5},{5,4},{6,7},{7,6},{8,9},{9,8},{10,11... | collective-permute-start | bytes 44040200 | tf_op jit(solution)/shard_map/ppermute | solution.py:594
  60.6 22.4 %collective-permute-start.16 = (bf16[512,256]{1,0:T(8,128)(2,1)}, bf16[512,256]{1,0:T(8,128)(2,1)S(1)}, u32[]{:S(2)}, u32[]{:S(2)}) collective-permute-start(bf16[512,256]{1,0:T(8,128)(2,1)} %copy-done.12), channel_id=1, source_target_pairs={{0,8},{8,0},{16,24},{24,16},{1,9},{9,1},{17,25},{25,17},{2,10},{10... | collective-permute-start | bytes 786440 | tf_op jit(solution)/shard_map/ppermute | solution.py:657
  61.7 21.3 %collective-permute-start.15 = (bf16[512,256]{1,0:T(8,128)(2,1)}, bf16[512,256]{1,0:T(8,128)(2,1)S(1)}, u32[]{:S(2)}, u32[]{:S(2)}) collective-permute-start(bf16[512,256]{1,0:T(8,128)(2,1)} %copy-done.9), channel_id=1, source_target_pairs={{0,16},{8,24},{16,0},{24,8},{1,17},{9,25},{17,1},{25,9},{2,18},{10... | collective-permute-start | bytes 786440 | tf_op jit(solution)/shard_map/ppermute | solution.py:657
  64.3 18.6 %collective-permute-start.11 = (bf16[512,256]{1,0:T(8,128)(2,1)}, bf16[512,256]{1,0:T(8,128)(2,1)S(1)}, u32[]{:S(2)}, u32[]{:S(2)}) collective-permute-start(bf16[512,256]{1,0:T(8,128)(2,1)} %copy-done.18), channel_id=1, source_target_pairs={{0,4},{4,0},{1,5},{5,1},{2,6},{6,2},{3,7},{7,3},{8,12},{12,8},{9,1... | collective-permute-start | bytes 786440 | tf_op jit(solution)/shard_map/ppermute | solution.py:641
  84.4 32.3 %collective-permute-start.14 = (bf16[512,256]{1,0:T(8,128)(2,1)S(1)}, bf16[512,256]{1,0:T(8,128)(2,1)S(1)}, u32[]{:S(2)}, u32[]{:S(2)}) collective-permute-start(bf16[512,256]{1,0:T(8,128)(2,1)S(1)} %get-tuple-element.149.refs_1_.refs_7_), channel_id=1, source_target_pairs={{0,8},{8,0},{16,24},{24,16},{1,9},{9,1},{17,25},{25,17},{2,10},{10... | collective-permute-start | bytes 786440 | tf_op jit(solution)/shard_map/ppermute | solution.py:657
  84.4 33.8 %collective-permute-start.20 = (bf16[512,256]{1,0:T(8,128)(2,1)S(1)}, bf16[512,256]{1,0:T(8,128)(2,1)S(1)}, u32[]{:S(2)}, u32[]{:S(2)}) collective-permute-start(bf16[512,256]{1,0:T(8,128)(2,1)S(1)} %get-tuple-element.152.refs_1_.refs_6_), channel_id=1, source_target_pairs={{0,16},{8,24},{16,0},{24,8},{1,17},{9,25},{17,1},{25,9},{2,18},{10... | collective-permute-start | bytes 786440 | tf_op jit(solution)/shard_map/ppermute | solution.py:657
  85.7 33.6 %collective-permute-start.19 = (bf16[512,128]{1,0:T(8,128)(2,1)S(1)}, bf16[512,128]{1,0:T(8,128)(2,1)S(1)}, u32[]{:S(2)}, u32[]{:S(2)}) collective-permute-start(bf16[512,128]{1,0:T(8,128)(2,1)S(1)} %get-tuple-element.147.refs_1_), channel_id=1, source_target_pairs={{0,4},{4,0},{1,5},{5,1},{2,6},{6,2},{3,7},{7,3},{8,12},{12,8},{9,1... | collective-permute-start | bytes 393224 | tf_op jit(solution)/shard_map/ppermute | solution.py:641
  116.7 18.8 %collective-permute-start.18 = (bf16[512,256]{1,0:T(8,128)(2,1)S(1)}, bf16[512,256]{1,0:T(8,128)(2,1)S(1)}, u32[]{:S(2)}, u32[]{:S(2)}) collective-permute-start(bf16[512,256]{1,0:T(8,128)(2,1)S(1)} %get-tuple-element.155.refs_1_.refs_6_), channel_id=1, source_target_pairs={{0,16},{8,24},{16,0},{24,8},{1,17},{9,25},{17,1},{25,9},{2,18},{10... | collective-permute-start | bytes 786440 | tf_op jit(solution)/shard_map/ppermute | solution.py:657
  117.1 19.0 %collective-permute-start.22 = (bf16[512,128]{1,0:T(8,128)(2,1)S(1)}, bf16[512,128]{1,0:T(8,128)(2,1)S(1)}, u32[]{:S(2)}, u32[]{:S(2)}) collective-permute-start(bf16[512,128]{1,0:T(8,128)(2,1)S(1)} %get-tuple-element.160), channel_id=1, source_target_pairs={{0,4},{4,0},{1,5},{5,1},{2,6},{6,2},{3,7},{7,3},{8,12},{12,8},{9,1... | collective-permute-start | bytes 393224 | tf_op jit(solution)/shard_map/ppermute | solution.py:641
  118.3 21.6 %collective-permute-start.24 = (bf16[512,256]{1,0:T(8,128)(2,1)S(1)}, bf16[512,256]{1,0:T(8,128)(2,1)S(1)}, u32[]{:S(2)}, u32[]{:S(2)}) collective-permute-start(bf16[512,256]{1,0:T(8,128)(2,1)S(1)} %hop.50.refs_1_.refs_5_.refs_0_), channel_id=1, source_target_pairs={{0,4},{4,0},{1,5},{5,1},{2,6},{6,2},{3,7},{7,3},{8,12},{12,8},{9,1... | collective-permute-start | bytes 786440 | tf_op jit(solution)/shard_map/ppermute | solution.py:669
  119.3 17.9 %collective-permute-start.25 = (bf16[512,128]{1,0:T(8,128)(2,1)S(1)}, bf16[512,128]{1,0:T(8,128)(2,1)S(1)}, u32[]{:S(2)}, u32[]{:S(2)}) collective-permute-start(bf16[512,128]{1,0:T(8,128)(2,1)S(1)} %get-tuple-element.157.refs_4_), channel_id=1, source_target_pairs={{0,8},{8,0},{16,24},{24,16},{1,9},{9,1},{17,25},{25,17},{2,10},{10... | collective-permute-start | bytes 393224 | tf_op jit(solution)/shard_map/ppermute | solution.py:657
  135.5 21.7 %collective-permute-start.27 = (bf16[512,256]{1,0:T(8,128)(2,1)S(1)}, bf16[512,256]{1,0:T(8,128)(2,1)S(1)}, u32[]{:S(2)}, u32[]{:S(2)}) collective-permute-start(bf16[512,256]{1,0:T(8,128)(2,1)S(1)} %hop.52.refs_1_.refs_6_.refs_0_), channel_id=1, source_target_pairs={{0,4},{4,0},{1,5},{5,1},{2,6},{6,2},{3,7},{7,3},{8,12},{12,8},{9,1... | collective-permute-start | bytes 786440 | tf_op jit(solution)/shard_map/ppermute | solution.py:669
  136.1 19.4 %collective-permute-start.23 = (bf16[512,128]{1,0:T(8,128)(2,1)S(1)}, bf16[512,128]{1,0:T(8,128)(2,1)S(1)}, u32[]{:S(2)}, u32[]{:S(2)}) collective-permute-start(bf16[512,128]{1,0:T(8,128)(2,1)S(1)} %get-tuple-element.162.refs_1_.refs_5_), channel_id=1, source_target_pairs={{0,8},{8,0},{16,24},{24,16},{1,9},{9,1},{17,25},{25,17},{2,10},{10... | collective-permute-start | bytes 393224 | tf_op jit(solution)/shard_map/ppermute | solution.py:657
  137.3 18.7 %collective-permute-start.28 = (bf16[512,128]{1,0:T(8,128)(2,1)S(1)}, bf16[512,128]{1,0:T(8,128)(2,1)S(1)}, u32[]{:S(2)}, u32[]{:S(2)}) collective-permute-start(bf16[512,128]{1,0:T(8,128)(2,1)S(1)} %get-tuple-element.164.refs_4_), channel_id=1, source_target_pairs={{0,16},{8,24},{16,0},{24,8},{1,17},{9,25},{17,1},{25,9},{2,18},{10... | collective-permute-start | bytes 393224 | tf_op jit(solution)/shard_map/ppermute | solution.py:657
  154.7 27.7 %collective-permute-start.29 = (bf16[512,128]{1,0:T(8,128)(2,1)S(1)}, bf16[512,128]{1,0:T(8,128)(2,1)S(1)}, u32[]{:S(2)}, u32[]{:S(2)}) collective-permute-start(bf16[512,128]{1,0:T(8,128)(2,1)S(1)} %get-tuple-element.165.refs_1_), channel_id=1, source_target_pairs={{0,4},{4,0},{1,5},{5,1},{2,6},{6,2},{3,7},{7,3},{8,12},{12,8},{9,1... | collective-permute-start | bytes 393224 | tf_op jit(solution)/shard_map/ppermute | solution.py:641
  155.6 28.5 %collective-permute-start.26 = (bf16[512,128]{1,0:T(8,128)(2,1)S(1)}, bf16[512,128]{1,0:T(8,128)(2,1)S(1)}, u32[]{:S(2)}, u32[]{:S(2)}) collective-permute-start(bf16[512,128]{1,0:T(8,128)(2,1)S(1)} %get-tuple-element.167.refs_1_.refs_6_), channel_id=1, source_target_pairs={{0,16},{8,24},{16,0},{24,8},{1,17},{9,25},{17,1},{25,9},{2,18},{10... | collective-permute-start | bytes 393224 | tf_op jit(solution)/shard_map/ppermute | solution.py:657
  156.0 47.3 %collective-permute-start.32 = (bf16[512,128]{1,0:T(8,128)(2,1)S(1)}, bf16[512,128]{1,0:T(8,128)(2,1)S(1)}, u32[]{:S(2)}, u32[]{:S(2)}) collective-permute-start(bf16[512,128]{1,0:T(8,128)(2,1)S(1)} %hop.56.refs_5_.refs_0_), channel_id=1, source_target_pairs={{0,4},{4,0},{1,5},{5,1},{2,6},{6,2},{3,7},{7,3},{8,12},{12,8},{9,1... | collective-permute-start | bytes 393224 | tf_op jit(solution)/shard_map/ppermute | solution.py:669
  181.5 18.0 %collective-permute-start.30 = (bf16[512,128]{1,0:T(8,128)(2,1)S(1)}, bf16[512,128]{1,0:T(8,128)(2,1)S(1)}, u32[]{:S(2)}, u32[]{:S(2)}) collective-permute-start(bf16[512,128]{1,0:T(8,128)(2,1)S(1)} %get-tuple-element.172), channel_id=1, source_target_pairs={{0,4},{4,0},{1,5},{5,1},{2,6},{6,2},{3,7},{7,3},{8,12},{12,8},{9,1... | collective-permute-start | bytes 393224 | tf_op jit(solution)/shard_map/ppermute | solution.py:641
  182.4 18.3 %collective-permute-start.33 = (bf16[512,128]{1,0:T(8,128)(2,1)S(1)}, bf16[512,128]{1,0:T(8,128)(2,1)S(1)}, u32[]{:S(2)}, u32[]{:S(2)}) collective-permute-start(bf16[512,128]{1,0:T(8,128)(2,1)S(1)} %get-tuple-element.170.refs_1_.refs_5_), channel_id=1, source_target_pairs={{0,8},{8,0},{16,24},{24,16},{1,9},{9,1},{17,25},{25,17},{2,10},{10... | collective-permute-start | bytes 393224 | tf_op jit(solution)/shard_map/ppermute | solution.py:657
  184.1 26.3 %collective-permute-start.35 = (bf16[512,128]{1,0:T(8,128)(2,1)S(1)}, bf16[512,128]{1,0:T(8,128)(2,1)S(1)}, u32[]{:S(2)}, u32[]{:S(2)}) collective-permute-start(bf16[512,128]{1,0:T(8,128)(2,1)S(1)} %hop.58.refs_4_.refs_1_.refs_0_), channel_id=1, source_target_pairs={{0,4},{4,0},{1,5},{5,1},{2,6},{6,2},{3,7},{7,3},{8,12},{12,8},{9,1... | collective-permute-start | bytes 393224 | tf_op jit(solution)/shard_map/ppermute | solution.py:669
  223.0 14.9 %collective-permute-start.37 = (bf16[512,128]{1,0:T(8,128)(2,1)S(1)}, bf16[512,128]{1,0:T(8,128)(2,1)S(1)}, u32[]{:S(2)}, u32[]{:S(2)}) collective-permute-start(bf16[512,128]{1,0:T(8,128)(2,1)S(1)} %hop.63.refs_3_.refs_0_), channel_id=1, source_target_pairs={{0,4},{4,0},{1,5},{5,1},{2,6},{6,2},{3,7},{7,3},{8,12},{12,8},{9,1... | collective-permute-start | bytes 393224 | tf_op jit(solution)/shard_map/ppermute | solution.py:669
  273.8 14.9 %collective-permute-start.42 = (bf16[512,128]{1,0:T(8,128)(2,1)S(1)}, bf16[512,128]{1,0:T(8,128)(2,1)S(1)}, u32[]{:S(2)}, u32[]{:S(2)}) collective-permute-start(bf16[512,128]{1,0:T(8,128)(2,1)S(1)} %image.7), channel_id=1, source_target_pairs={{0,4},{4,0},{1,5},{5,1},{2,6},{6,2},{3,7},{7,3},{8,12},{12,8},{9,1... | collective-permute-start | bytes 393224 | tf_op jit(solution)/shard_map/ppermute | solution.py:641
  307.6 16.7 %collective-permute-start.48 = (bf16[512,128]{1,0:T(8,128)(2,1)S(1)}, bf16[512,128]{1,0:T(8,128)(2,1)S(1)}, u32[]{:S(2)}, u32[]{:S(2)}) collective-permute-start(bf16[512,128]{1,0:T(8,128)(2,1)S(1)} %image.9.refs_1_), channel_id=1, source_target_pairs={{0,4},{4,0},{1,5},{5,1},{2,6},{6,2},{3,7},{7,3},{8,12},{12,8},{9,1... | collective-permute-start | bytes 393224 | tf_op jit(solution)/shard_map/ppermute | solution.py:641
  308.6 17.2 %collective-permute-start.47 = (bf16[512,128]{1,0:T(8,128)(2,1)S(1)}, bf16[512,128]{1,0:T(8,128)(2,1)S(1)}, u32[]{:S(2)}, u32[]{:S(2)}) collective-permute-start(bf16[512,128]{1,0:T(8,128)(2,1)S(1)} %get-tuple-element.204.refs_1_), channel_id=1, source_target_pairs={{0,16},{8,24},{16,0},{24,8},{1,17},{9,25},{17,1},{25,9},{2,18},{10... | collective-permute-start | bytes 393224 | tf_op jit(solution)/shard_map/ppermute | solution.py:657
  322.2 15.4 %collective-permute-start.53 = (bf16[512,128]{1,0:T(8,128)(2,1)S(1)}, bf16[512,128]{1,0:T(8,128)(2,1)S(1)}, u32[]{:S(2)}, u32[]{:S(2)}) collective-permute-start(bf16[512,128]{1,0:T(8,128)(2,1)S(1)} %hop.68.refs_0_.refs_1_), channel_id=1, source_target_pairs={{0,4},{4,0},{1,5},{5,1},{2,6},{6,2},{3,7},{7,3},{8,12},{12,8},{9,1... | collective-permute-start | bytes 393224 | tf_op jit(solution)/shard_map/ppermute | solution.py:669
  401.9 52.4 %all-to-all-start = ((bf16[8,256,256]{2,1,0:T(8,128)(2,1)}), bf16[8,256,256]{2,1,0:T(8,128)(2,1)}, u32[]{:S(2)}, u32[]{:S(2)}) async-start(bf16[8,256,256]{2,1,0:T(8,128)(2,1)} %broadcast_in_dim.2.refs_3_), calls=%async_computation | async-start | bytes 2097152 | tf_op jit(solution)/shard_map/all_to_all | solution.py:764
  451.5 19.3 %collective-permute-start.71 = (bf16[896,256]{1,0:T(8,128)(2,1)S(1)}, bf16[896,256]{1,0:T(8,128)(2,1)}, u32[]{:S(2)}, u32[]{:S(2)}) collective-permute-start(bf16[896,256]{1,0:T(8,128)(2,1)S(1)} %hop.77.refs_1_), channel_id=1, source_target_pairs={{0,8},{8,0},{16,24},{24,16},{1,9},{9,1},{17,25},{25,17},{2,10},{10... | collective-permute-start | bytes 1376264 | tf_op jit(solution)/shard_map/ppermute | solution.py:657
  454.3 28.9 %all-to-all-start.1 = ((bf16[4,512,256]{2,1,0:T(8,128)(2,1)}), bf16[4,512,256]{2,1,0:T(8,128)(2,1)}, u32[]{:S(2)}, u32[]{:S(2)}) async-start(bf16[4,512,256]{2,1,0:T(8,128)(2,1)} %bitcast.4), calls=%async_computation.1 | async-start | bytes 2097152 | tf_op jit(solution)/shard_map/all_to_all | solution.py:767
  490.9 20.3 %all-to-all-start.2 = ((bf16[4,128,256]{1,2,0:T(8,128)(2,1)}), bf16[4,128,256]{1,2,0:T(8,128)(2,1)}, u32[]{:S(2)}, u32[]{:S(2)}) async-start(bf16[4,128,256]{1,2,0:T(8,128)(2,1)} %bitcast.22), calls=%async_computation.2 | async-start | bytes 524288 | tf_op jit(solution)/shard_map/all_to_all | solution.py:704
  (69 other events, 1111.9 us)

commit v11 on v10

--- a/solution.py
+++ b/solution.py
@@ -785,22 +785,22 @@
         their_pieces = [swap_cores(each, n_width) for each in their_pieces]
         hidden = (jax.nn.silu(gate_pre.astype(f32)) * up_pre.astype(f32)).astype(bf16)
         hops = boundary([mine_in], turning)
-        total_in, sent_in, got_in = last_hop(after(mine_in, hops) + theirs_in)
-        last = [sent_in]
+        total_in, sent_in, got_in = last_hop(mine_in + theirs_in)
+        basis = lax.dynamic_slice_in_dim(start, core * COLS, COLS, 1)
+        last = [sent_in, *hops]
         for at in range(1, count):
             sends, keep = (own_pieces + their_pieces)[2 * at : 2 * at + 2]
             turning.append(Reduction(after(sends, last), n_grp, n_dp, keep=keep))
             if turning[0].parts is None:
-                last = boundary(last + [hidden] if at == 2 else last, turning)[:1]
+                last = boundary(last + [hidden, basis] if at == 2 else last, turning)[:1]
         rot_in = (total_in + got_in.astype(f32)).astype(bf16)
         eig_sent = after(eigvals, [rot_in, *turning[0].parts, *their_pieces])
         eig_theirs = swap_cores(eig_sent, n_width)
-        basis = lax.dynamic_slice_in_dim(start, core * COLS, COLS, 1)
         calls = []
         for begin in range(0, count, PIECES):
             span = list(range(begin, begin + PIECES))
             calls += zip([None] + span, span + [None])
-        rotated, ties = [None] * len(calls), [hidden]
+        rotated, ties = [None] * len(calls), []
 
         def parts_of(reductions, pieces):
             for piece in pieces:

time: 527 us -> 526 us (level)
  transfers between devices with their start and end apart: 82 -> 82, of which waited for: 23 -> 19; matrix products, arithmetic and copies ran while one was open for 3% -> 3% of each run, Pallas kernels for 48% -> 49%
where the time goes in v11:
time: 526 us; the launch traced here: 517 us
  Pallas kernels  304 us (58%)
  starting transfers between devices  96.5 us (18%)
  waiting for transfers between devices  89.3 us (17%)
  other arithmetic  14.7 us (3%)
  local copies, waits for them, and re-layouts  9.92 us (2%)
    pallas_call x6, Pallas kernels, form_parts(): pl.pallas_call(functools.partial(form_kernel, n_keep, n_parts, len(ties))...  107 us
    pallas_call x12, Pallas kernels, return_parts(): pl.pallas_call(functools.partial(return_kernel, n_parts, not before), in_...  91.1 us
    pallas_call x6, Pallas kernels, image_parts(): pl.pallas_call(functools.partial(image_kernel, n_keep, len(ties)), grid=(...  54.8 us
    ppermute x28, starting transfers between devices, run(): got = [lax.ppermute(sent, 'grp', crossed(n_grp, step))]  39.8 us
    ppermute x28, waiting for transfers between devices, run(): got = [lax.ppermute(sent, 'grp', crossed(n_grp, step))]  23.6 us
    ppermute x14, waiting for transfers between devices, run(): lax.ppermute(sends[at * rows:(at + 1) * rows], 'dp', turned_by(n_dp, at +...  17.5 us
    ppermute x14, waiting for transfers between devices, run(): lax.ppermute(own, 'dp', turned_by(n_dp, n_dp - 1 - at))  16.3 us
    ppermute x14, starting transfers between devices, run(): lax.ppermute(own, 'dp', turned_by(n_dp, n_dp - 1 - at))  15.6 us
  transfers between devices with their start and end apart: 82, of which 19 were waited for; matrix products, arithmetic and copies ran while one was open for 3% of the time, Pallas kernels for 49%

profile of v11, /device:TPU:0, one launch (start us, length us, event | category | flops | bytes accessed | tf_op | source)
XLA Modules:
  0.0 516.9 jit_solution(2769126566634355541)
XLA Ops:
  0.7 12.5 %rotate_in.1 = (f32[256,1792]{1,0:T(8,128)S(1)}, f32[256,1792]{1,0:T(8,128)S(1)}) custom-call(s32[3]{0:T(128)S(1)} %pad_add_fusion.place_ref, bf16[512,3584]{1,0:T(8,128)(2,1)} %query_ref.2, bf16[3584,1792]{1,0:T(8,128)(2,1)} %eigen_ref.9), custom_call_target="tpu_custom_call" | custom-call | flops 6576668672 | bytes 12845056 | tf_op jit(solution)/shard_map/rotate_in/pallas_call | solution.py:328
  21.5 7.0 %collective-permute-done.2.refs_0_ = bf16[512,256]{1,0:T(8,128)(2,1)S(1)} collective-permute-done((bf16[512,256]{1,0:T(8,128)(2,1)S(1)}, bf16[512,256]{1,0:T(8,128)(2,1)S(1)}, u32[]{:S(2)}, u32[]{:S(2)}) %collective-permute-start.2) | collective-permute-done | bytes 262176 | tf_op jit(solution)/shard_map/ppermute | solution.py:641
  60.2 6.4 %collective-permute-done.12.refs_0_ = bf16[512,256]{1,0:T(8,128)(2,1)S(1)} collective-permute-done((bf16[512,256]{1,0:T(8,128)(2,1)S(1)}, bf16[512,256]{1,0:T(8,128)(2,1)S(1)}, u32[]{:S(2)}, u32[]{:S(2)}) %collective-permute-start.12) | collective-permute-done | bytes 262176 | tf_op jit(solution)/shard_map/ppermute | solution.py:669
  68.0 14.6 %form.6 = (bf16[8,512,1792]{2,1,0:T(8,128)(2,1)}, bf16[512,128]{1,0:T(8,128)(2,1)S(1)}) custom-call(s32[3]{0:T(128)S(1)} %pad_add_fusion.place_ref, bf16[512,256]{1,0:T(8,128)(2,1)S(1)} %collective-permute-done.12.refs_0_, bf16[256,1792]{1,0:T(8,128)(2,1)S(1)} %add_convert_fusion.refs_1_.refs_2_, f32[2048,1792]{1,0:T(8,128)} %refs_2_.3, ...), custom_call_target="tpu_custom_call" | custom-call | flops 5872025600 | bytes 14680064 | tf_op jit(solution)/shard_map/form/pallas_call | solution.py:138
  91.6 24.2 %form.7 = (bf16[8,1024,1792]{2,1,0:T(8,128)(2,1)}, f32[512,128]{1,0:T(8,128)S(1)}, bf16[512,128]{1,0:T(8,128)(2,1)S(1)}) custom-call(s32[3]{0:T(128)S(1)} %pad_add_fusion.place_ref, bf16[512,256]{1,0:T(8,128)(2,1)S(1)} %hop.45.refs_0_, bf16[512,256]{1,0:T(8,128)(2,1)S(1)} %collective-permute-done.17.refs_1_, ...), custom_call_target="tpu_custom_call" | custom-call | flops 11744051200 | bytes 29360128 | tf_op jit(solution)/shard_map/form/pallas_call | solution.py:138
  122.8 14.6 %form.8 = (bf16[8,512,1792]{2,1,0:T(8,128)(2,1)}, f32[512,128]{1,0:T(8,128)S(1)}) custom-call(s32[3]{0:T(128)S(1)} %pad_add_fusion.place_ref, bf16[512,256]{1,0:T(8,128)(2,1)S(1)} %hop.48.refs_5_.refs_0_, bf16[256,1792]{1,0:T(8,128)(2,1)S(1)} %add_convert_fusion.refs_1_.refs_2_, f32[2048,1792]{1,0:T(8,128)} %refs_2_.3, ...), custom_call_target="tpu_custom_call" | custom-call | flops 5872025600 | bytes 14680064 | tf_op jit(solution)/shard_map/form/pallas_call | solution.py:138
  139.9 14.7 %form.9 = (bf16[8,512,1792]{2,1,0:T(8,128)(2,1)}, bf16[512,128]{1,0:T(8,128)(2,1)S(1)}) custom-call(s32[3]{0:T(128)S(1)} %pad_add_fusion.place_ref, bf16[512,256]{1,0:T(8,128)(2,1)S(1)} %collective-permute-done.24.refs_0_, bf16[256,1792]{1,0:T(8,128)(2,1)S(1)} %add_convert_fusion.refs_1_.refs_2_, f32[2048,1792]{1,0:T(8,128)} %collective-permute-done.21.refs_2_.refs_3_, ...), custom_call_target="tpu_custom_call" | custom-call | flops 5872025600 | bytes 14680064 | tf_op jit(solution)/shard_map/form/pallas_call | solution.py:138
  159.4 24.2 %form.10 = (bf16[8,1024,1792]{2,1,0:T(8,128)(2,1)}, f32[512,128]{1,0:T(8,128)S(1)}, bf16[512,128]{1,0:T(8,128)(2,1)S(1)}) custom-call(s32[3]{0:T(128)S(1)} %pad_add_fusion.place_ref, bf16[512,256]{1,0:T(8,128)(2,1)S(1)} %hop.50.refs_1_.refs_5_.refs_0_, bf16[512,256]{1,0:T(8,128)(2,1)S(1)} %collective-permute-done.27.refs_1_, ...), custom_call_target="tpu_custom_call" | custom-call | flops 11744051200 | bytes 29360128 | tf_op jit(solution)/shard_map/form/pallas_call | solution.py:138
  187.4 14.9 %form.11 = (bf16[8,512,1792]{2,1,0:T(8,128)(2,1)}, f32[512,128]{1,0:T(8,128)S(1)}) custom-call(s32[3]{0:T(128)S(1)} %pad_add_fusion.place_ref, bf16[512,256]{1,0:T(8,128)(2,1)S(1)} %hop.52.refs_1_.refs_6_.refs_0_, bf16[256,1792]{1,0:T(8,128)(2,1)S(1)} %add_convert_fusion.refs_1_.refs_2_, f32[2048,1792]{1,0:T(8,128)} %collective-permute-done.21.refs_2_.refs_3_, ...), custom_call_target="tpu_custom_call" | custom-call | flops 5872025600 | bytes 14680064 | tf_op jit(solution)/shard_map/form/pallas_call | solution.py:138
  203.3 5.9 %returned.12 = (f32[128,1792]{1,0:T(8,128)S(1)}, bf16[128,1792]{1,0:T(8,128)(2,1)S(1)}) custom-call(bf16[512,128]{1,0:T(8,128)(2,1)S(1)} %collective-permute-done.32.refs_0_, bf16[8,512,1792]{2,1,0:T(8,128)(2,1)} %get-tuple-element.173.refs_1_.rotated_ref, bf16[512,128]{1,0:T(8,128)(2,1)S(1)} %get-tuple-element.175.refs_2_, ...), custom_call_target="tpu_custom_call" | custom-call | flops 3758096384 | bytes 14680064 | tf_op jit(solution)/shard_map/returned/pallas_call | solution.py:260
  212.0 10.1 %returned.13 = (f32[128,1792]{1,0:T(8,128)S(1)}, bf16[128,1792]{1,0:T(8,128)(2,1)S(1)}) custom-call(bf16[512,128]{1,0:T(8,128)(2,1)S(1)} %hop.56.refs_5_.refs_0_, bf16[512,128]{1,0:T(8,128)(2,1)S(1)} %collective-permute-done.35.refs_1_, bf16[8,1024,1792]{2,1,0:T(8,128)(2,1)} %get-tuple-element.179.refs_2_.rotated_ref, ...), custom_call_target="tpu_custom_call" | custom-call | flops 7516192768 | bytes 29360128 | tf_op jit(solution)/shard_map/returned/pallas_call | solution.py:260
  226.8 6.0 %returned.14 = (f32[128,1792]{1,0:T(8,128)S(1)}, bf16[128,1792]{1,0:T(8,128)(2,1)S(1)}) custom-call(bf16[512,128]{1,0:T(8,128)(2,1)S(1)} %hop.58.refs_4_.refs_1_.refs_0_, bf16[8,512,1792]{2,1,0:T(8,128)(2,1)} %get-tuple-element.186.refs_1_.rotated_ref, f32[128,1792]{1,0:T(8,128)S(1)} %get-tuple-element.187.refs_2_, ...), custom_call_target="tpu_custom_call" | custom-call | flops 3758096384 | bytes 14680064 | tf_op jit(solution)/shard_map/returned/pallas_call | solution.py:260
  232.8 6.7 %returned.15 = (f32[128,1792]{1,0:T(8,128)S(1)}, bf16[128,1792]{1,0:T(8,128)(2,1)}) custom-call(bf16[512,128]{1,0:T(8,128)(2,1)S(1)} %collective-permute-done.38.refs_0_, bf16[8,512,1792]{2,1,0:T(8,128)(2,1)} %get-tuple-element.185.refs_1_.rotated_ref, f32[128,1792]{1,0:T(8,128)S(1)} %get-tuple-element.188.refs_2_), custom_call_target="tpu_custom_call" | custom-call | flops 3758096384 | bytes 14680064 | tf_op jit(solution)/shard_map/returned/pallas_call | solution.py:260
  239.5 10.9 %returned.16 = (f32[128,1792]{1,0:T(8,128)S(1)}, bf16[128,1792]{1,0:T(8,128)(2,1)}) custom-call(bf16[512,128]{1,0:T(8,128)(2,1)S(1)} %hop.62.refs_4_.refs_2_.refs_0_, bf16[512,128]{1,0:T(8,128)(2,1)S(1)} %collective-permute-done.37.refs_1_, bf16[8,1024,1792]{2,1,0:T(8,128)(2,1)} %get-tuple-element.184.refs_2_.rotated_ref, ...), custom_call_target="tpu_custom_call" | custom-call | flops 7516192768 | bytes 29360128 | tf_op jit(solution)/shard_map/returned/pallas_call | solution.py:260
  250.4 5.9 %returned.17 = (f32[128,1792]{1,0:T(8,128)S(1)}, bf16[128,1792]{1,0:T(8,128)(2,1)S(1)}) custom-call(bf16[512,128]{1,0:T(8,128)(2,1)S(1)} %hop.63.refs_3_.refs_0_, bf16[8,512,1792]{2,1,0:T(8,128)(2,1)} %get-tuple-element.183.refs_1_.rotated_ref, f32[128,1792]{1,0:T(8,128)S(1)} %get-tuple-element.190.refs_2_), custom_call_target="tpu_custom_call" | custom-call | flops 3758096384 | bytes 14680064 | tf_op jit(solution)/shard_map/returned/pallas_call | solution.py:260
  258.5 7.2 %collective-permute-done.41.gram_got_ref = f32[128,128]{1,0:T(8,128)S(1)} collective-permute-done((f32[128,128]{1,0:T(8,128)S(1)}, f32[128,128]{1,0:T(8,128)S(1)}, u32[]{:S(2)}, u32[]{:S(2)}) %collective-permute-start.41) | collective-permute-done | bytes 65568 | tf_op jit(solution)/shard_map/ppermute | solution.py:739
  268.1 7.3 %image.7 = bf16[512,128]{1,0:T(8,128)(2,1)S(1)} custom-call(bf16[1792,128]{1,0:T(8,128)(2,1)S(1)} %normalize.2.basis_ref, bf16[8,512,1792]{2,1,0:T(8,128)(2,1)} %get-tuple-element.173.refs_1_.rotated_ref), custom_call_target="tpu_custom_call" | custom-call | flops 3758096384 | bytes 14680064 | tf_op jit(solution)/shard_map/image/pallas_call | solution.py:217
  276.0 12.7 %image.6 = (f32[512,128]{1,0:T(8,128)S(1)}, bf16[512,128]{1,0:T(8,128)(2,1)S(1)}) custom-call(bf16[1792,128]{1,0:T(8,128)(2,1)S(1)} %normalize.2.basis_ref, bf16[8,1024,1792]{2,1,0:T(8,128)(2,1)} %get-tuple-element.179.refs_2_.rotated_ref), custom_call_target="tpu_custom_call" | custom-call | flops 7516192768 | bytes 29360128 | tf_op jit(solution)/shard_map/image/pallas_call | solution.py:217
  292.0 7.3 %image.8.total_ref.refs_1_ = f32[512,128]{1,0:T(8,128)S(1)} custom-call(bf16[1792,128]{1,0:T(8,128)(2,1)S(1)} %normalize.2.basis_ref, bf16[8,512,1792]{2,1,0:T(8,128)(2,1)} %get-tuple-element.186.refs_1_.rotated_ref, bf16[512,128]{1,0:T(8,128)(2,1)S(1)} %get-tuple-element.196.refs_0_), custom_call_target="tpu_custom_call" | custom-call | flops 3758096384 | bytes 14680064 | tf_op jit(solution)/shard_map/image/pallas_call | solution.py:217
  300.3 7.3 %image.9.refs_1_ = bf16[512,128]{1,0:T(8,128)(2,1)S(1)} custom-call(bf16[1792,128]{1,0:T(8,128)(2,1)S(1)} %normalize.2.basis_ref, bf16[8,512,1792]{2,1,0:T(8,128)(2,1)} %get-tuple-element.185.refs_1_.rotated_ref, bf16[512,128]{1,0:T(8,128)(2,1)S(1)} %get-tuple-element.200.refs_0_, bf16[512,128]{1,0:T(8,128)(2,1)S(1)} %get-tuple-element.198.refs_1_), custom_call_target="tpu_custom_call" | custom-call | flops 3758096384 | bytes 14680064 | tf_op jit(solution)/shard_map/image/pallas_call | solution.py:217
  310.9 13.0 %image.10 = (f32[512,128]{1,0:T(8,128)S(1)}, bf16[512,128]{1,0:T(8,128)(2,1)S(1)}) custom-call(bf16[1792,128]{1,0:T(8,128)(2,1)S(1)} %normalize.2.basis_ref, bf16[8,1024,1792]{2,1,0:T(8,128)(2,1)} %get-tuple-element.184.refs_2_.rotated_ref, bf16[512,128]{1,0:T(8,128)(2,1)S(1)} %hop.68.refs_0_.refs_1_, bf16[512,128]{1,0:T(8,128)(2,1)S(1)} %get-tuple-element.202.refs_1_), custom_call_target="tpu_custom_call" | custom-call | flops 7516192768 | bytes 29360128 | tf_op jit(solution)/shard_map/image/pallas_call | solution.py:217
  327.7 7.3 %image.11.total_ref.refs_1_ = f32[512,128]{1,0:T(8,128)S(1)} custom-call(bf16[1792,128]{1,0:T(8,128)(2,1)S(1)} %normalize.2.basis_ref, bf16[8,512,1792]{2,1,0:T(8,128)(2,1)} %get-tuple-element.183.refs_1_.rotated_ref, bf16[512,128]{1,0:T(8,128)(2,1)S(1)} %hop.70.refs_0_.refs_1_.refs_3_, bf16[512,128]{1,0:T(8,128)(2,1)S(1)} %get-tuple-element.205.refs_1_), custom_call_target="tpu_custom_call" | custom-call | flops 3758096384 | bytes 14680064 | tf_op jit(solution)/shard_map/image/pallas_call | solution.py:217
  337.5 5.9 %returned.18 = (f32[128,1792]{1,0:T(8,128)S(1)}, bf16[128,1792]{1,0:T(8,128)(2,1)S(1)}) custom-call(bf16[512,128]{1,0:T(8,128)(2,1)S(1)} %collective-permute-done.53.refs_0_, bf16[8,512,1792]{2,1,0:T(8,128)(2,1)} %get-tuple-element.173.refs_1_.rotated_ref, bf16[512,128]{1,0:T(8,128)(2,1)S(1)} %get-tuple-element.210.refs_2_, ...), custom_call_target="tpu_custom_call" | custom-call | flops 3758096384 | bytes 14680064 | tf_op jit(solution)/shard_map/returned/pallas_call | solution.py:260
  346.2 10.1 %returned.19 = (f32[128,1792]{1,0:T(8,128)S(1)}, bf16[128,1792]{1,0:T(8,128)(2,1)S(1)}) custom-call(bf16[512,128]{1,0:T(8,128)(2,1)S(1)} %hop.68.refs_0_.refs_1_, bf16[512,128]{1,0:T(8,128)(2,1)S(1)} %collective-permute-done.55.refs_1_.refs_2_, bf16[8,1024,1792]{2,1,0:T(8,128)(2,1)} %get-tuple-element.179.refs_2_.rotated_ref, ...), custom_call_target="tpu_custom_call" | custom-call | flops 7516192768 | bytes 29360128 | tf_op jit(solution)/shard_map/returned/pallas_call | solution.py:260
  372.6 5.9 %returned.21 = (f32[128,1792]{1,0:T(8,128)S(1)}, bf16[128,1792]{1,0:T(8,128)(2,1)S(1)}) custom-call(bf16[512,128]{1,0:T(8,128)(2,1)S(1)} %collective-permute-done.58.refs_4_.refs_0_, bf16[8,512,1792]{2,1,0:T(8,128)(2,1)} %get-tuple-element.185.refs_1_.rotated_ref, f32[128,1792]{1,0:T(8,128)S(1)} %get-tuple-element.221.refs_2_, ...), custom_call_target="tpu_custom_call" | custom-call | flops 3758096384 | bytes 14680064 | tf_op jit(solution)/shard_map/returned/pallas_call | solution.py:260
  384.1 10.9 %returned.22 = (f32[128,1792]{1,0:T(8,128)S(1)}, bf16[128,1792]{1,0:T(8,128)(2,1)}) custom-call(bf16[512,128]{1,0:T(8,128)(2,1)S(1)} %hop.74.refs_4_.refs_2_.refs_5_.refs_0_, bf16[512,128]{1,0:T(8,128)(2,1)S(1)} %collective-permute-done.59.refs_6_.refs_1_, bf16[8,1024,1792]{2,1,0:T(8,128)(2,1)} %get-tuple-element.184.refs_2_.rotated_ref, ...), custom_call_target="tpu_custom_call" | custom-call | flops 7516192768 | bytes 29360128 | tf_op jit(solution)/shard_map/returned/pallas_call | solution.py:260
  396.1 6.7 %returned.23 = (f32[128,1792]{1,0:T(8,128)S(1)}, bf16[128,1792]{1,0:T(8,128)(2,1)}) custom-call(bf16[512,128]{1,0:T(8,128)(2,1)S(1)} %hop.75.refs_3_.refs_7_.refs_0_, bf16[8,512,1792]{2,1,0:T(8,128)(2,1)} %get-tuple-element.183.refs_1_.rotated_ref, f32[128,1792]{1,0:T(8,128)S(1)} %get-tuple-element.228.refs_2_, bf16[8,256,256]{2,1,0:T(8,128)(2,1)} %broadcast_in_dim.2.refs_3_), custom_call_target="tpu_custom_call" | custom-call | flops 3758096384 | bytes 14680064 | tf_op jit(solution)/shard_map/returned/pallas_call | solution.py:260
  407.7 8.5 %collective-permute-done.64.got_ref = bf16[128,1792]{1,0:T(8,128)(2,1)S(1)} collective-permute-done((bf16[128,1792]{1,0:T(8,128)(2,1)}, bf16[128,1792]{1,0:T(8,128)(2,1)S(1)}, u32[]{:S(2)}, u32[]{:S(2)}) %collective-permute-start.64) | collective-permute-done | bytes 458784 | tf_op jit(solution)/shard_map/ppermute | solution.py:726
  429.8 7.8 %collective-permute-done.66.refs_0_ = bf16[896,256]{1,0:T(8,128)(2,1)S(1)} collective-permute-done((bf16[896,256]{1,0:T(8,128)(2,1)S(1)}, bf16[896,256]{1,0:T(8,128)(2,1)S(1)}, u32[]{:S(2)}, u32[]{:S(2)}) %collective-permute-start.66) | collective-permute-done | bytes 458784 | tf_op jit(solution)/shard_map/ppermute | solution.py:641
  439.8 10.5 %collective-permute-done.67 = bf16[896,256]{1,0:T(8,128)(2,1)} collective-permute-done((bf16[896,256]{1,0:T(8,128)(2,1)S(1)}, bf16[896,256]{1,0:T(8,128)(2,1)}, u32[]{:S(2)}, u32[]{:S(2)}) %collective-permute-start.67) | collective-permute-done | bytes 458784 | tf_op jit(solution)/shard_map/ppermute | solution.py:657
  459.1 8.8 %collective-permute-done.68.refs_0_ = bf16[448,256]{1,0:T(8,128)(2,1)S(1)} collective-permute-done((bf16[448,256]{1,0:T(8,128)(2,1)}, bf16[448,256]{1,0:T(8,128)(2,1)S(1)}, u32[]{:S(2)}, u32[]{:S(2)}) %collective-permute-start.68) | collective-permute-done | bytes 229408 | tf_op jit(solution)/shard_map/ppermute | solution.py:657
  496.7 6.2 %collective-permute-done.75.refs_2_ = bf16[896,256]{1,0:T(8,128)(2,1)S(1)} collective-permute-done((bf16[896,256]{1,0:T(8,128)(2,1)S(1)}, bf16[896,256]{1,0:T(8,128)(2,1)S(1)}, u32[]{:S(2)}, u32[]{:S(2)}) %collective-permute-start.75) | collective-permute-done | bytes 458784 | tf_op jit(solution)/shard_map/ppermute | solution.py:669
  (254 shorter events, 193.0 us)
Async XLA Ops:
  13.2 15.3 %collective-permute-start.4 = (f32[256,1792]{1,0:T(8,128)S(1)}, f32[256,1792]{1,0:T(8,128)S(1)}, u32[]{:S(2)}, u32[]{:S(2)}) collective-permute-start(f32[256,1792]{1,0:T(8,128)S(1)} %get-tuple-element.133), channel_id=1, source_target_pairs={{0,1},{1,0},{2,3},{3,2},{4,5},{5,4},{6,7},{7,6},{8,9},{9,8},{10,11... | collective-permute-start | bytes 5505032 | tf_op jit(solution)/shard_map/ppermute | solution.py:594
  33.3 18.9 %collective-permute-start.8 = (bf16[512,256]{1,0:T(8,128)(2,1)}, bf16[512,256]{1,0:T(8,128)(2,1)}, u32[]{:S(2)}, u32[]{:S(2)}) collective-permute-start(bf16[512,256]{1,0:T(8,128)(2,1)} %get-tuple-element.139), channel_id=1, source_target_pairs={{0,1},{1,0},{2,3},{3,2},{4,5},{5,4},{6,7},{7,6},{8,9},{9,8},{10,11... | collective-permute-start | bytes 786440 | tf_op jit(solution)/shard_map/ppermute | solution.py:594
  33.8 24.9 %collective-permute-start.13 = (bf16[256,1792]{1,0:T(8,128)(2,1)S(1)}, bf16[256,1792]{1,0:T(8,128)(2,1)}, u32[]{:S(2)}, u32[]{:S(2)}) collective-permute-start(bf16[256,1792]{1,0:T(8,128)(2,1)S(1)} %get-tuple-element.245.refs_1_), channel_id=1, source_target_pairs={{0,2},{1,3},{2,0},{3,1},{4,6},{5,7},{6,4},{7,5},{8,10},{9,11},{10,... | collective-permute-start | bytes 2752520 | tf_op jit(solution)/shard_map/ppermute | solution.py:726
  38.9 17.3 %collective-permute-start.7 = (bf16[512,256]{1,0:T(8,128)(2,1)}, bf16[512,256]{1,0:T(8,128)(2,1)}, u32[]{:S(2)}, u32[]{:S(2)}) collective-permute-start(bf16[512,256]{1,0:T(8,128)(2,1)} %get-tuple-element.135.refs_1_), channel_id=1, source_target_pairs={{0,8},{8,0},{16,24},{24,16},{1,9},{9,1},{17,25},{25,17},{2,10},{10... | collective-permute-start | bytes 786440 | tf_op jit(solution)/shard_map/ppermute | solution.py:657
  42.0 15.1 %collective-permute-start.6 = (bf16[512,256]{1,0:T(8,128)(2,1)}, bf16[512,256]{1,0:T(8,128)(2,1)}, u32[]{:S(2)}, u32[]{:S(2)}) collective-permute-start(bf16[512,256]{1,0:T(8,128)(2,1)} %get-tuple-element.137.refs_1_), channel_id=1, source_target_pairs={{0,16},{8,24},{16,0},{24,8},{1,17},{9,25},{17,1},{25,9},{2,18},{10... | collective-permute-start | bytes 786440 | tf_op jit(solution)/shard_map/ppermute | solution.py:657
  66.5 73.3 %collective-permute-start.21 = (f32[2048,1792]{1,0:T(8,128)}, f32[2048,1792]{1,0:T(8,128)}, u32[]{:S(2)}, u32[]{:S(2)}) collective-permute-start(f32[2048,1792]{1,0:T(8,128)} %refs_2_.3), channel_id=1, source_target_pairs={{0,1},{1,0},{2,3},{3,2},{4,5},{5,4},{6,7},{7,6},{8,9},{9,8},{10,11... | collective-permute-start | bytes 44040200 | tf_op jit(solution)/shard_map/ppermute | solution.py:594
  66.5 16.1 %collective-permute-start.16 = (bf16[512,256]{1,0:T(8,128)(2,1)S(1)}, bf16[512,256]{1,0:T(8,128)(2,1)S(1)}, u32[]{:S(2)}, u32[]{:S(2)}) collective-permute-start(bf16[512,256]{1,0:T(8,128)(2,1)S(1)} %get-tuple-element.142.refs_1_), channel_id=1, source_target_pairs={{0,8},{8,0},{16,24},{24,16},{1,9},{9,1},{17,25},{25,17},{2,10},{10... | collective-permute-start | bytes 786440 | tf_op jit(solution)/shard_map/ppermute | solution.py:657
  67.0 15.8 %collective-permute-start.15 = (bf16[512,256]{1,0:T(8,128)(2,1)S(1)}, bf16[512,256]{1,0:T(8,128)(2,1)S(1)}, u32[]{:S(2)}, u32[]{:S(2)}) collective-permute-start(bf16[512,256]{1,0:T(8,128)(2,1)S(1)} %get-tuple-element.143.refs_1_), channel_id=1, source_target_pairs={{0,16},{8,24},{16,0},{24,8},{1,17},{9,25},{17,1},{25,9},{2,18},{10... | collective-permute-start | bytes 786440 | tf_op jit(solution)/shard_map/ppermute | solution.py:657
  67.3 15.3 %collective-permute-start.11 = (bf16[512,256]{1,0:T(8,128)(2,1)S(1)}, bf16[512,256]{1,0:T(8,128)(2,1)S(1)}, u32[]{:S(2)}, u32[]{:S(2)}) collective-permute-start(bf16[512,256]{1,0:T(8,128)(2,1)S(1)} %collective-permute-done.1), channel_id=1, source_target_pairs={{0,4},{4,0},{1,5},{5,1},{2,6},{6,2},{3,7},{7,3},{8,12},{12,8},{9,1... | collective-permute-start | bytes 786440 | tf_op jit(solution)/shard_map/ppermute | solution.py:641
  84.3 31.6 %collective-permute-start.14 = (bf16[512,256]{1,0:T(8,128)(2,1)S(1)}, bf16[512,256]{1,0:T(8,128)(2,1)S(1)}, u32[]{:S(2)}, u32[]{:S(2)}) collective-permute-start(bf16[512,256]{1,0:T(8,128)(2,1)S(1)} %get-tuple-element.147.refs_1_.refs_7_), channel_id=1, source_target_pairs={{0,8},{8,0},{16,24},{24,16},{1,9},{9,1},{17,25},{25,17},{2,10},{10... | collective-permute-start | bytes 786440 | tf_op jit(solution)/shard_map/ppermute | solution.py:657
  85.8 34.6 %collective-permute-start.20 = (bf16[512,256]{1,0:T(8,128)(2,1)S(1)}, bf16[512,256]{1,0:T(8,128)(2,1)S(1)}, u32[]{:S(2)}, u32[]{:S(2)}) collective-permute-start(bf16[512,256]{1,0:T(8,128)(2,1)S(1)} %get-tuple-element.150.refs_1_.refs_6_), channel_id=1, source_target_pairs={{0,16},{8,24},{16,0},{24,8},{1,17},{9,25},{17,1},{25,9},{2,18},{10... | collective-permute-start | bytes 786440 | tf_op jit(solution)/shard_map/ppermute | solution.py:657
  88.4 32.7 %collective-permute-start.19 = (bf16[512,128]{1,0:T(8,128)(2,1)S(1)}, bf16[512,128]{1,0:T(8,128)(2,1)S(1)}, u32[]{:S(2)}, u32[]{:S(2)}) collective-permute-start(bf16[512,128]{1,0:T(8,128)(2,1)S(1)} %get-tuple-element.145.refs_1_), channel_id=1, source_target_pairs={{0,4},{4,0},{1,5},{5,1},{2,6},{6,2},{3,7},{7,3},{8,12},{12,8},{9,1... | collective-permute-start | bytes 393224 | tf_op jit(solution)/shard_map/ppermute | solution.py:641
  115.9 21.4 %collective-permute-start.18 = (bf16[512,256]{1,0:T(8,128)(2,1)S(1)}, bf16[512,256]{1,0:T(8,128)(2,1)S(1)}, u32[]{:S(2)}, u32[]{:S(2)}) collective-permute-start(bf16[512,256]{1,0:T(8,128)(2,1)S(1)} %get-tuple-element.153.refs_1_.refs_6_), channel_id=1, source_target_pairs={{0,16},{8,24},{16,0},{24,8},{1,17},{9,25},{17,1},{25,9},{2,18},{10... | collective-permute-start | bytes 786440 | tf_op jit(solution)/shard_map/ppermute | solution.py:657
  118.9 19.9 %collective-permute-start.22 = (bf16[512,128]{1,0:T(8,128)(2,1)S(1)}, bf16[512,128]{1,0:T(8,128)(2,1)S(1)}, u32[]{:S(2)}, u32[]{:S(2)}) collective-permute-start(bf16[512,128]{1,0:T(8,128)(2,1)S(1)} %get-tuple-element.158), channel_id=1, source_target_pairs={{0,4},{4,0},{1,5},{5,1},{2,6},{6,2},{3,7},{7,3},{8,12},{12,8},{9,1... | collective-permute-start | bytes 393224 | tf_op jit(solution)/shard_map/ppermute | solution.py:641
  120.5 19.4 %collective-permute-start.24 = (bf16[512,256]{1,0:T(8,128)(2,1)S(1)}, bf16[512,256]{1,0:T(8,128)(2,1)S(1)}, u32[]{:S(2)}, u32[]{:S(2)}) collective-permute-start(bf16[512,256]{1,0:T(8,128)(2,1)S(1)} %hop.50.refs_1_.refs_5_.refs_0_), channel_id=1, source_target_pairs={{0,4},{4,0},{1,5},{5,1},{2,6},{6,2},{3,7},{7,3},{8,12},{12,8},{9,1... | collective-permute-start | bytes 786440 | tf_op jit(solution)/shard_map/ppermute | solution.py:669
  121.1 18.3 %collective-permute-start.25 = (bf16[512,128]{1,0:T(8,128)(2,1)S(1)}, bf16[512,128]{1,0:T(8,128)(2,1)S(1)}, u32[]{:S(2)}, u32[]{:S(2)}) collective-permute-start(bf16[512,128]{1,0:T(8,128)(2,1)S(1)} %get-tuple-element.155.refs_4_), channel_id=1, source_target_pairs={{0,8},{8,0},{16,24},{24,16},{1,9},{9,1},{17,25},{25,17},{2,10},{10... | collective-permute-start | bytes 393224 | tf_op jit(solution)/shard_map/ppermute | solution.py:657
  137.4 22.0 %collective-permute-start.27 = (bf16[512,256]{1,0:T(8,128)(2,1)S(1)}, bf16[512,256]{1,0:T(8,128)(2,1)S(1)}, u32[]{:S(2)}, u32[]{:S(2)}) collective-permute-start(bf16[512,256]{1,0:T(8,128)(2,1)S(1)} %hop.52.refs_1_.refs_6_.refs_0_), channel_id=1, source_target_pairs={{0,4},{4,0},{1,5},{5,1},{2,6},{6,2},{3,7},{7,3},{8,12},{12,8},{9,1... | collective-permute-start | bytes 786440 | tf_op jit(solution)/shard_map/ppermute | solution.py:669
  138.9 16.0 %collective-permute-start.23 = (bf16[512,128]{1,0:T(8,128)(2,1)S(1)}, bf16[512,128]{1,0:T(8,128)(2,1)S(1)}, u32[]{:S(2)}, u32[]{:S(2)}) collective-permute-start(bf16[512,128]{1,0:T(8,128)(2,1)S(1)} %get-tuple-element.160.refs_1_.refs_5_), channel_id=1, source_target_pairs={{0,8},{8,0},{16,24},{24,16},{1,9},{9,1},{17,25},{25,17},{2,10},{10... | collective-permute-start | bytes 393224 | tf_op jit(solution)/shard_map/ppermute | solution.py:657
  139.5 18.4 %collective-permute-start.28 = (bf16[512,128]{1,0:T(8,128)(2,1)S(1)}, bf16[512,128]{1,0:T(8,128)(2,1)S(1)}, u32[]{:S(2)}, u32[]{:S(2)}) collective-permute-start(bf16[512,128]{1,0:T(8,128)(2,1)S(1)} %get-tuple-element.162.refs_4_), channel_id=1, source_target_pairs={{0,16},{8,24},{16,0},{24,8},{1,17},{9,25},{17,1},{25,9},{2,18},{10... | collective-permute-start | bytes 393224 | tf_op jit(solution)/shard_map/ppermute | solution.py:657
  154.6 29.6 %collective-permute-start.29 = (bf16[512,128]{1,0:T(8,128)(2,1)S(1)}, bf16[512,128]{1,0:T(8,128)(2,1)S(1)}, u32[]{:S(2)}, u32[]{:S(2)}) collective-permute-start(bf16[512,128]{1,0:T(8,128)(2,1)S(1)} %get-tuple-element.163.refs_1_), channel_id=1, source_target_pairs={{0,4},{4,0},{1,5},{5,1},{2,6},{6,2},{3,7},{7,3},{8,12},{12,8},{9,1... | collective-permute-start | bytes 393224 | tf_op jit(solution)/shard_map/ppermute | solution.py:641
  154.9 30.9 %collective-permute-start.26 = (bf16[512,128]{1,0:T(8,128)(2,1)S(1)}, bf16[512,128]{1,0:T(8,128)(2,1)S(1)}, u32[]{:S(2)}, u32[]{:S(2)}) collective-permute-start(bf16[512,128]{1,0:T(8,128)(2,1)S(1)} %get-tuple-element.165.refs_1_.refs_6_), channel_id=1, source_target_pairs={{0,16},{8,24},{16,0},{24,8},{1,17},{9,25},{17,1},{25,9},{2,18},{10... | collective-permute-start | bytes 393224 | tf_op jit(solution)/shard_map/ppermute | solution.py:657
  157.9 45.4 %collective-permute-start.32 = (bf16[512,128]{1,0:T(8,128)(2,1)S(1)}, bf16[512,128]{1,0:T(8,128)(2,1)S(1)}, u32[]{:S(2)}, u32[]{:S(2)}) collective-permute-start(bf16[512,128]{1,0:T(8,128)(2,1)S(1)} %hop.56.refs_5_.refs_0_), channel_id=1, source_target_pairs={{0,4},{4,0},{1,5},{5,1},{2,6},{6,2},{3,7},{7,3},{8,12},{12,8},{9,1... | collective-permute-start | bytes 393224 | tf_op jit(solution)/shard_map/ppermute | solution.py:669
  183.6 18.7 %collective-permute-start.30 = (bf16[512,128]{1,0:T(8,128)(2,1)S(1)}, bf16[512,128]{1,0:T(8,128)(2,1)S(1)}, u32[]{:S(2)}, u32[]{:S(2)}) collective-permute-start(bf16[512,128]{1,0:T(8,128)(2,1)S(1)} %get-tuple-element.170), channel_id=1, source_target_pairs={{0,4},{4,0},{1,5},{5,1},{2,6},{6,2},{3,7},{7,3},{8,12},{12,8},{9,1... | collective-permute-start | bytes 393224 | tf_op jit(solution)/shard_map/ppermute | solution.py:641
  184.2 18.6 %collective-permute-start.33 = (bf16[512,128]{1,0:T(8,128)(2,1)S(1)}, bf16[512,128]{1,0:T(8,128)(2,1)S(1)}, u32[]{:S(2)}, u32[]{:S(2)}) collective-permute-start(bf16[512,128]{1,0:T(8,128)(2,1)S(1)} %get-tuple-element.168.refs_1_.refs_5_), channel_id=1, source_target_pairs={{0,8},{8,0},{16,24},{24,16},{1,9},{9,1},{17,25},{25,17},{2,10},{10... | collective-permute-start | bytes 393224 | tf_op jit(solution)/shard_map/ppermute | solution.py:657
  185.9 26.0 %collective-permute-start.35 = (bf16[512,128]{1,0:T(8,128)(2,1)S(1)}, bf16[512,128]{1,0:T(8,128)(2,1)S(1)}, u32[]{:S(2)}, u32[]{:S(2)}) collective-permute-start(bf16[512,128]{1,0:T(8,128)(2,1)S(1)} %hop.58.refs_4_.refs_1_.refs_0_), channel_id=1, source_target_pairs={{0,4},{4,0},{1,5},{5,1},{2,6},{6,2},{3,7},{7,3},{8,12},{12,8},{9,1... | collective-permute-start | bytes 393224 | tf_op jit(solution)/shard_map/ppermute | solution.py:669
  224.6 14.9 %collective-permute-start.37 = (bf16[512,128]{1,0:T(8,128)(2,1)S(1)}, bf16[512,128]{1,0:T(8,128)(2,1)S(1)}, u32[]{:S(2)}, u32[]{:S(2)}) collective-permute-start(bf16[512,128]{1,0:T(8,128)(2,1)S(1)} %hop.63.refs_3_.refs_0_), channel_id=1, source_target_pairs={{0,4},{4,0},{1,5},{5,1},{2,6},{6,2},{3,7},{7,3},{8,12},{12,8},{9,1... | collective-permute-start | bytes 393224 | tf_op jit(solution)/shard_map/ppermute | solution.py:669
  307.5 18.4 %collective-permute-start.48 = (bf16[512,128]{1,0:T(8,128)(2,1)S(1)}, bf16[512,128]{1,0:T(8,128)(2,1)S(1)}, u32[]{:S(2)}, u32[]{:S(2)}) collective-permute-start(bf16[512,128]{1,0:T(8,128)(2,1)S(1)} %image.9.refs_1_), channel_id=1, source_target_pairs={{0,4},{4,0},{1,5},{5,1},{2,6},{6,2},{3,7},{7,3},{8,12},{12,8},{9,1... | collective-permute-start | bytes 393224 | tf_op jit(solution)/shard_map/ppermute | solution.py:641
  308.0 19.7 %collective-permute-start.47 = (bf16[512,128]{1,0:T(8,128)(2,1)S(1)}, bf16[512,128]{1,0:T(8,128)(2,1)S(1)}, u32[]{:S(2)}, u32[]{:S(2)}) collective-permute-start(bf16[512,128]{1,0:T(8,128)(2,1)S(1)} %get-tuple-element.202.refs_1_), channel_id=1, source_target_pairs={{0,16},{8,24},{16,0},{24,8},{1,17},{9,25},{17,1},{25,9},{2,18},{10... | collective-permute-start | bytes 393224 | tf_op jit(solution)/shard_map/ppermute | solution.py:657
  403.5 51.3 %all-to-all-start = ((bf16[8,256,256]{2,1,0:T(8,128)(2,1)}), bf16[8,256,256]{2,1,0:T(8,128)(2,1)}, u32[]{:S(2)}, u32[]{:S(2)}) async-start(bf16[8,256,256]{2,1,0:T(8,128)(2,1)} %broadcast_in_dim.2.refs_3_), calls=%async_computation | async-start | bytes 2097152 | tf_op jit(solution)/shard_map/all_to_all | solution.py:764
  453.1 18.4 %collective-permute-start.71 = (bf16[896,256]{1,0:T(8,128)(2,1)S(1)}, bf16[896,256]{1,0:T(8,128)(2,1)}, u32[]{:S(2)}, u32[]{:S(2)}) collective-permute-start(bf16[896,256]{1,0:T(8,128)(2,1)S(1)} %hop.77.refs_1_), channel_id=1, source_target_pairs={{0,8},{8,0},{16,24},{24,16},{1,9},{9,1},{17,25},{25,17},{2,10},{10... | collective-permute-start | bytes 1376264 | tf_op jit(solution)/shard_map/ppermute | solution.py:657
  454.8 28.9 %all-to-all-start.1 = ((bf16[4,512,256]{2,1,0:T(8,128)(2,1)}), bf16[4,512,256]{2,1,0:T(8,128)(2,1)}, u32[]{:S(2)}, u32[]{:S(2)}) async-start(bf16[4,512,256]{2,1,0:T(8,128)(2,1)} %bitcast.4), calls=%async_computation.1 | async-start | bytes 2097152 | tf_op jit(solution)/shard_map/all_to_all | solution.py:767
  491.7 19.2 %all-to-all-start.2 = ((bf16[4,128,256]{1,2,0:T(8,128)(2,1)}), bf16[4,128,256]{1,2,0:T(8,128)(2,1)}, u32[]{:S(2)}, u32[]{:S(2)}) async-start(bf16[4,128,256]{1,2,0:T(8,128)(2,1)} %bitcast.22), calls=%async_computation.2 | async-start | bytes 524288 | tf_op jit(solution)/shard_map/all_to_all | solution.py:704
  (62 other events, 1043.8 us)
